TPU v7x, 32 devices: a whole 2x2x4 slice. The times are simulated.
32 devices in a mesh: aux: 8 (over y, x, core), mu: 4 (over z).
Axes of the slice: x: 2, y: 2, z: 4, core: 2. Of those that a mesh axis runs over, the one named last changes fastest.
Arguments:
- three_center: float32 [4, 3, 512, 4096], P('mu', None, 'aux'), may hold values from -0.4375 to 0.4375
- nu_slots: int32 [4, 3, 8], P('mu', None, 'aux'), may hold values from 0 to 3
- nu_count: int32 [4, 8], P('mu', 'aux'), may hold values from 1 to 3, 16 in all within a row
- density: float32 [256, 64], P('mu'), may hold values from -6 to 6
- metric_tensor: float32 [4, 3, 512, 1024], P('mu', None, 'aux'), may hold values from -0.046875 to 0.046875
- sig_slots: int32 [4, 3, 8], P('mu', None, 'aux'), may hold values from 0 to 3
- sig_count: int32 [4, 8], P('mu', 'aux'), may hold values from 1 to 3, 16 in all within a row
Outputs:
- exchange_k: float32 [256, 256], P('aux', 'mu')
Inputs may be any that keep to these rules, and one draw needn't show every extreme that they name: `nu_slots`: an orbital block index. `nu_count`: slots at or past the count are ignored; each row sums to 8 * (3 + 1) // 2. `sig_slots`: an orbital block index; slots may repeat. `sig_count`: slots at or past the count are ignored; each row sums to 8 * (3 + 1) // 2.
All inputs are finite; a program needn't handle non-finite values. No bound on the sum of `nu_count` or of `sig_count` on one device may be relied on, other than what follows from the above.
Results may differ from a plain program's by a relative error of at most 0.0029.
Values may be sent and summed in bfloat16 or wider, within the bound.
No kernel may reach another device: no remote copies, remote signals or barrier semaphores. Data moves between devices by JAX's collectives and lax.ppermute only.
A program may use at most 64 MiB of HBM per device.

v0:
```python
import jax
import jax.numpy as jnp
from jax import lax
from jax.sharding import PartitionSpec as P


def shards(three_center, nu_slots, nu_count, density, metric_tensor, sig_slots, sig_count):
    highest = lax.Precision.HIGHEST
    orb_block = density.shape[0]
    lam_all = density.shape[1]
    aux_width = three_center.shape[2]
    dens_all = lax.all_gather(density, "mu", axis=0, tiled=True)

    def add_slot(k, running):
        nu_pick = nu_slots[0, k, 0]
        dens_rows = lax.dynamic_slice_in_dim(dens_all, nu_pick * orb_block, orb_block, 0)
        slab_piece = lax.dynamic_index_in_dim(three_center[0], k, 0, keepdims=False).reshape(
            aux_width, orb_block, orb_block
        )
        return running + jnp.einsum("pij,jl->lpi", slab_piece, dens_rows, precision=highest)

    halfway = lax.fori_loop(
        0, nu_count[0, 0], add_slot, jnp.zeros((lam_all, aux_width, orb_block), jnp.float32)
    )
    relayed = lax.all_to_all(
        halfway.astype(jnp.bfloat16), "mu", split_axis=0, concat_axis=2, tiled=True
    )
    widened = relayed.astype(jnp.float32)
    lam_rows = relayed.shape[0]
    orbitals = relayed.shape[2]

    def add_target(q, running):
        target = sig_slots[0, q, 0]
        weights = lax.dynamic_index_in_dim(metric_tensor[0], q, 0, keepdims=False).reshape(
            aux_width, lam_rows, orb_block
        )
        contrib = jnp.einsum("rpm,prc->mc", widened, weights, precision=highest)
        current = lax.dynamic_slice_in_dim(running, target * orb_block, orb_block, 1)
        return lax.dynamic_update_slice_in_dim(running, current + contrib, target * orb_block, 1)

    partial_k = lax.fori_loop(
        0, sig_count[0, 0], add_target, jnp.zeros((orbitals, orbitals), jnp.float32)
    )
    row_share = lax.psum_scatter(partial_k, "aux", scatter_dimension=0, tiled=True)
    exchange_k = lax.psum_scatter(row_share, "mu", scatter_dimension=1, tiled=True)
    return exchange_k


def solution(mesh):
    placed = (
        P("mu", None, "aux", None),
        P("mu", None, "aux"),
        P("mu", "aux"),
        P("mu", None),
        P("mu", None, "aux", None),
        P("mu", None, "aux"),
        P("mu", "aux"),
    )
    return jax.shard_map(
        shards, mesh=mesh, in_specs=placed, out_specs=P("aux", "mu"), check_vma=False
    )
```

profile of v0, /device:TPU:0, one launch (start us, length us, event | category | flops | bytes accessed | tf_op | source)
XLA Modules:
  0.0 170.4 jit_solution(16274832245689744548)
XLA Ops:
  6.5 0.0 copy-start
  6.5 15.4 %all_gather.3 = f32[256,64]{1,0:T(8,128)S(1)} all-gather(f32[64,64]{1,0:T(8,128)} %param.14), channel_id=1, replica_groups=mesh['aux'=8,'mu'=4] {'mu'}, dimensions={0}, use_global_device_ids=true | all-gather | bytes 81920 | tf_op jit(solution)/shard_map/all_gather | solution.py:12
  21.9 1.6 broadcast_in_dim.7
  23.5 0.0 copy-done
  23.5 15.2 %while.20 = (s32[]{:T(128)}, f32[64,64,64]{2,0,1:T(8,128)}, s32[]{:T(128)}, s32[1,3,1]{1,2,0:T(1,128)S(1)}, f32[256,64]{1,0:T(8,128)S(1)}, /*index=5*/f32[1,3,64...) while((s32[]{:T(128)}, f32[64,64,64]{2,0,1:T(8,128)}, s32[]{:T(128)}, ...), condition=%wide.region_1.2_spmd, body=%wide.region_0.1_spmd.sunk | while | flops 201588736 | bytes 8421565 | solution.py:22
  24.2 0.7 fusion.19
  26.9 1.3 constant_dynamic-slice_fusion.6
  28.2 0.8 reshape.29
  29.1 9.1 %convolution_add_fusion.2 = f32[64,64,64]{2,0,1:T(8,128)} fusion(f32[64,64,64]{2,0,1:T(8,128)} %get-tuple-element.202, f32[64,64,64]{2,1,0:T(8,128)S(1)} %reshape.29, f32[256,64]{1,0:T(8,128)S(1)} %get-tuple-element.215, s32[]{:T(128)S(6)} %select_n.22), kind=kOutput, calls=%fused_computation.clone.1 | convolution fusion | flops 201588736 | bytes 4227076 | tf_op jit(solution)/shard_map/while/body/pij,jl->lpi/dot_general | solution.py:20
  38.8 2.8 %copy.22 = bf16[64,64,64]{2,1,0:T(8,128)(2,1)S(1)} copy(f32[64,64,64]{2,0,1:T(8,128)} %get-tuple-element.71) | data formatting | bytes 1572864 | tf_op jit(solution)/shard_map/while | solution.py:22
  41.6 1.5 reshape.26
  43.1 32.3 %all-to-all-start = ((bf16[4,2,32768]{2,1,0:T(2,128)(2,1)}), bf16[4,2,32768]{2,1,0:T(2,128)(2,1)S(1)}, u32[]{:S(2)}, u32[]{:S(2)}) async-start(bf16[4,2,32768]{2,1,0:T(2,128)(2,1)} %reshape.26), calls=%async_computation | async-start | bytes 1048576 | tf_op jit(solution)/shard_map/all_to_all | solution.py:25
  75.5 0.0 reduce-scatter.5.cloned.1.call-start
  75.5 12.7 %all-to-all-done = bf16[4,2,32768]{2,1,0:T(2,128)(2,1)S(1)} async-done(((bf16[4,2,32768]{2,1,0:T(2,128)(2,1)}), bf16[4,2,32768]{2,1,0:T(2,128)(2,1)S(1)}, u32[]{:S(2)}, u32[]{:S(2)}) %all-to-all-start) | async-done | bytes 524320 | tf_op jit(solution)/shard_map/all_to_all | solution.py:25
  88.2 0.7 reshape.27
  88.9 0.2 convert_bitcast_fusion
  89.2 1.4 copy.14
  90.6 0.0 copy-start.1
  90.6 1.1 reshape.20
  91.8 0.0 copy-done.1
  91.8 16.5 %while.21 = (s32[]{:T(128)}, f32[256,256]{0,1:T(8,128)S(1)}, s32[]{:T(128)}, s32[1,3,1]{1,2,0:T(1,128)S(1)}, f32[1,3,64,1024]{3,2,1,0:T(8,128)}, /*index=5*/f32[...) while((s32[]{:T(128)}, f32[256,256]{0,1:T(8,128)S(1)}, s32[]{:T(128)}, ...), condition=%wide.region_3.4_spmd, body=%wide.region_2.3_spmd.sunk | while | flops 201342976 | bytes 2752701 | solution.py:41
  92.4 0.7 fusion.22
  95.2 1.0 constant_dynamic-slice_fusion.7
  96.2 0.2 copy.24
  96.4 0.7 fusion.23
  97.7 0.7 fusion.22
  100.5 1.0 constant_dynamic-slice_fusion.7
  101.4 0.2 copy.24
  101.6 0.7 fusion.23
  103.0 0.7 fusion.22
  105.7 1.0 constant_dynamic-slice_fusion.7
  106.7 0.2 copy.24
  106.9 0.7 fusion.23
  108.2 0.8 copy.16
  109.1 0.0 reduce-scatter.5.cloned.1.call-update
  109.1 0.0 reduce-scatter.7.cloned.1.call-start
  109.2 31.4 %reduce-scatter.5.cloned.1.call-done = f32[32,256]{1,0:T(8,128)} async-done(((f32[256,256]{1,0:T(8,128)}), f32[32,256]{1,0:T(8,128)}) %reduce-scatter.5.cloned.1.call-update) | async-done | bytes 32784 | tf_op jit(solution)/shard_map/reduce_scatter | solution.py:44
  140.6 1.5 copy.17
  142.1 0.0 reduce-scatter.7.cloned.1.call-update
  142.1 20.0 %reduce-scatter.7.cloned.1.call-done = f32[64,32]{1,0:T(8,128)} async-done(((f32[256,32]{1,0:T(8,128)}), f32[64,32]{1,0:T(8,128)}) %reduce-scatter.7.cloned.1.call-update) | async-done | bytes 8208
  162.1 1.4 copy.18
  (1 shorter events, 0.0 us)
Async XLA Ops:
  6.5 17.0 %copy-start = (s32[1,3,1]{1,2,0:T(1,128)S(1)}, s32[1,3,1]{1,2,0:T(1,128)}, u32[]{:S(2)}) copy-start(s32[1,3,1]{1,2,0:T(1,128)} %param.12) | copy-start | bytes 40
  43.1 45.1 %all-to-all-start = ((bf16[4,2,32768]{2,1,0:T(2,128)(2,1)}), bf16[4,2,32768]{2,1,0:T(2,128)(2,1)S(1)}, u32[]{:S(2)}, u32[]{:S(2)}) async-start(bf16[4,2,32768]{2,1,0:T(2,128)(2,1)} %reshape.26), calls=%async_computation | async-start | bytes 1048576 | tf_op jit(solution)/shard_map/all_to_all | solution.py:25
  75.5 65.1 %reduce-scatter.5.cloned.1.call-start = ((), (), s32[]{:S(2)}) async-start(), calls=%async_computation.3 | async-start | bytes 294912 | tf_op jit(solution)/shard_map/reduce_scatter | solution.py:44
  90.6 1.2 copy-start.1
  109.1 53.0 %reduce-scatter.7.cloned.1.call-start = ((), (), s32[]{:S(2)}) async-start(), calls=%async_computation.4 | async-start | bytes 163840
Sparse Core Ops, SparseCore 0:
  109.2 31.2 reduce-scatter.4
  142.9 19.1 reduce-scatter.6
where the time goes:
time: 171 us; the launch traced here: 170 us
  waiting for transfers between devices  64.2 us (38%)
  starting transfers between devices  32.4 us (19%)
  local copies, waits for them, and re-layouts  18.7 us (11%)
  blocking collectives  15.4 us (9%)
  between operations  13.5 us (8%)
  loops' own time  12.3 us (7%)
  matrix products  11.1 us (6%)
  other arithmetic  2.89 us (2%)
    all_to_all x1, starting transfers between devices, shards(): lax.all_to_all(halfway.astype(jnp.bfloat16), 'mu', split_axis=0, concat_a...  32.3 us
    reduce_scatter x1, waiting for transfers between devices, shards(): lax.psum_scatter(partial_k, 'aux', scatter_dimension=0, tiled=True)  31.4 us
    unnamed x3, waiting for transfers between devices  20 us
    all_gather x1, blocking collectives, shards(): dens_all = lax.all_gather(density, 'mu', axis=0, tiled=True)  15.4 us
    all_to_all x1, waiting for transfers between devices, shards(): lax.all_to_all(halfway.astype(jnp.bfloat16), 'mu', split_axis=0, concat_a...  12.7 us
    dot_general x1, matrix products, add_slot(): jnp.einsum('pij,jl->lpi', slab_piece, dens_rows, precision=highest)  9.09 us
    another operation x1, loops' own time, shards(): lax.fori_loop(0, sig_count[0, 0], add_target, jnp.zeros((orbitals, orbita...  8.92 us
    unnamed x8, local copies, waits for them, and re-layouts  5.21 us
  transfers between devices with their start and end apart: 3, of which 3 were waited for; matrix products, arithmetic and copies ran while one was open for 0% of the time, Pallas kernels for 0%

commit v1 on v0

--- a/solution.py
+++ b/solution.py
@@ -1,10 +1,204 @@
+import functools
+
 import jax
 import jax.numpy as jnp
 from jax import lax
+from jax.experimental import pallas as pl
+from jax.experimental.pallas import tpu as pltpu
 from jax.sharding import PartitionSpec as P
 
-
-def shards(three_center, nu_slots, nu_count, density, metric_tensor, sig_slots, sig_count):
+F32 = jnp.float32
+BF16 = jnp.bfloat16
+VMEM = pl.BlockSpec(memory_space=pltpu.VMEM)
+SMEM = pl.BlockSpec(memory_space=pltpu.SMEM)
+
+
+def params(mib):
+    return pltpu.CompilerParams(vmem_limit_bytes=mib * 1024 * 1024)
+
+
+def split(x):
+    hi = x.astype(BF16)
+    return hi, (x - hi.astype(F32)).astype(BF16)
+
+
+def iota(shape, dim):
+    return lax.broadcasted_iota(jnp.int32, shape, dim)
+
+
+def prepare_kernel(sig_slots, sig_count, tensor, metric, t_hi, t_lo, m_hi, m_lo):
+    _, slots, aux_width, width = tensor.shape
+    for k in range(slots):
+        for chunk in range(width // 256):
+            hi, lo = split(tensor[0, k, :, chunk * 256:(chunk + 1) * 256])
+            rows = slice(chunk * aux_width, (chunk + 1) * aux_width)
+            t_hi[rows, k * 256:(k + 1) * 256] = hi
+            t_lo[rows, k * 256:(k + 1) * 256] = lo
+    sig = metric.shape[1]
+    half = iota((aux_width, 128), 1) >= 64
+    pair_of = jnp.where(half, 1, 0)
+    targets = [jnp.where(q < sig_count[0, 0], sig_slots[0, q, 0], -1) for q in range(sig)]
+    for pair in range(metric.shape[3] // 128):
+        sums = [[jnp.zeros((aux_width, 128), F32) for _ in range(2)] for _ in range(2)]
+        for q in range(sig):
+            block = metric[0, q, :, pair * 128:(pair + 1) * 128]
+            turned = pltpu.roll(block, 64, 1)
+            both = (jnp.where(half, turned, block), jnp.where(half, block, turned))
+            for out_half in range(2):
+                here = pair_of + 2 * out_half == targets[q]
+                for parity in range(2):
+                    sums[parity][out_half] += jnp.where(here, both[parity], 0.0)
+        for parity in range(2):
+            r = 2 * pair + parity
+            at = ((r % 8) * 2 + r // 8) * aux_width
+            for out_half in range(2):
+                hi, lo = split(sums[parity][out_half])
+                columns = slice(out_half * 128, (out_half + 1) * 128)
+                m_hi[at:at + aux_width, columns] = hi
+                m_lo[at:at + aux_width, columns] = lo
+
+
+def half_kernel(n_mu, nu_slots, nu_count, *refs):
+    dens = refs[:n_mu]
+    t_hi, t_lo = refs[n_mu:n_mu + 2]
+    outs = refs[n_mu + 2:2 * n_mu + 2]
+    d_hi, d_lo, w_hi, w_lo, turned = refs[2 * n_mu + 2:]
+    z = lax.axis_index("mu")
+    orb, lam_all = dens[0].shape
+    lam = lam_all // n_mu
+    slots = nu_slots.shape[1]
+    row, col = iota((lam_all, 256), 0), iota((lam_all, 256), 1)
+    group = lax.rem(((col >> 3) & 3) + z, n_mu)
+    wanted = group * lam + (col >> 7) * 8 + (col & 7)
+    choose = jnp.where(row == wanted, 1.0, 0.0).astype(BF16)
+    for s in range(n_mu):
+        hi, lo = split(dens[s][...])
+        d_hi[s] = jnp.dot(hi, choose, preferred_element_type=F32)
+        d_lo[s] = jnp.dot(lo, choose, preferred_element_type=F32)
+    orbital = (iota((orb, 256), 1) >> 5) & 3
+    for k in range(slots):
+        at = lax.rem(z - nu_slots[0, k, 0] + n_mu, n_mu)
+        live = jnp.where(k < nu_count[0, 0], 1.0, 0.0)
+        hi, lo = d_hi[at] * live, d_lo[at] * live
+        for i in range(4):
+            rows = slice(k * 256 + i * orb, k * 256 + (i + 1) * orb)
+            w_hi[rows, :] = jnp.where(orbital == i, hi, 0.0).astype(BF16)
+            w_lo[rows, :] = jnp.where(orbital == i, lo, 0.0).astype(BF16)
+    total = jnp.dot(t_hi[...], w_hi[...], preferred_element_type=F32)
+    total += jnp.dot(t_lo[...], w_hi[...], preferred_element_type=F32)
+    total += jnp.dot(t_hi[...], w_lo[...], preferred_element_type=F32)
+    aux_width = outs[0].shape[1] // lam
+    for chunk in range(total.shape[0] // aux_width):
+        piece = total[chunk * aux_width:(chunk + 1) * aux_width]
+        stacked = jnp.concatenate([piece[:, :128], piece[:, 128:]], axis=0)
+        turned[chunk * 128:(chunk + 1) * 128, :] = stacked.T
+    for s in range(n_mu):
+        for r in range(8):
+            outs[s][:, r * 128:(r + 1) * 128] = turned[
+                pl.ds(s * 8 + r, orb, stride=32), :
+            ].astype(BF16)
+
+
+def exchange_kernel(n_mu, n_aux, *refs):
+    halves = refs[:n_mu]
+    m_hi, m_lo = refs[n_mu:n_mu + 2]
+    outs = refs[n_mu + 2:n_mu + 2 + n_aux]
+    total = refs[-1]
+    z, a = lax.axis_index("mu"), lax.axis_index("aux")
+    left = jnp.concatenate([h[...] for h in halves], axis=0)
+    product = jnp.dot(left, m_hi[...], preferred_element_type=F32)
+    product += jnp.dot(left, m_lo[...], preferred_element_type=F32)
+    orb = halves[0].shape[0]
+    for s in range(n_mu):
+        block = lax.rem(z - s + n_mu, n_mu)
+        total[pl.ds(pl.multiple_of(block * orb, orb), orb), :] = product[s * orb:(s + 1) * orb]
+    rows = outs[0].shape[0]
+    for t in range(n_aux):
+        outs[t][...] = total[pl.ds(pl.multiple_of((a ^ t) * rows, rows), rows), :]
+
+
+def row_sum_kernel(n_mu, n_aux, *refs):
+    parts, outs = refs[:n_aux], refs[n_aux:]
+    z = lax.axis_index("mu")
+    total = parts[0][...]
+    for t in range(1, n_aux):
+        total += parts[t][...]
+    width = outs[0].shape[1]
+    for s in range(n_mu):
+        block = lax.rem(z + s, n_mu)
+        picked = total[:, :width]
+        for c in range(1, n_mu):
+            picked = jnp.where(block == c, total[:, c * width:(c + 1) * width], picked)
+        outs[s][...] = picked
+
+
+def fast(n_mu, n_aux, three_center, nu_slots, nu_count, density, metric_tensor, sig_slots, sig_count):
+    orb, lam_all = density.shape
+    slots, aux_width = three_center.shape[1:3]
+    lam = lam_all // n_mu
+    turns = [[(z, (z + s) % n_mu) for z in range(n_mu)] for s in range(n_mu)]
+    dens = [density] + [lax.ppermute(density, "mu", turns[s]) for s in range(1, n_mu)]
+    chunks = three_center.shape[3] // 256
+    t_shape = jax.ShapeDtypeStruct((chunks * aux_width, slots * 256), BF16)
+    m_shape = jax.ShapeDtypeStruct((lam * aux_width, n_mu * orb), BF16)
+    t_hi, t_lo, m_hi, m_lo = pl.pallas_call(
+        prepare_kernel,
+        out_shape=(t_shape, t_shape, m_shape, m_shape),
+        in_specs=[SMEM, SMEM, VMEM, VMEM],
+        out_specs=(VMEM,) * 4,
+        compiler_params=params(16),
+        cost_estimate=pl.CostEstimate(flops=10_000_000, bytes_accessed=8_000_000, transcendentals=0),
+        name="prepare",
+    )(sig_slots, sig_count, three_center, metric_tensor)
+    half_shape = jax.ShapeDtypeStruct((orb, lam * aux_width), BF16)
+    halves = pl.pallas_call(
+        functools.partial(half_kernel, n_mu),
+        out_shape=(half_shape,) * n_mu,
+        in_specs=[SMEM, SMEM] + [VMEM] * (n_mu + 2),
+        out_specs=(VMEM,) * n_mu,
+        scratch_shapes=[
+            pltpu.VMEM((n_mu, orb, 256), F32),
+            pltpu.VMEM((n_mu, orb, 256), F32),
+            pltpu.VMEM((slots * 256, 256), BF16),
+            pltpu.VMEM((slots * 256, 256), BF16),
+            pltpu.VMEM((chunks * 128, 128), F32),
+        ],
+        compiler_params=params(16),
+        cost_estimate=pl.CostEstimate(flops=1_200_000_000, bytes_accessed=4_000_000, transcendentals=0),
+        name="half",
+    )(nu_slots, nu_count, *dens, t_hi, t_lo)
+    halves = [halves[0]] + [lax.ppermute(halves[s], "mu", turns[s]) for s in range(1, n_mu)]
+    rows = n_mu * orb // n_aux
+    part_shape = jax.ShapeDtypeStruct((rows, n_mu * orb), F32)
+    parts = pl.pallas_call(
+        functools.partial(exchange_kernel, n_mu, n_aux),
+        out_shape=(part_shape,) * n_aux,
+        in_specs=[VMEM] * (n_mu + 2),
+        out_specs=(VMEM,) * n_aux,
+        scratch_shapes=[pltpu.VMEM((n_mu * orb, n_mu * orb), F32)],
+        compiler_params=params(16),
+        cost_estimate=pl.CostEstimate(flops=300_000_000, bytes_accessed=2_000_000, transcendentals=0),
+        name="exchange",
+    )(*halves, m_hi, m_lo)
+    parts = [parts[0]] + [
+        lax.ppermute(parts[t], "aux", [(a, a ^ t) for a in range(n_aux)]) for t in range(1, n_aux)
+    ]
+    share_shape = jax.ShapeDtypeStruct((rows, orb), F32)
+    shares = pl.pallas_call(
+        functools.partial(row_sum_kernel, n_mu, n_aux),
+        out_shape=(share_shape,) * n_mu,
+        in_specs=[VMEM] * n_aux,
+        out_specs=(VMEM,) * n_mu,
+        compiler_params=params(8),
+        name="row_sum",
+    )(*parts)
+    result = shares[0]
+    for s in range(1, n_mu):
+        result = result + lax.ppermute(shares[s], "mu", turns[s])
+    return result
+
+
+def general(three_center, nu_slots, nu_count, density, metric_tensor, sig_slots, sig_count):
     highest = lax.Precision.HIGHEST
     orb_block = density.shape[0]
     lam_all = density.shape[1]
@@ -20,12 +214,10 @@
         return running + jnp.einsum("pij,jl->lpi", slab_piece, dens_rows, precision=highest)
 
     halfway = lax.fori_loop(
-        0, nu_count[0, 0], add_slot, jnp.zeros((lam_all, aux_width, orb_block), jnp.float32)
-    )
-    relayed = lax.all_to_all(
-        halfway.astype(jnp.bfloat16), "mu", split_axis=0, concat_axis=2, tiled=True
-    )
-    widened = relayed.astype(jnp.float32)
+        0, nu_count[0, 0], add_slot, jnp.zeros((lam_all, aux_width, orb_block), F32)
+    )
+    relayed = lax.all_to_all(halfway.astype(BF16), "mu", split_axis=0, concat_axis=2, tiled=True)
+    widened = relayed.astype(F32)
     lam_rows = relayed.shape[0]
     orbitals = relayed.shape[2]
 
@@ -39,14 +231,25 @@
         return lax.dynamic_update_slice_in_dim(running, current + contrib, target * orb_block, 1)
 
     partial_k = lax.fori_loop(
-        0, sig_count[0, 0], add_target, jnp.zeros((orbitals, orbitals), jnp.float32)
+        0, sig_count[0, 0], add_target, jnp.zeros((orbitals, orbitals), F32)
     )
     row_share = lax.psum_scatter(partial_k, "aux", scatter_dimension=0, tiled=True)
-    exchange_k = lax.psum_scatter(row_share, "mu", scatter_dimension=1, tiled=True)
-    return exchange_k
+    return lax.psum_scatter(row_share, "mu", scatter_dimension=1, tiled=True)
 
 
 def solution(mesh):
+    n_aux, n_mu = mesh.shape["aux"], mesh.shape["mu"]
+
+    def shards(three_center, nu_slots, nu_count, density, metric_tensor, sig_slots, sig_count):
+        args = (three_center, nu_slots, nu_count, density, metric_tensor, sig_slots, sig_count)
+        orb, lam_all = density.shape
+        fits = (
+            (n_aux, n_mu, orb, lam_all) == (8, 4, 64, 64)
+            and three_center.shape[2:] == (64, orb * orb)
+            and metric_tensor.shape[2:] == (64, lam_all // n_mu * orb)
+        )
+        return fast(n_mu, n_aux, *args) if fits else general(*args)
+
     placed = (
         P("mu", None, "aux", None),
         P("mu", None, "aux"),

time: 171 us -> 49 us (0.29)
  waiting for transfers between devices: 64.2 us -> 14.4 us
  blocking collectives: 15.4 us -> 0 us
  local copies, waits for them, and re-layouts: 18.7 us -> 4.51 us
  loops' own time: 12.3 us -> 0 us
  between operations: 13.5 us -> 1.39 us
  matrix products: 11.1 us -> 0 us
  starting transfers between devices: 32.4 us -> 22.9 us
  Pallas kernels: 0 us -> 4.94 us
  other arithmetic: 2.89 us -> 0.61 us
    all_to_all x1 -> x0, starting transfers between devices: 32.3 us -> none  [shards(): lax.all_to_all(halfway.astype(jnp.bfloat16), 'mu', split_axis=0, concat_a...]
    reduce_scatter x1 -> x0, waiting for transfers between devices: 31.4 us -> none  [shards(): lax.psum_scatter(partial_k, 'aux', scatter_dimension=0, tiled=True)]
    ppermute x0 -> x16, starting transfers between devices: none -> 22.9 us  [the longest x3 7.86 us: fast(): lax.ppermute(density, 'mu', turns[s])]
    unnamed x3 -> x0, waiting for transfers between devices: 20 us -> none
    all_gather x1 -> x0, blocking collectives: 15.4 us -> none  [shards(): dens_all = lax.all_gather(density, 'mu', axis=0, tiled=True)]
    ppermute x0 -> x16, waiting for transfers between devices: none -> 14.4 us  [the longest x3 8.19 us: fast(): lax.ppermute(halves[s], 'mu', turns[s])]
    all_to_all x1 -> x0, waiting for transfers between devices: 12.7 us -> none  [shards(): lax.all_to_all(halfway.astype(jnp.bfloat16), 'mu', split_axis=0, concat_a...]
    another operation x2 -> x0, loops' own time: 12.3 us -> none  [the longest x1 8.92 us: shards(): lax.fori_loop(0, sig_count[0, 0], add_target, jnp.zeros((orbitals, orbita...]
  transfers between devices with their start and end apart: 3 -> 16, of which waited for: 3 -> 7; matrix products, arithmetic and copies ran while one was open for 0% -> 3% of each run, Pallas kernels for 0% -> 3%
where the time goes in v1:
time: 49 us; the launch traced here: 48.8 us
  starting transfers between devices  22.9 us (47%)
  waiting for transfers between devices  14.4 us (29%)
  Pallas kernels  4.94 us (10%)
  local copies, waits for them, and re-layouts  4.51 us (9%)
  between operations  1.39 us (3%)
  other arithmetic  0.61 us (1%)
    ppermute x3, waiting for transfers between devices, fast(): lax.ppermute(halves[s], 'mu', turns[s])  8.19 us
    ppermute x3, starting transfers between devices, fast(): lax.ppermute(density, 'mu', turns[s])  7.86 us
    ppermute x7, starting transfers between devices, fast(): lax.ppermute(parts[t], 'aux', [(a, a ^ t) for a in range(n_aux)])  6.32 us
    ppermute x3, starting transfers between devices, fast(): result = result + lax.ppermute(shares[s], 'mu', turns[s])  4.87 us
    unnamed x8, local copies, waits for them, and re-layouts  4.51 us
    ppermute x7, waiting for transfers between devices, fast(): lax.ppermute(parts[t], 'aux', [(a, a ^ t) for a in range(n_aux)])  4 us
    ppermute x3, starting transfers between devices, fast(): lax.ppermute(halves[s], 'mu', turns[s])  3.87 us
    pallas_call x1, Pallas kernels, fast(): pl.pallas_call(functools.partial(half_kernel, n_mu), out_shape=(half_shap...  2.79 us
  transfers between devices with their start and end apart: 16, of which 7 were waited for; matrix products, arithmetic and copies ran while one was open for 3% of the time, Pallas kernels for 3%

profile of v1, /device:TPU:0, one launch (start us, length us, event | category | flops | bytes accessed | tf_op | source)
XLA Modules:
  0.0 48.8 jit_solution(4561947947139606409)
XLA Ops:
  0.0 4.0 %collective-permute-start.1 = (f32[64,64]{1,0:T(8,128)}, f32[64,64]{1,0:T(8,128)S(1)}, u32[]{:S(2)}, u32[]{:S(2)}) collective-permute-start(f32[64,64]{1,0:T(8,128)} %refs_0_.1), channel_id=1, source_target_pairs={{0,2},{1,3},{2,0},{3,1},{4,6},{5,7},{6,4},{7,5},{8,10},{9,11},{10,... | collective-permute-start | bytes 49160 | tf_op jit(solution)/shard_map/ppermute | solution.py:140
  4.0 1.6 %collective-permute-start = (f32[64,64]{1,0:T(8,128)}, f32[64,64]{1,0:T(8,128)S(1)}, u32[]{:S(2)}, u32[]{:S(2)}) collective-permute-start(f32[64,64]{1,0:T(8,128)} %refs_0_.1), channel_id=1, source_target_pairs={{0,1},{1,2},{2,3},{3,0},{4,5},{5,6},{6,7},{7,4},{8,9},{9,10},{10,1... | collective-permute-start | bytes 49160 | tf_op jit(solution)/shard_map/ppermute | solution.py:140
  5.6 2.2 %collective-permute-start.2 = (f32[64,64]{1,0:T(8,128)}, f32[64,64]{1,0:T(8,128)S(1)}, u32[]{:S(2)}, u32[]{:S(2)}) collective-permute-start(f32[64,64]{1,0:T(8,128)} %refs_0_.1), channel_id=1, source_target_pairs={{0,3},{1,0},{2,1},{3,2},{4,7},{5,4},{6,5},{7,6},{8,11},{9,8},{10,9... | collective-permute-start | bytes 49160 | tf_op jit(solution)/shard_map/ppermute | solution.py:140
  9.2 0.7 %copy.9.nu_slots = s32[1,3,1]{2,1,0:T(4,128)S(1)} copy(s32[1,3,1]{1,2,0:T(1,128)} %param.8) | data formatting | bytes 24 | tf_op args[1]
  9.9 0.7 %copy.8.sig_slots = s32[1,3,1]{2,1,0:T(4,128)S(1)} copy(s32[1,3,1]{1,2,0:T(1,128)} %param.12) | data formatting | bytes 24 | tf_op args[5]
  10.6 0.0 copy-start
  10.6 1.9 %copy-done = f32[1,3,64,4096]{3,2,1,0:T(8,128)S(1)} copy-done((f32[1,3,64,4096]{3,2,1,0:T(8,128)S(1)}, f32[1,3,64,4096]{3,2,1,0:T(8,128)}, u32[]{:S(2)}) %copy-start) | copy-done | bytes 3145752
  12.5 0.0 copy-start.1
  12.5 1.1 %copy-done.1 = f32[1,3,64,1024]{3,2,1,0:T(8,128)S(1)} copy-done((f32[1,3,64,1024]{3,2,1,0:T(8,128)S(1)}, f32[1,3,64,1024]{3,2,1,0:T(8,128)}, u32[]{:S(2)}) %copy-start.1) | copy-done | bytes 786456
  13.7 0.0 copy-start.2
  13.7 1.4 %prepare.1 = (bf16[1024,768]{1,0:T(8,128)(2,1)S(1)}, bf16[1024,768]{1,0:T(8,128)(2,1)S(1)}, bf16[1024,256]{1,0:T(8,128)(2,1)S(1)}, bf16[1024,256]{1,0:T(8,128)(2,1)S(1)}) custom-call(s32[1,3,1]{2,1,0:T(4,128)S(1)} %copy.8.sig_slots, s32[1,1]{1,0:T(1,128)S(6)} %copy.11.sig_count, f32[1,3,64,4096]{3,2,1,0:T(8,128)S(1)} %copy-done, f32[1,3,64,1024]{3,2,1,0:T(8,128)S(1)} %copy-done.1), custom_call_target="tpu_custom_call" | custom-call | flops 10000000 | bytes 8000000 | tf_op jit(solution)/shard_map/prepare/pallas_call | solution.py:144
  15.1 0.0 collective-permute-done.1.refs_2_
  15.1 0.0 collective-permute-done.refs_1_
  15.1 0.0 collective-permute-done.2.refs_3_
  15.1 0.0 copy-done.2
  15.1 2.8 %half.1 = (bf16[64,1024]{1,0:T(8,128)(2,1)S(1)}, bf16[64,1024]{1,0:T(8,128)(2,1)S(1)}, bf16[64,1024]{1,0:T(8,128)(2,1)S(1)}, bf16[64,1024]{1,0:T(8,128)(2,1)S(1)}) custom-call(s32[1,3,1]{2,1,0:T(4,128)S(1)} %copy.9.nu_slots, s32[1,1]{1,0:T(1,128)S(6)} %copy.10.nu_count, f32[64,64]{1,0:T(8,128)S(1)} %copy-done.2, f32[64,64]{1,0:T(8,128)S(1)} %collective-permute-done.refs_1_, ...), custom_call_target="tpu_custom_call" | custom-call | flops 1200000000 | bytes 4000000 | tf_op jit(solution)/shard_map/half/pallas_call | solution.py:154
  17.9 0.1 collective-permute-start.3
  18.0 0.6 %collective-permute-start.4 = (bf16[64,1024]{1,0:T(8,128)(2,1)S(1)}, bf16[64,1024]{1,0:T(8,128)(2,1)S(1)}, u32[]{:S(2)}, u32[]{:S(2)}) collective-permute-start(bf16[64,1024]{1,0:T(8,128)(2,1)S(1)} %get-tuple-element.29), channel_id=1, source_target_pairs={{0,2},{1,3},{2,0},{3,1},{4,6},{5,7},{6,4},{7,5},{8,10},{9,11},{10,... | collective-permute-start | bytes 393224 | tf_op jit(solution)/shard_map/ppermute | solution.py:170
  18.5 3.3 %collective-permute-start.5 = (bf16[64,1024]{1,0:T(8,128)(2,1)S(1)}, bf16[64,1024]{1,0:T(8,128)(2,1)S(1)}, u32[]{:S(2)}, u32[]{:S(2)}) collective-permute-start(bf16[64,1024]{1,0:T(8,128)(2,1)S(1)} %get-tuple-element.30), channel_id=1, source_target_pairs={{0,3},{1,0},{2,1},{3,2},{4,7},{5,4},{6,5},{7,6},{8,11},{9,8},{10,9... | collective-permute-start | bytes 393224 | tf_op jit(solution)/shard_map/ppermute | solution.py:170
  21.8 4.5 %collective-permute-done.3.refs_1_ = bf16[64,1024]{1,0:T(8,128)(2,1)S(1)} collective-permute-done((bf16[64,1024]{1,0:T(8,128)(2,1)S(1)}, bf16[64,1024]{1,0:T(8,128)(2,1)S(1)}, u32[]{:S(2)}, u32[]{:S(2)}) %collective-permute-start.3) | collective-permute-done | bytes 131104 | tf_op jit(solution)/shard_map/ppermute | solution.py:170
  26.3 3.7 %collective-permute-done.4.refs_2_ = bf16[64,1024]{1,0:T(8,128)(2,1)S(1)} collective-permute-done((bf16[64,1024]{1,0:T(8,128)(2,1)S(1)}, bf16[64,1024]{1,0:T(8,128)(2,1)S(1)}, u32[]{:S(2)}, u32[]{:S(2)}) %collective-permute-start.4) | collective-permute-done | bytes 131104 | tf_op jit(solution)/shard_map/ppermute | solution.py:170
  30.0 0.0 collective-permute-done.5.refs_3_
  30.0 0.5 exchange.1
  30.5 0.1 collective-permute-start.6
  30.5 1.6 %collective-permute-start.7 = (f32[32,256]{1,0:T(8,128)S(1)}, f32[32,256]{1,0:T(8,128)S(1)}, u32[]{:S(2)}, u32[]{:S(2)}) collective-permute-start(f32[32,256]{1,0:T(8,128)S(1)} %get-tuple-element.35), channel_id=1, source_target_pairs={{0,8},{4,12},{8,0},{12,4},{16,24},{20,28},{24,16},{28,20},{1,9},{5... | collective-permute-start | bytes 98312 | tf_op jit(solution)/shard_map/ppermute | solution.py:184
  32.1 0.3 collective-permute-start.8
  32.4 1.5 %collective-permute-start.9 = (f32[32,256]{1,0:T(8,128)S(1)}, f32[32,256]{1,0:T(8,128)S(1)}, u32[]{:S(2)}, u32[]{:S(2)}) collective-permute-start(f32[32,256]{1,0:T(8,128)S(1)} %get-tuple-element.37), channel_id=1, source_target_pairs={{0,16},{4,20},{8,24},{12,28},{16,0},{20,4},{24,8},{28,12},{1,17},{... | collective-permute-start | bytes 98312 | tf_op jit(solution)/shard_map/ppermute | solution.py:184
  33.9 0.2 collective-permute-start.10
  34.1 0.0 collective-permute-done.6.refs_1_
  34.1 2.4 %collective-permute-start.11 = (f32[32,256]{1,0:T(8,128)S(1)}, f32[32,256]{1,0:T(8,128)S(1)}, u32[]{:S(2)}, u32[]{:S(2)}) collective-permute-start(f32[32,256]{1,0:T(8,128)S(1)} %get-tuple-element.39), channel_id=1, source_target_pairs={{0,24},{4,28},{8,16},{12,20},{16,8},{20,12},{24,0},{28,4},{1,25},{... | collective-permute-start | bytes 98312 | tf_op jit(solution)/shard_map/ppermute | solution.py:184
  36.5 0.0 collective-permute-done.7.refs_2_
  36.5 0.2 collective-permute-start.12
  36.8 0.0 collective-permute-done.8.refs_3_
  36.8 0.0 collective-permute-done.9.refs_4_
  36.8 0.6 %collective-permute-done.10.refs_5_ = f32[32,256]{1,0:T(8,128)S(1)} collective-permute-done((f32[32,256]{1,0:T(8,128)S(1)}, f32[32,256]{1,0:T(8,128)S(1)}, u32[]{:S(2)}, u32[]{:S(2)}) %collective-permute-start.10) | collective-permute-done | bytes 32800 | tf_op jit(solution)/shard_map/ppermute | solution.py:184
  37.4 1.5 %collective-permute-done.11.refs_6_ = f32[32,256]{1,0:T(8,128)S(1)} collective-permute-done((f32[32,256]{1,0:T(8,128)S(1)}, f32[32,256]{1,0:T(8,128)S(1)}, u32[]{:S(2)}, u32[]{:S(2)}) %collective-permute-start.11) | collective-permute-done | bytes 32800 | tf_op jit(solution)/shard_map/ppermute | solution.py:184
  38.9 1.9 %collective-permute-done.12.refs_7_ = f32[32,256]{1,0:T(8,128)S(1)} collective-permute-done((f32[32,256]{1,0:T(8,128)S(1)}, f32[32,256]{1,0:T(8,128)S(1)}, u32[]{:S(2)}, u32[]{:S(2)}) %collective-permute-start.12) | collective-permute-done | bytes 32800 | tf_op jit(solution)/shard_map/ppermute | solution.py:184
  40.8 0.3 row_sum.1
  41.1 2.4 %collective-permute-start.13 = (f32[32,64]{1,0:T(8,128)S(1)}, f32[32,64]{1,0:T(8,128)S(1)}, u32[]{:S(2)}, u32[]{:S(2)}) collective-permute-start(f32[32,64]{1,0:T(8,128)S(1)} %get-tuple-element.42), channel_id=1, source_target_pairs={{0,1},{1,2},{2,3},{3,0},{4,5},{5,6},{6,7},{7,4},{8,9},{9,10},{10,1... | collective-permute-start | bytes 24584 | tf_op jit(solution)/shard_map/ppermute | solution.py:197
  43.5 0.0 collective-permute-start.14
  43.5 2.4 %collective-permute-start.15 = (f32[32,64]{1,0:T(8,128)S(1)}, f32[32,64]{1,0:T(8,128)S(1)}, u32[]{:S(2)}, u32[]{:S(2)}) collective-permute-start(f32[32,64]{1,0:T(8,128)S(1)} %get-tuple-element.44), channel_id=1, source_target_pairs={{0,3},{1,0},{2,1},{3,2},{4,7},{5,4},{6,5},{7,6},{8,11},{9,8},{10,9... | collective-permute-start | bytes 24584 | tf_op jit(solution)/shard_map/ppermute | solution.py:197
  46.0 0.7 %collective-permute-done.13 = f32[32,64]{1,0:T(8,128)S(1)} collective-permute-done((f32[32,64]{1,0:T(8,128)S(1)}, f32[32,64]{1,0:T(8,128)S(1)}, u32[]{:S(2)}, u32[]{:S(2)}) %collective-permute-start.13) | collective-permute-done | bytes 8224 | tf_op jit(solution)/shard_map/ppermute | solution.py:197
  46.7 1.5 %collective-permute-done.14 = f32[32,64]{1,0:T(8,128)S(1)} collective-permute-done((f32[32,64]{1,0:T(8,128)S(1)}, f32[32,64]{1,0:T(8,128)S(1)}, u32[]{:S(2)}, u32[]{:S(2)}) %collective-permute-start.14) | collective-permute-done | bytes 8224 | tf_op jit(solution)/shard_map/ppermute | solution.py:197
  48.2 0.0 collective-permute-done.15
  48.2 0.6 %add_add_fusion = f32[32,64]{1,0:T(8,128)} fusion(f32[32,64]{1,0:T(8,128)S(1)} %collective-permute-done.15, f32[32,64]{1,0:T(8,128)S(1)} %collective-permute-done.14, f32[32,64]{1,0:T(8,128)S(1)} %get-tuple-element.41, f32[32,64]{1,0:T(8,128)S(1)} %collective-permute-done.13), kind=kLoop, calls=%fused_computation | loop fusion | flops 6144 | bytes 40960 | tf_op jit(solution)/shard_map/add | solution.py:197
Async XLA Ops:
  0.0 15.1 %collective-permute-start.1 = (f32[64,64]{1,0:T(8,128)}, f32[64,64]{1,0:T(8,128)S(1)}, u32[]{:S(2)}, u32[]{:S(2)}) collective-permute-start(f32[64,64]{1,0:T(8,128)} %refs_0_.1), channel_id=1, source_target_pairs={{0,2},{1,3},{2,0},{3,1},{4,6},{5,7},{6,4},{7,5},{8,10},{9,11},{10,... | collective-permute-start | bytes 49160 | tf_op jit(solution)/shard_map/ppermute | solution.py:140
  4.0 11.1 %collective-permute-start = (f32[64,64]{1,0:T(8,128)}, f32[64,64]{1,0:T(8,128)S(1)}, u32[]{:S(2)}, u32[]{:S(2)}) collective-permute-start(f32[64,64]{1,0:T(8,128)} %refs_0_.1), channel_id=1, source_target_pairs={{0,1},{1,2},{2,3},{3,0},{4,5},{5,6},{6,7},{7,4},{8,9},{9,10},{10,1... | collective-permute-start | bytes 49160 | tf_op jit(solution)/shard_map/ppermute | solution.py:140
  5.6 9.5 %collective-permute-start.2 = (f32[64,64]{1,0:T(8,128)}, f32[64,64]{1,0:T(8,128)S(1)}, u32[]{:S(2)}, u32[]{:S(2)}) collective-permute-start(f32[64,64]{1,0:T(8,128)} %refs_0_.1), channel_id=1, source_target_pairs={{0,3},{1,0},{2,1},{3,2},{4,7},{5,4},{6,5},{7,6},{8,11},{9,8},{10,9... | collective-permute-start | bytes 49160 | tf_op jit(solution)/shard_map/ppermute | solution.py:140
  10.6 1.9 %copy-start = (f32[1,3,64,4096]{3,2,1,0:T(8,128)S(1)}, f32[1,3,64,4096]{3,2,1,0:T(8,128)}, u32[]{:S(2)}) copy-start(f32[1,3,64,4096]{3,2,1,0:T(8,128)} %tensor.1) | copy-start | bytes 9437188
  12.5 1.1 %copy-start.1 = (f32[1,3,64,1024]{3,2,1,0:T(8,128)S(1)}, f32[1,3,64,1024]{3,2,1,0:T(8,128)}, u32[]{:S(2)}) copy-start(f32[1,3,64,1024]{3,2,1,0:T(8,128)} %metric.1) | copy-start | bytes 2359300
  13.7 1.4 %copy-start.2 = (f32[64,64]{1,0:T(8,128)S(1)}, f32[64,64]{1,0:T(8,128)}, u32[]{:S(2)}) copy-start(f32[64,64]{1,0:T(8,128)} %refs_0_.1) | copy-start | bytes 49156
  17.9 8.3 %collective-permute-start.3 = (bf16[64,1024]{1,0:T(8,128)(2,1)S(1)}, bf16[64,1024]{1,0:T(8,128)(2,1)S(1)}, u32[]{:S(2)}, u32[]{:S(2)}) collective-permute-start(bf16[64,1024]{1,0:T(8,128)(2,1)S(1)} %get-tuple-element.28), channel_id=1, source_target_pairs={{0,1},{1,2},{2,3},{3,0},{4,5},{5,6},{6,7},{7,4},{8,9},{9,10},{10,1... | collective-permute-start | bytes 393224 | tf_op jit(solution)/shard_map/ppermute | solution.py:170
  18.0 12.0 %collective-permute-start.4 = (bf16[64,1024]{1,0:T(8,128)(2,1)S(1)}, bf16[64,1024]{1,0:T(8,128)(2,1)S(1)}, u32[]{:S(2)}, u32[]{:S(2)}) collective-permute-start(bf16[64,1024]{1,0:T(8,128)(2,1)S(1)} %get-tuple-element.29), channel_id=1, source_target_pairs={{0,2},{1,3},{2,0},{3,1},{4,6},{5,7},{6,4},{7,5},{8,10},{9,11},{10,... | collective-permute-start | bytes 393224 | tf_op jit(solution)/shard_map/ppermute | solution.py:170
  18.5 11.5 %collective-permute-start.5 = (bf16[64,1024]{1,0:T(8,128)(2,1)S(1)}, bf16[64,1024]{1,0:T(8,128)(2,1)S(1)}, u32[]{:S(2)}, u32[]{:S(2)}) collective-permute-start(bf16[64,1024]{1,0:T(8,128)(2,1)S(1)} %get-tuple-element.30), channel_id=1, source_target_pairs={{0,3},{1,0},{2,1},{3,2},{4,7},{5,4},{6,5},{7,6},{8,11},{9,8},{10,9... | collective-permute-start | bytes 393224 | tf_op jit(solution)/shard_map/ppermute | solution.py:170
  30.5 3.6 %collective-permute-start.6 = (f32[32,256]{1,0:T(8,128)S(1)}, f32[32,256]{1,0:T(8,128)S(1)}, u32[]{:S(2)}, u32[]{:S(2)}) collective-permute-start(f32[32,256]{1,0:T(8,128)S(1)} %get-tuple-element.34), channel_id=1, source_target_pairs={{0,4},{4,0},{8,12},{12,8},{16,20},{20,16},{24,28},{28,24},{1,5},{5... | collective-permute-start | bytes 98312 | tf_op jit(solution)/shard_map/ppermute | solution.py:184
  30.5 6.0 %collective-permute-start.7 = (f32[32,256]{1,0:T(8,128)S(1)}, f32[32,256]{1,0:T(8,128)S(1)}, u32[]{:S(2)}, u32[]{:S(2)}) collective-permute-start(f32[32,256]{1,0:T(8,128)S(1)} %get-tuple-element.35), channel_id=1, source_target_pairs={{0,8},{4,12},{8,0},{12,4},{16,24},{20,28},{24,16},{28,20},{1,9},{5... | collective-permute-start | bytes 98312 | tf_op jit(solution)/shard_map/ppermute | solution.py:184
  32.1 4.7 %collective-permute-start.8 = (f32[32,256]{1,0:T(8,128)S(1)}, f32[32,256]{1,0:T(8,128)S(1)}, u32[]{:S(2)}, u32[]{:S(2)}) collective-permute-start(f32[32,256]{1,0:T(8,128)S(1)} %get-tuple-element.36), channel_id=1, source_target_pairs={{0,12},{4,8},{8,4},{12,0},{16,28},{20,24},{24,20},{28,16},{1,13},{... | collective-permute-start | bytes 98312 | tf_op jit(solution)/shard_map/ppermute | solution.py:184
  32.4 4.4 %collective-permute-start.9 = (f32[32,256]{1,0:T(8,128)S(1)}, f32[32,256]{1,0:T(8,128)S(1)}, u32[]{:S(2)}, u32[]{:S(2)}) collective-permute-start(f32[32,256]{1,0:T(8,128)S(1)} %get-tuple-element.37), channel_id=1, source_target_pairs={{0,16},{4,20},{8,24},{12,28},{16,0},{20,4},{24,8},{28,12},{1,17},{... | collective-permute-start | bytes 98312 | tf_op jit(solution)/shard_map/ppermute | solution.py:184
  33.9 3.4 %collective-permute-start.10 = (f32[32,256]{1,0:T(8,128)S(1)}, f32[32,256]{1,0:T(8,128)S(1)}, u32[]{:S(2)}, u32[]{:S(2)}) collective-permute-start(f32[32,256]{1,0:T(8,128)S(1)} %get-tuple-element.38), channel_id=1, source_target_pairs={{0,20},{4,16},{8,28},{12,24},{16,4},{20,0},{24,12},{28,8},{1,21},{... | collective-permute-start | bytes 98312 | tf_op jit(solution)/shard_map/ppermute | solution.py:184
  34.1 4.8 %collective-permute-start.11 = (f32[32,256]{1,0:T(8,128)S(1)}, f32[32,256]{1,0:T(8,128)S(1)}, u32[]{:S(2)}, u32[]{:S(2)}) collective-permute-start(f32[32,256]{1,0:T(8,128)S(1)} %get-tuple-element.39), channel_id=1, source_target_pairs={{0,24},{4,28},{8,16},{12,20},{16,8},{20,12},{24,0},{28,4},{1,25},{... | collective-permute-start | bytes 98312 | tf_op jit(solution)/shard_map/ppermute | solution.py:184
  36.5 4.2 %collective-permute-start.12 = (f32[32,256]{1,0:T(8,128)S(1)}, f32[32,256]{1,0:T(8,128)S(1)}, u32[]{:S(2)}, u32[]{:S(2)}) collective-permute-start(f32[32,256]{1,0:T(8,128)S(1)} %get-tuple-element.40), channel_id=1, source_target_pairs={{0,28},{4,24},{8,20},{12,16},{16,12},{20,8},{24,4},{28,0},{1,29},{... | collective-permute-start | bytes 98312 | tf_op jit(solution)/shard_map/ppermute | solution.py:184
  41.1 5.6 %collective-permute-start.13 = (f32[32,64]{1,0:T(8,128)S(1)}, f32[32,64]{1,0:T(8,128)S(1)}, u32[]{:S(2)}, u32[]{:S(2)}) collective-permute-start(f32[32,64]{1,0:T(8,128)S(1)} %get-tuple-element.42), channel_id=1, source_target_pairs={{0,1},{1,2},{2,3},{3,0},{4,5},{5,6},{6,7},{7,4},{8,9},{9,10},{10,1... | collective-permute-start | bytes 24584 | tf_op jit(solution)/shard_map/ppermute | solution.py:197
  43.5 4.6 %collective-permute-start.14 = (f32[32,64]{1,0:T(8,128)S(1)}, f32[32,64]{1,0:T(8,128)S(1)}, u32[]{:S(2)}, u32[]{:S(2)}) collective-permute-start(f32[32,64]{1,0:T(8,128)S(1)} %get-tuple-element.43), channel_id=1, source_target_pairs={{0,2},{1,3},{2,0},{3,1},{4,6},{5,7},{6,4},{7,5},{8,10},{9,11},{10,... | collective-permute-start | bytes 24584 | tf_op jit(solution)/shard_map/ppermute | solution.py:197
  43.5 4.6 %collective-permute-start.15 = (f32[32,64]{1,0:T(8,128)S(1)}, f32[32,64]{1,0:T(8,128)S(1)}, u32[]{:S(2)}, u32[]{:S(2)}) collective-permute-start(f32[32,64]{1,0:T(8,128)S(1)} %get-tuple-element.44), channel_id=1, source_target_pairs={{0,3},{1,0},{2,1},{3,2},{4,7},{5,4},{6,5},{7,6},{8,11},{9,8},{10,9... | collective-permute-start | bytes 24584 | tf_op jit(solution)/shard_map/ppermute | solution.py:197

commit v2 on v1

--- a/solution.py
+++ b/solution.py
@@ -11,6 +11,8 @@
 BF16 = jnp.bfloat16
 VMEM = pl.BlockSpec(memory_space=pltpu.VMEM)
 SMEM = pl.BlockSpec(memory_space=pltpu.SMEM)
+ANY = pl.BlockSpec(memory_space=pl.ANY)
+HBM = pl.BlockSpec(memory_space=pltpu.HBM)
 
 
 def params(mib):
@@ -26,19 +28,36 @@
     return lax.broadcasted_iota(jnp.int32, shape, dim)
 
 
-def prepare_kernel(sig_slots, sig_count, tensor, metric, t_hi, t_lo, m_hi, m_lo):
+def tensor_kernel(tensor, t_hi, t_lo, buffer, arrived):
     _, slots, aux_width, width = tensor.shape
-    for k in range(slots):
-        for chunk in range(width // 256):
-            hi, lo = split(tensor[0, k, :, chunk * 256:(chunk + 1) * 256])
-            rows = slice(chunk * aux_width, (chunk + 1) * aux_width)
-            t_hi[rows, k * 256:(k + 1) * 256] = hi
-            t_lo[rows, k * 256:(k + 1) * 256] = lo
-    sig = metric.shape[1]
+    parts = buffer.shape[0] // slots
+    span = width // parts
+
+    def fetch(k, part):
+        return pltpu.make_async_copy(
+            tensor.at[0, k, :, pl.ds(part * span, span)],
+            buffer.at[k * parts + part],
+            arrived.at[k * parts + part],
+        )
+
+    order = [(k, part) for k in range(slots) for part in range(parts)]
+    for k, part in order:
+        fetch(k, part).start()
+    for k, part in order:
+        fetch(k, part).wait()
+        for chunk in range(span // 256):
+            hi, lo = split(buffer[k * parts + part, :, chunk * 256:(chunk + 1) * 256])
+            at = (part * (span // 256) + chunk) * aux_width
+            t_hi[at:at + aux_width, k * 256:(k + 1) * 256] = hi
+            t_lo[at:at + aux_width, k * 256:(k + 1) * 256] = lo
+
+
+def metric_kernel(sig_slots, sig_count, after, metric, m_hi, m_lo):
+    _, sig, aux_width, width = metric.shape
     half = iota((aux_width, 128), 1) >= 64
     pair_of = jnp.where(half, 1, 0)
-    targets = [jnp.where(q < sig_count[0, 0], sig_slots[0, q, 0], -1) for q in range(sig)]
-    for pair in range(metric.shape[3] // 128):
+    targets = [jnp.where(q < sig_count[0, 0], sig_slots[0, 0, q], -1) for q in range(sig)]
+    for pair in range(width // 128):
         sums = [[jnp.zeros((aux_width, 128), F32) for _ in range(2)] for _ in range(2)]
         for q in range(sig):
             block = metric[0, q, :, pair * 128:(pair + 1) * 128]
@@ -66,7 +85,7 @@
     z = lax.axis_index("mu")
     orb, lam_all = dens[0].shape
     lam = lam_all // n_mu
-    slots = nu_slots.shape[1]
+    slots = nu_slots.shape[2]
     row, col = iota((lam_all, 256), 0), iota((lam_all, 256), 1)
     group = lax.rem(((col >> 3) & 3) + z, n_mu)
     wanted = group * lam + (col >> 7) * 8 + (col & 7)
@@ -77,7 +96,7 @@
         d_lo[s] = jnp.dot(lo, choose, preferred_element_type=F32)
     orbital = (iota((orb, 256), 1) >> 5) & 3
     for k in range(slots):
-        at = lax.rem(z - nu_slots[0, k, 0] + n_mu, n_mu)
+        at = lax.rem(z - nu_slots[0, 0, k] + n_mu, n_mu)
         live = jnp.where(k < nu_count[0, 0], 1.0, 0.0)
         hi, lo = d_hi[at] * live, d_lo[at] * live
         for i in range(4):
@@ -101,10 +120,8 @@
 
 def exchange_kernel(n_mu, n_aux, *refs):
     halves = refs[:n_mu]
-    m_hi, m_lo = refs[n_mu:n_mu + 2]
-    outs = refs[n_mu + 2:n_mu + 2 + n_aux]
-    total = refs[-1]
-    z, a = lax.axis_index("mu"), lax.axis_index("aux")
+    m_hi, m_lo, out, total = refs[n_mu:]
+    z = lax.axis_index("mu")
     left = jnp.concatenate([h[...] for h in halves], axis=0)
     product = jnp.dot(left, m_hi[...], preferred_element_type=F32)
     product += jnp.dot(left, m_lo[...], preferred_element_type=F32)
@@ -112,24 +129,25 @@
     for s in range(n_mu):
         block = lax.rem(z - s + n_mu, n_mu)
         total[pl.ds(pl.multiple_of(block * orb, orb), orb), :] = product[s * orb:(s + 1) * orb]
-    rows = outs[0].shape[0]
-    for t in range(n_aux):
-        outs[t][...] = total[pl.ds(pl.multiple_of((a ^ t) * rows, rows), rows), :]
-
-
-def row_sum_kernel(n_mu, n_aux, *refs):
-    parts, outs = refs[:n_aux], refs[n_aux:]
-    z = lax.axis_index("mu")
-    total = parts[0][...]
-    for t in range(1, n_aux):
-        total += parts[t][...]
-    width = outs[0].shape[1]
-    for s in range(n_mu):
-        block = lax.rem(z + s, n_mu)
-        picked = total[:, :width]
-        for c in range(1, n_mu):
-            picked = jnp.where(block == c, total[:, c * width:(c + 1) * width], picked)
-        outs[s][...] = picked
+    rows = out.shape[1]
+    lower = iota((rows, 128), 1) < 64
+    for a in range(n_aux):
+        for pair in range(n_mu // 2):
+            columns = slice(pair * 128, (pair + 1) * 128)
+            top = total[a * 2 * rows:(a * 2 + 1) * rows, columns]
+            bottom = total[(a * 2 + 1) * rows:(a * 2 + 2) * rows, columns]
+            at = a * n_mu + pair * 2
+            out[at] = jnp.where(lower, top, pltpu.roll(bottom, 64, 1))
+            out[at + 1] = jnp.where(lower, pltpu.roll(top, 64, 1), bottom)
+
+
+def sum_kernel(parts, out):
+    total = parts[0]
+    for d in range(1, parts.shape[0]):
+        total += parts[d]
+    rows = parts.shape[1]
+    out[:rows, :] = total[:, :64]
+    out[rows:, :] = total[:, 64:]
 
 
 def fast(n_mu, n_aux, three_center, nu_slots, nu_count, density, metric_tensor, sig_slots, sig_count):
@@ -138,18 +156,23 @@
     lam = lam_all // n_mu
     turns = [[(z, (z + s) % n_mu) for z in range(n_mu)] for s in range(n_mu)]
     dens = [density] + [lax.ppermute(density, "mu", turns[s]) for s in range(1, n_mu)]
+    nu_slots, sig_slots = jnp.swapaxes(nu_slots, 1, 2), jnp.swapaxes(sig_slots, 1, 2)
     chunks = three_center.shape[3] // 256
     t_shape = jax.ShapeDtypeStruct((chunks * aux_width, slots * 256), BF16)
     m_shape = jax.ShapeDtypeStruct((lam * aux_width, n_mu * orb), BF16)
-    t_hi, t_lo, m_hi, m_lo = pl.pallas_call(
-        prepare_kernel,
-        out_shape=(t_shape, t_shape, m_shape, m_shape),
-        in_specs=[SMEM, SMEM, VMEM, VMEM],
-        out_specs=(VMEM,) * 4,
-        compiler_params=params(16),
-        cost_estimate=pl.CostEstimate(flops=10_000_000, bytes_accessed=8_000_000, transcendentals=0),
-        name="prepare",
-    )(sig_slots, sig_count, three_center, metric_tensor)
+    t_hi, t_lo = pl.pallas_call(
+        tensor_kernel,
+        out_shape=(t_shape, t_shape),
+        in_specs=[HBM],
+        out_specs=(VMEM, VMEM),
+        scratch_shapes=[
+            pltpu.VMEM((slots * 4, aux_width, chunks * 64), F32),
+            pltpu.SemaphoreType.DMA((slots * 4,)),
+        ],
+        compiler_params=params(16),
+        cost_estimate=pl.CostEstimate(flops=10_000_000, bytes_accessed=6_000_000, transcendentals=0),
+        name="tensor",
+    )(three_center)
     half_shape = jax.ShapeDtypeStruct((orb, lam * aux_width), BF16)
     halves = pl.pallas_call(
         functools.partial(half_kernel, n_mu),
@@ -167,35 +190,36 @@
         cost_estimate=pl.CostEstimate(flops=1_200_000_000, bytes_accessed=4_000_000, transcendentals=0),
         name="half",
     )(nu_slots, nu_count, *dens, t_hi, t_lo)
+    m_hi, m_lo = pl.pallas_call(
+        metric_kernel,
+        out_shape=(m_shape, m_shape),
+        in_specs=[SMEM, SMEM, ANY, VMEM],
+        out_specs=(VMEM, VMEM),
+        compiler_params=params(16),
+        cost_estimate=pl.CostEstimate(flops=10_000_000, bytes_accessed=2_000_000, transcendentals=0),
+        name="metric",
+    )(sig_slots, sig_count, halves[0], metric_tensor)
     halves = [halves[0]] + [lax.ppermute(halves[s], "mu", turns[s]) for s in range(1, n_mu)]
     rows = n_mu * orb // n_aux
-    part_shape = jax.ShapeDtypeStruct((rows, n_mu * orb), F32)
     parts = pl.pallas_call(
         functools.partial(exchange_kernel, n_mu, n_aux),
-        out_shape=(part_shape,) * n_aux,
+        out_shape=jax.ShapeDtypeStruct((n_aux * n_mu, rows // 2, 128), F32),
         in_specs=[VMEM] * (n_mu + 2),
-        out_specs=(VMEM,) * n_aux,
+        out_specs=VMEM,
         scratch_shapes=[pltpu.VMEM((n_mu * orb, n_mu * orb), F32)],
         compiler_params=params(16),
         cost_estimate=pl.CostEstimate(flops=300_000_000, bytes_accessed=2_000_000, transcendentals=0),
         name="exchange",
     )(*halves, m_hi, m_lo)
-    parts = [parts[0]] + [
-        lax.ppermute(parts[t], "aux", [(a, a ^ t) for a in range(n_aux)]) for t in range(1, n_aux)
-    ]
-    share_shape = jax.ShapeDtypeStruct((rows, orb), F32)
-    shares = pl.pallas_call(
-        functools.partial(row_sum_kernel, n_mu, n_aux),
-        out_shape=(share_shape,) * n_mu,
-        in_specs=[VMEM] * n_aux,
-        out_specs=(VMEM,) * n_mu,
+    parts = lax.all_to_all(parts, ("aux", "mu"), 0, 0)
+    return pl.pallas_call(
+        sum_kernel,
+        out_shape=jax.ShapeDtypeStruct((rows, orb), F32),
+        in_specs=[VMEM],
+        out_specs=VMEM,
         compiler_params=params(8),
-        name="row_sum",
-    )(*parts)
-    result = shares[0]
-    for s in range(1, n_mu):
-        result = result + lax.ppermute(shares[s], "mu", turns[s])
-    return result
+        name="sum",
+    )(parts)
 
 
 def general(three_center, nu_slots, nu_count, density, metric_tensor, sig_slots, sig_count):

time: 49 us -> 41.6 us (0.85)
  blocking collectives: 0 us -> 15 us
  starting transfers between devices: 22.9 us -> 10.8 us
  waiting for transfers between devices: 14.4 us -> 6.52 us
  local copies, waits for them, and re-layouts: 4.51 us -> 1.9 us
  Pallas kernels: 4.94 us -> 5.77 us
  other arithmetic: 0.61 us -> 0 us
    all_to_all x0 -> x1, blocking collectives: none -> 15 us  [fast(): parts = lax.all_to_all(parts, ('aux', 'mu'), 0, 0)]
    ppermute x10 -> x0, starting transfers between devices: 11.2 us -> none  [the longest x7 6.32 us: fast(): lax.ppermute(parts[t], 'aux', [(a, a ^ t) for a in range(n_aux)])]
    ppermute x10 -> x0, waiting for transfers between devices: 6.2 us -> none  [the longest x7 4 us: fast(): lax.ppermute(parts[t], 'aux', [(a, a ^ t) for a in range(n_aux)])]
    unnamed x8 -> x10, local copies, waits for them, and re-layouts: 4.51 us -> 1.9 us
    ppermute x3, waiting for transfers between devices: 8.19 us -> 6.52 us  [fast(): lax.ppermute(halves[s], 'mu', turns[s])]
    ppermute x3, starting transfers between devices: 7.86 us -> 6.96 us  [fast(): lax.ppermute(density, 'mu', turns[s])]
    pallas_call x2 -> x3, Pallas kernels: 1.69 us -> 2.45 us  [the longest x1 1 us: fast(): pl.pallas_call(metric_kernel, out_shape=(m_shape, m_shape), in_specs=[SME...]
    add x1 -> x0, other arithmetic: 0.61 us -> none  [fast(): result = result + lax.ppermute(shares[s], 'mu', turns[s])]
  transfers between devices with their start and end apart: 16 -> 6, of which waited for: 7 -> 2; matrix products, arithmetic and copies ran while one was open for 3% -> 0% of each run, Pallas kernels for 3% -> 4%
where the time goes in v2:
time: 41.6 us; the launch traced here: 41.4 us
  blocking collectives  15 us (36%)
  starting transfers between devices  10.8 us (26%)
  waiting for transfers between devices  6.52 us (16%)
  Pallas kernels  5.77 us (14%)
  local copies, waits for them, and re-layouts  1.9 us (5%)
  between operations  1.42 us (3%)
    all_to_all x1, blocking collectives, fast(): parts = lax.all_to_all(parts, ('aux', 'mu'), 0, 0)  15 us
    ppermute x3, starting transfers between devices, fast(): lax.ppermute(density, 'mu', turns[s])  6.96 us
    ppermute x3, waiting for transfers between devices, fast(): lax.ppermute(halves[s], 'mu', turns[s])  6.52 us
    ppermute x3, starting transfers between devices, fast(): lax.ppermute(halves[s], 'mu', turns[s])  3.88 us
    pallas_call x1, Pallas kernels, fast(): pl.pallas_call(functools.partial(half_kernel, n_mu), out_shape=(half_shap...  2.75 us
    unnamed x10, local copies, waits for them, and re-layouts  1.9 us
    pallas_call x1, Pallas kernels, fast(): pl.pallas_call(metric_kernel, out_shape=(m_shape, m_shape), in_specs=[SME...  1 us
  transfers between devices with their start and end apart: 6, of which 2 were waited for; matrix products, arithmetic and copies ran while one was open for 0% of the time, Pallas kernels for 4%

profile of v2, /device:TPU:0, one launch (start us, length us, event | category | flops | bytes accessed | tf_op | source)
XLA Modules:
  0.0 41.4 jit_solution(1802485802716825922)
XLA Ops:
  0.0 3.0 %collective-permute-start = (f32[64,64]{1,0:T(8,128)}, f32[64,64]{1,0:T(8,128)S(1)}, u32[]{:S(2)}, u32[]{:S(2)}) collective-permute-start(f32[64,64]{1,0:T(8,128)} %refs_0_.1), channel_id=1, source_target_pairs={{0,1},{1,2},{2,3},{3,0},{4,5},{5,6},{6,7},{7,4},{8,9},{9,10},{10,1... | collective-permute-start | bytes 49160 | tf_op jit(solution)/shard_map/ppermute | solution.py:158
  3.0 2.6 %collective-permute-start.1 = (f32[64,64]{1,0:T(8,128)}, f32[64,64]{1,0:T(8,128)S(1)}, u32[]{:S(2)}, u32[]{:S(2)}) collective-permute-start(f32[64,64]{1,0:T(8,128)} %refs_0_.1), channel_id=1, source_target_pairs={{0,2},{1,3},{2,0},{3,1},{4,6},{5,7},{6,4},{7,5},{8,10},{9,11},{10,... | collective-permute-start | bytes 49160 | tf_op jit(solution)/shard_map/ppermute | solution.py:158
  5.6 1.3 %collective-permute-start.2 = (f32[64,64]{1,0:T(8,128)}, f32[64,64]{1,0:T(8,128)S(1)}, u32[]{:S(2)}, u32[]{:S(2)}) collective-permute-start(f32[64,64]{1,0:T(8,128)} %refs_0_.1), channel_id=1, source_target_pairs={{0,3},{1,0},{2,1},{3,2},{4,7},{5,4},{6,5},{7,6},{8,11},{9,8},{10,9... | collective-permute-start | bytes 49160 | tf_op jit(solution)/shard_map/ppermute | solution.py:158
  7.6 0.0 copy-start
  7.6 1.9 %copy-done = f32[1,3,64,4096]{3,2,1,0:T(8,128)S(1)} copy-done((f32[1,3,64,4096]{3,2,1,0:T(8,128)S(1)}, f32[1,3,64,4096]{3,2,1,0:T(8,128)}, u32[]{:S(2)}) %copy-start) | copy-done | bytes 3145752
  9.5 0.0 copy-start.3
  9.5 0.0 copy-start.4
  9.5 0.7 %tensor.2 = (bf16[1024,768]{1,0:T(8,128)(2,1)S(1)}, bf16[1024,768]{1,0:T(8,128)(2,1)S(1)}) custom-call(f32[1,3,64,4096]{3,2,1,0:T(8,128)S(1)} %copy-done), custom_call_target="tpu_custom_call" | custom-call | flops 10000000 | bytes 6000000 | tf_op jit(solution)/shard_map/tensor/pallas_call | solution.py:163
  10.3 0.0 collective-permute-done.refs_1_
  10.3 0.0 collective-permute-done.1.refs_2_
  10.3 0.0 collective-permute-done.2.refs_3_
  10.3 0.0 copy-done.3
  10.3 0.0 copy-done.4
  10.3 0.0 copy-start.1
  10.3 0.0 copy-start.2
  10.3 2.8 %half.1 = (bf16[64,1024]{1,0:T(8,128)(2,1)S(1)}, bf16[64,1024]{1,0:T(8,128)(2,1)S(1)}, bf16[64,1024]{1,0:T(8,128)(2,1)S(1)}, bf16[64,1024]{1,0:T(8,128)(2,1)S(1)}) custom-call(s32[1,1,3]{2,1,0:T(1,128)S(1)} %bitcast.3, s32[1,1]{1,0:T(1,128)S(6)} %copy.8.nu_count, f32[64,64]{1,0:T(8,128)S(1)} %copy-done.3, f32[64,64]{1,0:T(8,128)S(1)} %collective-permute-done.refs_1_, ...), custom_call_target="tpu_custom_call" | custom-call | flops 1200000000 | bytes 4000000 | tf_op jit(solution)/shard_map/half/pallas_call | solution.py:177
  13.1 0.7 %collective-permute-start.3 = (bf16[64,1024]{1,0:T(8,128)(2,1)S(1)}, bf16[64,1024]{1,0:T(8,128)(2,1)S(1)}, u32[]{:S(2)}, u32[]{:S(2)}) collective-permute-start(bf16[64,1024]{1,0:T(8,128)(2,1)S(1)} %get-tuple-element.16), channel_id=1, source_target_pairs={{0,1},{1,2},{2,3},{3,0},{4,5},{5,6},{6,7},{7,4},{8,9},{9,10},{10,1... | collective-permute-start | bytes 393224 | tf_op jit(solution)/shard_map/ppermute | solution.py:202
  13.8 2.5 %collective-permute-start.4 = (bf16[64,1024]{1,0:T(8,128)(2,1)S(1)}, bf16[64,1024]{1,0:T(8,128)(2,1)S(1)}, u32[]{:S(2)}, u32[]{:S(2)}) collective-permute-start(bf16[64,1024]{1,0:T(8,128)(2,1)S(1)} %get-tuple-element.17), channel_id=1, source_target_pairs={{0,2},{1,3},{2,0},{3,1},{4,6},{5,7},{6,4},{7,5},{8,10},{9,11},{10,... | collective-permute-start | bytes 393224 | tf_op jit(solution)/shard_map/ppermute | solution.py:202
  16.3 0.7 %collective-permute-start.5 = (bf16[64,1024]{1,0:T(8,128)(2,1)S(1)}, bf16[64,1024]{1,0:T(8,128)(2,1)S(1)}, u32[]{:S(2)}, u32[]{:S(2)}) collective-permute-start(bf16[64,1024]{1,0:T(8,128)(2,1)S(1)} %get-tuple-element.18), channel_id=1, source_target_pairs={{0,3},{1,0},{2,1},{3,2},{4,7},{5,4},{6,5},{7,6},{8,11},{9,8},{10,9... | collective-permute-start | bytes 393224 | tf_op jit(solution)/shard_map/ppermute | solution.py:202
  17.6 0.0 copy-done.1
  17.6 0.0 copy-done.2
  17.6 1.0 %metric.2 = (bf16[1024,256]{1,0:T(8,128)(2,1)S(1)}, bf16[1024,256]{1,0:T(8,128)(2,1)S(1)}) custom-call(s32[1,1,3]{2,1,0:T(1,128)S(1)} %bitcast.2, s32[1,1]{1,0:T(1,128)S(6)} %copy.9.sig_count, bf16[64,1024]{1,0:T(8,128)(2,1)S(1)} %get-tuple-element.15.after.refs_0_, f32[1,3,64,1024]{3,2,1,0:T(8,128)S(1)} %copy-done.1), custom_call_target="tpu_custom_call" | custom-call | flops 10000000 | bytes 2000000 | tf_op jit(solution)/shard_map/metric/pallas_call | solution.py:193
  18.7 2.8 %collective-permute-done.3.refs_1_ = bf16[64,1024]{1,0:T(8,128)(2,1)S(1)} collective-permute-done((bf16[64,1024]{1,0:T(8,128)(2,1)S(1)}, bf16[64,1024]{1,0:T(8,128)(2,1)S(1)}, u32[]{:S(2)}, u32[]{:S(2)}) %collective-permute-start.3) | collective-permute-done | bytes 131104 | tf_op jit(solution)/shard_map/ppermute | solution.py:202
  21.4 3.7 %collective-permute-done.4.refs_2_ = bf16[64,1024]{1,0:T(8,128)(2,1)S(1)} collective-permute-done((bf16[64,1024]{1,0:T(8,128)(2,1)S(1)}, bf16[64,1024]{1,0:T(8,128)(2,1)S(1)}, u32[]{:S(2)}, u32[]{:S(2)}) %collective-permute-start.4) | collective-permute-done | bytes 131104 | tf_op jit(solution)/shard_map/ppermute | solution.py:202
  25.2 0.0 collective-permute-done.5.refs_3_
  25.2 0.6 %exchange.1 = f32[32,16,128]{2,1,0:T(8,128)S(1)} custom-call(bf16[64,1024]{1,0:T(8,128)(2,1)S(1)} %get-tuple-element.15.after.refs_0_, bf16[64,1024]{1,0:T(8,128)(2,1)S(1)} %collective-permute-done.3.refs_1_, bf16[64,1024]{1,0:T(8,128)(2,1)S(1)} %collective-permute-done.4.refs_2_, bf16[64,1024]{1,0:T(8,128)(2,1)S(1)} %collective-permute-done.5.refs_3_, ...), custom_call_target="tpu_custom_call" | custom-call | flops 300000000 | bytes 2000000 | tf_op jit(solution)/shard_map/exchange/pallas_call | solution.py:204
  25.7 15.0 %all_to_all.5.parts = f32[32,16,128]{2,1,0:T(8,128)S(1)} all-to-all(f32[32,16,128]{2,1,0:T(8,128)S(1)} %exchange.1), channel_id=1, replica_groups=mesh['aux'=8,'mu'=4] {'aux','mu'}, dimensions={0} | all-to-all | bytes 524288 | tf_op jit(solution)/shard_map/all_to_all | solution.py:214
  40.7 0.7 %sum.1 = f32[32,64]{1,0:T(8,128)} custom-call(f32[32,16,128]{2,1,0:T(8,128)S(1)} %all_to_all.5.parts), custom_call_target="tpu_custom_call" | custom-call | tf_op jit(solution)/shard_map/sum/pallas_call | solution.py:215
Async XLA Ops:
  0.0 10.3 %collective-permute-start = (f32[64,64]{1,0:T(8,128)}, f32[64,64]{1,0:T(8,128)S(1)}, u32[]{:S(2)}, u32[]{:S(2)}) collective-permute-start(f32[64,64]{1,0:T(8,128)} %refs_0_.1), channel_id=1, source_target_pairs={{0,1},{1,2},{2,3},{3,0},{4,5},{5,6},{6,7},{7,4},{8,9},{9,10},{10,1... | collective-permute-start | bytes 49160 | tf_op jit(solution)/shard_map/ppermute | solution.py:158
  3.0 7.2 %collective-permute-start.1 = (f32[64,64]{1,0:T(8,128)}, f32[64,64]{1,0:T(8,128)S(1)}, u32[]{:S(2)}, u32[]{:S(2)}) collective-permute-start(f32[64,64]{1,0:T(8,128)} %refs_0_.1), channel_id=1, source_target_pairs={{0,2},{1,3},{2,0},{3,1},{4,6},{5,7},{6,4},{7,5},{8,10},{9,11},{10,... | collective-permute-start | bytes 49160 | tf_op jit(solution)/shard_map/ppermute | solution.py:158
  5.6 4.7 %collective-permute-start.2 = (f32[64,64]{1,0:T(8,128)}, f32[64,64]{1,0:T(8,128)S(1)}, u32[]{:S(2)}, u32[]{:S(2)}) collective-permute-start(f32[64,64]{1,0:T(8,128)} %refs_0_.1), channel_id=1, source_target_pairs={{0,3},{1,0},{2,1},{3,2},{4,7},{5,4},{6,5},{7,6},{8,11},{9,8},{10,9... | collective-permute-start | bytes 49160 | tf_op jit(solution)/shard_map/ppermute | solution.py:158
  7.6 1.9 %copy-start = (f32[1,3,64,4096]{3,2,1,0:T(8,128)S(1)}, f32[1,3,64,4096]{3,2,1,0:T(8,128)}, u32[]{:S(2)}) copy-start(f32[1,3,64,4096]{3,2,1,0:T(8,128)} %tensor.3) | copy-start | bytes 9437188
  9.5 0.8 %copy-start.3 = (f32[64,64]{1,0:T(8,128)S(1)}, f32[64,64]{1,0:T(8,128)}, u32[]{:S(2)}) copy-start(f32[64,64]{1,0:T(8,128)} %refs_0_.1) | copy-start | bytes 49156
  9.5 0.8 %copy-start.4 = (s32[1,3,1]{1,2,0:T(1,128)S(1)}, s32[1,3,1]{1,2,0:T(1,128)}, u32[]{:S(2)}) copy-start(s32[1,3,1]{1,2,0:T(1,128)} %param.8) | copy-start | bytes 40
  10.3 7.3 %copy-start.1 = (f32[1,3,64,1024]{3,2,1,0:T(8,128)S(1)}, f32[1,3,64,1024]{3,2,1,0:T(8,128)}, u32[]{:S(2)}) copy-start(f32[1,3,64,1024]{3,2,1,0:T(8,128)} %metric.3) | copy-start | bytes 2359300
  10.3 7.3 %copy-start.2 = (s32[1,3,1]{1,2,0:T(1,128)S(1)}, s32[1,3,1]{1,2,0:T(1,128)}, u32[]{:S(2)}) copy-start(s32[1,3,1]{1,2,0:T(1,128)} %param.12) | copy-start | bytes 40
  13.1 8.3 %collective-permute-start.3 = (bf16[64,1024]{1,0:T(8,128)(2,1)S(1)}, bf16[64,1024]{1,0:T(8,128)(2,1)S(1)}, u32[]{:S(2)}, u32[]{:S(2)}) collective-permute-start(bf16[64,1024]{1,0:T(8,128)(2,1)S(1)} %get-tuple-element.16), channel_id=1, source_target_pairs={{0,1},{1,2},{2,3},{3,0},{4,5},{5,6},{6,7},{7,4},{8,9},{9,10},{10,1... | collective-permute-start | bytes 393224 | tf_op jit(solution)/shard_map/ppermute | solution.py:202
  13.8 11.3 %collective-permute-start.4 = (bf16[64,1024]{1,0:T(8,128)(2,1)S(1)}, bf16[64,1024]{1,0:T(8,128)(2,1)S(1)}, u32[]{:S(2)}, u32[]{:S(2)}) collective-permute-start(bf16[64,1024]{1,0:T(8,128)(2,1)S(1)} %get-tuple-element.17), channel_id=1, source_target_pairs={{0,2},{1,3},{2,0},{3,1},{4,6},{5,7},{6,4},{7,5},{8,10},{9,11},{10,... | collective-permute-start | bytes 393224 | tf_op jit(solution)/shard_map/ppermute | solution.py:202
  16.3 8.9 %collective-permute-start.5 = (bf16[64,1024]{1,0:T(8,128)(2,1)S(1)}, bf16[64,1024]{1,0:T(8,128)(2,1)S(1)}, u32[]{:S(2)}, u32[]{:S(2)}) collective-permute-start(bf16[64,1024]{1,0:T(8,128)(2,1)S(1)} %get-tuple-element.18), channel_id=1, source_target_pairs={{0,3},{1,0},{2,1},{3,2},{4,7},{5,4},{6,5},{7,6},{8,11},{9,8},{10,9... | collective-permute-start | bytes 393224 | tf_op jit(solution)/shard_map/ppermute | solution.py:202

commit v3 on v2

--- a/solution.py
+++ b/solution.py
@@ -103,19 +103,23 @@
             rows = slice(k * 256 + i * orb, k * 256 + (i + 1) * orb)
             w_hi[rows, :] = jnp.where(orbital == i, hi, 0.0).astype(BF16)
             w_lo[rows, :] = jnp.where(orbital == i, lo, 0.0).astype(BF16)
-    total = jnp.dot(t_hi[...], w_hi[...], preferred_element_type=F32)
-    total += jnp.dot(t_lo[...], w_hi[...], preferred_element_type=F32)
-    total += jnp.dot(t_hi[...], w_lo[...], preferred_element_type=F32)
     aux_width = outs[0].shape[1] // lam
-    for chunk in range(total.shape[0] // aux_width):
-        piece = total[chunk * aux_width:(chunk + 1) * aux_width]
-        stacked = jnp.concatenate([piece[:, :128], piece[:, 128:]], axis=0)
-        turned[chunk * 128:(chunk + 1) * 128, :] = stacked.T
-    for s in range(n_mu):
-        for r in range(8):
-            outs[s][:, r * 128:(r + 1) * 128] = turned[
-                pl.ds(s * 8 + r, orb, stride=32), :
-            ].astype(BF16)
+    per_group = 256 // aux_width
+    span = per_group * 4
+    for group in range(t_hi.shape[0] // 256):
+        rows = slice(group * 256, (group + 1) * 256)
+        total = jnp.dot(t_hi[rows, :], w_hi[...], preferred_element_type=F32)
+        total += jnp.dot(t_lo[rows, :], w_hi[...], preferred_element_type=F32)
+        total += jnp.dot(t_hi[rows, :], w_lo[...], preferred_element_type=F32)
+        for chunk in range(per_group):
+            piece = total[chunk * aux_width:(chunk + 1) * aux_width]
+            stacked = jnp.concatenate([piece[:, :128], piece[:, 128:]], axis=0)
+            at = (group * per_group + chunk) * 128
+            turned[at:at + 128, :] = stacked.T
+        for s in range(n_mu):
+            for r in range(8):
+                picked = turned[pl.ds(group * per_group * 128 + s * 8 + r, span, stride=32), :]
+                outs[s][group * span:(group + 1) * span, r * 128:(r + 1) * 128] = picked.astype(BF16)
 
 
 def exchange_kernel(n_mu, n_aux, *refs):
@@ -137,14 +141,14 @@
             top = total[a * 2 * rows:(a * 2 + 1) * rows, columns]
             bottom = total[(a * 2 + 1) * rows:(a * 2 + 2) * rows, columns]
             at = a * n_mu + pair * 2
-            out[at] = jnp.where(lower, top, pltpu.roll(bottom, 64, 1))
-            out[at + 1] = jnp.where(lower, pltpu.roll(top, 64, 1), bottom)
+            out[at] = jnp.where(lower, top, pltpu.roll(bottom, 64, 1)).astype(BF16)
+            out[at + 1] = jnp.where(lower, pltpu.roll(top, 64, 1), bottom).astype(BF16)
 
 
 def sum_kernel(parts, out):
-    total = parts[0]
+    total = parts[0].astype(F32)
     for d in range(1, parts.shape[0]):
-        total += parts[d]
+        total += parts[d].astype(F32)
     rows = parts.shape[1]
     out[:rows, :] = total[:, :64]
     out[rows:, :] = total[:, 64:]
@@ -169,7 +173,7 @@
             pltpu.VMEM((slots * 4, aux_width, chunks * 64), F32),
             pltpu.SemaphoreType.DMA((slots * 4,)),
         ],
-        compiler_params=params(16),
+        compiler_params=params(50),
         cost_estimate=pl.CostEstimate(flops=10_000_000, bytes_accessed=6_000_000, transcendentals=0),
         name="tensor",
     )(three_center)
@@ -203,7 +207,7 @@
     rows = n_mu * orb // n_aux
     parts = pl.pallas_call(
         functools.partial(exchange_kernel, n_mu, n_aux),
-        out_shape=jax.ShapeDtypeStruct((n_aux * n_mu, rows // 2, 128), F32),
+        out_shape=jax.ShapeDtypeStruct((n_aux * n_mu, rows // 2, 128), BF16),
         in_specs=[VMEM] * (n_mu + 2),
         out_specs=VMEM,
         scratch_shapes=[pltpu.VMEM((n_mu * orb, n_mu * orb), F32)],

time: 41.6 us -> 39.6 us (0.952)
  local copies, waits for them, and re-layouts: 1.9 us -> 0.02 us
  blocking collectives: 15 us -> 13.8 us
  Pallas kernels: 5.77 us -> 6.92 us
    unnamed x10 -> x8, local copies, waits for them, and re-layouts: 1.9 us -> 0.02 us
    pallas_call x1, Pallas kernels: 0.74 us -> 1.97 us  [fast(): pl.pallas_call(tensor_kernel, out_shape=(t_shape, t_shape), in_specs=[HBM...]
    all_to_all x1, blocking collectives: 15 us -> 13.8 us  [fast(): parts = lax.all_to_all(parts, ('aux', 'mu'), 0, 0)]
  transfers between devices with their start and end apart: 6 -> 6, of which waited for: 2 -> 3; matrix products, arithmetic and copies ran while one was open for 0% -> 0% of each run, Pallas kernels for 4% -> 8%
where the time goes in v3:
time: 39.6 us; the launch traced here: 39.5 us
  blocking collectives  13.8 us (35%)
  starting transfers between devices  10.9 us (28%)
  Pallas kernels  6.92 us (17%)
  waiting for transfers between devices  6.49 us (16%)
  between operations  1.4 us (4%)
    all_to_all x1, blocking collectives, fast(): parts = lax.all_to_all(parts, ('aux', 'mu'), 0, 0)  13.8 us
    ppermute x3, starting transfers between devices, fast(): lax.ppermute(density, 'mu', turns[s])  6.96 us
    ppermute x3, waiting for transfers between devices, fast(): lax.ppermute(halves[s], 'mu', turns[s])  6.38 us
    ppermute x3, starting transfers between devices, fast(): lax.ppermute(halves[s], 'mu', turns[s])  3.9 us
    pallas_call x1, Pallas kernels, fast(): pl.pallas_call(functools.partial(half_kernel, n_mu), out_shape=(half_shap...  2.69 us
    pallas_call x1, Pallas kernels, fast(): pl.pallas_call(tensor_kernel, out_shape=(t_shape, t_shape), in_specs=[HBM...  1.97 us
    pallas_call x1, Pallas kernels, fast(): pl.pallas_call(metric_kernel, out_shape=(m_shape, m_shape), in_specs=[SME...  1 us
  transfers between devices with their start and end apart: 6, of which 3 were waited for; matrix products, arithmetic and copies ran while one was open for 0% of the time, Pallas kernels for 8%

profile of v3, /device:TPU:0, one launch (start us, length us, event | category | flops | bytes accessed | tf_op | source)
XLA Modules:
  0.0 39.5 jit_solution(11033622245812267546)
XLA Ops:
  0.0 3.0 %collective-permute-start = (f32[64,64]{1,0:T(8,128)}, f32[64,64]{1,0:T(8,128)S(1)}, u32[]{:S(2)}, u32[]{:S(2)}) collective-permute-start(f32[64,64]{1,0:T(8,128)} %refs_0_.1), channel_id=1, source_target_pairs={{0,1},{1,2},{2,3},{3,0},{4,5},{5,6},{6,7},{7,4},{8,9},{9,10},{10,1... | collective-permute-start | bytes 49160 | tf_op jit(solution)/shard_map/ppermute | solution.py:162
  3.0 2.6 %collective-permute-start.1 = (f32[64,64]{1,0:T(8,128)}, f32[64,64]{1,0:T(8,128)S(1)}, u32[]{:S(2)}, u32[]{:S(2)}) collective-permute-start(f32[64,64]{1,0:T(8,128)} %refs_0_.1), channel_id=1, source_target_pairs={{0,2},{1,3},{2,0},{3,1},{4,6},{5,7},{6,4},{7,5},{8,10},{9,11},{10,... | collective-permute-start | bytes 49160 | tf_op jit(solution)/shard_map/ppermute | solution.py:162
  5.6 1.3 %collective-permute-start.2 = (f32[64,64]{1,0:T(8,128)}, f32[64,64]{1,0:T(8,128)S(1)}, u32[]{:S(2)}, u32[]{:S(2)}) collective-permute-start(f32[64,64]{1,0:T(8,128)} %refs_0_.1), channel_id=1, source_target_pairs={{0,3},{1,0},{2,1},{3,2},{4,7},{5,4},{6,5},{7,6},{8,11},{9,8},{10,9... | collective-permute-start | bytes 49160 | tf_op jit(solution)/shard_map/ppermute | solution.py:162
  7.6 0.0 copy-start.2
  7.6 0.0 copy-start.3
  7.6 2.0 %tensor.2 = (bf16[1024,768]{1,0:T(8,128)(2,1)S(1)}, bf16[1024,768]{1,0:T(8,128)(2,1)S(1)}) custom-call(f32[1,3,64,4096]{3,2,1,0:T(8,128)} %tensor.3), custom_call_target="tpu_custom_call" | custom-call | flops 10000000 | bytes 6000000 | tf_op jit(solution)/shard_map/tensor/pallas_call | solution.py:167
  9.6 0.0 collective-permute-done.refs_1_
  9.6 0.0 collective-permute-done.1.refs_2_
  9.6 0.1 collective-permute-done.2.refs_3_
  9.7 0.0 copy-done.2
  9.7 0.0 copy-done.3
  9.7 0.0 copy-start
  9.7 0.0 copy-start.1
  9.8 2.7 %half.1 = (bf16[64,1024]{1,0:T(8,128)(2,1)S(1)}, bf16[64,1024]{1,0:T(8,128)(2,1)S(1)}, bf16[64,1024]{1,0:T(8,128)(2,1)S(1)}, bf16[64,1024]{1,0:T(8,128)(2,1)S(1)}) custom-call(s32[1,1,3]{2,1,0:T(1,128)S(1)} %bitcast.3, s32[1,1]{1,0:T(1,128)S(6)} %copy.8.nu_count, f32[64,64]{1,0:T(8,128)S(1)} %copy-done.2, f32[64,64]{1,0:T(8,128)S(1)} %collective-permute-done.refs_1_, ...), custom_call_target="tpu_custom_call" | custom-call | flops 1200000000 | bytes 4000000 | tf_op jit(solution)/shard_map/half/pallas_call | solution.py:181
  12.5 0.7 %collective-permute-start.3 = (bf16[64,1024]{1,0:T(8,128)(2,1)S(1)}, bf16[64,1024]{1,0:T(8,128)(2,1)S(1)}, u32[]{:S(2)}, u32[]{:S(2)}) collective-permute-start(bf16[64,1024]{1,0:T(8,128)(2,1)S(1)} %get-tuple-element.16), channel_id=1, source_target_pairs={{0,1},{1,2},{2,3},{3,0},{4,5},{5,6},{6,7},{7,4},{8,9},{9,10},{10,1... | collective-permute-start | bytes 393224 | tf_op jit(solution)/shard_map/ppermute | solution.py:206
  13.1 3.1 %collective-permute-start.4 = (bf16[64,1024]{1,0:T(8,128)(2,1)S(1)}, bf16[64,1024]{1,0:T(8,128)(2,1)S(1)}, u32[]{:S(2)}, u32[]{:S(2)}) collective-permute-start(bf16[64,1024]{1,0:T(8,128)(2,1)S(1)} %get-tuple-element.17), channel_id=1, source_target_pairs={{0,2},{1,3},{2,0},{3,1},{4,6},{5,7},{6,4},{7,5},{8,10},{9,11},{10,... | collective-permute-start | bytes 393224 | tf_op jit(solution)/shard_map/ppermute | solution.py:206
  16.2 0.1 collective-permute-start.5
  17.0 0.0 copy-done
  17.0 0.0 copy-done.1
  17.0 1.0 %metric.2 = (bf16[1024,256]{1,0:T(8,128)(2,1)S(1)}, bf16[1024,256]{1,0:T(8,128)(2,1)S(1)}) custom-call(s32[1,1,3]{2,1,0:T(1,128)S(1)} %bitcast.2, s32[1,1]{1,0:T(1,128)S(6)} %copy.9.sig_count, bf16[64,1024]{1,0:T(8,128)(2,1)S(1)} %get-tuple-element.15.after.refs_0_, f32[1,3,64,1024]{3,2,1,0:T(8,128)S(1)} %copy-done), custom_call_target="tpu_custom_call" | custom-call | flops 10000000 | bytes 2000000 | tf_op jit(solution)/shard_map/metric/pallas_call | solution.py:197
  18.0 2.8 %collective-permute-done.3.refs_1_ = bf16[64,1024]{1,0:T(8,128)(2,1)S(1)} collective-permute-done((bf16[64,1024]{1,0:T(8,128)(2,1)S(1)}, bf16[64,1024]{1,0:T(8,128)(2,1)S(1)}, u32[]{:S(2)}, u32[]{:S(2)}) %collective-permute-start.3) | collective-permute-done | bytes 131104 | tf_op jit(solution)/shard_map/ppermute | solution.py:206
  20.8 3.6 %collective-permute-done.4.refs_2_ = bf16[64,1024]{1,0:T(8,128)(2,1)S(1)} collective-permute-done((bf16[64,1024]{1,0:T(8,128)(2,1)S(1)}, bf16[64,1024]{1,0:T(8,128)(2,1)S(1)}, u32[]{:S(2)}, u32[]{:S(2)}) %collective-permute-start.4) | collective-permute-done | bytes 131104 | tf_op jit(solution)/shard_map/ppermute | solution.py:206
  24.4 0.0 collective-permute-done.5.refs_3_
  24.4 0.6 %exchange.1 = bf16[32,16,128]{2,1,0:T(8,128)(2,1)S(1)} custom-call(bf16[64,1024]{1,0:T(8,128)(2,1)S(1)} %get-tuple-element.15.after.refs_0_, bf16[64,1024]{1,0:T(8,128)(2,1)S(1)} %collective-permute-done.3.refs_1_, bf16[64,1024]{1,0:T(8,128)(2,1)S(1)} %collective-permute-done.4.refs_2_, bf16[64,1024]{1,0:T(8,128)(2,1)S(1)} %collective-permute-done.5.refs_3_, ...), custom_call_target="tpu_custom_call" | custom-call | flops 300000000 | bytes 2000000 | tf_op jit(solution)/shard_map/exchange/pallas_call | solution.py:208
  25.0 13.8 %all_to_all.5.parts = bf16[32,16,128]{2,1,0:T(8,128)(2,1)S(1)} all-to-all(bf16[32,16,128]{2,1,0:T(8,128)(2,1)S(1)} %exchange.1), channel_id=1, replica_groups=mesh['aux'=8,'mu'=4] {'aux','mu'}, dimensions={0} | all-to-all | bytes 262144 | tf_op jit(solution)/shard_map/all_to_all | solution.py:218
  38.7 0.7 %sum.1 = f32[32,64]{1,0:T(8,128)} custom-call(bf16[32,16,128]{2,1,0:T(8,128)(2,1)S(1)} %all_to_all.5.parts), custom_call_target="tpu_custom_call" | custom-call | tf_op jit(solution)/shard_map/sum/pallas_call | solution.py:219
Async XLA Ops:
  0.0 9.6 %collective-permute-start = (f32[64,64]{1,0:T(8,128)}, f32[64,64]{1,0:T(8,128)S(1)}, u32[]{:S(2)}, u32[]{:S(2)}) collective-permute-start(f32[64,64]{1,0:T(8,128)} %refs_0_.1), channel_id=1, source_target_pairs={{0,1},{1,2},{2,3},{3,0},{4,5},{5,6},{6,7},{7,4},{8,9},{9,10},{10,1... | collective-permute-start | bytes 49160 | tf_op jit(solution)/shard_map/ppermute | solution.py:162
  3.0 6.6 %collective-permute-start.1 = (f32[64,64]{1,0:T(8,128)}, f32[64,64]{1,0:T(8,128)S(1)}, u32[]{:S(2)}, u32[]{:S(2)}) collective-permute-start(f32[64,64]{1,0:T(8,128)} %refs_0_.1), channel_id=1, source_target_pairs={{0,2},{1,3},{2,0},{3,1},{4,6},{5,7},{6,4},{7,5},{8,10},{9,11},{10,... | collective-permute-start | bytes 49160 | tf_op jit(solution)/shard_map/ppermute | solution.py:162
  5.6 4.1 %collective-permute-start.2 = (f32[64,64]{1,0:T(8,128)}, f32[64,64]{1,0:T(8,128)S(1)}, u32[]{:S(2)}, u32[]{:S(2)}) collective-permute-start(f32[64,64]{1,0:T(8,128)} %refs_0_.1), channel_id=1, source_target_pairs={{0,3},{1,0},{2,1},{3,2},{4,7},{5,4},{6,5},{7,6},{8,11},{9,8},{10,9... | collective-permute-start | bytes 49160 | tf_op jit(solution)/shard_map/ppermute | solution.py:162
  7.6 2.1 %copy-start.2 = (f32[64,64]{1,0:T(8,128)S(1)}, f32[64,64]{1,0:T(8,128)}, u32[]{:S(2)}) copy-start(f32[64,64]{1,0:T(8,128)} %refs_0_.1) | copy-start | bytes 49156
  7.6 2.1 %copy-start.3 = (s32[1,3,1]{1,2,0:T(1,128)S(1)}, s32[1,3,1]{1,2,0:T(1,128)}, u32[]{:S(2)}) copy-start(s32[1,3,1]{1,2,0:T(1,128)} %param.8) | copy-start | bytes 40
  9.7 7.3 %copy-start = (f32[1,3,64,1024]{3,2,1,0:T(8,128)S(1)}, f32[1,3,64,1024]{3,2,1,0:T(8,128)}, u32[]{:S(2)}) copy-start(f32[1,3,64,1024]{3,2,1,0:T(8,128)} %metric.3) | copy-start | bytes 2359300
  9.7 7.3 %copy-start.1 = (s32[1,3,1]{1,2,0:T(1,128)S(1)}, s32[1,3,1]{1,2,0:T(1,128)}, u32[]{:S(2)}) copy-start(s32[1,3,1]{1,2,0:T(1,128)} %param.12) | copy-start | bytes 40
  12.5 8.4 %collective-permute-start.3 = (bf16[64,1024]{1,0:T(8,128)(2,1)S(1)}, bf16[64,1024]{1,0:T(8,128)(2,1)S(1)}, u32[]{:S(2)}, u32[]{:S(2)}) collective-permute-start(bf16[64,1024]{1,0:T(8,128)(2,1)S(1)} %get-tuple-element.16), channel_id=1, source_target_pairs={{0,1},{1,2},{2,3},{3,0},{4,5},{5,6},{6,7},{7,4},{8,9},{9,10},{10,1... | collective-permute-start | bytes 393224 | tf_op jit(solution)/shard_map/ppermute | solution.py:206
  13.1 11.3 %collective-permute-start.4 = (bf16[64,1024]{1,0:T(8,128)(2,1)S(1)}, bf16[64,1024]{1,0:T(8,128)(2,1)S(1)}, u32[]{:S(2)}, u32[]{:S(2)}) collective-permute-start(bf16[64,1024]{1,0:T(8,128)(2,1)S(1)} %get-tuple-element.17), channel_id=1, source_target_pairs={{0,2},{1,3},{2,0},{3,1},{4,6},{5,7},{6,4},{7,5},{8,10},{9,11},{10,... | collective-permute-start | bytes 393224 | tf_op jit(solution)/shard_map/ppermute | solution.py:206
  16.2 8.2 %collective-permute-start.5 = (bf16[64,1024]{1,0:T(8,128)(2,1)S(1)}, bf16[64,1024]{1,0:T(8,128)(2,1)S(1)}, u32[]{:S(2)}, u32[]{:S(2)}) collective-permute-start(bf16[64,1024]{1,0:T(8,128)(2,1)S(1)} %get-tuple-element.18), channel_id=1, source_target_pairs={{0,3},{1,0},{2,1},{3,2},{4,7},{5,4},{6,5},{7,6},{8,11},{9,8},{10,9... | collective-permute-start | bytes 393224 | tf_op jit(solution)/shard_map/ppermute | solution.py:206

commit v4 on v3

--- a/solution.py
+++ b/solution.py
@@ -81,13 +81,13 @@
     dens = refs[:n_mu]
     t_hi, t_lo = refs[n_mu:n_mu + 2]
     outs = refs[n_mu + 2:2 * n_mu + 2]
-    d_hi, d_lo, w_hi, w_lo, turned = refs[2 * n_mu + 2:]
+    d_hi, d_lo, weights, turned = refs[2 * n_mu + 2:]
     z = lax.axis_index("mu")
     orb, lam_all = dens[0].shape
     lam = lam_all // n_mu
     slots = nu_slots.shape[2]
     row, col = iota((lam_all, 256), 0), iota((lam_all, 256), 1)
-    group = lax.rem(((col >> 3) & 3) + z, n_mu)
+    group = ((col >> 3) & 3) ^ z
     wanted = group * lam + (col >> 7) * 8 + (col & 7)
     choose = jnp.where(row == wanted, 1.0, 0.0).astype(BF16)
     for s in range(n_mu):
@@ -95,22 +95,27 @@
         d_hi[s] = jnp.dot(hi, choose, preferred_element_type=F32)
         d_lo[s] = jnp.dot(lo, choose, preferred_element_type=F32)
     orbital = (iota((orb, 256), 1) >> 5) & 3
+    depth = slots * 256
     for k in range(slots):
-        at = lax.rem(z - nu_slots[0, 0, k] + n_mu, n_mu)
+        at = z ^ nu_slots[0, 0, k]
         live = jnp.where(k < nu_count[0, 0], 1.0, 0.0)
         hi, lo = d_hi[at] * live, d_lo[at] * live
         for i in range(4):
-            rows = slice(k * 256 + i * orb, k * 256 + (i + 1) * orb)
-            w_hi[rows, :] = jnp.where(orbital == i, hi, 0.0).astype(BF16)
-            w_lo[rows, :] = jnp.where(orbital == i, lo, 0.0).astype(BF16)
+            rows = k * 256 + i * orb
+            w_hi = jnp.where(orbital == i, hi, 0.0).astype(BF16)
+            weights[rows:rows + orb, :] = w_hi
+            weights[rows + depth:rows + depth + orb, :] = w_hi
+            weights[rows + 2 * depth:rows + 2 * depth + orb, :] = jnp.where(
+                orbital == i, lo, 0.0
+            ).astype(BF16)
     aux_width = outs[0].shape[1] // lam
     per_group = 256 // aux_width
     span = per_group * 4
     for group in range(t_hi.shape[0] // 256):
         rows = slice(group * 256, (group + 1) * 256)
-        total = jnp.dot(t_hi[rows, :], w_hi[...], preferred_element_type=F32)
-        total += jnp.dot(t_lo[rows, :], w_hi[...], preferred_element_type=F32)
-        total += jnp.dot(t_hi[rows, :], w_lo[...], preferred_element_type=F32)
+        high = t_hi[rows, :]
+        left = jnp.concatenate([high, t_lo[rows, :], high], axis=1)
+        total = jnp.dot(left, weights[...], preferred_element_type=F32)
         for chunk in range(per_group):
             piece = total[chunk * aux_width:(chunk + 1) * aux_width]
             stacked = jnp.concatenate([piece[:, :128], piece[:, 128:]], axis=0)
@@ -131,7 +136,7 @@
     product += jnp.dot(left, m_lo[...], preferred_element_type=F32)
     orb = halves[0].shape[0]
     for s in range(n_mu):
-        block = lax.rem(z - s + n_mu, n_mu)
+        block = z ^ s
         total[pl.ds(pl.multiple_of(block * orb, orb), orb), :] = product[s * orb:(s + 1) * orb]
     rows = out.shape[1]
     lower = iota((rows, 128), 1) < 64
@@ -158,8 +163,10 @@
     orb, lam_all = density.shape
     slots, aux_width = three_center.shape[1:3]
     lam = lam_all // n_mu
-    turns = [[(z, (z + s) % n_mu) for z in range(n_mu)] for s in range(n_mu)]
-    dens = [density] + [lax.ppermute(density, "mu", turns[s]) for s in range(1, n_mu)]
+    turns = [[(z, z ^ s) for z in range(n_mu)] for s in range(n_mu)]
+    dens = [density] * n_mu
+    for s in (2, 3, 1):
+        dens[s] = lax.ppermute(density, "mu", turns[s])
     nu_slots, sig_slots = jnp.swapaxes(nu_slots, 1, 2), jnp.swapaxes(sig_slots, 1, 2)
     chunks = three_center.shape[3] // 256
     t_shape = jax.ShapeDtypeStruct((chunks * aux_width, slots * 256), BF16)
@@ -186,8 +193,7 @@
         scratch_shapes=[
             pltpu.VMEM((n_mu, orb, 256), F32),
             pltpu.VMEM((n_mu, orb, 256), F32),
-            pltpu.VMEM((slots * 256, 256), BF16),
-            pltpu.VMEM((slots * 256, 256), BF16),
+            pltpu.VMEM((3 * slots * 256, 256), BF16),
             pltpu.VMEM((chunks * 128, 128), F32),
         ],
         compiler_params=params(16),
@@ -203,7 +209,9 @@
         cost_estimate=pl.CostEstimate(flops=10_000_000, bytes_accessed=2_000_000, transcendentals=0),
         name="metric",
     )(sig_slots, sig_count, halves[0], metric_tensor)
-    halves = [halves[0]] + [lax.ppermute(halves[s], "mu", turns[s]) for s in range(1, n_mu)]
+    halves = list(halves)
+    for s in (3, 2, 1):
+        halves[s] = lax.ppermute(halves[s], "mu", turns[s])
     rows = n_mu * orb // n_aux
     parts = pl.pallas_call(
         functools.partial(exchange_kernel, n_mu, n_aux),

time: 39.6 us -> 39.8 us (level)
  waiting for transfers between devices: 6.49 us -> 8.87 us
  blocking collectives: 13.8 us -> 12.4 us
  starting transfers between devices: 10.9 us -> 10.1 us
    ppermute x6, waiting for transfers between devices: 6.49 us -> 8.87 us  [the longest x3 5.61 us: fast(): halves[s] = lax.ppermute(halves[s], 'mu', turns[s])]
    all_to_all x1, blocking collectives: 13.8 us -> 12.4 us  [fast(): parts = lax.all_to_all(parts, ('aux', 'mu'), 0, 0)]
    ppermute x6, starting transfers between devices: 10.9 us -> 10.1 us  [the longest x3 5.62 us: fast(): dens[s] = lax.ppermute(density, 'mu', turns[s])]
  transfers between devices with their start and end apart: 6 -> 6, of which waited for: 3 -> 3; matrix products, arithmetic and copies ran while one was open for 0% -> 0% of each run, Pallas kernels for 8% -> 7%
where the time goes in v4:
time: 39.8 us; the launch traced here: 39.7 us
  blocking collectives  12.4 us (31%)
  starting transfers between devices  10.1 us (25%)
  waiting for transfers between devices  8.87 us (22%)
  Pallas kernels  6.89 us (17%)
  between operations  1.4 us (4%)
    all_to_all x1, blocking collectives, fast(): parts = lax.all_to_all(parts, ('aux', 'mu'), 0, 0)  12.4 us
    ppermute x3, starting transfers between devices, fast(): dens[s] = lax.ppermute(density, 'mu', turns[s])  5.62 us
    ppermute x3, waiting for transfers between devices, fast(): halves[s] = lax.ppermute(halves[s], 'mu', turns[s])  5.61 us
    ppermute x3, starting transfers between devices, fast(): halves[s] = lax.ppermute(halves[s], 'mu', turns[s])  4.44 us
    ppermute x3, waiting for transfers between devices, fast(): dens[s] = lax.ppermute(density, 'mu', turns[s])  3.26 us
    pallas_call x1, Pallas kernels, fast(): pl.pallas_call(functools.partial(half_kernel, n_mu), out_shape=(half_shap...  2.67 us
    pallas_call x1, Pallas kernels, fast(): pl.pallas_call(tensor_kernel, out_shape=(t_shape, t_shape), in_specs=[HBM...  1.97 us
    pallas_call x1, Pallas kernels, fast(): pl.pallas_call(metric_kernel, out_shape=(m_shape, m_shape), in_specs=[SME...  1 us
  transfers between devices with their start and end apart: 6, of which 3 were waited for; matrix products, arithmetic and copies ran while one was open for 0% of the time, Pallas kernels for 7%

profile of v4, /device:TPU:0, one launch (start us, length us, event | category | flops | bytes accessed | tf_op | source)
XLA Modules:
  0.0 39.7 jit_solution(4644515793873252138)
XLA Ops:
  0.0 3.0 %collective-permute-start = (f32[64,64]{1,0:T(8,128)}, f32[64,64]{1,0:T(8,128)S(1)}, u32[]{:S(2)}, u32[]{:S(2)}) collective-permute-start(f32[64,64]{1,0:T(8,128)} %refs_0_.1), channel_id=1, source_target_pairs={{0,1},{1,0},{2,3},{3,2},{4,5},{5,4},{6,7},{7,6},{8,9},{9,8},{10,11... | collective-permute-start | bytes 49160 | tf_op jit(solution)/shard_map/ppermute | solution.py:169
  3.0 2.6 %collective-permute-start.1 = (f32[64,64]{1,0:T(8,128)}, f32[64,64]{1,0:T(8,128)S(1)}, u32[]{:S(2)}, u32[]{:S(2)}) collective-permute-start(f32[64,64]{1,0:T(8,128)} %refs_0_.1), channel_id=1, source_target_pairs={{0,2},{1,3},{2,0},{3,1},{4,6},{5,7},{6,4},{7,5},{8,10},{9,11},{10,... | collective-permute-start | bytes 49160 | tf_op jit(solution)/shard_map/ppermute | solution.py:169
  5.6 0.0 collective-permute-start.2
  6.3 0.0 copy-start.2
  6.3 0.0 copy-start.3
  6.3 2.0 %tensor.2 = (bf16[1024,768]{1,0:T(8,128)(2,1)S(1)}, bf16[1024,768]{1,0:T(8,128)(2,1)S(1)}) custom-call(f32[1,3,64,4096]{3,2,1,0:T(8,128)} %tensor.3), custom_call_target="tpu_custom_call" | custom-call | flops 10000000 | bytes 6000000 | tf_op jit(solution)/shard_map/tensor/pallas_call | solution.py:174
  8.3 0.0 collective-permute-done.refs_1_
  8.3 0.4 collective-permute-done.1.refs_2_
  8.6 2.9 %collective-permute-done.2.refs_3_ = f32[64,64]{1,0:T(8,128)S(1)} collective-permute-done((f32[64,64]{1,0:T(8,128)}, f32[64,64]{1,0:T(8,128)S(1)}, u32[]{:S(2)}, u32[]{:S(2)}) %collective-permute-start.2) | collective-permute-done | bytes 16416 | tf_op jit(solution)/shard_map/ppermute | solution.py:169
  11.5 0.0 copy-done.2
  11.5 0.0 copy-done.3
  11.5 0.0 copy-start
  11.5 0.0 copy-start.1
  11.6 2.7 %half.1 = (bf16[64,1024]{1,0:T(8,128)(2,1)S(1)}, bf16[64,1024]{1,0:T(8,128)(2,1)S(1)}, bf16[64,1024]{1,0:T(8,128)(2,1)S(1)}, bf16[64,1024]{1,0:T(8,128)(2,1)S(1)}) custom-call(s32[1,1,3]{2,1,0:T(1,128)S(1)} %bitcast.3, s32[1,1]{1,0:T(1,128)S(6)} %copy.8.nu_count, f32[64,64]{1,0:T(8,128)S(1)} %copy-done.2, f32[64,64]{1,0:T(8,128)S(1)} %collective-permute-done.refs_1_, ...), custom_call_target="tpu_custom_call" | custom-call | flops 1200000000 | bytes 4000000 | tf_op jit(solution)/shard_map/half/pallas_call | solution.py:188
  14.2 0.1 collective-permute-start.3
  14.3 1.2 %collective-permute-start.4 = (bf16[64,1024]{1,0:T(8,128)(2,1)S(1)}, bf16[64,1024]{1,0:T(8,128)(2,1)S(1)}, u32[]{:S(2)}, u32[]{:S(2)}) collective-permute-start(bf16[64,1024]{1,0:T(8,128)(2,1)S(1)} %get-tuple-element.17), channel_id=1, source_target_pairs={{0,2},{1,3},{2,0},{3,1},{4,6},{5,7},{6,4},{7,5},{8,10},{9,11},{10,... | collective-permute-start | bytes 393224 | tf_op jit(solution)/shard_map/ppermute | solution.py:214
  15.5 3.2 %collective-permute-start.5 = (bf16[64,1024]{1,0:T(8,128)(2,1)S(1)}, bf16[64,1024]{1,0:T(8,128)(2,1)S(1)}, u32[]{:S(2)}, u32[]{:S(2)}) collective-permute-start(bf16[64,1024]{1,0:T(8,128)(2,1)S(1)} %get-tuple-element.18), channel_id=1, source_target_pairs={{0,3},{1,2},{2,1},{3,0},{4,7},{5,6},{6,5},{7,4},{8,11},{9,10},{10,... | collective-permute-start | bytes 393224 | tf_op jit(solution)/shard_map/ppermute | solution.py:214
  19.3 0.0 copy-done
  19.3 0.0 copy-done.1
  19.4 1.0 %metric.2 = (bf16[1024,256]{1,0:T(8,128)(2,1)S(1)}, bf16[1024,256]{1,0:T(8,128)(2,1)S(1)}) custom-call(s32[1,1,3]{2,1,0:T(1,128)S(1)} %bitcast.2, s32[1,1]{1,0:T(1,128)S(6)} %copy.9.sig_count, bf16[64,1024]{1,0:T(8,128)(2,1)S(1)} %get-tuple-element.15.after.refs_0_, f32[1,3,64,1024]{3,2,1,0:T(8,128)S(1)} %copy-done), custom_call_target="tpu_custom_call" | custom-call | flops 10000000 | bytes 2000000 | tf_op jit(solution)/shard_map/metric/pallas_call | solution.py:203
  20.4 0.0 collective-permute-done.3.refs_1_
  20.4 5.6 %collective-permute-done.4.refs_2_ = bf16[64,1024]{1,0:T(8,128)(2,1)S(1)} collective-permute-done((bf16[64,1024]{1,0:T(8,128)(2,1)S(1)}, bf16[64,1024]{1,0:T(8,128)(2,1)S(1)}, u32[]{:S(2)}, u32[]{:S(2)}) %collective-permute-start.4) | collective-permute-done | bytes 131104 | tf_op jit(solution)/shard_map/ppermute | solution.py:214
  26.0 0.0 collective-permute-done.5.refs_3_
  26.0 0.5 %exchange.1 = bf16[32,16,128]{2,1,0:T(8,128)(2,1)S(1)} custom-call(bf16[64,1024]{1,0:T(8,128)(2,1)S(1)} %get-tuple-element.15.after.refs_0_, bf16[64,1024]{1,0:T(8,128)(2,1)S(1)} %collective-permute-done.3.refs_1_, bf16[64,1024]{1,0:T(8,128)(2,1)S(1)} %collective-permute-done.4.refs_2_, bf16[64,1024]{1,0:T(8,128)(2,1)S(1)} %collective-permute-done.5.refs_3_, ...), custom_call_target="tpu_custom_call" | custom-call | flops 300000000 | bytes 2000000 | tf_op jit(solution)/shard_map/exchange/pallas_call | solution.py:216
  26.5 12.4 %all_to_all.5.parts = bf16[32,16,128]{2,1,0:T(8,128)(2,1)S(1)} all-to-all(bf16[32,16,128]{2,1,0:T(8,128)(2,1)S(1)} %exchange.1), channel_id=1, replica_groups=mesh['aux'=8,'mu'=4] {'aux','mu'}, dimensions={0} | all-to-all | bytes 262144 | tf_op jit(solution)/shard_map/all_to_all | solution.py:226
  39.0 0.7 %sum.1 = f32[32,64]{1,0:T(8,128)} custom-call(bf16[32,16,128]{2,1,0:T(8,128)(2,1)S(1)} %all_to_all.5.parts), custom_call_target="tpu_custom_call" | custom-call | tf_op jit(solution)/shard_map/sum/pallas_call | solution.py:227
Async XLA Ops:
  0.0 8.3 %collective-permute-start = (f32[64,64]{1,0:T(8,128)}, f32[64,64]{1,0:T(8,128)S(1)}, u32[]{:S(2)}, u32[]{:S(2)}) collective-permute-start(f32[64,64]{1,0:T(8,128)} %refs_0_.1), channel_id=1, source_target_pairs={{0,1},{1,0},{2,3},{3,2},{4,5},{5,4},{6,7},{7,6},{8,9},{9,8},{10,11... | collective-permute-start | bytes 49160 | tf_op jit(solution)/shard_map/ppermute | solution.py:169
  3.0 5.6 %collective-permute-start.1 = (f32[64,64]{1,0:T(8,128)}, f32[64,64]{1,0:T(8,128)S(1)}, u32[]{:S(2)}, u32[]{:S(2)}) collective-permute-start(f32[64,64]{1,0:T(8,128)} %refs_0_.1), channel_id=1, source_target_pairs={{0,2},{1,3},{2,0},{3,1},{4,6},{5,7},{6,4},{7,5},{8,10},{9,11},{10,... | collective-permute-start | bytes 49160 | tf_op jit(solution)/shard_map/ppermute | solution.py:169
  5.6 5.9 %collective-permute-start.2 = (f32[64,64]{1,0:T(8,128)}, f32[64,64]{1,0:T(8,128)S(1)}, u32[]{:S(2)}, u32[]{:S(2)}) collective-permute-start(f32[64,64]{1,0:T(8,128)} %refs_0_.1), channel_id=1, source_target_pairs={{0,3},{1,2},{2,1},{3,0},{4,7},{5,6},{6,5},{7,4},{8,11},{9,10},{10,... | collective-permute-start | bytes 49160 | tf_op jit(solution)/shard_map/ppermute | solution.py:169
  6.3 5.3 %copy-start.2 = (f32[64,64]{1,0:T(8,128)S(1)}, f32[64,64]{1,0:T(8,128)}, u32[]{:S(2)}) copy-start(f32[64,64]{1,0:T(8,128)} %refs_0_.1) | copy-start | bytes 49156
  6.3 5.3 %copy-start.3 = (s32[1,3,1]{1,2,0:T(1,128)S(1)}, s32[1,3,1]{1,2,0:T(1,128)}, u32[]{:S(2)}) copy-start(s32[1,3,1]{1,2,0:T(1,128)} %param.8) | copy-start | bytes 40
  11.5 7.8 %copy-start = (f32[1,3,64,1024]{3,2,1,0:T(8,128)S(1)}, f32[1,3,64,1024]{3,2,1,0:T(8,128)}, u32[]{:S(2)}) copy-start(f32[1,3,64,1024]{3,2,1,0:T(8,128)} %metric.3) | copy-start | bytes 2359300
  11.5 7.8 %copy-start.1 = (s32[1,3,1]{1,2,0:T(1,128)S(1)}, s32[1,3,1]{1,2,0:T(1,128)}, u32[]{:S(2)}) copy-start(s32[1,3,1]{1,2,0:T(1,128)} %param.12) | copy-start | bytes 40
  14.2 6.1 %collective-permute-start.3 = (bf16[64,1024]{1,0:T(8,128)(2,1)S(1)}, bf16[64,1024]{1,0:T(8,128)(2,1)S(1)}, u32[]{:S(2)}, u32[]{:S(2)}) collective-permute-start(bf16[64,1024]{1,0:T(8,128)(2,1)S(1)} %get-tuple-element.16), channel_id=1, source_target_pairs={{0,1},{1,0},{2,3},{3,2},{4,5},{5,4},{6,7},{7,6},{8,9},{9,8},{10,11... | collective-permute-start | bytes 393224 | tf_op jit(solution)/shard_map/ppermute | solution.py:214
  14.3 11.7 %collective-permute-start.4 = (bf16[64,1024]{1,0:T(8,128)(2,1)S(1)}, bf16[64,1024]{1,0:T(8,128)(2,1)S(1)}, u32[]{:S(2)}, u32[]{:S(2)}) collective-permute-start(bf16[64,1024]{1,0:T(8,128)(2,1)S(1)} %get-tuple-element.17), channel_id=1, source_target_pairs={{0,2},{1,3},{2,0},{3,1},{4,6},{5,7},{6,4},{7,5},{8,10},{9,11},{10,... | collective-permute-start | bytes 393224 | tf_op jit(solution)/shard_map/ppermute | solution.py:214
  15.5 10.5 %collective-permute-start.5 = (bf16[64,1024]{1,0:T(8,128)(2,1)S(1)}, bf16[64,1024]{1,0:T(8,128)(2,1)S(1)}, u32[]{:S(2)}, u32[]{:S(2)}) collective-permute-start(bf16[64,1024]{1,0:T(8,128)(2,1)S(1)} %get-tuple-element.18), channel_id=1, source_target_pairs={{0,3},{1,2},{2,1},{3,0},{4,7},{5,6},{6,5},{7,4},{8,11},{9,10},{10,... | collective-permute-start | bytes 393224 | tf_op jit(solution)/shard_map/ppermute | solution.py:214

commit v5 on v4

--- a/solution.py
+++ b/solution.py
@@ -52,11 +52,17 @@
             t_lo[at:at + aux_width, k * 256:(k + 1) * 256] = lo
 
 
-def metric_kernel(sig_slots, sig_count, after, metric, m_hi, m_lo):
+def live_targets(sig_slots, sig_count):
+    return [
+        jnp.where(q < sig_count[0, 0], sig_slots[0, 0, q], -1).astype(F32)
+        for q in range(sig_slots.shape[2])
+    ]
+
+
+def place(targets, metric, m_hi, m_lo):
     _, sig, aux_width, width = metric.shape
     half = iota((aux_width, 128), 1) >= 64
-    pair_of = jnp.where(half, 1, 0)
-    targets = [jnp.where(q < sig_count[0, 0], sig_slots[0, 0, q], -1) for q in range(sig)]
+    pair_of = jnp.where(half, 1.0, 0.0)
     for pair in range(width // 128):
         sums = [[jnp.zeros((aux_width, 128), F32) for _ in range(2)] for _ in range(2)]
         for q in range(sig):
@@ -77,11 +83,46 @@
                 m_lo[at:at + aux_width, columns] = lo
 
 
-def half_kernel(n_mu, nu_slots, nu_count, *refs):
+def product(halves, rows, m_hi, m_lo):
+    left = jnp.concatenate([h[:rows, :] for h in halves], axis=0)
+    total = jnp.dot(left, m_hi[...], preferred_element_type=F32)
+    return total + jnp.dot(left, m_lo[...], preferred_element_type=F32)
+
+
+def metric_kernel(n_mu, slots, count, received, metric, metric_other, *refs):
+    near = refs[:n_mu]
+    total, m_hi, m_lo, own_hi, own_lo = refs[n_mu:]
+    note = received[received.shape[0] - 16:, :128].astype(F32)
+    targets = [note[q:q + 1, :] for q in range(slots.shape[2])]
+    place(targets, metric_other, m_hi, m_lo)
+    place(live_targets(slots, count), metric, own_hi, own_lo)
+    total[...] = product(near, near[0].shape[0], own_hi, own_lo)
+
+
+def contract(first, weights, t_hi, t_lo, outs, turned):
+    span = outs[1].shape[0] // 2
+    aux_width = 1024 // span
+    for group in range(2):
+        rows = pl.ds(pl.multiple_of(first + group * 256, 256), 256)
+        high = t_hi[rows, :]
+        left = jnp.concatenate([high, t_lo[rows, :], high], axis=1)
+        total = jnp.dot(left, weights[...], preferred_element_type=F32)
+        for chunk in range(256 // aux_width):
+            piece = total[chunk * aux_width:(chunk + 1) * aux_width]
+            stacked = jnp.concatenate([piece[:, :128], piece[:, 128:]], axis=0)
+            at = group * span * 32 + chunk * 128
+            turned[at:at + 128, :] = stacked.T
+        for s in range(len(outs)):
+            for r in range(8):
+                picked = turned[pl.ds(group * span * 32 + s * 8 + r, span, stride=32), :]
+                outs[s][group * span:(group + 1) * span, r * 128:(r + 1) * 128] = picked.astype(BF16)
+
+
+def near_kernel(n_mu, nu_slots, nu_count, after, *refs):
     dens = refs[:n_mu]
     t_hi, t_lo = refs[n_mu:n_mu + 2]
     outs = refs[n_mu + 2:2 * n_mu + 2]
-    d_hi, d_lo, weights, turned = refs[2 * n_mu + 2:]
+    weights, d_hi, d_lo, turned = refs[2 * n_mu + 2:]
     z = lax.axis_index("mu")
     orb, lam_all = dens[0].shape
     lam = lam_all // n_mu
@@ -108,44 +149,38 @@
             weights[rows + 2 * depth:rows + 2 * depth + orb, :] = jnp.where(
                 orbital == i, lo, 0.0
             ).astype(BF16)
-    aux_width = outs[0].shape[1] // lam
-    per_group = 256 // aux_width
-    span = per_group * 4
-    for group in range(t_hi.shape[0] // 256):
-        rows = slice(group * 256, (group + 1) * 256)
-        high = t_hi[rows, :]
-        left = jnp.concatenate([high, t_lo[rows, :], high], axis=1)
-        total = jnp.dot(left, weights[...], preferred_element_type=F32)
-        for chunk in range(per_group):
-            piece = total[chunk * aux_width:(chunk + 1) * aux_width]
-            stacked = jnp.concatenate([piece[:, :128], piece[:, 128:]], axis=0)
-            at = (group * per_group + chunk) * 128
-            turned[at:at + 128, :] = stacked.T
-        for s in range(n_mu):
-            for r in range(8):
-                picked = turned[pl.ds(group * per_group * 128 + s * 8 + r, span, stride=32), :]
-                outs[s][group * span:(group + 1) * span, r * 128:(r + 1) * 128] = picked.astype(BF16)
-
-
-def exchange_kernel(n_mu, n_aux, *refs):
-    halves = refs[:n_mu]
+    core = lax.axis_index("aux") & 1
+    contract(core * 512, weights, t_hi, t_lo, outs, turned)
+
+
+def far_kernel(sig_slots, sig_count, weights, t_hi, t_lo, *refs):
+    outs, turned = refs[:-1], refs[-1]
+    core = lax.axis_index("aux") & 1
+    contract((1 - core) * 512, weights, t_hi, t_lo, outs, turned)
+    shape = (16, outs[0].shape[1])
+    note = jnp.full(shape, -1.0, F32)
+    for q, target in enumerate(live_targets(sig_slots, sig_count)):
+        note = jnp.where(iota(shape, 0) == q, target, note)
+    outs[0][outs[0].shape[0] - 16:, :] = note.astype(BF16)
+
+
+def exchange_kernel(n_mu, n_chip, near_total, *refs):
+    far = refs[:n_mu]
     m_hi, m_lo, out, total = refs[n_mu:]
     z = lax.axis_index("mu")
-    left = jnp.concatenate([h[...] for h in halves], axis=0)
-    product = jnp.dot(left, m_hi[...], preferred_element_type=F32)
-    product += jnp.dot(left, m_lo[...], preferred_element_type=F32)
-    orb = halves[0].shape[0]
+    orb_half = far[1].shape[0]
+    whole = near_total[...] + product(far, orb_half, m_hi, m_lo)
     for s in range(n_mu):
-        block = z ^ s
-        total[pl.ds(pl.multiple_of(block * orb, orb), orb), :] = product[s * orb:(s + 1) * orb]
+        at = pl.multiple_of((z ^ s) * orb_half, orb_half)
+        total[pl.ds(at, orb_half), :] = whole[s * orb_half:(s + 1) * orb_half]
     rows = out.shape[1]
     lower = iota((rows, 128), 1) < 64
-    for a in range(n_aux):
+    for c in range(n_chip):
         for pair in range(n_mu // 2):
             columns = slice(pair * 128, (pair + 1) * 128)
-            top = total[a * 2 * rows:(a * 2 + 1) * rows, columns]
-            bottom = total[(a * 2 + 1) * rows:(a * 2 + 2) * rows, columns]
-            at = a * n_mu + pair * 2
+            top = total[c * 2 * rows:(c * 2 + 1) * rows, columns]
+            bottom = total[(c * 2 + 1) * rows:(c * 2 + 2) * rows, columns]
+            at = c * n_mu + pair * 2
             out[at] = jnp.where(lower, top, pltpu.roll(bottom, 64, 1)).astype(BF16)
             out[at + 1] = jnp.where(lower, pltpu.roll(top, 64, 1), bottom).astype(BF16)
 
@@ -163,14 +198,17 @@
     orb, lam_all = density.shape
     slots, aux_width = three_center.shape[1:3]
     lam = lam_all // n_mu
+    both = ("aux", "mu")
     turns = [[(z, z ^ s) for z in range(n_mu)] for s in range(n_mu)]
-    dens = [density] * n_mu
-    for s in (2, 3, 1):
-        dens[s] = lax.ppermute(density, "mu", turns[s])
+    cross = [
+        [(a * n_mu + z, (a ^ 1) * n_mu + (z ^ s)) for a in range(n_aux) for z in range(n_mu)]
+        for s in range(n_mu)
+    ]
     nu_slots, sig_slots = jnp.swapaxes(nu_slots, 1, 2), jnp.swapaxes(sig_slots, 1, 2)
+    dens = [density] + [lax.ppermute(density, "mu", turns[s]) for s in range(1, n_mu)]
+    metric_other = lax.ppermute(metric_tensor, both, cross[0])
     chunks = three_center.shape[3] // 256
     t_shape = jax.ShapeDtypeStruct((chunks * aux_width, slots * 256), BF16)
-    m_shape = jax.ShapeDtypeStruct((lam * aux_width, n_mu * orb), BF16)
     t_hi, t_lo = pl.pallas_call(
         tensor_kernel,
         out_shape=(t_shape, t_shape),
@@ -184,46 +222,61 @@
         cost_estimate=pl.CostEstimate(flops=10_000_000, bytes_accessed=6_000_000, transcendentals=0),
         name="tensor",
     )(three_center)
-    half_shape = jax.ShapeDtypeStruct((orb, lam * aux_width), BF16)
-    halves = pl.pallas_call(
-        functools.partial(half_kernel, n_mu),
-        out_shape=(half_shape,) * n_mu,
-        in_specs=[SMEM, SMEM] + [VMEM] * (n_mu + 2),
-        out_specs=(VMEM,) * n_mu,
+    half_shape = jax.ShapeDtypeStruct((orb // 2, lam * aux_width), BF16)
+    *near, weights = pl.pallas_call(
+        functools.partial(near_kernel, n_mu),
+        out_shape=(half_shape,) * n_mu + (jax.ShapeDtypeStruct((3 * slots * 256, 256), BF16),),
+        in_specs=[SMEM, SMEM, ANY] + [VMEM] * (n_mu + 2),
+        out_specs=(VMEM,) * (n_mu + 1),
         scratch_shapes=[
             pltpu.VMEM((n_mu, orb, 256), F32),
             pltpu.VMEM((n_mu, orb, 256), F32),
-            pltpu.VMEM((3 * slots * 256, 256), BF16),
-            pltpu.VMEM((chunks * 128, 128), F32),
+            pltpu.VMEM((chunks * 64, 128), F32),
         ],
         compiler_params=params(16),
-        cost_estimate=pl.CostEstimate(flops=1_200_000_000, bytes_accessed=4_000_000, transcendentals=0),
-        name="half",
-    )(nu_slots, nu_count, *dens, t_hi, t_lo)
-    m_hi, m_lo = pl.pallas_call(
-        metric_kernel,
-        out_shape=(m_shape, m_shape),
-        in_specs=[SMEM, SMEM, ANY, VMEM],
-        out_specs=(VMEM, VMEM),
+        cost_estimate=pl.CostEstimate(flops=600_000_000, bytes_accessed=4_000_000, transcendentals=0),
+        name="near",
+    )(nu_slots, nu_count, metric_other, *dens, t_hi, t_lo)
+    note_shape = jax.ShapeDtypeStruct((orb // 2 + 16, lam * aux_width), BF16)
+    far = pl.pallas_call(
+        far_kernel,
+        out_shape=(note_shape,) + (half_shape,) * (n_mu - 1),
+        in_specs=[SMEM, SMEM] + [VMEM] * 3,
+        out_specs=(VMEM,) * n_mu,
+        scratch_shapes=[pltpu.VMEM((chunks * 64, 128), F32)],
         compiler_params=params(16),
-        cost_estimate=pl.CostEstimate(flops=10_000_000, bytes_accessed=2_000_000, transcendentals=0),
+        cost_estimate=pl.CostEstimate(flops=600_000_000, bytes_accessed=4_000_000, transcendentals=0),
+        name="far",
+    )(sig_slots, sig_count, weights, t_hi, t_lo)
+    near = [near[0]] + [lax.ppermute(near[s], "mu", turns[s]) for s in range(1, n_mu)]
+    far = [lax.ppermute(far[s], both, cross[s]) for s in range(n_mu)]
+    m_shape = jax.ShapeDtypeStruct((lam * aux_width, n_mu * orb), BF16)
+    near_total, m_hi, m_lo = pl.pallas_call(
+        functools.partial(metric_kernel, n_mu),
+        out_shape=(jax.ShapeDtypeStruct((n_mu * orb // 2, n_mu * orb), F32), m_shape, m_shape),
+        in_specs=[SMEM, SMEM] + [VMEM] * (n_mu + 3),
+        out_specs=(VMEM,) * 3,
+        scratch_shapes=[pltpu.VMEM(m_shape.shape, BF16)] * 2,
+        compiler_params=params(16),
+        cost_estimate=pl.CostEstimate(flops=10_000_000, bytes_accessed=4_000_000, transcendentals=0),
         name="metric",
-    )(sig_slots, sig_count, halves[0], metric_tensor)
-    halves = list(halves)
-    for s in (3, 2, 1):
-        halves[s] = lax.ppermute(halves[s], "mu", turns[s])
+    )(sig_slots, sig_count, far[0], metric_tensor, metric_other, *near)
     rows = n_mu * orb // n_aux
+    n_chip = n_aux // 2
     parts = pl.pallas_call(
-        functools.partial(exchange_kernel, n_mu, n_aux),
-        out_shape=jax.ShapeDtypeStruct((n_aux * n_mu, rows // 2, 128), BF16),
-        in_specs=[VMEM] * (n_mu + 2),
+        functools.partial(exchange_kernel, n_mu, n_chip),
+        out_shape=jax.ShapeDtypeStruct((n_chip * n_mu, rows // 2, 128), BF16),
+        in_specs=[VMEM] * (n_mu + 3),
         out_specs=VMEM,
-        scratch_shapes=[pltpu.VMEM((n_mu * orb, n_mu * orb), F32)],
+        scratch_shapes=[pltpu.VMEM((n_mu * orb // 2, n_mu * orb), F32)],
         compiler_params=params(16),
         cost_estimate=pl.CostEstimate(flops=300_000_000, bytes_accessed=2_000_000, transcendentals=0),
         name="exchange",
-    )(*halves, m_hi, m_lo)
-    parts = lax.all_to_all(parts, ("aux", "mu"), 0, 0)
+    )(near_total, *far, m_hi, m_lo)
+    same_core = [
+        [(c * 2 + h) * n_mu + z for c in range(n_chip) for z in range(n_mu)] for h in range(2)
+    ]
+    parts = lax.all_to_all(parts, both, 0, 0, axis_index_groups=same_core)
     return pl.pallas_call(
         sum_kernel,
         out_shape=jax.ShapeDtypeStruct((rows, orb), F32),

time: 39.8 us -> 42.6 us (1.070)
  starting transfers between devices: 10.1 us -> 14.1 us
  waiting for transfers between devices: 8.87 us -> 4.94 us
  blocking collectives: 12.4 us -> 13.8 us
  Pallas kernels: 6.89 us -> 8.22 us
    ppermute x6 -> x11, starting transfers between devices: 10.1 us -> 14.1 us  [the longest x3 5.17 us: fast(): lax.ppermute(density, 'mu', turns[s])]
    ppermute x6 -> x11, waiting for transfers between devices: 8.87 us -> 4.94 us  [the longest x3 2.61 us: fast(): lax.ppermute(density, 'mu', turns[s])]
    pallas_call x3 -> x4, Pallas kernels: 4.21 us -> 5.55 us  [the longest x1 1.94 us: fast(): pl.pallas_call(functools.partial(near_kernel, n_mu), out_shape=(half_shap...]
    all_to_all x1, blocking collectives: 12.4 us -> 13.8 us  [fast(): parts = lax.all_to_all(parts, both, 0, 0, axis_index_groups=same_core)]
  transfers between devices with their start and end apart: 6 -> 11, of which waited for: 3 -> 4; matrix products, arithmetic and copies ran while one was open for 0% -> 0% of each run, Pallas kernels for 7% -> 12%
where the time goes in v5:
time: 42.6 us; the launch traced here: 42.4 us
  starting transfers between devices  14.1 us (33%)
  blocking collectives  13.8 us (32%)
  Pallas kernels  8.22 us (19%)
  waiting for transfers between devices  4.94 us (12%)
  between operations  1.41 us (3%)
    all_to_all x1, blocking collectives, fast(): parts = lax.all_to_all(parts, both, 0, 0, axis_index_groups=same_core)  13.8 us
    ppermute x3, starting transfers between devices, fast(): lax.ppermute(density, 'mu', turns[s])  5.17 us
    ppermute x3, starting transfers between devices, fast(): lax.ppermute(near[s], 'mu', turns[s])  4.51 us
    ppermute x4, starting transfers between devices, fast(): far = [lax.ppermute(far[s], both, cross[s]) for s in range(n_mu)]  3.95 us
    ppermute x3, waiting for transfers between devices, fast(): lax.ppermute(density, 'mu', turns[s])  2.61 us
    ppermute x4, waiting for transfers between devices, fast(): far = [lax.ppermute(far[s], both, cross[s]) for s in range(n_mu)]  2.07 us
    pallas_call x1, Pallas kernels, fast(): pl.pallas_call(tensor_kernel, out_shape=(t_shape, t_shape), in_specs=[HBM...  1.97 us
    pallas_call x1, Pallas kernels, fast(): pl.pallas_call(functools.partial(near_kernel, n_mu), out_shape=(half_shap...  1.94 us
  transfers between devices with their start and end apart: 11, of which 4 were waited for; matrix products, arithmetic and copies ran while one was open for 0% of the time, Pallas kernels for 12%

profile of v5, /device:TPU:0, one launch (start us, length us, event | category | flops | bytes accessed | tf_op | source)
XLA Modules:
  0.0 42.4 jit_solution(10002754145639020429)
XLA Ops:
  0.0 0.5 %collective-permute-start = (f32[1,3,64,1024]{3,2,1,0:T(8,128)}, f32[1,3,64,1024]{3,2,1,0:T(8,128)S(1)}, u32[]{:S(2)}, u32[]{:S(2)}) collective-permute-start(f32[1,3,64,1024]{3,2,1,0:T(8,128)} %metric.3), channel_id=1, source_target_pairs={{0,4},{1,5},{2,6},{3,7},{4,0},{5,1},{6,2},{7,3},{8,12},{9,13},{10,... | collective-permute-start | bytes 2359304 | tf_op jit(solution)/shard_map/ppermute | solution.py:209
  0.5 3.6 %collective-permute-start.2 = (f32[64,64]{1,0:T(8,128)}, f32[64,64]{1,0:T(8,128)S(1)}, u32[]{:S(2)}, u32[]{:S(2)}) collective-permute-start(f32[64,64]{1,0:T(8,128)} %refs_0_.1), channel_id=1, source_target_pairs={{0,2},{1,3},{2,0},{3,1},{4,6},{5,7},{6,4},{7,5},{8,10},{9,11},{10,... | collective-permute-start | bytes 49160 | tf_op jit(solution)/shard_map/ppermute | solution.py:208
  4.0 1.6 %collective-permute-start.1 = (f32[64,64]{1,0:T(8,128)}, f32[64,64]{1,0:T(8,128)S(1)}, u32[]{:S(2)}, u32[]{:S(2)}) collective-permute-start(f32[64,64]{1,0:T(8,128)} %refs_0_.1), channel_id=1, source_target_pairs={{0,1},{1,0},{2,3},{3,2},{4,5},{5,4},{6,7},{7,6},{8,9},{9,8},{10,11... | collective-permute-start | bytes 49160 | tf_op jit(solution)/shard_map/ppermute | solution.py:208
  5.6 0.0 collective-permute-start.3
  6.9 0.0 copy-start.1
  6.9 0.0 copy-start.3
  6.9 2.0 %tensor.2 = (bf16[1024,768]{1,0:T(8,128)(2,1)S(1)}, bf16[1024,768]{1,0:T(8,128)(2,1)S(1)}) custom-call(f32[1,3,64,4096]{3,2,1,0:T(8,128)} %tensor.3), custom_call_target="tpu_custom_call" | custom-call | flops 10000000 | bytes 6000000 | tf_op jit(solution)/shard_map/tensor/pallas_call | solution.py:212
  8.9 0.0 collective-permute-done.2.refs_2_
  8.9 0.0 collective-permute-done.1.refs_1_
  8.9 2.6 %collective-permute-done.3.refs_3_ = f32[64,64]{1,0:T(8,128)S(1)} collective-permute-done((f32[64,64]{1,0:T(8,128)}, f32[64,64]{1,0:T(8,128)S(1)}, u32[]{:S(2)}, u32[]{:S(2)}) %collective-permute-start.3) | collective-permute-done | bytes 16416 | tf_op jit(solution)/shard_map/ppermute | solution.py:208
  11.5 0.0 collective-permute-done.after.metric_other
  11.5 0.0 copy-done.1
  11.5 0.0 copy-done.3
  11.6 0.0 copy-start.2
  11.6 1.9 %near.1 = (bf16[32,1024]{1,0:T(8,128)(2,1)S(1)}, bf16[32,1024]{1,0:T(8,128)(2,1)S(1)}, bf16[32,1024]{1,0:T(8,128)(2,1)S(1)}, bf16[32,1024]{1,0:T(8,128)(2,1)S(1)}, bf16[2304,256]{1,0:T(8,128)(2,1)S(1)}) custom-call(s32[1,1,3]{2,1,0:T(1,128)S(1)} %bitcast.4, s32[1,1]{1,0:T(1,128)S(6)} %copy.8.nu_count, ...), custom_call_target="tpu_custom_call" | custom-call | flops 600000000 | bytes 4000000 | tf_op jit(solution)/shard_map/near/pallas_call | solution.py:226
  13.5 0.1 collective-permute-start.5
  13.6 1.8 %collective-permute-start.6 = (bf16[32,1024]{1,0:T(8,128)(2,1)S(1)}, bf16[32,1024]{1,0:T(8,128)(2,1)S(1)}, u32[]{:S(2)}, u32[]{:S(2)}) collective-permute-start(bf16[32,1024]{1,0:T(8,128)(2,1)S(1)} %get-tuple-element.25), channel_id=1, source_target_pairs={{0,2},{1,3},{2,0},{3,1},{4,6},{5,7},{6,4},{7,5},{8,10},{9,11},{10,... | collective-permute-start | bytes 196616 | tf_op jit(solution)/shard_map/ppermute | solution.py:251
  15.4 0.0 copy-done.2
  15.4 0.0 copy-start
  15.4 1.7 %far.1 = (bf16[48,1024]{1,0:T(8,128)(2,1)S(1)}, bf16[32,1024]{1,0:T(8,128)(2,1)S(1)}, bf16[32,1024]{1,0:T(8,128)(2,1)S(1)}, bf16[32,1024]{1,0:T(8,128)(2,1)S(1)}) custom-call(s32[1,1,3]{2,1,0:T(1,128)S(1)} %bitcast.2, s32[1,1]{1,0:T(1,128)S(6)} %copy.9.sig_count.count, bf16[2304,256]{1,0:T(8,128)(2,1)S(1)} %get-tuple-element.21.weights, ...), custom_call_target="tpu_custom_call" | custom-call | flops 600000000 | bytes 4000000 | tf_op jit(solution)/shard_map/far/pallas_call | solution.py:241
  17.1 0.1 collective-permute-start.4
  17.2 2.6 %collective-permute-start.7 = (bf16[32,1024]{1,0:T(8,128)(2,1)S(1)}, bf16[32,1024]{1,0:T(8,128)(2,1)S(1)}, u32[]{:S(2)}, u32[]{:S(2)}) collective-permute-start(bf16[32,1024]{1,0:T(8,128)(2,1)S(1)} %get-tuple-element.26), channel_id=1, source_target_pairs={{0,3},{1,2},{2,1},{3,0},{4,7},{5,6},{6,5},{7,4},{8,11},{9,10},{10,... | collective-permute-start | bytes 196616 | tf_op jit(solution)/shard_map/ppermute | solution.py:251
  19.8 0.0 collective-permute-start.8
  19.8 0.0 collective-permute-done.5.refs_1_
  19.8 1.5 %collective-permute-start.9 = (bf16[32,1024]{1,0:T(8,128)(2,1)S(1)}, bf16[32,1024]{1,0:T(8,128)(2,1)S(1)}, u32[]{:S(2)}, u32[]{:S(2)}) collective-permute-start(bf16[32,1024]{1,0:T(8,128)(2,1)S(1)} %get-tuple-element.29), channel_id=1, source_target_pairs={{0,6},{1,7},{2,4},{3,5},{4,2},{5,3},{6,0},{7,1},{8,14},{9,15},{10,... | collective-permute-start | bytes 196616 | tf_op jit(solution)/shard_map/ppermute | solution.py:252
  21.4 0.0 collective-permute-done.6.refs_2_
  21.4 2.3 %collective-permute-start.10 = (bf16[32,1024]{1,0:T(8,128)(2,1)S(1)}, bf16[32,1024]{1,0:T(8,128)(2,1)S(1)}, u32[]{:S(2)}, u32[]{:S(2)}) collective-permute-start(bf16[32,1024]{1,0:T(8,128)(2,1)S(1)} %get-tuple-element.30), channel_id=1, source_target_pairs={{0,7},{1,6},{2,5},{3,4},{4,3},{5,2},{6,1},{7,0},{8,15},{9,14},{10,... | collective-permute-start | bytes 196616 | tf_op jit(solution)/shard_map/ppermute | solution.py:252
  23.7 0.3 collective-permute-done.7.refs_3_
  24.0 0.0 collective-permute-done.4.received.refs_0_
  24.0 0.0 copy-done
  24.0 1.5 %metric.2 = (f32[128,256]{1,0:T(8,128)S(1)}, bf16[1024,256]{1,0:T(8,128)(2,1)S(1)}, bf16[1024,256]{1,0:T(8,128)(2,1)S(1)}) custom-call(s32[1,1,3]{2,1,0:T(1,128)S(1)} %bitcast.3, s32[1,1]{1,0:T(1,128)S(6)} %copy.9.sig_count.count, bf16[48,1024]{1,0:T(8,128)(2,1)S(1)} %collective-permute-done.4.received.refs_0_, f32[1,3,64,1024]{3,2,1,0:T(8,128)S(1)} %copy-done, ...), custom_call_target="tpu_custom_call" | custom-call | flops 10000000 | bytes 4000000 | tf_op jit(solution)/shard_map/metric/pallas_call | solution.py:254
  25.5 0.5 %collective-permute-done.8.refs_1_ = bf16[32,1024]{1,0:T(8,128)(2,1)S(1)} collective-permute-done((bf16[32,1024]{1,0:T(8,128)(2,1)S(1)}, bf16[32,1024]{1,0:T(8,128)(2,1)S(1)}, u32[]{:S(2)}, u32[]{:S(2)}) %collective-permute-start.8) | collective-permute-done | bytes 65568 | tf_op jit(solution)/shard_map/ppermute | solution.py:252
  26.0 0.0 collective-permute-done.9.refs_2_
  26.0 1.5 %collective-permute-done.10.refs_3_ = bf16[32,1024]{1,0:T(8,128)(2,1)S(1)} collective-permute-done((bf16[32,1024]{1,0:T(8,128)(2,1)S(1)}, bf16[32,1024]{1,0:T(8,128)(2,1)S(1)}, u32[]{:S(2)}, u32[]{:S(2)}) %collective-permute-start.10) | collective-permute-done | bytes 65568 | tf_op jit(solution)/shard_map/ppermute | solution.py:252
  27.6 0.4 exchange.1
  28.0 13.8 %all_to_all.5.parts = bf16[16,16,128]{2,1,0:T(8,128)(2,1)S(1)} all-to-all(bf16[16,16,128]{2,1,0:T(8,128)(2,1)S(1)} %exchange.1), channel_id=1, replica_groups={{0,1,2,3,8,9,10,11,16,17,18,19,24,25,26,27},{4,5,6,7,12,13,14,15,20,21,..., dimensions={0} | all-to-all | bytes 131072 | tf_op jit(solution)/shard_map/all_to_all | solution.py:279
  41.7 0.7 %sum.1 = f32[32,64]{1,0:T(8,128)} custom-call(bf16[16,16,128]{2,1,0:T(8,128)(2,1)S(1)} %all_to_all.5.parts), custom_call_target="tpu_custom_call" | custom-call | tf_op jit(solution)/shard_map/sum/pallas_call | solution.py:280
Async XLA Ops:
  0.0 11.5 %collective-permute-start = (f32[1,3,64,1024]{3,2,1,0:T(8,128)}, f32[1,3,64,1024]{3,2,1,0:T(8,128)S(1)}, u32[]{:S(2)}, u32[]{:S(2)}) collective-permute-start(f32[1,3,64,1024]{3,2,1,0:T(8,128)} %metric.3), channel_id=1, source_target_pairs={{0,4},{1,5},{2,6},{3,7},{4,0},{5,1},{6,2},{7,3},{8,12},{9,13},{10,... | collective-permute-start | bytes 2359304 | tf_op jit(solution)/shard_map/ppermute | solution.py:209
  0.5 8.5 %collective-permute-start.2 = (f32[64,64]{1,0:T(8,128)}, f32[64,64]{1,0:T(8,128)S(1)}, u32[]{:S(2)}, u32[]{:S(2)}) collective-permute-start(f32[64,64]{1,0:T(8,128)} %refs_0_.1), channel_id=1, source_target_pairs={{0,2},{1,3},{2,0},{3,1},{4,6},{5,7},{6,4},{7,5},{8,10},{9,11},{10,... | collective-permute-start | bytes 49160 | tf_op jit(solution)/shard_map/ppermute | solution.py:208
  4.0 4.9 %collective-permute-start.1 = (f32[64,64]{1,0:T(8,128)}, f32[64,64]{1,0:T(8,128)S(1)}, u32[]{:S(2)}, u32[]{:S(2)}) collective-permute-start(f32[64,64]{1,0:T(8,128)} %refs_0_.1), channel_id=1, source_target_pairs={{0,1},{1,0},{2,3},{3,2},{4,5},{5,4},{6,7},{7,6},{8,9},{9,8},{10,11... | collective-permute-start | bytes 49160 | tf_op jit(solution)/shard_map/ppermute | solution.py:208
  5.6 5.9 %collective-permute-start.3 = (f32[64,64]{1,0:T(8,128)}, f32[64,64]{1,0:T(8,128)S(1)}, u32[]{:S(2)}, u32[]{:S(2)}) collective-permute-start(f32[64,64]{1,0:T(8,128)} %refs_0_.1), channel_id=1, source_target_pairs={{0,3},{1,2},{2,1},{3,0},{4,7},{5,6},{6,5},{7,4},{8,11},{9,10},{10,... | collective-permute-start | bytes 49160 | tf_op jit(solution)/shard_map/ppermute | solution.py:208
  6.9 4.6 %copy-start.1 = (f32[64,64]{1,0:T(8,128)S(1)}, f32[64,64]{1,0:T(8,128)}, u32[]{:S(2)}) copy-start(f32[64,64]{1,0:T(8,128)} %refs_0_.1) | copy-start | bytes 49156
  6.9 4.6 %copy-start.3 = (s32[1,3,1]{1,2,0:T(1,128)S(1)}, s32[1,3,1]{1,2,0:T(1,128)}, u32[]{:S(2)}) copy-start(s32[1,3,1]{1,2,0:T(1,128)} %param.8) | copy-start | bytes 40
  11.6 3.8 %copy-start.2 = (s32[1,3,1]{1,2,0:T(1,128)S(1)}, s32[1,3,1]{1,2,0:T(1,128)}, u32[]{:S(2)}) copy-start(s32[1,3,1]{1,2,0:T(1,128)} %param.12) | copy-start | bytes 40
  13.5 6.3 %collective-permute-start.5 = (bf16[32,1024]{1,0:T(8,128)(2,1)S(1)}, bf16[32,1024]{1,0:T(8,128)(2,1)S(1)}, u32[]{:S(2)}, u32[]{:S(2)}) collective-permute-start(bf16[32,1024]{1,0:T(8,128)(2,1)S(1)} %get-tuple-element.24), channel_id=1, source_target_pairs={{0,1},{1,0},{2,3},{3,2},{4,5},{5,4},{6,7},{7,6},{8,9},{9,8},{10,11... | collective-permute-start | bytes 196616 | tf_op jit(solution)/shard_map/ppermute | solution.py:251
  13.6 7.8 %collective-permute-start.6 = (bf16[32,1024]{1,0:T(8,128)(2,1)S(1)}, bf16[32,1024]{1,0:T(8,128)(2,1)S(1)}, u32[]{:S(2)}, u32[]{:S(2)}) collective-permute-start(bf16[32,1024]{1,0:T(8,128)(2,1)S(1)} %get-tuple-element.25), channel_id=1, source_target_pairs={{0,2},{1,3},{2,0},{3,1},{4,6},{5,7},{6,4},{7,5},{8,10},{9,11},{10,... | collective-permute-start | bytes 196616 | tf_op jit(solution)/shard_map/ppermute | solution.py:251
  15.4 8.6 %copy-start = (f32[1,3,64,1024]{3,2,1,0:T(8,128)S(1)}, f32[1,3,64,1024]{3,2,1,0:T(8,128)}, u32[]{:S(2)}) copy-start(f32[1,3,64,1024]{3,2,1,0:T(8,128)} %metric.3) | copy-start | bytes 2359300
  17.1 6.9 %collective-permute-start.4 = (bf16[48,1024]{1,0:T(8,128)(2,1)S(1)}, bf16[48,1024]{1,0:T(8,128)(2,1)S(1)}, u32[]{:S(2)}, u32[]{:S(2)}) collective-permute-start(bf16[48,1024]{1,0:T(8,128)(2,1)S(1)} %get-tuple-element.22), channel_id=1, source_target_pairs={{0,4},{1,5},{2,6},{3,7},{4,0},{5,1},{6,2},{7,3},{8,12},{9,13},{10,... | collective-permute-start | bytes 294920 | tf_op jit(solution)/shard_map/ppermute | solution.py:252
  17.2 6.8 %collective-permute-start.7 = (bf16[32,1024]{1,0:T(8,128)(2,1)S(1)}, bf16[32,1024]{1,0:T(8,128)(2,1)S(1)}, u32[]{:S(2)}, u32[]{:S(2)}) collective-permute-start(bf16[32,1024]{1,0:T(8,128)(2,1)S(1)} %get-tuple-element.26), channel_id=1, source_target_pairs={{0,3},{1,2},{2,1},{3,0},{4,7},{5,6},{6,5},{7,4},{8,11},{9,10},{10,... | collective-permute-start | bytes 196616 | tf_op jit(solution)/shard_map/ppermute | solution.py:251
  19.8 6.2 %collective-permute-start.8 = (bf16[32,1024]{1,0:T(8,128)(2,1)S(1)}, bf16[32,1024]{1,0:T(8,128)(2,1)S(1)}, u32[]{:S(2)}, u32[]{:S(2)}) collective-permute-start(bf16[32,1024]{1,0:T(8,128)(2,1)S(1)} %get-tuple-element.28), channel_id=1, source_target_pairs={{0,5},{1,4},{2,7},{3,6},{4,1},{5,0},{6,3},{7,2},{8,13},{9,12},{10,... | collective-permute-start | bytes 196616 | tf_op jit(solution)/shard_map/ppermute | solution.py:252
  19.8 6.2 %collective-permute-start.9 = (bf16[32,1024]{1,0:T(8,128)(2,1)S(1)}, bf16[32,1024]{1,0:T(8,128)(2,1)S(1)}, u32[]{:S(2)}, u32[]{:S(2)}) collective-permute-start(bf16[32,1024]{1,0:T(8,128)(2,1)S(1)} %get-tuple-element.29), channel_id=1, source_target_pairs={{0,6},{1,7},{2,4},{3,5},{4,2},{5,3},{6,0},{7,1},{8,14},{9,15},{10,... | collective-permute-start | bytes 196616 | tf_op jit(solution)/shard_map/ppermute | solution.py:252
  21.4 6.2 %collective-permute-start.10 = (bf16[32,1024]{1,0:T(8,128)(2,1)S(1)}, bf16[32,1024]{1,0:T(8,128)(2,1)S(1)}, u32[]{:S(2)}, u32[]{:S(2)}) collective-permute-start(bf16[32,1024]{1,0:T(8,128)(2,1)S(1)} %get-tuple-element.30), channel_id=1, source_target_pairs={{0,7},{1,6},{2,5},{3,4},{4,3},{5,2},{6,1},{7,0},{8,15},{9,14},{10,... | collective-permute-start | bytes 196616 | tf_op jit(solution)/shard_map/ppermute | solution.py:252

commit v6 on v4

--- a/solution.py
+++ b/solution.py
@@ -13,6 +13,14 @@
 SMEM = pl.BlockSpec(memory_space=pltpu.SMEM)
 ANY = pl.BlockSpec(memory_space=pl.ANY)
 HBM = pl.BlockSpec(memory_space=pltpu.HBM)
+
+
+DENSITY_ORDER = (2, 3, 1)
+HALF_ORDER = (3, 2, 1)
+
+
+def by_distance(refs, order):
+    return [refs[0]] + [refs[1 + order.index(s)] for s in range(1, len(refs))]
 
 
 def params(mib):
@@ -78,7 +86,7 @@
 
 
 def half_kernel(n_mu, nu_slots, nu_count, *refs):
-    dens = refs[:n_mu]
+    dens = by_distance(refs[:n_mu], DENSITY_ORDER)
     t_hi, t_lo = refs[n_mu:n_mu + 2]
     outs = refs[n_mu + 2:2 * n_mu + 2]
     d_hi, d_lo, weights, turned = refs[2 * n_mu + 2:]
@@ -128,7 +136,7 @@
 
 
 def exchange_kernel(n_mu, n_aux, *refs):
-    halves = refs[:n_mu]
+    halves = by_distance(refs[:n_mu], HALF_ORDER)
     m_hi, m_lo, out, total = refs[n_mu:]
     z = lax.axis_index("mu")
     left = jnp.concatenate([h[...] for h in halves], axis=0)
@@ -164,9 +172,7 @@
     slots, aux_width = three_center.shape[1:3]
     lam = lam_all // n_mu
     turns = [[(z, z ^ s) for z in range(n_mu)] for s in range(n_mu)]
-    dens = [density] * n_mu
-    for s in (2, 3, 1):
-        dens[s] = lax.ppermute(density, "mu", turns[s])
+    dens = [density] + [lax.ppermute(density, "mu", turns[s]) for s in DENSITY_ORDER]
     nu_slots, sig_slots = jnp.swapaxes(nu_slots, 1, 2), jnp.swapaxes(sig_slots, 1, 2)
     chunks = three_center.shape[3] // 256
     t_shape = jax.ShapeDtypeStruct((chunks * aux_width, slots * 256), BF16)
@@ -209,9 +215,7 @@
         cost_estimate=pl.CostEstimate(flops=10_000_000, bytes_accessed=2_000_000, transcendentals=0),
         name="metric",
     )(sig_slots, sig_count, halves[0], metric_tensor)
-    halves = list(halves)
-    for s in (3, 2, 1):
-        halves[s] = lax.ppermute(halves[s], "mu", turns[s])
+    halves = [halves[0]] + [lax.ppermute(halves[s], "mu", turns[s]) for s in HALF_ORDER]
     rows = n_mu * orb // n_aux
     parts = pl.pallas_call(
         functools.partial(exchange_kernel, n_mu, n_aux),

time: 39.8 us -> 39.7 us (level)
  waiting for transfers between devices: 8.87 us -> 8.25 us
  blocking collectives: 12.4 us -> 12.9 us
    ppermute x6, waiting for transfers between devices: 8.87 us -> 8.25 us  [the longest x3 6.56 us: fast(): lax.ppermute(halves[s], 'mu', turns[s])]
    all_to_all x1, blocking collectives: 12.4 us -> 12.9 us  [fast(): parts = lax.all_to_all(parts, ('aux', 'mu'), 0, 0)]
where the time goes in v6:
time: 39.7 us; the launch traced here: 39.6 us
  blocking collectives  12.9 us (32%)
  starting transfers between devices  10.1 us (25%)
  waiting for transfers between devices  8.25 us (21%)
  Pallas kernels  6.89 us (17%)
  between operations  1.4 us (4%)
    all_to_all x1, blocking collectives, fast(): parts = lax.all_to_all(parts, ('aux', 'mu'), 0, 0)  12.9 us
    ppermute x3, waiting for transfers between devices, fast(): lax.ppermute(halves[s], 'mu', turns[s])  6.56 us
    ppermute x3, starting transfers between devices, fast(): lax.ppermute(density, 'mu', turns[s])  5.62 us
    ppermute x3, starting transfers between devices, fast(): lax.ppermute(halves[s], 'mu', turns[s])  4.45 us
    pallas_call x1, Pallas kernels, fast(): pl.pallas_call(functools.partial(half_kernel, n_mu), out_shape=(half_shap...  2.66 us
    pallas_call x1, Pallas kernels, fast(): pl.pallas_call(tensor_kernel, out_shape=(t_shape, t_shape), in_specs=[HBM...  1.97 us
    ppermute x3, waiting for transfers between devices, fast(): lax.ppermute(density, 'mu', turns[s])  1.69 us
    pallas_call x1, Pallas kernels, fast(): pl.pallas_call(metric_kernel, out_shape=(m_shape, m_shape), in_specs=[SME...  1 us
  transfers between devices with their start and end apart: 6, of which 3 were waited for; matrix products, arithmetic and copies ran while one was open for 0% of the time, Pallas kernels for 7%

profile of v6, /device:TPU:0, one launch (start us, length us, event | category | flops | bytes accessed | tf_op | source)
XLA Modules:
  0.0 39.6 jit_solution(6690851908423838915)
XLA Ops:
  0.0 4.0 %collective-permute-start = (f32[64,64]{1,0:T(8,128)}, f32[64,64]{1,0:T(8,128)S(1)}, u32[]{:S(2)}, u32[]{:S(2)}) collective-permute-start(f32[64,64]{1,0:T(8,128)} %refs_0_.1), channel_id=1, source_target_pairs={{0,2},{1,3},{2,0},{3,1},{4,6},{5,7},{6,4},{7,5},{8,10},{9,11},{10,... | collective-permute-start | bytes 49160 | tf_op jit(solution)/shard_map/ppermute | solution.py:175
  4.0 1.3 %collective-permute-start.1 = (f32[64,64]{1,0:T(8,128)}, f32[64,64]{1,0:T(8,128)S(1)}, u32[]{:S(2)}, u32[]{:S(2)}) collective-permute-start(f32[64,64]{1,0:T(8,128)} %refs_0_.1), channel_id=1, source_target_pairs={{0,3},{1,2},{2,1},{3,0},{4,7},{5,6},{6,5},{7,4},{8,11},{9,10},{10,... | collective-permute-start | bytes 49160 | tf_op jit(solution)/shard_map/ppermute | solution.py:175
  5.4 0.2 collective-permute-start.2
  6.3 0.0 copy-start.2
  6.3 0.0 copy-start.3
  6.3 2.0 %tensor.2 = (bf16[1024,768]{1,0:T(8,128)(2,1)S(1)}, bf16[1024,768]{1,0:T(8,128)(2,1)S(1)}) custom-call(f32[1,3,64,4096]{3,2,1,0:T(8,128)} %tensor.3), custom_call_target="tpu_custom_call" | custom-call | flops 10000000 | bytes 6000000 | tf_op jit(solution)/shard_map/tensor/pallas_call | solution.py:180
  8.3 0.0 collective-permute-done.refs_1_
  8.3 1.7 %collective-permute-done.1.refs_2_ = f32[64,64]{1,0:T(8,128)S(1)} collective-permute-done((f32[64,64]{1,0:T(8,128)}, f32[64,64]{1,0:T(8,128)S(1)}, u32[]{:S(2)}, u32[]{:S(2)}) %collective-permute-start.1) | collective-permute-done | bytes 16416 | tf_op jit(solution)/shard_map/ppermute | solution.py:175
  10.0 0.0 collective-permute-done.2.refs_3_
  10.0 0.0 copy-done.2
  10.0 0.0 copy-done.3
  10.0 0.0 copy-start
  10.0 0.0 copy-start.1
  10.0 2.7 %half.1 = (bf16[64,1024]{1,0:T(8,128)(2,1)S(1)}, bf16[64,1024]{1,0:T(8,128)(2,1)S(1)}, bf16[64,1024]{1,0:T(8,128)(2,1)S(1)}, bf16[64,1024]{1,0:T(8,128)(2,1)S(1)}) custom-call(s32[1,1,3]{2,1,0:T(1,128)S(1)} %bitcast.3, s32[1,1]{1,0:T(1,128)S(6)} %copy.8.nu_count, f32[64,64]{1,0:T(8,128)S(1)} %copy-done.2, f32[64,64]{1,0:T(8,128)S(1)} %collective-permute-done.refs_1_, ...), custom_call_target="tpu_custom_call" | custom-call | flops 1200000000 | bytes 4000000 | tf_op jit(solution)/shard_map/half/pallas_call | solution.py:194
  12.7 2.1 %collective-permute-start.3 = (bf16[64,1024]{1,0:T(8,128)(2,1)S(1)}, bf16[64,1024]{1,0:T(8,128)(2,1)S(1)}, u32[]{:S(2)}, u32[]{:S(2)}) collective-permute-start(bf16[64,1024]{1,0:T(8,128)(2,1)S(1)} %get-tuple-element.16), channel_id=1, source_target_pairs={{0,3},{1,2},{2,1},{3,0},{4,7},{5,6},{6,5},{7,4},{8,11},{9,10},{10,... | collective-permute-start | bytes 393224 | tf_op jit(solution)/shard_map/ppermute | solution.py:218
  14.7 0.0 collective-permute-start.4
  14.7 2.4 %collective-permute-start.5 = (bf16[64,1024]{1,0:T(8,128)(2,1)S(1)}, bf16[64,1024]{1,0:T(8,128)(2,1)S(1)}, u32[]{:S(2)}, u32[]{:S(2)}) collective-permute-start(bf16[64,1024]{1,0:T(8,128)(2,1)S(1)} %get-tuple-element.18), channel_id=1, source_target_pairs={{0,1},{1,0},{2,3},{3,2},{4,5},{5,4},{6,7},{7,6},{8,9},{9,8},{10,11... | collective-permute-start | bytes 393224 | tf_op jit(solution)/shard_map/ppermute | solution.py:218
  17.8 0.0 copy-done
  17.8 0.0 copy-done.1
  17.8 1.0 %metric.2 = (bf16[1024,256]{1,0:T(8,128)(2,1)S(1)}, bf16[1024,256]{1,0:T(8,128)(2,1)S(1)}) custom-call(s32[1,1,3]{2,1,0:T(1,128)S(1)} %bitcast.2, s32[1,1]{1,0:T(1,128)S(6)} %copy.9.sig_count, bf16[64,1024]{1,0:T(8,128)(2,1)S(1)} %get-tuple-element.15.after.refs_0_, f32[1,3,64,1024]{3,2,1,0:T(8,128)S(1)} %copy-done), custom_call_target="tpu_custom_call" | custom-call | flops 10000000 | bytes 2000000 | tf_op jit(solution)/shard_map/metric/pallas_call | solution.py:209
  18.8 2.2 %collective-permute-done.3.refs_1_ = bf16[64,1024]{1,0:T(8,128)(2,1)S(1)} collective-permute-done((bf16[64,1024]{1,0:T(8,128)(2,1)S(1)}, bf16[64,1024]{1,0:T(8,128)(2,1)S(1)}, u32[]{:S(2)}, u32[]{:S(2)}) %collective-permute-start.3) | collective-permute-done | bytes 131104 | tf_op jit(solution)/shard_map/ppermute | solution.py:218
  21.0 4.4 %collective-permute-done.4.refs_2_ = bf16[64,1024]{1,0:T(8,128)(2,1)S(1)} collective-permute-done((bf16[64,1024]{1,0:T(8,128)(2,1)S(1)}, bf16[64,1024]{1,0:T(8,128)(2,1)S(1)}, u32[]{:S(2)}, u32[]{:S(2)}) %collective-permute-start.4) | collective-permute-done | bytes 131104 | tf_op jit(solution)/shard_map/ppermute | solution.py:218
  25.4 0.0 collective-permute-done.5.refs_3_
  25.4 0.5 %exchange.1 = bf16[32,16,128]{2,1,0:T(8,128)(2,1)S(1)} custom-call(bf16[64,1024]{1,0:T(8,128)(2,1)S(1)} %get-tuple-element.15.after.refs_0_, bf16[64,1024]{1,0:T(8,128)(2,1)S(1)} %collective-permute-done.3.refs_1_, bf16[64,1024]{1,0:T(8,128)(2,1)S(1)} %collective-permute-done.4.refs_2_, bf16[64,1024]{1,0:T(8,128)(2,1)S(1)} %collective-permute-done.5.refs_3_, ...), custom_call_target="tpu_custom_call" | custom-call | flops 300000000 | bytes 2000000 | tf_op jit(solution)/shard_map/exchange/pallas_call | solution.py:220
  25.9 12.9 %all_to_all.5.parts = bf16[32,16,128]{2,1,0:T(8,128)(2,1)S(1)} all-to-all(bf16[32,16,128]{2,1,0:T(8,128)(2,1)S(1)} %exchange.1), channel_id=1, replica_groups=mesh['aux'=8,'mu'=4] {'aux','mu'}, dimensions={0} | all-to-all | bytes 262144 | tf_op jit(solution)/shard_map/all_to_all | solution.py:230
  38.9 0.7 %sum.1 = f32[32,64]{1,0:T(8,128)} custom-call(bf16[32,16,128]{2,1,0:T(8,128)(2,1)S(1)} %all_to_all.5.parts), custom_call_target="tpu_custom_call" | custom-call | tf_op jit(solution)/shard_map/sum/pallas_call | solution.py:231
Async XLA Ops:
  0.0 8.3 %collective-permute-start = (f32[64,64]{1,0:T(8,128)}, f32[64,64]{1,0:T(8,128)S(1)}, u32[]{:S(2)}, u32[]{:S(2)}) collective-permute-start(f32[64,64]{1,0:T(8,128)} %refs_0_.1), channel_id=1, source_target_pairs={{0,2},{1,3},{2,0},{3,1},{4,6},{5,7},{6,4},{7,5},{8,10},{9,11},{10,... | collective-permute-start | bytes 49160 | tf_op jit(solution)/shard_map/ppermute | solution.py:175
  4.0 5.9 %collective-permute-start.1 = (f32[64,64]{1,0:T(8,128)}, f32[64,64]{1,0:T(8,128)S(1)}, u32[]{:S(2)}, u32[]{:S(2)}) collective-permute-start(f32[64,64]{1,0:T(8,128)} %refs_0_.1), channel_id=1, source_target_pairs={{0,3},{1,2},{2,1},{3,0},{4,7},{5,6},{6,5},{7,4},{8,11},{9,10},{10,... | collective-permute-start | bytes 49160 | tf_op jit(solution)/shard_map/ppermute | solution.py:175
  5.4 4.6 %collective-permute-start.2 = (f32[64,64]{1,0:T(8,128)}, f32[64,64]{1,0:T(8,128)S(1)}, u32[]{:S(2)}, u32[]{:S(2)}) collective-permute-start(f32[64,64]{1,0:T(8,128)} %refs_0_.1), channel_id=1, source_target_pairs={{0,1},{1,0},{2,3},{3,2},{4,5},{5,4},{6,7},{7,6},{8,9},{9,8},{10,11... | collective-permute-start | bytes 49160 | tf_op jit(solution)/shard_map/ppermute | solution.py:175
  6.3 3.7 %copy-start.2 = (f32[64,64]{1,0:T(8,128)S(1)}, f32[64,64]{1,0:T(8,128)}, u32[]{:S(2)}) copy-start(f32[64,64]{1,0:T(8,128)} %refs_0_.1) | copy-start | bytes 49156
  6.3 3.7 %copy-start.3 = (s32[1,3,1]{1,2,0:T(1,128)S(1)}, s32[1,3,1]{1,2,0:T(1,128)}, u32[]{:S(2)}) copy-start(s32[1,3,1]{1,2,0:T(1,128)} %param.8) | copy-start | bytes 40
  10.0 7.8 %copy-start = (f32[1,3,64,1024]{3,2,1,0:T(8,128)S(1)}, f32[1,3,64,1024]{3,2,1,0:T(8,128)}, u32[]{:S(2)}) copy-start(f32[1,3,64,1024]{3,2,1,0:T(8,128)} %metric.3) | copy-start | bytes 2359300
  10.0 7.8 %copy-start.1 = (s32[1,3,1]{1,2,0:T(1,128)S(1)}, s32[1,3,1]{1,2,0:T(1,128)}, u32[]{:S(2)}) copy-start(s32[1,3,1]{1,2,0:T(1,128)} %param.12) | copy-start | bytes 40
  12.7 8.3 %collective-permute-start.3 = (bf16[64,1024]{1,0:T(8,128)(2,1)S(1)}, bf16[64,1024]{1,0:T(8,128)(2,1)S(1)}, u32[]{:S(2)}, u32[]{:S(2)}) collective-permute-start(bf16[64,1024]{1,0:T(8,128)(2,1)S(1)} %get-tuple-element.16), channel_id=1, source_target_pairs={{0,3},{1,2},{2,1},{3,0},{4,7},{5,6},{6,5},{7,4},{8,11},{9,10},{10,... | collective-permute-start | bytes 393224 | tf_op jit(solution)/shard_map/ppermute | solution.py:218
  14.7 10.6 %collective-permute-start.4 = (bf16[64,1024]{1,0:T(8,128)(2,1)S(1)}, bf16[64,1024]{1,0:T(8,128)(2,1)S(1)}, u32[]{:S(2)}, u32[]{:S(2)}) collective-permute-start(bf16[64,1024]{1,0:T(8,128)(2,1)S(1)} %get-tuple-element.17), channel_id=1, source_target_pairs={{0,2},{1,3},{2,0},{3,1},{4,6},{5,7},{6,4},{7,5},{8,10},{9,11},{10,... | collective-permute-start | bytes 393224 | tf_op jit(solution)/shard_map/ppermute | solution.py:218
  14.7 10.6 %collective-permute-start.5 = (bf16[64,1024]{1,0:T(8,128)(2,1)S(1)}, bf16[64,1024]{1,0:T(8,128)(2,1)S(1)}, u32[]{:S(2)}, u32[]{:S(2)}) collective-permute-start(bf16[64,1024]{1,0:T(8,128)(2,1)S(1)} %get-tuple-element.18), channel_id=1, source_target_pairs={{0,1},{1,0},{2,3},{3,2},{4,5},{5,4},{6,7},{7,6},{8,9},{9,8},{10,11... | collective-permute-start | bytes 393224 | tf_op jit(solution)/shard_map/ppermute | solution.py:218

commit v7 on v6

--- a/solution.py
+++ b/solution.py
@@ -16,7 +16,9 @@
 
 
 DENSITY_ORDER = (2, 3, 1)
-HALF_ORDER = (3, 2, 1)
+OUTER = ((0, 2), (3, 1))
+MIDDLE = ((1, 2), (2, 1))
+EDGE = ((0, 1), (3, 2))
 
 
 def by_distance(refs, order):
@@ -36,39 +38,48 @@
     return lax.broadcasted_iota(jnp.int32, shape, dim)
 
 
-def tensor_kernel(tensor, t_hi, t_lo, buffer, arrived):
+def tensor_kernel(tensor, t_hi, t_lo):
     _, slots, aux_width, width = tensor.shape
-    parts = buffer.shape[0] // slots
-    span = width // parts
-
-    def fetch(k, part):
-        return pltpu.make_async_copy(
-            tensor.at[0, k, :, pl.ds(part * span, span)],
-            buffer.at[k * parts + part],
-            arrived.at[k * parts + part],
-        )
-
-    order = [(k, part) for k in range(slots) for part in range(parts)]
-    for k, part in order:
-        fetch(k, part).start()
-    for k, part in order:
-        fetch(k, part).wait()
-        for chunk in range(span // 256):
-            hi, lo = split(buffer[k * parts + part, :, chunk * 256:(chunk + 1) * 256])
-            at = (part * (span // 256) + chunk) * aux_width
-            t_hi[at:at + aux_width, k * 256:(k + 1) * 256] = hi
-            t_lo[at:at + aux_width, k * 256:(k + 1) * 256] = lo
-
-
-def metric_kernel(sig_slots, sig_count, after, metric, m_hi, m_lo):
+    for k in range(slots):
+        for chunk in range(width // 256):
+            hi, lo = split(tensor[0, k, :, chunk * 256:(chunk + 1) * 256])
+            rows = slice(chunk * aux_width, (chunk + 1) * aux_width)
+            t_hi[rows, k * 256:(k + 1) * 256] = hi
+            t_lo[rows, k * 256:(k + 1) * 256] = lo
+
+
+def live_targets(sig_slots, sig_count):
+    return [
+        jnp.where(q < sig_count[0, 0], sig_slots[0, 0, q], -1).astype(F32)
+        for q in range(sig_slots.shape[2])
+    ]
+
+
+def share_kernel(sig_slots, sig_count, metric, out, buffer, arrived):
     _, sig, aux_width, width = metric.shape
+    copies = [
+        pltpu.make_async_copy(metric.at[0, q], buffer.at[q], arrived.at[q]) for q in range(sig)
+    ]
+    for copy in copies:
+        copy.start()
+    shape = (16, width)
+    note = jnp.full(shape, -1.0, F32)
+    for q, target in enumerate(live_targets(sig_slots, sig_count)):
+        note = jnp.where(iota(shape, 0) == q, target, note)
+    out[sig * aux_width:, :] = note.astype(BF16)
+    for q in range(sig):
+        copies[q].wait()
+        out[q * aux_width:(q + 1) * aux_width, :] = buffer[q].astype(BF16)
+
+
+def place(blocks, targets, m_hi, m_lo):
+    aux_width, width = blocks[0].shape
     half = iota((aux_width, 128), 1) >= 64
-    pair_of = jnp.where(half, 1, 0)
-    targets = [jnp.where(q < sig_count[0, 0], sig_slots[0, 0, q], -1) for q in range(sig)]
+    pair_of = jnp.where(half, 1.0, 0.0)
     for pair in range(width // 128):
         sums = [[jnp.zeros((aux_width, 128), F32) for _ in range(2)] for _ in range(2)]
-        for q in range(sig):
-            block = metric[0, q, :, pair * 128:(pair + 1) * 128]
+        for q in range(len(blocks)):
+            block = blocks[q][:, pair * 128:(pair + 1) * 128].astype(F32)
             turned = pltpu.roll(block, 64, 1)
             both = (jnp.where(half, turned, block), jnp.where(half, block, turned))
             for out_half in range(2):
@@ -83,6 +94,28 @@
                 columns = slice(out_half * 128, (out_half + 1) * 128)
                 m_hi[at:at + aux_width, columns] = hi
                 m_lo[at:at + aux_width, columns] = lo
+
+
+def product(left, m_hi, m_lo):
+    total = jnp.dot(left, m_hi[...], preferred_element_type=F32)
+    return total + jnp.dot(left, m_lo[...], preferred_element_type=F32)
+
+
+def own_kernel(sig_slots, sig_count, metric, half, base, m_hi, m_lo):
+    blocks = [metric.at[0, q] for q in range(metric.shape[1])]
+    place(blocks, live_targets(sig_slots, sig_count), m_hi, m_lo)
+    base[...] = product(half[...], m_hi, m_lo)
+
+
+def neighbour_kernel(sig, near, far, near_half, far_half, base, out, n_hi, n_lo, f_hi, f_lo):
+    aux_width = (near.shape[0] - 16) // sig
+    total = base[...]
+    for shared, half, hi, lo in ((near, near_half, n_hi, n_lo), (far, far_half, f_hi, f_lo)):
+        note = shared[sig * aux_width:, :128].astype(F32)
+        blocks = [shared.at[pl.ds(q * aux_width, aux_width)] for q in range(sig)]
+        place(blocks, [note[q:q + 1, :] for q in range(sig)], hi, lo)
+        total += product(half[...], hi, lo)
+    out[...] = total
 
 
 def half_kernel(n_mu, nu_slots, nu_count, *refs):
@@ -135,17 +168,14 @@
                 outs[s][group * span:(group + 1) * span, r * 128:(r + 1) * 128] = picked.astype(BF16)
 
 
-def exchange_kernel(n_mu, n_aux, *refs):
-    halves = by_distance(refs[:n_mu], HALF_ORDER)
-    m_hi, m_lo, out, total = refs[n_mu:]
+def exchange_kernel(n_mu, n_aux, base, outer, middle, edge, n_hi, n_lo, f_hi, f_lo, out, total):
     z = lax.axis_index("mu")
-    left = jnp.concatenate([h[...] for h in halves], axis=0)
-    product = jnp.dot(left, m_hi[...], preferred_element_type=F32)
-    product += jnp.dot(left, m_lo[...], preferred_element_type=F32)
-    orb = halves[0].shape[0]
-    for s in range(n_mu):
-        block = z ^ s
-        total[pl.ds(pl.multiple_of(block * orb, orb), orb), :] = product[s * orb:(s + 1) * orb]
+    orb = base.shape[0]
+    by_near = product(jnp.concatenate([outer[...], middle[...]], axis=0), n_hi, n_lo)
+    by_far = product(edge[...], f_hi, f_lo)
+    pieces = ((z, base[...]), (z ^ 2, by_near[:orb]), (z ^ 3, by_near[orb:]), (z ^ 1, by_far))
+    for block, piece in pieces:
+        total[pl.ds(pl.multiple_of(block * orb, orb), orb), :] = piece
     rows = out.shape[1]
     lower = iota((rows, 128), 1) < 64
     for a in range(n_aux):
@@ -175,18 +205,29 @@
     dens = [density] + [lax.ppermute(density, "mu", turns[s]) for s in DENSITY_ORDER]
     nu_slots, sig_slots = jnp.swapaxes(nu_slots, 1, 2), jnp.swapaxes(sig_slots, 1, 2)
     chunks = three_center.shape[3] // 256
+    sig = metric_tensor.shape[1]
+    shared = pl.pallas_call(
+        share_kernel,
+        out_shape=jax.ShapeDtypeStruct((sig * aux_width + 16, lam * orb), BF16),
+        in_specs=[SMEM, SMEM, HBM],
+        out_specs=VMEM,
+        scratch_shapes=[
+            pltpu.VMEM((sig, aux_width, lam * orb), F32),
+            pltpu.SemaphoreType.DMA((sig,)),
+        ],
+        compiler_params=params(58),
+        cost_estimate=pl.CostEstimate(flops=1_000_000, bytes_accessed=6_000_000, transcendentals=0),
+        name="share",
+    )(sig_slots, sig_count, metric_tensor)
+    near = lax.ppermute(shared, "mu", turns[1])
+    far = lax.ppermute(shared, "mu", MIDDLE)
     t_shape = jax.ShapeDtypeStruct((chunks * aux_width, slots * 256), BF16)
-    m_shape = jax.ShapeDtypeStruct((lam * aux_width, n_mu * orb), BF16)
     t_hi, t_lo = pl.pallas_call(
         tensor_kernel,
         out_shape=(t_shape, t_shape),
-        in_specs=[HBM],
+        in_specs=[VMEM],
         out_specs=(VMEM, VMEM),
-        scratch_shapes=[
-            pltpu.VMEM((slots * 4, aux_width, chunks * 64), F32),
-            pltpu.SemaphoreType.DMA((slots * 4,)),
-        ],
-        compiler_params=params(50),
+        compiler_params=params(16),
         cost_estimate=pl.CostEstimate(flops=10_000_000, bytes_accessed=6_000_000, transcendentals=0),
         name="tensor",
     )(three_center)
@@ -206,27 +247,42 @@
         cost_estimate=pl.CostEstimate(flops=1_200_000_000, bytes_accessed=4_000_000, transcendentals=0),
         name="half",
     )(nu_slots, nu_count, *dens, t_hi, t_lo)
-    m_hi, m_lo = pl.pallas_call(
-        metric_kernel,
-        out_shape=(m_shape, m_shape),
-        in_specs=[SMEM, SMEM, ANY, VMEM],
-        out_specs=(VMEM, VMEM),
-        compiler_params=params(16),
-        cost_estimate=pl.CostEstimate(flops=10_000_000, bytes_accessed=2_000_000, transcendentals=0),
-        name="metric",
-    )(sig_slots, sig_count, halves[0], metric_tensor)
-    halves = [halves[0]] + [lax.ppermute(halves[s], "mu", turns[s]) for s in HALF_ORDER]
+    outer = lax.ppermute(halves[3], "mu", OUTER)
+    middle = lax.ppermute(halves[2], "mu", MIDDLE)
+    edge = lax.ppermute(halves[2], "mu", EDGE)
+    base_shape = jax.ShapeDtypeStruct((orb, n_mu * orb), F32)
+    m_size = (lam * aux_width, n_mu * orb)
+    m_shape = jax.ShapeDtypeStruct(m_size, BF16)
+    base = pl.pallas_call(
+        own_kernel,
+        out_shape=base_shape,
+        in_specs=[SMEM, SMEM, VMEM, VMEM],
+        out_specs=VMEM,
+        scratch_shapes=[pltpu.VMEM(m_size, BF16)] * 2,
+        compiler_params=params(16),
+        cost_estimate=pl.CostEstimate(flops=80_000_000, bytes_accessed=2_000_000, transcendentals=0),
+        name="own",
+    )(sig_slots, sig_count, metric_tensor, halves[0])
+    base, *placed = pl.pallas_call(
+        functools.partial(neighbour_kernel, sig),
+        out_shape=(base_shape,) + (m_shape,) * 4,
+        in_specs=[VMEM] * 5,
+        out_specs=(VMEM,) * 5,
+        compiler_params=params(16),
+        cost_estimate=pl.CostEstimate(flops=160_000_000, bytes_accessed=4_000_000, transcendentals=0),
+        name="neighbour",
+    )(near, far, halves[1], halves[3], base)
     rows = n_mu * orb // n_aux
     parts = pl.pallas_call(
         functools.partial(exchange_kernel, n_mu, n_aux),
         out_shape=jax.ShapeDtypeStruct((n_aux * n_mu, rows // 2, 128), BF16),
-        in_specs=[VMEM] * (n_mu + 2),
+        in_specs=[VMEM] * 8,
         out_specs=VMEM,
         scratch_shapes=[pltpu.VMEM((n_mu * orb, n_mu * orb), F32)],
         compiler_params=params(16),
         cost_estimate=pl.CostEstimate(flops=300_000_000, bytes_accessed=2_000_000, transcendentals=0),
         name="exchange",
-    )(*halves, m_hi, m_lo)
+    )(base, outer, middle, edge, *placed)
     parts = lax.all_to_all(parts, ("aux", "mu"), 0, 0)
     return pl.pallas_call(
         sum_kernel,

time: 39.7 us -> 50.5 us (1.27)
  starting transfers between devices: 10.1 us -> 18.3 us
  Pallas kernels: 6.89 us -> 9.4 us
  waiting for transfers between devices: 8.25 us -> 6.29 us
  local copies, waits for them, and re-layouts: 0.02 us -> 1.9 us
    ppermute x3 -> x5, starting transfers between devices: 4.45 us -> 11.5 us  [the longest x1 3.99 us: fast(): outer = lax.ppermute(halves[3], 'mu', OUTER)]
    ppermute x3 -> x5, waiting for transfers between devices: 6.56 us -> 0.01 us  [the longest x1 0.01 us: fast(): far = lax.ppermute(shared, 'mu', MIDDLE)]
    ppermute x3, waiting for transfers between devices: 1.69 us -> 6.27 us  [fast(): lax.ppermute(density, 'mu', turns[s])]
    pallas_call x2 -> x4, Pallas kernels: 2.97 us -> 5.46 us  [the longest x1 2.57 us: fast(): pl.pallas_call(share_kernel, out_shape=jax.ShapeDtypeStruct((sig * aux_wi...]
    unnamed x8 -> x10, local copies, waits for them, and re-layouts: 0.02 us -> 1.9 us
    ppermute x3, starting transfers between devices: 5.62 us -> 6.82 us  [fast(): lax.ppermute(density, 'mu', turns[s])]
  transfers between devices with their start and end apart: 6 -> 8, of which waited for: 3 -> 1; matrix products, arithmetic and copies ran while one was open for 0% -> 0% of each run, Pallas kernels for 7% -> 11%
where the time goes in v7:
time: 50.5 us; the launch traced here: 50.2 us
  starting transfers between devices  18.3 us (36%)
  blocking collectives  12.8 us (25%)
  Pallas kernels  9.4 us (19%)
  waiting for transfers between devices  6.29 us (12%)
  local copies, waits for them, and re-layouts  1.9 us (4%)
  between operations  1.47 us (3%)
    all_to_all x1, blocking collectives, fast(): parts = lax.all_to_all(parts, ('aux', 'mu'), 0, 0)  12.8 us
    ppermute x3, starting transfers between devices, fast(): lax.ppermute(density, 'mu', turns[s])  6.82 us
    ppermute x3, waiting for transfers between devices, fast(): lax.ppermute(density, 'mu', turns[s])  6.27 us
    ppermute x1, starting transfers between devices, fast(): outer = lax.ppermute(halves[3], 'mu', OUTER)  3.99 us
    ppermute x1, starting transfers between devices, fast(): edge = lax.ppermute(halves[2], 'mu', EDGE)  3.1 us
    ppermute x1, starting transfers between devices, fast(): near = lax.ppermute(shared, 'mu', turns[1])  3.09 us
    pallas_call x1, Pallas kernels, fast(): pl.pallas_call(functools.partial(half_kernel, n_mu), out_shape=(half_shap...  2.67 us
    pallas_call x1, Pallas kernels, fast(): pl.pallas_call(share_kernel, out_shape=jax.ShapeDtypeStruct((sig * aux_wi...  2.57 us
  transfers between devices with their start and end apart: 8, of which 1 were waited for; matrix products, arithmetic and copies ran while one was open for 0% of the time, Pallas kernels for 11%

profile of v7, /device:TPU:0, one launch (start us, length us, event | category | flops | bytes accessed | tf_op | source)
XLA Modules:
  0.0 50.2 jit_solution(7600757213583607302)
XLA Ops:
  0.7 2.6 %share.1 = bf16[208,1024]{1,0:T(8,128)(2,1)} custom-call(s32[1,1,3]{2,1,0:T(1,128)} %bitcast.2, s32[1,1]{1,0:T(1,128)S(6)} %copy.9.sig_count, f32[1,3,64,1024]{3,2,1,0:T(8,128)} %metric.3), custom_call_target="tpu_custom_call" | custom-call | flops 1000000 | bytes 6000000 | tf_op jit(solution)/shard_map/share/pallas_call | solution.py:209
  3.2 3.1 %collective-permute-start = (bf16[208,1024]{1,0:T(8,128)(2,1)}, bf16[208,1024]{1,0:T(8,128)(2,1)S(1)}, u32[]{:S(2)}, u32[]{:S(2)}) collective-permute-start(bf16[208,1024]{1,0:T(8,128)(2,1)} %share.1), channel_id=1, source_target_pairs={{0,1},{1,0},{2,3},{3,2},{4,5},{5,4},{6,7},{7,6},{8,9},{9,8},{10,11... | collective-permute-start | bytes 1277960 | tf_op jit(solution)/shard_map/ppermute | solution.py:222
  6.3 0.7 %collective-permute-start.1 = (bf16[208,1024]{1,0:T(8,128)(2,1)}, bf16[208,1024]{1,0:T(8,128)(2,1)S(1)}, u32[]{:S(2)}, u32[]{:S(2)}) collective-permute-start(bf16[208,1024]{1,0:T(8,128)(2,1)} %share.1), channel_id=1, source_target_pairs={{1,2},{2,1},{5,6},{6,5},{9,10},{10,9},{13,14},{14,13},{17,18},{18,... | collective-permute-start | bytes 1277960 | tf_op jit(solution)/shard_map/ppermute | solution.py:223
  7.0 3.9 %collective-permute-start.2 = (f32[64,64]{1,0:T(8,128)}, f32[64,64]{1,0:T(8,128)S(1)}, u32[]{:S(2)}, u32[]{:S(2)}) collective-permute-start(f32[64,64]{1,0:T(8,128)} %refs_0_.1), channel_id=1, source_target_pairs={{0,2},{1,3},{2,0},{3,1},{4,6},{5,7},{6,4},{7,5},{8,10},{9,11},{10,... | collective-permute-start | bytes 49160 | tf_op jit(solution)/shard_map/ppermute | solution.py:205
  10.9 2.9 %collective-permute-start.3 = (f32[64,64]{1,0:T(8,128)}, f32[64,64]{1,0:T(8,128)S(1)}, u32[]{:S(2)}, u32[]{:S(2)}) collective-permute-start(f32[64,64]{1,0:T(8,128)} %refs_0_.1), channel_id=1, source_target_pairs={{0,3},{1,2},{2,1},{3,0},{4,7},{5,6},{6,5},{7,4},{8,11},{9,10},{10,... | collective-permute-start | bytes 49160 | tf_op jit(solution)/shard_map/ppermute | solution.py:205
  13.8 0.0 collective-permute-start.4
  14.5 0.0 copy-start
  14.5 1.9 %copy-done = f32[1,3,64,4096]{3,2,1,0:T(8,128)S(1)} copy-done((f32[1,3,64,4096]{3,2,1,0:T(8,128)S(1)}, f32[1,3,64,4096]{3,2,1,0:T(8,128)}, u32[]{:S(2)}) %copy-start) | copy-done | bytes 3145752
  16.4 0.0 copy-start.3
  16.4 0.0 copy-start.4
  16.4 0.4 tensor.2
  16.7 6.3 %collective-permute-done.2.refs_1_ = f32[64,64]{1,0:T(8,128)S(1)} collective-permute-done((f32[64,64]{1,0:T(8,128)}, f32[64,64]{1,0:T(8,128)S(1)}, u32[]{:S(2)}, u32[]{:S(2)}) %collective-permute-start.2) | collective-permute-done | bytes 16416 | tf_op jit(solution)/shard_map/ppermute | solution.py:205
  23.0 0.0 collective-permute-done.3.refs_2_
  23.0 0.0 collective-permute-done.4.refs_3_
  23.0 0.0 copy-done.3
  23.0 0.0 copy-done.4
  23.0 0.0 copy-start.1
  23.0 0.0 copy-start.2
  23.1 2.7 %half.1 = (bf16[64,1024]{1,0:T(8,128)(2,1)S(1)}, bf16[64,1024]{1,0:T(8,128)(2,1)S(1)}, bf16[64,1024]{1,0:T(8,128)(2,1)S(1)}, bf16[64,1024]{1,0:T(8,128)(2,1)S(1)}) custom-call(s32[1,1,3]{2,1,0:T(1,128)S(1)} %bitcast.4, s32[1,1]{1,0:T(1,128)S(6)} %copy.8.nu_count, f32[64,64]{1,0:T(8,128)S(1)} %copy-done.3, f32[64,64]{1,0:T(8,128)S(1)} %collective-permute-done.2.refs_1_, ...), custom_call_target="tpu_custom_call" | custom-call | flops 1200000000 | bytes 4000000 | tf_op jit(solution)/shard_map/half/pallas_call | solution.py:235
  25.7 4.0 %collective-permute-start.5 = (bf16[64,1024]{1,0:T(8,128)(2,1)S(1)}, bf16[64,1024]{1,0:T(8,128)(2,1)S(1)}, u32[]{:S(2)}, u32[]{:S(2)}) collective-permute-start(bf16[64,1024]{1,0:T(8,128)(2,1)S(1)} %get-tuple-element.19.far_half), channel_id=1, source_target_pairs={{0,2},{3,1},{4,6},{7,5},{8,10},{11,9},{12,14},{15,13},{16,18},{19,... | collective-permute-start | bytes 393224 | tf_op jit(solution)/shard_map/ppermute | solution.py:250
  29.7 0.7 %collective-permute-start.6 = (bf16[64,1024]{1,0:T(8,128)(2,1)S(1)}, bf16[64,1024]{1,0:T(8,128)(2,1)S(1)}, u32[]{:S(2)}, u32[]{:S(2)}) collective-permute-start(bf16[64,1024]{1,0:T(8,128)(2,1)S(1)} %get-tuple-element.22), channel_id=1, source_target_pairs={{1,2},{2,1},{5,6},{6,5},{9,10},{10,9},{13,14},{14,13},{17,18},{18,... | collective-permute-start | bytes 393224 | tf_op jit(solution)/shard_map/ppermute | solution.py:251
  30.4 3.1 %collective-permute-start.7 = (bf16[64,1024]{1,0:T(8,128)(2,1)S(1)}, bf16[64,1024]{1,0:T(8,128)(2,1)S(1)}, u32[]{:S(2)}, u32[]{:S(2)}) collective-permute-start(bf16[64,1024]{1,0:T(8,128)(2,1)S(1)} %get-tuple-element.22), channel_id=1, source_target_pairs={{0,1},{3,2},{4,5},{7,6},{8,9},{11,10},{12,13},{15,14},{16,17},{19,... | collective-permute-start | bytes 393224 | tf_op jit(solution)/shard_map/ppermute | solution.py:252
  33.5 0.0 copy-done.1
  33.5 0.0 copy-done.2
  33.5 1.2 %own.1.base = f32[64,256]{1,0:T(8,128)S(1)} custom-call(s32[1,1,3]{2,1,0:T(1,128)S(1)} %bitcast.3, s32[1,1]{1,0:T(1,128)S(6)} %copy.9.sig_count, f32[1,3,64,1024]{3,2,1,0:T(8,128)S(1)} %copy-done.1, bf16[64,1024]{1,0:T(8,128)(2,1)S(1)} %get-tuple-element.20.half), custom_call_target="tpu_custom_call" | custom-call | flops 80000000 | bytes 2000000 | tf_op jit(solution)/shard_map/own/pallas_call | solution.py:256
  34.7 0.0 collective-permute-done.near
  34.8 0.0 collective-permute-done.1.far
  34.8 1.3 %neighbour.1 = (f32[64,256]{1,0:T(8,128)S(1)}, bf16[1024,256]{1,0:T(8,128)(2,1)S(1)}, bf16[1024,256]{1,0:T(8,128)(2,1)S(1)}, bf16[1024,256]{1,0:T(8,128)(2,1)S(1)}, bf16[1024,256]{1,0:T(8,128)(2,1)S(1)}) custom-call(bf16[208,1024]{1,0:T(8,128)(2,1)S(1)} %collective-permute-done.near, bf16[208,1024]{1,0:T(8,128)(2,1)S(1)} %collective-permute-done.1.far, ...), custom_call_target="tpu_custom_call" | custom-call | flops 160000000 | bytes 4000000 | tf_op jit(solution)/shard_map/neighbour/pallas_call | solution.py:266
  36.1 0.0 collective-permute-done.5.outer
  36.1 0.0 collective-permute-done.6.middle
  36.1 0.0 collective-permute-done.7.edge
  36.1 0.6 %exchange.1 = bf16[32,16,128]{2,1,0:T(8,128)(2,1)S(1)} custom-call(f32[64,256]{1,0:T(8,128)S(1)} %get-tuple-element.21.base, bf16[64,1024]{1,0:T(8,128)(2,1)S(1)} %collective-permute-done.5.outer, bf16[64,1024]{1,0:T(8,128)(2,1)S(1)} %collective-permute-done.6.middle, bf16[64,1024]{1,0:T(8,128)(2,1)S(1)} %collective-permute-done.7.edge, ...), custom_call_target="tpu_custom_call" | custom-call | flops 300000000 | bytes 2000000 | tf_op jit(solution)/shard_map/exchange/pallas_call | solution.py:276
  36.7 12.8 %all_to_all.5.parts = bf16[32,16,128]{2,1,0:T(8,128)(2,1)S(1)} all-to-all(bf16[32,16,128]{2,1,0:T(8,128)(2,1)S(1)} %exchange.1), channel_id=1, replica_groups=mesh['aux'=8,'mu'=4] {'aux','mu'}, dimensions={0} | all-to-all | bytes 262144 | tf_op jit(solution)/shard_map/all_to_all | solution.py:286
  49.5 0.7 %sum.1 = f32[32,64]{1,0:T(8,128)} custom-call(bf16[32,16,128]{2,1,0:T(8,128)(2,1)S(1)} %all_to_all.5.parts), custom_call_target="tpu_custom_call" | custom-call | tf_op jit(solution)/shard_map/sum/pallas_call | solution.py:287
Async XLA Ops:
  3.2 31.5 %collective-permute-start = (bf16[208,1024]{1,0:T(8,128)(2,1)}, bf16[208,1024]{1,0:T(8,128)(2,1)S(1)}, u32[]{:S(2)}, u32[]{:S(2)}) collective-permute-start(bf16[208,1024]{1,0:T(8,128)(2,1)} %share.1), channel_id=1, source_target_pairs={{0,1},{1,0},{2,3},{3,2},{4,5},{5,4},{6,7},{7,6},{8,9},{9,8},{10,11... | collective-permute-start | bytes 1277960 | tf_op jit(solution)/shard_map/ppermute | solution.py:222
  6.3 28.4 %collective-permute-start.1 = (bf16[208,1024]{1,0:T(8,128)(2,1)}, bf16[208,1024]{1,0:T(8,128)(2,1)S(1)}, u32[]{:S(2)}, u32[]{:S(2)}) collective-permute-start(bf16[208,1024]{1,0:T(8,128)(2,1)} %share.1), channel_id=1, source_target_pairs={{1,2},{2,1},{5,6},{6,5},{9,10},{10,9},{13,14},{14,13},{17,18},{18,... | collective-permute-start | bytes 1277960 | tf_op jit(solution)/shard_map/ppermute | solution.py:223
  7.0 16.0 %collective-permute-start.2 = (f32[64,64]{1,0:T(8,128)}, f32[64,64]{1,0:T(8,128)S(1)}, u32[]{:S(2)}, u32[]{:S(2)}) collective-permute-start(f32[64,64]{1,0:T(8,128)} %refs_0_.1), channel_id=1, source_target_pairs={{0,2},{1,3},{2,0},{3,1},{4,6},{5,7},{6,4},{7,5},{8,10},{9,11},{10,... | collective-permute-start | bytes 49160 | tf_op jit(solution)/shard_map/ppermute | solution.py:205
  10.9 12.1 %collective-permute-start.3 = (f32[64,64]{1,0:T(8,128)}, f32[64,64]{1,0:T(8,128)S(1)}, u32[]{:S(2)}, u32[]{:S(2)}) collective-permute-start(f32[64,64]{1,0:T(8,128)} %refs_0_.1), channel_id=1, source_target_pairs={{0,3},{1,2},{2,1},{3,0},{4,7},{5,6},{6,5},{7,4},{8,11},{9,10},{10,... | collective-permute-start | bytes 49160 | tf_op jit(solution)/shard_map/ppermute | solution.py:205
  13.8 9.2 %collective-permute-start.4 = (f32[64,64]{1,0:T(8,128)}, f32[64,64]{1,0:T(8,128)S(1)}, u32[]{:S(2)}, u32[]{:S(2)}) collective-permute-start(f32[64,64]{1,0:T(8,128)} %refs_0_.1), channel_id=1, source_target_pairs={{0,1},{1,0},{2,3},{3,2},{4,5},{5,4},{6,7},{7,6},{8,9},{9,8},{10,11... | collective-permute-start | bytes 49160 | tf_op jit(solution)/shard_map/ppermute | solution.py:205
  14.5 1.9 %copy-start = (f32[1,3,64,4096]{3,2,1,0:T(8,128)S(1)}, f32[1,3,64,4096]{3,2,1,0:T(8,128)}, u32[]{:S(2)}) copy-start(f32[1,3,64,4096]{3,2,1,0:T(8,128)} %tensor.3) | copy-start | bytes 9437188
  16.4 6.6 %copy-start.3 = (f32[64,64]{1,0:T(8,128)S(1)}, f32[64,64]{1,0:T(8,128)}, u32[]{:S(2)}) copy-start(f32[64,64]{1,0:T(8,128)} %refs_0_.1) | copy-start | bytes 49156
  16.4 6.6 %copy-start.4 = (s32[1,3,1]{1,2,0:T(1,128)S(1)}, s32[1,3,1]{1,2,0:T(1,128)}, u32[]{:S(2)}) copy-start(s32[1,3,1]{1,2,0:T(1,128)} %param.8) | copy-start | bytes 40
  23.0 10.5 %copy-start.1 = (f32[1,3,64,1024]{3,2,1,0:T(8,128)S(1)}, f32[1,3,64,1024]{3,2,1,0:T(8,128)}, u32[]{:S(2)}) copy-start(f32[1,3,64,1024]{3,2,1,0:T(8,128)} %metric.3) | copy-start | bytes 2359300
  23.0 10.5 %copy-start.2 = (s32[1,3,1]{1,2,0:T(1,128)S(1)}, s32[1,3,1]{1,2,0:T(1,128)}, u32[]{:S(2)}) copy-start(s32[1,3,1]{1,2,0:T(1,128)} %param.12) | copy-start | bytes 40
  25.7 10.4 %collective-permute-start.5 = (bf16[64,1024]{1,0:T(8,128)(2,1)S(1)}, bf16[64,1024]{1,0:T(8,128)(2,1)S(1)}, u32[]{:S(2)}, u32[]{:S(2)}) collective-permute-start(bf16[64,1024]{1,0:T(8,128)(2,1)S(1)} %get-tuple-element.19.far_half), channel_id=1, source_target_pairs={{0,2},{3,1},{4,6},{7,5},{8,10},{11,9},{12,14},{15,13},{16,18},{19,... | collective-permute-start | bytes 393224 | tf_op jit(solution)/shard_map/ppermute | solution.py:250
  29.7 6.4 %collective-permute-start.6 = (bf16[64,1024]{1,0:T(8,128)(2,1)S(1)}, bf16[64,1024]{1,0:T(8,128)(2,1)S(1)}, u32[]{:S(2)}, u32[]{:S(2)}) collective-permute-start(bf16[64,1024]{1,0:T(8,128)(2,1)S(1)} %get-tuple-element.22), channel_id=1, source_target_pairs={{1,2},{2,1},{5,6},{6,5},{9,10},{10,9},{13,14},{14,13},{17,18},{18,... | collective-permute-start | bytes 393224 | tf_op jit(solution)/shard_map/ppermute | solution.py:251
  30.4 5.7 %collective-permute-start.7 = (bf16[64,1024]{1,0:T(8,128)(2,1)S(1)}, bf16[64,1024]{1,0:T(8,128)(2,1)S(1)}, u32[]{:S(2)}, u32[]{:S(2)}) collective-permute-start(bf16[64,1024]{1,0:T(8,128)(2,1)S(1)} %get-tuple-element.22), channel_id=1, source_target_pairs={{0,1},{3,2},{4,5},{7,6},{8,9},{11,10},{12,13},{15,14},{16,17},{19,... | collective-permute-start | bytes 393224 | tf_op jit(solution)/shard_map/ppermute | solution.py:252

commit v8 on v6

--- a/solution.py
+++ b/solution.py
@@ -16,7 +16,11 @@
 
 
 DENSITY_ORDER = (2, 3, 1)
-HALF_ORDER = (3, 2, 1)
+FACTORS = (1, 4, 2, 3)
+
+
+def goes_to(factor, z):
+    return (z + 1) * factor % 5 - 1
 
 
 def by_distance(refs, order):
@@ -95,7 +99,9 @@
     lam = lam_all // n_mu
     slots = nu_slots.shape[2]
     row, col = iota((lam_all, 256), 0), iota((lam_all, 256), 1)
-    group = ((col >> 3) & 3) ^ z
+    group = z
+    for slot in range(1, n_mu):
+        group = jnp.where((col >> 3) & 3 == slot, lax.rem((z + 1) * FACTORS[slot], 5) - 1, group)
     wanted = group * lam + (col >> 7) * 8 + (col & 7)
     choose = jnp.where(row == wanted, 1.0, 0.0).astype(BF16)
     for s in range(n_mu):
@@ -136,7 +142,7 @@
 
 
 def exchange_kernel(n_mu, n_aux, *refs):
-    halves = by_distance(refs[:n_mu], HALF_ORDER)
+    halves = refs[:n_mu]
     m_hi, m_lo, out, total = refs[n_mu:]
     z = lax.axis_index("mu")
     left = jnp.concatenate([h[...] for h in halves], axis=0)
@@ -144,7 +150,8 @@
     product += jnp.dot(left, m_lo[...], preferred_element_type=F32)
     orb = halves[0].shape[0]
     for s in range(n_mu):
-        block = z ^ s
+        back = pow(FACTORS[s], -1, 5)
+        block = lax.rem((z + 1) * back, 5) - 1
         total[pl.ds(pl.multiple_of(block * orb, orb), orb), :] = product[s * orb:(s + 1) * orb]
     rows = out.shape[1]
     lower = iota((rows, 128), 1) < 64
@@ -215,7 +222,10 @@
         cost_estimate=pl.CostEstimate(flops=10_000_000, bytes_accessed=2_000_000, transcendentals=0),
         name="metric",
     )(sig_slots, sig_count, halves[0], metric_tensor)
-    halves = [halves[0]] + [lax.ppermute(halves[s], "mu", turns[s]) for s in HALF_ORDER]
+    halves = [halves[0]] + [
+        lax.ppermute(halves[s], "mu", [(z, goes_to(FACTORS[s], z)) for z in range(n_mu)])
+        for s in range(1, n_mu)
+    ]
     rows = n_mu * orb // n_aux
     parts = pl.pallas_call(
         functools.partial(exchange_kernel, n_mu, n_aux),

time: 39.7 us -> 39.7 us (level)
  waiting for transfers between devices: 8.25 us -> 7.71 us
  starting transfers between devices: 10.1 us -> 10.6 us
    ppermute x3, starting transfers between devices: 4.45 us -> 5 us  [fast(): lax.ppermute(halves[s], 'mu', [(z, goes_to(FACTORS[s], z)) for z in range...]
    ppermute x3, waiting for transfers between devices: 6.56 us -> 6.02 us  [fast(): lax.ppermute(halves[s], 'mu', [(z, goes_to(FACTORS[s], z)) for z in range...]
where the time goes in v8:
time: 39.7 us; the launch traced here: 39.6 us
  blocking collectives  12.9 us (32%)
  starting transfers between devices  10.6 us (27%)
  waiting for transfers between devices  7.71 us (19%)
  Pallas kernels  6.9 us (17%)
  between operations  1.4 us (4%)
    all_to_all x1, blocking collectives, fast(): parts = lax.all_to_all(parts, ('aux', 'mu'), 0, 0)  12.9 us
    ppermute x3, waiting for transfers between devices, fast(): lax.ppermute(halves[s], 'mu', [(z, goes_to(FACTORS[s], z)) for z in range...  6.02 us
    ppermute x3, starting transfers between devices, fast(): lax.ppermute(density, 'mu', turns[s])  5.62 us
    ppermute x3, starting transfers between devices, fast(): lax.ppermute(halves[s], 'mu', [(z, goes_to(FACTORS[s], z)) for z in range...  5 us
    pallas_call x1, Pallas kernels, fast(): pl.pallas_call(functools.partial(half_kernel, n_mu), out_shape=(half_shap...  2.67 us
    pallas_call x1, Pallas kernels, fast(): pl.pallas_call(tensor_kernel, out_shape=(t_shape, t_shape), in_specs=[HBM...  1.97 us
    ppermute x3, waiting for transfers between devices, fast(): lax.ppermute(density, 'mu', turns[s])  1.69 us
    pallas_call x1, Pallas kernels, fast(): pl.pallas_call(metric_kernel, out_shape=(m_shape, m_shape), in_specs=[SME...  1 us
  transfers between devices with their start and end apart: 6, of which 3 were waited for; matrix products, arithmetic and copies ran while one was open for 0% of the time, Pallas kernels for 7%

profile of v8, /device:TPU:0, one launch (start us, length us, event | category | flops | bytes accessed | tf_op | source)
XLA Modules:
  0.0 39.6 jit_solution(3300490212623297548)
XLA Ops:
  0.0 4.0 %collective-permute-start = (f32[64,64]{1,0:T(8,128)}, f32[64,64]{1,0:T(8,128)S(1)}, u32[]{:S(2)}, u32[]{:S(2)}) collective-permute-start(f32[64,64]{1,0:T(8,128)} %refs_0_.1), channel_id=1, source_target_pairs={{0,2},{1,3},{2,0},{3,1},{4,6},{5,7},{6,4},{7,5},{8,10},{9,11},{10,... | collective-permute-start | bytes 49160 | tf_op jit(solution)/shard_map/ppermute | solution.py:182
  4.0 1.3 %collective-permute-start.1 = (f32[64,64]{1,0:T(8,128)}, f32[64,64]{1,0:T(8,128)S(1)}, u32[]{:S(2)}, u32[]{:S(2)}) collective-permute-start(f32[64,64]{1,0:T(8,128)} %refs_0_.1), channel_id=1, source_target_pairs={{0,3},{1,2},{2,1},{3,0},{4,7},{5,6},{6,5},{7,4},{8,11},{9,10},{10,... | collective-permute-start | bytes 49160 | tf_op jit(solution)/shard_map/ppermute | solution.py:182
  5.4 0.2 collective-permute-start.2
  6.3 0.0 copy-start.2
  6.3 0.0 copy-start.3
  6.3 2.0 %tensor.2 = (bf16[1024,768]{1,0:T(8,128)(2,1)S(1)}, bf16[1024,768]{1,0:T(8,128)(2,1)S(1)}) custom-call(f32[1,3,64,4096]{3,2,1,0:T(8,128)} %tensor.3), custom_call_target="tpu_custom_call" | custom-call | flops 10000000 | bytes 6000000 | tf_op jit(solution)/shard_map/tensor/pallas_call | solution.py:187
  8.3 0.0 collective-permute-done.refs_1_
  8.3 1.7 %collective-permute-done.1.refs_2_ = f32[64,64]{1,0:T(8,128)S(1)} collective-permute-done((f32[64,64]{1,0:T(8,128)}, f32[64,64]{1,0:T(8,128)S(1)}, u32[]{:S(2)}, u32[]{:S(2)}) %collective-permute-start.1) | collective-permute-done | bytes 16416 | tf_op jit(solution)/shard_map/ppermute | solution.py:182
  10.0 0.0 collective-permute-done.2.refs_3_
  10.0 0.0 copy-done.2
  10.0 0.0 copy-done.3
  10.0 0.0 copy-start
  10.0 0.0 copy-start.1
  10.0 2.7 %half.1 = (bf16[64,1024]{1,0:T(8,128)(2,1)S(1)}, bf16[64,1024]{1,0:T(8,128)(2,1)S(1)}, bf16[64,1024]{1,0:T(8,128)(2,1)S(1)}, bf16[64,1024]{1,0:T(8,128)(2,1)S(1)}) custom-call(s32[1,1,3]{2,1,0:T(1,128)S(1)} %bitcast.3, s32[1,1]{1,0:T(1,128)S(6)} %copy.8.nu_count, f32[64,64]{1,0:T(8,128)S(1)} %copy-done.2, f32[64,64]{1,0:T(8,128)S(1)} %collective-permute-done.refs_1_, ...), custom_call_target="tpu_custom_call" | custom-call | flops 1200000000 | bytes 4000000 | tf_op jit(solution)/shard_map/half/pallas_call | solution.py:201
  12.7 2.1 %collective-permute-start.3 = (bf16[64,1024]{1,0:T(8,128)(2,1)S(1)}, bf16[64,1024]{1,0:T(8,128)(2,1)S(1)}, u32[]{:S(2)}, u32[]{:S(2)}) collective-permute-start(bf16[64,1024]{1,0:T(8,128)(2,1)S(1)} %get-tuple-element.16), channel_id=1, source_target_pairs={{0,3},{1,2},{2,1},{3,0},{4,7},{5,6},{6,5},{7,4},{8,11},{9,10},{10,... | collective-permute-start | bytes 393224 | tf_op jit(solution)/shard_map/ppermute | solution.py:226
  14.8 0.0 collective-permute-start.4
  14.8 2.9 %collective-permute-start.5 = (bf16[64,1024]{1,0:T(8,128)(2,1)S(1)}, bf16[64,1024]{1,0:T(8,128)(2,1)S(1)}, u32[]{:S(2)}, u32[]{:S(2)}) collective-permute-start(bf16[64,1024]{1,0:T(8,128)(2,1)S(1)} %get-tuple-element.18), channel_id=1, source_target_pairs={{0,2},{1,0},{2,3},{3,1},{4,6},{5,4},{6,7},{7,5},{8,10},{9,8},{10,1... | collective-permute-start | bytes 393224 | tf_op jit(solution)/shard_map/ppermute | solution.py:226
  18.3 0.0 copy-done
  18.3 0.0 copy-done.1
  18.4 1.0 %metric.2 = (bf16[1024,256]{1,0:T(8,128)(2,1)S(1)}, bf16[1024,256]{1,0:T(8,128)(2,1)S(1)}) custom-call(s32[1,1,3]{2,1,0:T(1,128)S(1)} %bitcast.2, s32[1,1]{1,0:T(1,128)S(6)} %copy.9.sig_count, bf16[64,1024]{1,0:T(8,128)(2,1)S(1)} %get-tuple-element.15.after.refs_0_, f32[1,3,64,1024]{3,2,1,0:T(8,128)S(1)} %copy-done), custom_call_target="tpu_custom_call" | custom-call | flops 10000000 | bytes 2000000 | tf_op jit(solution)/shard_map/metric/pallas_call | solution.py:216
  19.4 1.7 %collective-permute-done.3.refs_1_ = bf16[64,1024]{1,0:T(8,128)(2,1)S(1)} collective-permute-done((bf16[64,1024]{1,0:T(8,128)(2,1)S(1)}, bf16[64,1024]{1,0:T(8,128)(2,1)S(1)}, u32[]{:S(2)}, u32[]{:S(2)}) %collective-permute-start.3) | collective-permute-done | bytes 131104 | tf_op jit(solution)/shard_map/ppermute | solution.py:226
  21.1 4.3 %collective-permute-done.4.refs_2_ = bf16[64,1024]{1,0:T(8,128)(2,1)S(1)} collective-permute-done((bf16[64,1024]{1,0:T(8,128)(2,1)S(1)}, bf16[64,1024]{1,0:T(8,128)(2,1)S(1)}, u32[]{:S(2)}, u32[]{:S(2)}) %collective-permute-start.4) | collective-permute-done | bytes 131104 | tf_op jit(solution)/shard_map/ppermute | solution.py:226
  25.4 0.0 collective-permute-done.5.refs_3_
  25.4 0.5 %exchange.1 = bf16[32,16,128]{2,1,0:T(8,128)(2,1)S(1)} custom-call(bf16[64,1024]{1,0:T(8,128)(2,1)S(1)} %get-tuple-element.15.after.refs_0_, bf16[64,1024]{1,0:T(8,128)(2,1)S(1)} %collective-permute-done.3.refs_1_, bf16[64,1024]{1,0:T(8,128)(2,1)S(1)} %collective-permute-done.4.refs_2_, bf16[64,1024]{1,0:T(8,128)(2,1)S(1)} %collective-permute-done.5.refs_3_, ...), custom_call_target="tpu_custom_call" | custom-call | flops 300000000 | bytes 2000000 | tf_op jit(solution)/shard_map/exchange/pallas_call | solution.py:230
  25.9 12.9 %all_to_all.5.parts = bf16[32,16,128]{2,1,0:T(8,128)(2,1)S(1)} all-to-all(bf16[32,16,128]{2,1,0:T(8,128)(2,1)S(1)} %exchange.1), channel_id=1, replica_groups=mesh['aux'=8,'mu'=4] {'aux','mu'}, dimensions={0} | all-to-all | bytes 262144 | tf_op jit(solution)/shard_map/all_to_all | solution.py:240
  38.9 0.7 %sum.1 = f32[32,64]{1,0:T(8,128)} custom-call(bf16[32,16,128]{2,1,0:T(8,128)(2,1)S(1)} %all_to_all.5.parts), custom_call_target="tpu_custom_call" | custom-call | tf_op jit(solution)/shard_map/sum/pallas_call | solution.py:241
Async XLA Ops:
  0.0 8.3 %collective-permute-start = (f32[64,64]{1,0:T(8,128)}, f32[64,64]{1,0:T(8,128)S(1)}, u32[]{:S(2)}, u32[]{:S(2)}) collective-permute-start(f32[64,64]{1,0:T(8,128)} %refs_0_.1), channel_id=1, source_target_pairs={{0,2},{1,3},{2,0},{3,1},{4,6},{5,7},{6,4},{7,5},{8,10},{9,11},{10,... | collective-permute-start | bytes 49160 | tf_op jit(solution)/shard_map/ppermute | solution.py:182
  4.0 5.9 %collective-permute-start.1 = (f32[64,64]{1,0:T(8,128)}, f32[64,64]{1,0:T(8,128)S(1)}, u32[]{:S(2)}, u32[]{:S(2)}) collective-permute-start(f32[64,64]{1,0:T(8,128)} %refs_0_.1), channel_id=1, source_target_pairs={{0,3},{1,2},{2,1},{3,0},{4,7},{5,6},{6,5},{7,4},{8,11},{9,10},{10,... | collective-permute-start | bytes 49160 | tf_op jit(solution)/shard_map/ppermute | solution.py:182
  5.4 4.6 %collective-permute-start.2 = (f32[64,64]{1,0:T(8,128)}, f32[64,64]{1,0:T(8,128)S(1)}, u32[]{:S(2)}, u32[]{:S(2)}) collective-permute-start(f32[64,64]{1,0:T(8,128)} %refs_0_.1), channel_id=1, source_target_pairs={{0,1},{1,0},{2,3},{3,2},{4,5},{5,4},{6,7},{7,6},{8,9},{9,8},{10,11... | collective-permute-start | bytes 49160 | tf_op jit(solution)/shard_map/ppermute | solution.py:182
  6.3 3.7 %copy-start.2 = (f32[64,64]{1,0:T(8,128)S(1)}, f32[64,64]{1,0:T(8,128)}, u32[]{:S(2)}) copy-start(f32[64,64]{1,0:T(8,128)} %refs_0_.1) | copy-start | bytes 49156
  6.3 3.7 %copy-start.3 = (s32[1,3,1]{1,2,0:T(1,128)S(1)}, s32[1,3,1]{1,2,0:T(1,128)}, u32[]{:S(2)}) copy-start(s32[1,3,1]{1,2,0:T(1,128)} %param.8) | copy-start | bytes 40
  10.0 8.4 %copy-start = (f32[1,3,64,1024]{3,2,1,0:T(8,128)S(1)}, f32[1,3,64,1024]{3,2,1,0:T(8,128)}, u32[]{:S(2)}) copy-start(f32[1,3,64,1024]{3,2,1,0:T(8,128)} %metric.3) | copy-start | bytes 2359300
  10.0 8.4 %copy-start.1 = (s32[1,3,1]{1,2,0:T(1,128)S(1)}, s32[1,3,1]{1,2,0:T(1,128)}, u32[]{:S(2)}) copy-start(s32[1,3,1]{1,2,0:T(1,128)} %param.12) | copy-start | bytes 40
  12.7 8.4 %collective-permute-start.3 = (bf16[64,1024]{1,0:T(8,128)(2,1)S(1)}, bf16[64,1024]{1,0:T(8,128)(2,1)S(1)}, u32[]{:S(2)}, u32[]{:S(2)}) collective-permute-start(bf16[64,1024]{1,0:T(8,128)(2,1)S(1)} %get-tuple-element.16), channel_id=1, source_target_pairs={{0,3},{1,2},{2,1},{3,0},{4,7},{5,6},{6,5},{7,4},{8,11},{9,10},{10,... | collective-permute-start | bytes 393224 | tf_op jit(solution)/shard_map/ppermute | solution.py:226
  14.8 10.6 %collective-permute-start.4 = (bf16[64,1024]{1,0:T(8,128)(2,1)S(1)}, bf16[64,1024]{1,0:T(8,128)(2,1)S(1)}, u32[]{:S(2)}, u32[]{:S(2)}) collective-permute-start(bf16[64,1024]{1,0:T(8,128)(2,1)S(1)} %get-tuple-element.17), channel_id=1, source_target_pairs={{0,1},{1,3},{2,0},{3,2},{4,5},{5,7},{6,4},{7,6},{8,9},{9,11},{10,8... | collective-permute-start | bytes 393224 | tf_op jit(solution)/shard_map/ppermute | solution.py:226
  14.8 10.6 %collective-permute-start.5 = (bf16[64,1024]{1,0:T(8,128)(2,1)S(1)}, bf16[64,1024]{1,0:T(8,128)(2,1)S(1)}, u32[]{:S(2)}, u32[]{:S(2)}) collective-permute-start(bf16[64,1024]{1,0:T(8,128)(2,1)S(1)} %get-tuple-element.18), channel_id=1, source_target_pairs={{0,2},{1,0},{2,3},{3,1},{4,6},{5,4},{6,7},{7,5},{8,10},{9,8},{10,1... | collective-permute-start | bytes 393224 | tf_op jit(solution)/shard_map/ppermute | solution.py:226

commit v9 on v8

--- a/solution.py
+++ b/solution.py
@@ -160,9 +160,9 @@
             columns = slice(pair * 128, (pair + 1) * 128)
             top = total[a * 2 * rows:(a * 2 + 1) * rows, columns]
             bottom = total[(a * 2 + 1) * rows:(a * 2 + 2) * rows, columns]
-            at = a * n_mu + pair * 2
+            at = n_aux * n_mu - 1 - (a * n_mu + pair * 2)
             out[at] = jnp.where(lower, top, pltpu.roll(bottom, 64, 1)).astype(BF16)
-            out[at + 1] = jnp.where(lower, pltpu.roll(top, 64, 1), bottom).astype(BF16)
+            out[at - 1] = jnp.where(lower, pltpu.roll(top, 64, 1), bottom).astype(BF16)
 
 
 def sum_kernel(parts, out):
@@ -237,7 +237,8 @@
         cost_estimate=pl.CostEstimate(flops=300_000_000, bytes_accessed=2_000_000, transcendentals=0),
         name="exchange",
     )(*halves, m_hi, m_lo)
-    parts = lax.all_to_all(parts, ("aux", "mu"), 0, 0)
+    down = list(reversed(range(n_aux * n_mu)))
+    parts = lax.all_to_all(parts, ("aux", "mu"), 0, 0, axis_index_groups=[down])
     return pl.pallas_call(
         sum_kernel,
         out_shape=jax.ShapeDtypeStruct((rows, orb), F32),

time: 39.7 us -> 39.2 us (0.987)
  blocking collectives: 12.9 us -> 12.4 us
    all_to_all x1, blocking collectives: 12.9 us -> 12.4 us  [fast(): parts = lax.all_to_all(parts, ('aux', 'mu'), 0, 0, axis_index_groups=[down])]
  transfers between devices with their start and end apart: 6 -> 6, of which waited for: 3 -> 3; matrix products, arithmetic and copies ran while one was open for 0% -> 0% of each run, Pallas kernels for 7% -> 8%
where the time goes in v9:
time: 39.2 us; the launch traced here: 39 us
  blocking collectives  12.4 us (32%)
  starting transfers between devices  10.6 us (27%)
  waiting for transfers between devices  7.71 us (20%)
  Pallas kernels  6.9 us (18%)
  between operations  1.4 us (4%)
    all_to_all x1, blocking collectives, fast(): parts = lax.all_to_all(parts, ('aux', 'mu'), 0, 0, axis_index_groups=[down])  12.4 us
    ppermute x3, waiting for transfers between devices, fast(): lax.ppermute(halves[s], 'mu', [(z, goes_to(FACTORS[s], z)) for z in range...  6.02 us
    ppermute x3, starting transfers between devices, fast(): lax.ppermute(density, 'mu', turns[s])  5.62 us
    ppermute x3, starting transfers between devices, fast(): lax.ppermute(halves[s], 'mu', [(z, goes_to(FACTORS[s], z)) for z in range...  5 us
    pallas_call x1, Pallas kernels, fast(): pl.pallas_call(functools.partial(half_kernel, n_mu), out_shape=(half_shap...  2.68 us
    pallas_call x1, Pallas kernels, fast(): pl.pallas_call(tensor_kernel, out_shape=(t_shape, t_shape), in_specs=[HBM...  1.97 us
    ppermute x3, waiting for transfers between devices, fast(): lax.ppermute(density, 'mu', turns[s])  1.69 us
    pallas_call x1, Pallas kernels, fast(): pl.pallas_call(metric_kernel, out_shape=(m_shape, m_shape), in_specs=[SME...  1 us
  transfers between devices with their start and end apart: 6, of which 3 were waited for; matrix products, arithmetic and copies ran while one was open for 0% of the time, Pallas kernels for 8%

profile of v9, /device:TPU:0, one launch (start us, length us, event | category | flops | bytes accessed | tf_op | source)
XLA Modules:
  0.0 39.0 jit_solution(14898503855839507726)
XLA Ops:
  0.0 4.0 %collective-permute-start = (f32[64,64]{1,0:T(8,128)}, f32[64,64]{1,0:T(8,128)S(1)}, u32[]{:S(2)}, u32[]{:S(2)}) collective-permute-start(f32[64,64]{1,0:T(8,128)} %refs_0_.1), channel_id=1, source_target_pairs={{0,2},{1,3},{2,0},{3,1},{4,6},{5,7},{6,4},{7,5},{8,10},{9,11},{10,... | collective-permute-start | bytes 49160 | tf_op jit(solution)/shard_map/ppermute | solution.py:182
  4.0 1.3 %collective-permute-start.1 = (f32[64,64]{1,0:T(8,128)}, f32[64,64]{1,0:T(8,128)S(1)}, u32[]{:S(2)}, u32[]{:S(2)}) collective-permute-start(f32[64,64]{1,0:T(8,128)} %refs_0_.1), channel_id=1, source_target_pairs={{0,3},{1,2},{2,1},{3,0},{4,7},{5,6},{6,5},{7,4},{8,11},{9,10},{10,... | collective-permute-start | bytes 49160 | tf_op jit(solution)/shard_map/ppermute | solution.py:182
  5.4 0.2 collective-permute-start.2
  6.3 0.0 copy-start.2
  6.3 0.0 copy-start.3
  6.3 2.0 %tensor.2 = (bf16[1024,768]{1,0:T(8,128)(2,1)S(1)}, bf16[1024,768]{1,0:T(8,128)(2,1)S(1)}) custom-call(f32[1,3,64,4096]{3,2,1,0:T(8,128)} %tensor.3), custom_call_target="tpu_custom_call" | custom-call | flops 10000000 | bytes 6000000 | tf_op jit(solution)/shard_map/tensor/pallas_call | solution.py:187
  8.3 0.0 collective-permute-done.refs_1_
  8.3 1.7 %collective-permute-done.1.refs_2_ = f32[64,64]{1,0:T(8,128)S(1)} collective-permute-done((f32[64,64]{1,0:T(8,128)}, f32[64,64]{1,0:T(8,128)S(1)}, u32[]{:S(2)}, u32[]{:S(2)}) %collective-permute-start.1) | collective-permute-done | bytes 16416 | tf_op jit(solution)/shard_map/ppermute | solution.py:182
  10.0 0.0 collective-permute-done.2.refs_3_
  10.0 0.0 copy-done.2
  10.0 0.0 copy-done.3
  10.0 0.0 copy-start
  10.0 0.0 copy-start.1
  10.0 2.7 %half.1 = (bf16[64,1024]{1,0:T(8,128)(2,1)S(1)}, bf16[64,1024]{1,0:T(8,128)(2,1)S(1)}, bf16[64,1024]{1,0:T(8,128)(2,1)S(1)}, bf16[64,1024]{1,0:T(8,128)(2,1)S(1)}) custom-call(s32[1,1,3]{2,1,0:T(1,128)S(1)} %bitcast.3, s32[1,1]{1,0:T(1,128)S(6)} %copy.8.nu_count, f32[64,64]{1,0:T(8,128)S(1)} %copy-done.2, f32[64,64]{1,0:T(8,128)S(1)} %collective-permute-done.refs_1_, ...), custom_call_target="tpu_custom_call" | custom-call | flops 1200000000 | bytes 4000000 | tf_op jit(solution)/shard_map/half/pallas_call | solution.py:201
  12.7 2.1 %collective-permute-start.3 = (bf16[64,1024]{1,0:T(8,128)(2,1)S(1)}, bf16[64,1024]{1,0:T(8,128)(2,1)S(1)}, u32[]{:S(2)}, u32[]{:S(2)}) collective-permute-start(bf16[64,1024]{1,0:T(8,128)(2,1)S(1)} %get-tuple-element.16), channel_id=1, source_target_pairs={{0,3},{1,2},{2,1},{3,0},{4,7},{5,6},{6,5},{7,4},{8,11},{9,10},{10,... | collective-permute-start | bytes 393224 | tf_op jit(solution)/shard_map/ppermute | solution.py:226
  14.8 0.0 collective-permute-start.4
  14.8 2.9 %collective-permute-start.5 = (bf16[64,1024]{1,0:T(8,128)(2,1)S(1)}, bf16[64,1024]{1,0:T(8,128)(2,1)S(1)}, u32[]{:S(2)}, u32[]{:S(2)}) collective-permute-start(bf16[64,1024]{1,0:T(8,128)(2,1)S(1)} %get-tuple-element.18), channel_id=1, source_target_pairs={{0,2},{1,0},{2,3},{3,1},{4,6},{5,4},{6,7},{7,5},{8,10},{9,8},{10,1... | collective-permute-start | bytes 393224 | tf_op jit(solution)/shard_map/ppermute | solution.py:226
  18.3 0.0 copy-done
  18.3 0.0 copy-done.1
  18.4 1.0 %metric.2 = (bf16[1024,256]{1,0:T(8,128)(2,1)S(1)}, bf16[1024,256]{1,0:T(8,128)(2,1)S(1)}) custom-call(s32[1,1,3]{2,1,0:T(1,128)S(1)} %bitcast.2, s32[1,1]{1,0:T(1,128)S(6)} %copy.9.sig_count, bf16[64,1024]{1,0:T(8,128)(2,1)S(1)} %get-tuple-element.15.after.refs_0_, f32[1,3,64,1024]{3,2,1,0:T(8,128)S(1)} %copy-done), custom_call_target="tpu_custom_call" | custom-call | flops 10000000 | bytes 2000000 | tf_op jit(solution)/shard_map/metric/pallas_call | solution.py:216
  19.4 1.7 %collective-permute-done.3.refs_1_ = bf16[64,1024]{1,0:T(8,128)(2,1)S(1)} collective-permute-done((bf16[64,1024]{1,0:T(8,128)(2,1)S(1)}, bf16[64,1024]{1,0:T(8,128)(2,1)S(1)}, u32[]{:S(2)}, u32[]{:S(2)}) %collective-permute-start.3) | collective-permute-done | bytes 131104 | tf_op jit(solution)/shard_map/ppermute | solution.py:226
  21.1 4.3 %collective-permute-done.4.refs_2_ = bf16[64,1024]{1,0:T(8,128)(2,1)S(1)} collective-permute-done((bf16[64,1024]{1,0:T(8,128)(2,1)S(1)}, bf16[64,1024]{1,0:T(8,128)(2,1)S(1)}, u32[]{:S(2)}, u32[]{:S(2)}) %collective-permute-start.4) | collective-permute-done | bytes 131104 | tf_op jit(solution)/shard_map/ppermute | solution.py:226
  25.4 0.0 collective-permute-done.5.refs_3_
  25.4 0.5 %exchange.1 = bf16[32,16,128]{2,1,0:T(8,128)(2,1)S(1)} custom-call(bf16[64,1024]{1,0:T(8,128)(2,1)S(1)} %get-tuple-element.15.after.refs_0_, bf16[64,1024]{1,0:T(8,128)(2,1)S(1)} %collective-permute-done.3.refs_1_, bf16[64,1024]{1,0:T(8,128)(2,1)S(1)} %collective-permute-done.4.refs_2_, bf16[64,1024]{1,0:T(8,128)(2,1)S(1)} %collective-permute-done.5.refs_3_, ...), custom_call_target="tpu_custom_call" | custom-call | flops 300000000 | bytes 2000000 | tf_op jit(solution)/shard_map/exchange/pallas_call | solution.py:230
  25.9 12.4 %all_to_all.5.parts = bf16[32,16,128]{2,1,0:T(8,128)(2,1)S(1)} all-to-all(bf16[32,16,128]{2,1,0:T(8,128)(2,1)S(1)} %exchange.1), channel_id=1, replica_groups={{31,30,29,28,27,26,25,24,23,22,21,20,19,18,17,16,15,14,13,12,11,10,9,8,..., dimensions={0} | all-to-all | bytes 262144 | tf_op jit(solution)/shard_map/all_to_all | solution.py:241
  38.3 0.7 %sum.1 = f32[32,64]{1,0:T(8,128)} custom-call(bf16[32,16,128]{2,1,0:T(8,128)(2,1)S(1)} %all_to_all.5.parts), custom_call_target="tpu_custom_call" | custom-call | tf_op jit(solution)/shard_map/sum/pallas_call | solution.py:242
Async XLA Ops:
  0.0 8.3 %collective-permute-start = (f32[64,64]{1,0:T(8,128)}, f32[64,64]{1,0:T(8,128)S(1)}, u32[]{:S(2)}, u32[]{:S(2)}) collective-permute-start(f32[64,64]{1,0:T(8,128)} %refs_0_.1), channel_id=1, source_target_pairs={{0,2},{1,3},{2,0},{3,1},{4,6},{5,7},{6,4},{7,5},{8,10},{9,11},{10,... | collective-permute-start | bytes 49160 | tf_op jit(solution)/shard_map/ppermute | solution.py:182
  4.0 5.9 %collective-permute-start.1 = (f32[64,64]{1,0:T(8,128)}, f32[64,64]{1,0:T(8,128)S(1)}, u32[]{:S(2)}, u32[]{:S(2)}) collective-permute-start(f32[64,64]{1,0:T(8,128)} %refs_0_.1), channel_id=1, source_target_pairs={{0,3},{1,2},{2,1},{3,0},{4,7},{5,6},{6,5},{7,4},{8,11},{9,10},{10,... | collective-permute-start | bytes 49160 | tf_op jit(solution)/shard_map/ppermute | solution.py:182
  5.4 4.6 %collective-permute-start.2 = (f32[64,64]{1,0:T(8,128)}, f32[64,64]{1,0:T(8,128)S(1)}, u32[]{:S(2)}, u32[]{:S(2)}) collective-permute-start(f32[64,64]{1,0:T(8,128)} %refs_0_.1), channel_id=1, source_target_pairs={{0,1},{1,0},{2,3},{3,2},{4,5},{5,4},{6,7},{7,6},{8,9},{9,8},{10,11... | collective-permute-start | bytes 49160 | tf_op jit(solution)/shard_map/ppermute | solution.py:182
  6.3 3.7 %copy-start.2 = (f32[64,64]{1,0:T(8,128)S(1)}, f32[64,64]{1,0:T(8,128)}, u32[]{:S(2)}) copy-start(f32[64,64]{1,0:T(8,128)} %refs_0_.1) | copy-start | bytes 49156
  6.3 3.7 %copy-start.3 = (s32[1,3,1]{1,2,0:T(1,128)S(1)}, s32[1,3,1]{1,2,0:T(1,128)}, u32[]{:S(2)}) copy-start(s32[1,3,1]{1,2,0:T(1,128)} %param.8) | copy-start | bytes 40
  10.0 8.4 %copy-start = (f32[1,3,64,1024]{3,2,1,0:T(8,128)S(1)}, f32[1,3,64,1024]{3,2,1,0:T(8,128)}, u32[]{:S(2)}) copy-start(f32[1,3,64,1024]{3,2,1,0:T(8,128)} %metric.3) | copy-start | bytes 2359300
  10.0 8.4 %copy-start.1 = (s32[1,3,1]{1,2,0:T(1,128)S(1)}, s32[1,3,1]{1,2,0:T(1,128)}, u32[]{:S(2)}) copy-start(s32[1,3,1]{1,2,0:T(1,128)} %param.12) | copy-start | bytes 40
  12.7 8.4 %collective-permute-start.3 = (bf16[64,1024]{1,0:T(8,128)(2,1)S(1)}, bf16[64,1024]{1,0:T(8,128)(2,1)S(1)}, u32[]{:S(2)}, u32[]{:S(2)}) collective-permute-start(bf16[64,1024]{1,0:T(8,128)(2,1)S(1)} %get-tuple-element.16), channel_id=1, source_target_pairs={{0,3},{1,2},{2,1},{3,0},{4,7},{5,6},{6,5},{7,4},{8,11},{9,10},{10,... | collective-permute-start | bytes 393224 | tf_op jit(solution)/shard_map/ppermute | solution.py:226
  14.8 10.6 %collective-permute-start.4 = (bf16[64,1024]{1,0:T(8,128)(2,1)S(1)}, bf16[64,1024]{1,0:T(8,128)(2,1)S(1)}, u32[]{:S(2)}, u32[]{:S(2)}) collective-permute-start(bf16[64,1024]{1,0:T(8,128)(2,1)S(1)} %get-tuple-element.17), channel_id=1, source_target_pairs={{0,1},{1,3},{2,0},{3,2},{4,5},{5,7},{6,4},{7,6},{8,9},{9,11},{10,8... | collective-permute-start | bytes 393224 | tf_op jit(solution)/shard_map/ppermute | solution.py:226
  14.8 10.6 %collective-permute-start.5 = (bf16[64,1024]{1,0:T(8,128)(2,1)S(1)}, bf16[64,1024]{1,0:T(8,128)(2,1)S(1)}, u32[]{:S(2)}, u32[]{:S(2)}) collective-permute-start(bf16[64,1024]{1,0:T(8,128)(2,1)S(1)} %get-tuple-element.18), channel_id=1, source_target_pairs={{0,2},{1,0},{2,3},{3,1},{4,6},{5,4},{6,7},{7,5},{8,10},{9,8},{10,1... | collective-permute-start | bytes 393224 | tf_op jit(solution)/shard_map/ppermute | solution.py:226

commit v10 on v8

--- a/solution.py
+++ b/solution.py
@@ -141,9 +141,20 @@
                 outs[s][group * span:(group + 1) * span, r * 128:(r + 1) * 128] = picked.astype(BF16)
 
 
+def walk(n_mu, n_aux):
+    order = []
+    for turn, chip in enumerate((0, 1, 3, 2)):
+        for z in range(n_mu) if turn % 2 == 0 else reversed(range(n_mu)):
+            order += [(2 * chip + core) * n_mu + z for core in range(2)]
+    assert sorted(order) == list(range(n_aux * n_mu))
+    return order
+
+
 def exchange_kernel(n_mu, n_aux, *refs):
     halves = refs[:n_mu]
     m_hi, m_lo, out, total = refs[n_mu:]
+    order = walk(n_mu, n_aux)
+    places = [order.index(f) for f in range(n_aux * n_mu)]
     z = lax.axis_index("mu")
     left = jnp.concatenate([h[...] for h in halves], axis=0)
     product = jnp.dot(left, m_hi[...], preferred_element_type=F32)
@@ -160,9 +171,9 @@
             columns = slice(pair * 128, (pair + 1) * 128)
             top = total[a * 2 * rows:(a * 2 + 1) * rows, columns]
             bottom = total[(a * 2 + 1) * rows:(a * 2 + 2) * rows, columns]
-            at = a * n_mu + pair * 2
-            out[at] = jnp.where(lower, top, pltpu.roll(bottom, 64, 1)).astype(BF16)
-            out[at + 1] = jnp.where(lower, pltpu.roll(top, 64, 1), bottom).astype(BF16)
+            first, second = places[a * n_mu + pair * 2], places[a * n_mu + pair * 2 + 1]
+            out[first] = jnp.where(lower, top, pltpu.roll(bottom, 64, 1)).astype(BF16)
+            out[second] = jnp.where(lower, pltpu.roll(top, 64, 1), bottom).astype(BF16)
 
 
 def sum_kernel(parts, out):
@@ -237,7 +248,9 @@
         cost_estimate=pl.CostEstimate(flops=300_000_000, bytes_accessed=2_000_000, transcendentals=0),
         name="exchange",
     )(*halves, m_hi, m_lo)
-    parts = lax.all_to_all(parts, ("aux", "mu"), 0, 0)
+    parts = lax.all_to_all(
+        parts, ("aux", "mu"), 0, 0, axis_index_groups=[walk(n_mu, n_aux)]
+    )
     return pl.pallas_call(
         sum_kernel,
         out_shape=jax.ShapeDtypeStruct((rows, orb), F32),

time: 39.7 us -> 39.7 us (level)
  transfers between devices with their start and end apart: 6 -> 6, of which waited for: 3 -> 3; matrix products, arithmetic and copies ran while one was open for 0% -> 0% of each run, Pallas kernels for 7% -> 8%
where the time goes in v10:
time: 39.7 us; the launch traced here: 39.5 us
  blocking collectives  12.9 us (32%)
  starting transfers between devices  10.6 us (27%)
  waiting for transfers between devices  7.71 us (19%)
  Pallas kernels  6.9 us (17%)
  between operations  1.4 us (4%)
    all_to_all x1, blocking collectives, fast(): lax.all_to_all(parts, ('aux', 'mu'), 0, 0, axis_index_groups=[walk(n_mu,...  12.9 us
    ppermute x3, waiting for transfers between devices, fast(): lax.ppermute(halves[s], 'mu', [(z, goes_to(FACTORS[s], z)) for z in range...  6.02 us
    ppermute x3, starting transfers between devices, fast(): lax.ppermute(density, 'mu', turns[s])  5.62 us
    ppermute x3, starting transfers between devices, fast(): lax.ppermute(halves[s], 'mu', [(z, goes_to(FACTORS[s], z)) for z in range...  5 us
    pallas_call x1, Pallas kernels, fast(): pl.pallas_call(functools.partial(half_kernel, n_mu), out_shape=(half_shap...  2.67 us
    pallas_call x1, Pallas kernels, fast(): pl.pallas_call(tensor_kernel, out_shape=(t_shape, t_shape), in_specs=[HBM...  1.97 us
    ppermute x3, waiting for transfers between devices, fast(): lax.ppermute(density, 'mu', turns[s])  1.69 us
    pallas_call x1, Pallas kernels, fast(): pl.pallas_call(metric_kernel, out_shape=(m_shape, m_shape), in_specs=[SME...  1 us
  transfers between devices with their start and end apart: 6, of which 3 were waited for; matrix products, arithmetic and copies ran while one was open for 0% of the time, Pallas kernels for 8%

profile of v10, /device:TPU:0, one launch (start us, length us, event | category | flops | bytes accessed | tf_op | source)
XLA Modules:
  0.0 39.5 jit_solution(8564271263825053570)
XLA Ops:
  0.0 4.0 %collective-permute-start = (f32[64,64]{1,0:T(8,128)}, f32[64,64]{1,0:T(8,128)S(1)}, u32[]{:S(2)}, u32[]{:S(2)}) collective-permute-start(f32[64,64]{1,0:T(8,128)} %refs_0_.1), channel_id=1, source_target_pairs={{0,2},{1,3},{2,0},{3,1},{4,6},{5,7},{6,4},{7,5},{8,10},{9,11},{10,... | collective-permute-start | bytes 49160 | tf_op jit(solution)/shard_map/ppermute | solution.py:193
  4.0 1.3 %collective-permute-start.1 = (f32[64,64]{1,0:T(8,128)}, f32[64,64]{1,0:T(8,128)S(1)}, u32[]{:S(2)}, u32[]{:S(2)}) collective-permute-start(f32[64,64]{1,0:T(8,128)} %refs_0_.1), channel_id=1, source_target_pairs={{0,3},{1,2},{2,1},{3,0},{4,7},{5,6},{6,5},{7,4},{8,11},{9,10},{10,... | collective-permute-start | bytes 49160 | tf_op jit(solution)/shard_map/ppermute | solution.py:193
  5.4 0.2 collective-permute-start.2
  6.3 0.0 copy-start.2
  6.3 0.0 copy-start.3
  6.3 2.0 %tensor.2 = (bf16[1024,768]{1,0:T(8,128)(2,1)S(1)}, bf16[1024,768]{1,0:T(8,128)(2,1)S(1)}) custom-call(f32[1,3,64,4096]{3,2,1,0:T(8,128)} %tensor.3), custom_call_target="tpu_custom_call" | custom-call | flops 10000000 | bytes 6000000 | tf_op jit(solution)/shard_map/tensor/pallas_call | solution.py:198
  8.3 0.0 collective-permute-done.refs_1_
  8.3 1.7 %collective-permute-done.1.refs_2_ = f32[64,64]{1,0:T(8,128)S(1)} collective-permute-done((f32[64,64]{1,0:T(8,128)}, f32[64,64]{1,0:T(8,128)S(1)}, u32[]{:S(2)}, u32[]{:S(2)}) %collective-permute-start.1) | collective-permute-done | bytes 16416 | tf_op jit(solution)/shard_map/ppermute | solution.py:193
  10.0 0.0 collective-permute-done.2.refs_3_
  10.0 0.0 copy-done.2
  10.0 0.0 copy-done.3
  10.0 0.0 copy-start
  10.0 0.0 copy-start.1
  10.0 2.7 %half.1 = (bf16[64,1024]{1,0:T(8,128)(2,1)S(1)}, bf16[64,1024]{1,0:T(8,128)(2,1)S(1)}, bf16[64,1024]{1,0:T(8,128)(2,1)S(1)}, bf16[64,1024]{1,0:T(8,128)(2,1)S(1)}) custom-call(s32[1,1,3]{2,1,0:T(1,128)S(1)} %bitcast.3, s32[1,1]{1,0:T(1,128)S(6)} %copy.8.nu_count, f32[64,64]{1,0:T(8,128)S(1)} %copy-done.2, f32[64,64]{1,0:T(8,128)S(1)} %collective-permute-done.refs_1_, ...), custom_call_target="tpu_custom_call" | custom-call | flops 1200000000 | bytes 4000000 | tf_op jit(solution)/shard_map/half/pallas_call | solution.py:212
  12.7 2.1 %collective-permute-start.3 = (bf16[64,1024]{1,0:T(8,128)(2,1)S(1)}, bf16[64,1024]{1,0:T(8,128)(2,1)S(1)}, u32[]{:S(2)}, u32[]{:S(2)}) collective-permute-start(bf16[64,1024]{1,0:T(8,128)(2,1)S(1)} %get-tuple-element.16), channel_id=1, source_target_pairs={{0,3},{1,2},{2,1},{3,0},{4,7},{5,6},{6,5},{7,4},{8,11},{9,10},{10,... | collective-permute-start | bytes 393224 | tf_op jit(solution)/shard_map/ppermute | solution.py:237
  14.8 0.0 collective-permute-start.4
  14.8 2.9 %collective-permute-start.5 = (bf16[64,1024]{1,0:T(8,128)(2,1)S(1)}, bf16[64,1024]{1,0:T(8,128)(2,1)S(1)}, u32[]{:S(2)}, u32[]{:S(2)}) collective-permute-start(bf16[64,1024]{1,0:T(8,128)(2,1)S(1)} %get-tuple-element.18), channel_id=1, source_target_pairs={{0,2},{1,0},{2,3},{3,1},{4,6},{5,4},{6,7},{7,5},{8,10},{9,8},{10,1... | collective-permute-start | bytes 393224 | tf_op jit(solution)/shard_map/ppermute | solution.py:237
  18.3 0.0 copy-done
  18.3 0.0 copy-done.1
  18.4 1.0 %metric.2 = (bf16[1024,256]{1,0:T(8,128)(2,1)S(1)}, bf16[1024,256]{1,0:T(8,128)(2,1)S(1)}) custom-call(s32[1,1,3]{2,1,0:T(1,128)S(1)} %bitcast.2, s32[1,1]{1,0:T(1,128)S(6)} %copy.9.sig_count, bf16[64,1024]{1,0:T(8,128)(2,1)S(1)} %get-tuple-element.15.after.refs_0_, f32[1,3,64,1024]{3,2,1,0:T(8,128)S(1)} %copy-done), custom_call_target="tpu_custom_call" | custom-call | flops 10000000 | bytes 2000000 | tf_op jit(solution)/shard_map/metric/pallas_call | solution.py:227
  19.4 1.7 %collective-permute-done.3.refs_1_ = bf16[64,1024]{1,0:T(8,128)(2,1)S(1)} collective-permute-done((bf16[64,1024]{1,0:T(8,128)(2,1)S(1)}, bf16[64,1024]{1,0:T(8,128)(2,1)S(1)}, u32[]{:S(2)}, u32[]{:S(2)}) %collective-permute-start.3) | collective-permute-done | bytes 131104 | tf_op jit(solution)/shard_map/ppermute | solution.py:237
  21.1 4.3 %collective-permute-done.4.refs_2_ = bf16[64,1024]{1,0:T(8,128)(2,1)S(1)} collective-permute-done((bf16[64,1024]{1,0:T(8,128)(2,1)S(1)}, bf16[64,1024]{1,0:T(8,128)(2,1)S(1)}, u32[]{:S(2)}, u32[]{:S(2)}) %collective-permute-start.4) | collective-permute-done | bytes 131104 | tf_op jit(solution)/shard_map/ppermute | solution.py:237
  25.4 0.0 collective-permute-done.5.refs_3_
  25.4 0.5 %exchange.1 = bf16[32,16,128]{2,1,0:T(8,128)(2,1)S(1)} custom-call(bf16[64,1024]{1,0:T(8,128)(2,1)S(1)} %get-tuple-element.15.after.refs_0_, bf16[64,1024]{1,0:T(8,128)(2,1)S(1)} %collective-permute-done.3.refs_1_, bf16[64,1024]{1,0:T(8,128)(2,1)S(1)} %collective-permute-done.4.refs_2_, bf16[64,1024]{1,0:T(8,128)(2,1)S(1)} %collective-permute-done.5.refs_3_, ...), custom_call_target="tpu_custom_call" | custom-call | flops 300000000 | bytes 2000000 | tf_op jit(solution)/shard_map/exchange/pallas_call | solution.py:241
  25.9 12.9 %all_to_all.5.parts = bf16[32,16,128]{2,1,0:T(8,128)(2,1)S(1)} all-to-all(bf16[32,16,128]{2,1,0:T(8,128)(2,1)S(1)} %exchange.1), channel_id=1, replica_groups={{0,4,1,5,2,6,3,7,11,15,10,14,9,13,8,12,24,28,25,29,26,30,27,31,19,23,18..., dimensions={0} | all-to-all | bytes 262144 | tf_op jit(solution)/shard_map/all_to_all | solution.py:251
  38.8 0.7 %sum.1 = f32[32,64]{1,0:T(8,128)} custom-call(bf16[32,16,128]{2,1,0:T(8,128)(2,1)S(1)} %all_to_all.5.parts), custom_call_target="tpu_custom_call" | custom-call | tf_op jit(solution)/shard_map/sum/pallas_call | solution.py:254
Async XLA Ops:
  0.0 8.3 %collective-permute-start = (f32[64,64]{1,0:T(8,128)}, f32[64,64]{1,0:T(8,128)S(1)}, u32[]{:S(2)}, u32[]{:S(2)}) collective-permute-start(f32[64,64]{1,0:T(8,128)} %refs_0_.1), channel_id=1, source_target_pairs={{0,2},{1,3},{2,0},{3,1},{4,6},{5,7},{6,4},{7,5},{8,10},{9,11},{10,... | collective-permute-start | bytes 49160 | tf_op jit(solution)/shard_map/ppermute | solution.py:193
  4.0 5.9 %collective-permute-start.1 = (f32[64,64]{1,0:T(8,128)}, f32[64,64]{1,0:T(8,128)S(1)}, u32[]{:S(2)}, u32[]{:S(2)}) collective-permute-start(f32[64,64]{1,0:T(8,128)} %refs_0_.1), channel_id=1, source_target_pairs={{0,3},{1,2},{2,1},{3,0},{4,7},{5,6},{6,5},{7,4},{8,11},{9,10},{10,... | collective-permute-start | bytes 49160 | tf_op jit(solution)/shard_map/ppermute | solution.py:193
  5.4 4.6 %collective-permute-start.2 = (f32[64,64]{1,0:T(8,128)}, f32[64,64]{1,0:T(8,128)S(1)}, u32[]{:S(2)}, u32[]{:S(2)}) collective-permute-start(f32[64,64]{1,0:T(8,128)} %refs_0_.1), channel_id=1, source_target_pairs={{0,1},{1,0},{2,3},{3,2},{4,5},{5,4},{6,7},{7,6},{8,9},{9,8},{10,11... | collective-permute-start | bytes 49160 | tf_op jit(solution)/shard_map/ppermute | solution.py:193
  6.3 3.7 %copy-start.2 = (f32[64,64]{1,0:T(8,128)S(1)}, f32[64,64]{1,0:T(8,128)}, u32[]{:S(2)}) copy-start(f32[64,64]{1,0:T(8,128)} %refs_0_.1) | copy-start | bytes 49156
  6.3 3.7 %copy-start.3 = (s32[1,3,1]{1,2,0:T(1,128)S(1)}, s32[1,3,1]{1,2,0:T(1,128)}, u32[]{:S(2)}) copy-start(s32[1,3,1]{1,2,0:T(1,128)} %param.8) | copy-start | bytes 40
  10.0 8.4 %copy-start = (f32[1,3,64,1024]{3,2,1,0:T(8,128)S(1)}, f32[1,3,64,1024]{3,2,1,0:T(8,128)}, u32[]{:S(2)}) copy-start(f32[1,3,64,1024]{3,2,1,0:T(8,128)} %metric.3) | copy-start | bytes 2359300
  10.0 8.4 %copy-start.1 = (s32[1,3,1]{1,2,0:T(1,128)S(1)}, s32[1,3,1]{1,2,0:T(1,128)}, u32[]{:S(2)}) copy-start(s32[1,3,1]{1,2,0:T(1,128)} %param.12) | copy-start | bytes 40
  12.7 8.4 %collective-permute-start.3 = (bf16[64,1024]{1,0:T(8,128)(2,1)S(1)}, bf16[64,1024]{1,0:T(8,128)(2,1)S(1)}, u32[]{:S(2)}, u32[]{:S(2)}) collective-permute-start(bf16[64,1024]{1,0:T(8,128)(2,1)S(1)} %get-tuple-element.16), channel_id=1, source_target_pairs={{0,3},{1,2},{2,1},{3,0},{4,7},{5,6},{6,5},{7,4},{8,11},{9,10},{10,... | collective-permute-start | bytes 393224 | tf_op jit(solution)/shard_map/ppermute | solution.py:237
  14.8 10.6 %collective-permute-start.4 = (bf16[64,1024]{1,0:T(8,128)(2,1)S(1)}, bf16[64,1024]{1,0:T(8,128)(2,1)S(1)}, u32[]{:S(2)}, u32[]{:S(2)}) collective-permute-start(bf16[64,1024]{1,0:T(8,128)(2,1)S(1)} %get-tuple-element.17), channel_id=1, source_target_pairs={{0,1},{1,3},{2,0},{3,2},{4,5},{5,7},{6,4},{7,6},{8,9},{9,11},{10,8... | collective-permute-start | bytes 393224 | tf_op jit(solution)/shard_map/ppermute | solution.py:237
  14.8 10.6 %collective-permute-start.5 = (bf16[64,1024]{1,0:T(8,128)(2,1)S(1)}, bf16[64,1024]{1,0:T(8,128)(2,1)S(1)}, u32[]{:S(2)}, u32[]{:S(2)}) collective-permute-start(bf16[64,1024]{1,0:T(8,128)(2,1)S(1)} %get-tuple-element.18), channel_id=1, source_target_pairs={{0,2},{1,0},{2,3},{3,1},{4,6},{5,4},{6,7},{7,5},{8,10},{9,8},{10,1... | collective-permute-start | bytes 393224 | tf_op jit(solution)/shard_map/ppermute | solution.py:237

commit v11 on v9

--- a/solution.py
+++ b/solution.py
@@ -40,7 +40,7 @@
     return lax.broadcasted_iota(jnp.int32, shape, dim)
 
 
-def tensor_kernel(tensor, t_hi, t_lo, buffer, arrived):
+def tensor_kernel(tensor, packed, buffer, arrived):
     _, slots, aux_width, width = tensor.shape
     parts = buffer.shape[0] // slots
     span = width // parts
@@ -57,11 +57,11 @@
         fetch(k, part).start()
     for k, part in order:
         fetch(k, part).wait()
-        for chunk in range(span // 256):
-            hi, lo = split(buffer[k * parts + part, :, chunk * 256:(chunk + 1) * 256])
-            at = (part * (span // 256) + chunk) * aux_width
-            t_hi[at:at + aux_width, k * 256:(k + 1) * 256] = hi
-            t_lo[at:at + aux_width, k * 256:(k + 1) * 256] = lo
+        for chunk in range(span // 128):
+            hi, lo = split(buffer[k * parts + part, :, chunk * 128:(chunk + 1) * 128])
+            at = (part * (span // 128) + chunk) * aux_width
+            packed[at:at + aux_width, k * 256:k * 256 + 128] = hi
+            packed[at:at + aux_width, k * 256 + 128:(k + 1) * 256] = lo
 
 
 def metric_kernel(sig_slots, sig_count, after, metric, m_hi, m_lo):
@@ -91,54 +91,52 @@
 
 def half_kernel(n_mu, nu_slots, nu_count, *refs):
     dens = by_distance(refs[:n_mu], DENSITY_ORDER)
-    t_hi, t_lo = refs[n_mu:n_mu + 2]
-    outs = refs[n_mu + 2:2 * n_mu + 2]
-    d_hi, d_lo, weights, turned = refs[2 * n_mu + 2:]
+    packed = refs[n_mu]
+    outs = refs[n_mu + 1:2 * n_mu + 1]
+    d_both, weights, turned = refs[2 * n_mu + 1:]
     z = lax.axis_index("mu")
     orb, lam_all = dens[0].shape
     lam = lam_all // n_mu
     slots = nu_slots.shape[2]
-    row, col = iota((lam_all, 256), 0), iota((lam_all, 256), 1)
+    row, col = iota((lam_all, 128), 0), iota((lam_all, 128), 1)
     group = z
     for slot in range(1, n_mu):
         group = jnp.where((col >> 3) & 3 == slot, lax.rem((z + 1) * FACTORS[slot], 5) - 1, group)
-    wanted = group * lam + (col >> 7) * 8 + (col & 7)
+    wanted = group * lam + (col >> 6) * 8 + (col & 7)
     choose = jnp.where(row == wanted, 1.0, 0.0).astype(BF16)
     for s in range(n_mu):
         hi, lo = split(dens[s][...])
-        d_hi[s] = jnp.dot(hi, choose, preferred_element_type=F32)
-        d_lo[s] = jnp.dot(lo, choose, preferred_element_type=F32)
-    orbital = (iota((orb, 256), 1) >> 5) & 3
-    depth = slots * 256
+        d_both[s, :, :128] = jnp.dot(hi, choose, preferred_element_type=F32)
+        d_both[s, :, 128:] = jnp.dot(lo, choose, preferred_element_type=F32)
+    orbital = (iota((orb, 256), 1) >> 5) & 1
     for k in range(slots):
-        at = z ^ nu_slots[0, 0, k]
         live = jnp.where(k < nu_count[0, 0], 1.0, 0.0)
-        hi, lo = d_hi[at] * live, d_lo[at] * live
-        for i in range(4):
-            rows = k * 256 + i * orb
-            w_hi = jnp.where(orbital == i, hi, 0.0).astype(BF16)
-            weights[rows:rows + orb, :] = w_hi
-            weights[rows + depth:rows + depth + orb, :] = w_hi
-            weights[rows + 2 * depth:rows + 2 * depth + orb, :] = jnp.where(
-                orbital == i, lo, 0.0
-            ).astype(BF16)
+        both = d_both[z ^ nu_slots[0, 0, k]] * live
+        for i in range(2):
+            block = jnp.where(orbital == i, both, 0.0).astype(BF16)
+            for part in range(2):
+                at = k * 256 + part * 128 + i * orb
+                weights[at:at + orb, :] = block
     aux_width = outs[0].shape[1] // lam
-    per_group = 256 // aux_width
+    lower = iota((aux_width, 128), 1) < 64
+    per_group = 512 // (2 * aux_width)
     span = per_group * 4
-    for group in range(t_hi.shape[0] // 256):
-        rows = slice(group * 256, (group + 1) * 256)
-        high = t_hi[rows, :]
-        left = jnp.concatenate([high, t_lo[rows, :], high], axis=1)
-        total = jnp.dot(left, weights[...], preferred_element_type=F32)
+    for part in range(packed.shape[0] // 512):
+        product = jnp.dot(
+            packed[part * 512:(part + 1) * 512, :], weights[...], preferred_element_type=F32
+        )
+        total = product[:, :128] + product[:, 128:]
         for chunk in range(per_group):
-            piece = total[chunk * aux_width:(chunk + 1) * aux_width]
-            stacked = jnp.concatenate([piece[:, :128], piece[:, 128:]], axis=0)
-            at = (group * per_group + chunk) * 128
-            turned[at:at + 128, :] = stacked.T
+            at = chunk * 2 * aux_width
+            one, two = total[at:at + aux_width], total[at + aux_width:at + 2 * aux_width]
+            top = jnp.where(lower, one, pltpu.roll(two, 64, 1))
+            bottom = jnp.where(lower, pltpu.roll(one, 64, 1), two)
+            at = (part * per_group + chunk) * 128
+            turned[at:at + 128, :] = jnp.concatenate([top, bottom], axis=0).T
         for s in range(n_mu):
             for r in range(8):
-                picked = turned[pl.ds(group * per_group * 128 + s * 8 + r, span, stride=32), :]
-                outs[s][group * span:(group + 1) * span, r * 128:(r + 1) * 128] = picked.astype(BF16)
+                picked = turned[pl.ds(part * per_group * 128 + s * 8 + r, span, stride=32), :]
+                outs[s][part * span:(part + 1) * span, r * 128:(r + 1) * 128] = picked.astype(BF16)
 
 
 def exchange_kernel(n_mu, n_aux, *refs):
@@ -182,13 +180,13 @@
     dens = [density] + [lax.ppermute(density, "mu", turns[s]) for s in DENSITY_ORDER]
     nu_slots, sig_slots = jnp.swapaxes(nu_slots, 1, 2), jnp.swapaxes(sig_slots, 1, 2)
     chunks = three_center.shape[3] // 256
-    t_shape = jax.ShapeDtypeStruct((chunks * aux_width, slots * 256), BF16)
+    t_shape = jax.ShapeDtypeStruct((2 * chunks * aux_width, slots * 256), BF16)
     m_shape = jax.ShapeDtypeStruct((lam * aux_width, n_mu * orb), BF16)
-    t_hi, t_lo = pl.pallas_call(
+    packed = pl.pallas_call(
         tensor_kernel,
-        out_shape=(t_shape, t_shape),
+        out_shape=t_shape,
         in_specs=[HBM],
-        out_specs=(VMEM, VMEM),
+        out_specs=VMEM,
         scratch_shapes=[
             pltpu.VMEM((slots * 4, aux_width, chunks * 64), F32),
             pltpu.SemaphoreType.DMA((slots * 4,)),
@@ -201,18 +199,17 @@
     halves = pl.pallas_call(
         functools.partial(half_kernel, n_mu),
         out_shape=(half_shape,) * n_mu,
-        in_specs=[SMEM, SMEM] + [VMEM] * (n_mu + 2),
+        in_specs=[SMEM, SMEM] + [VMEM] * (n_mu + 1),
         out_specs=(VMEM,) * n_mu,
         scratch_shapes=[
             pltpu.VMEM((n_mu, orb, 256), F32),
-            pltpu.VMEM((n_mu, orb, 256), F32),
-            pltpu.VMEM((3 * slots * 256, 256), BF16),
+            pltpu.VMEM((slots * 256, 256), BF16),
             pltpu.VMEM((chunks * 128, 128), F32),
         ],
         compiler_params=params(16),
         cost_estimate=pl.CostEstimate(flops=1_200_000_000, bytes_accessed=4_000_000, transcendentals=0),
         name="half",
-    )(nu_slots, nu_count, *dens, t_hi, t_lo)
+    )(nu_slots, nu_count, *dens, packed)
     m_hi, m_lo = pl.pallas_call(
         metric_kernel,
         out_shape=(m_shape, m_shape),

time: 39.2 us -> 38.9 us (level)
  no operation moved by 1% of the time
where the time goes in v11:
time: 38.9 us; the launch traced here: 38.8 us
  blocking collectives  12.4 us (32%)
  starting transfers between devices  10.6 us (27%)
  waiting for transfers between devices  7.66 us (20%)
  Pallas kernels  6.67 us (17%)
  between operations  1.4 us (4%)
    all_to_all x1, blocking collectives, fast(): parts = lax.all_to_all(parts, ('aux', 'mu'), 0, 0, axis_index_groups=[down])  12.4 us
    ppermute x3, waiting for transfers between devices, fast(): lax.ppermute(halves[s], 'mu', [(z, goes_to(FACTORS[s], z)) for z in range...  6.01 us
    ppermute x3, starting transfers between devices, fast(): lax.ppermute(density, 'mu', turns[s])  5.62 us
    ppermute x3, starting transfers between devices, fast(): lax.ppermute(halves[s], 'mu', [(z, goes_to(FACTORS[s], z)) for z in range...  5.01 us
    pallas_call x1, Pallas kernels, fast(): pl.pallas_call(functools.partial(half_kernel, n_mu), out_shape=(half_shap...  2.44 us
    pallas_call x1, Pallas kernels, fast(): pl.pallas_call(tensor_kernel, out_shape=t_shape, in_specs=[HBM], out_spec...  1.98 us
    ppermute x3, waiting for transfers between devices, fast(): lax.ppermute(density, 'mu', turns[s])  1.65 us
    pallas_call x1, Pallas kernels, fast(): pl.pallas_call(metric_kernel, out_shape=(m_shape, m_shape), in_specs=[SME...  1 us
  transfers between devices with their start and end apart: 6, of which 3 were waited for; matrix products, arithmetic and copies ran while one was open for 0% of the time, Pallas kernels for 8%

profile of v11, /device:TPU:0, one launch (start us, length us, event | category | flops | bytes accessed | tf_op | source)
XLA Modules:
  0.0 38.8 jit_solution(7256835850944678952)
XLA Ops:
  0.0 4.0 %collective-permute-start = (f32[64,64]{1,0:T(8,128)}, f32[64,64]{1,0:T(8,128)S(1)}, u32[]{:S(2)}, u32[]{:S(2)}) collective-permute-start(f32[64,64]{1,0:T(8,128)} %refs_0_.1), channel_id=1, source_target_pairs={{0,2},{1,3},{2,0},{3,1},{4,6},{5,7},{6,4},{7,5},{8,10},{9,11},{10,... | collective-permute-start | bytes 49160 | tf_op jit(solution)/shard_map/ppermute | solution.py:180
  4.0 1.3 %collective-permute-start.1 = (f32[64,64]{1,0:T(8,128)}, f32[64,64]{1,0:T(8,128)S(1)}, u32[]{:S(2)}, u32[]{:S(2)}) collective-permute-start(f32[64,64]{1,0:T(8,128)} %refs_0_.1), channel_id=1, source_target_pairs={{0,3},{1,2},{2,1},{3,0},{4,7},{5,6},{6,5},{7,4},{8,11},{9,10},{10,... | collective-permute-start | bytes 49160 | tf_op jit(solution)/shard_map/ppermute | solution.py:180
  5.4 0.2 collective-permute-start.2
  6.3 0.0 copy-start.2
  6.3 0.0 copy-start.3
  6.3 2.0 %tensor.2.refs_4_ = bf16[2048,768]{1,0:T(8,128)(2,1)S(1)} custom-call(f32[1,3,64,4096]{3,2,1,0:T(8,128)} %tensor.3), custom_call_target="tpu_custom_call" | custom-call | flops 10000000 | bytes 6000000 | tf_op jit(solution)/shard_map/tensor/pallas_call | solution.py:185
  8.3 0.0 copy-start
  8.3 0.0 copy-start.1
  8.3 0.0 collective-permute-done.refs_1_
  8.3 1.6 %collective-permute-done.1.refs_2_ = f32[64,64]{1,0:T(8,128)S(1)} collective-permute-done((f32[64,64]{1,0:T(8,128)}, f32[64,64]{1,0:T(8,128)S(1)}, u32[]{:S(2)}, u32[]{:S(2)}) %collective-permute-start.1) | collective-permute-done | bytes 16416 | tf_op jit(solution)/shard_map/ppermute | solution.py:180
  10.0 0.0 collective-permute-done.2.refs_3_
  10.0 0.0 copy-done.2
  10.0 0.0 copy-done.3
  10.0 2.4 %half.1 = (bf16[64,1024]{1,0:T(8,128)(2,1)S(1)}, bf16[64,1024]{1,0:T(8,128)(2,1)S(1)}, bf16[64,1024]{1,0:T(8,128)(2,1)S(1)}, bf16[64,1024]{1,0:T(8,128)(2,1)S(1)}) custom-call(s32[1,1,3]{2,1,0:T(1,128)S(1)} %bitcast.3, s32[1,1]{1,0:T(1,128)S(6)} %copy.8.nu_count, f32[64,64]{1,0:T(8,128)S(1)} %copy-done.2, f32[64,64]{1,0:T(8,128)S(1)} %collective-permute-done.refs_1_, ...), custom_call_target="tpu_custom_call" | custom-call | flops 1200000000 | bytes 4000000 | tf_op jit(solution)/shard_map/half/pallas_call | solution.py:199
  12.4 2.1 %collective-permute-start.3 = (bf16[64,1024]{1,0:T(8,128)(2,1)S(1)}, bf16[64,1024]{1,0:T(8,128)(2,1)S(1)}, u32[]{:S(2)}, u32[]{:S(2)}) collective-permute-start(bf16[64,1024]{1,0:T(8,128)(2,1)S(1)} %get-tuple-element.12), channel_id=1, source_target_pairs={{0,3},{1,2},{2,1},{3,0},{4,7},{5,6},{6,5},{7,4},{8,11},{9,10},{10,... | collective-permute-start | bytes 393224 | tf_op jit(solution)/shard_map/ppermute | solution.py:223
  14.5 0.0 collective-permute-start.4
  14.5 2.9 %collective-permute-start.5 = (bf16[64,1024]{1,0:T(8,128)(2,1)S(1)}, bf16[64,1024]{1,0:T(8,128)(2,1)S(1)}, u32[]{:S(2)}, u32[]{:S(2)}) collective-permute-start(bf16[64,1024]{1,0:T(8,128)(2,1)S(1)} %get-tuple-element.14), channel_id=1, source_target_pairs={{0,2},{1,0},{2,3},{3,1},{4,6},{5,4},{6,7},{7,5},{8,10},{9,8},{10,1... | collective-permute-start | bytes 393224 | tf_op jit(solution)/shard_map/ppermute | solution.py:223
  18.1 0.0 copy-done
  18.1 0.0 copy-done.1
  18.1 1.0 %metric.2 = (bf16[1024,256]{1,0:T(8,128)(2,1)S(1)}, bf16[1024,256]{1,0:T(8,128)(2,1)S(1)}) custom-call(s32[1,1,3]{2,1,0:T(1,128)S(1)} %bitcast.2, s32[1,1]{1,0:T(1,128)S(6)} %copy.9.sig_count, bf16[64,1024]{1,0:T(8,128)(2,1)S(1)} %get-tuple-element.11.after.refs_0_, f32[1,3,64,1024]{3,2,1,0:T(8,128)S(1)} %copy-done), custom_call_target="tpu_custom_call" | custom-call | flops 10000000 | bytes 2000000 | tf_op jit(solution)/shard_map/metric/pallas_call | solution.py:213
  19.1 1.7 %collective-permute-done.3.refs_1_ = bf16[64,1024]{1,0:T(8,128)(2,1)S(1)} collective-permute-done((bf16[64,1024]{1,0:T(8,128)(2,1)S(1)}, bf16[64,1024]{1,0:T(8,128)(2,1)S(1)}, u32[]{:S(2)}, u32[]{:S(2)}) %collective-permute-start.3) | collective-permute-done | bytes 131104 | tf_op jit(solution)/shard_map/ppermute | solution.py:223
  20.8 4.3 %collective-permute-done.4.refs_2_ = bf16[64,1024]{1,0:T(8,128)(2,1)S(1)} collective-permute-done((bf16[64,1024]{1,0:T(8,128)(2,1)S(1)}, bf16[64,1024]{1,0:T(8,128)(2,1)S(1)}, u32[]{:S(2)}, u32[]{:S(2)}) %collective-permute-start.4) | collective-permute-done | bytes 131104 | tf_op jit(solution)/shard_map/ppermute | solution.py:223
  25.1 0.0 collective-permute-done.5.refs_3_
  25.1 0.5 %exchange.1 = bf16[32,16,128]{2,1,0:T(8,128)(2,1)S(1)} custom-call(bf16[64,1024]{1,0:T(8,128)(2,1)S(1)} %get-tuple-element.11.after.refs_0_, bf16[64,1024]{1,0:T(8,128)(2,1)S(1)} %collective-permute-done.3.refs_1_, bf16[64,1024]{1,0:T(8,128)(2,1)S(1)} %collective-permute-done.4.refs_2_, bf16[64,1024]{1,0:T(8,128)(2,1)S(1)} %collective-permute-done.5.refs_3_, ...), custom_call_target="tpu_custom_call" | custom-call | flops 300000000 | bytes 2000000 | tf_op jit(solution)/shard_map/exchange/pallas_call | solution.py:227
  25.7 12.4 %all_to_all.5.parts = bf16[32,16,128]{2,1,0:T(8,128)(2,1)S(1)} all-to-all(bf16[32,16,128]{2,1,0:T(8,128)(2,1)S(1)} %exchange.1), channel_id=1, replica_groups={{31,30,29,28,27,26,25,24,23,22,21,20,19,18,17,16,15,14,13,12,11,10,9,8,..., dimensions={0} | all-to-all | bytes 262144 | tf_op jit(solution)/shard_map/all_to_all | solution.py:238
  38.1 0.7 %sum.1 = f32[32,64]{1,0:T(8,128)} custom-call(bf16[32,16,128]{2,1,0:T(8,128)(2,1)S(1)} %all_to_all.5.parts), custom_call_target="tpu_custom_call" | custom-call | tf_op jit(solution)/shard_map/sum/pallas_call | solution.py:239
Async XLA Ops:
  0.0 8.3 %collective-permute-start = (f32[64,64]{1,0:T(8,128)}, f32[64,64]{1,0:T(8,128)S(1)}, u32[]{:S(2)}, u32[]{:S(2)}) collective-permute-start(f32[64,64]{1,0:T(8,128)} %refs_0_.1), channel_id=1, source_target_pairs={{0,2},{1,3},{2,0},{3,1},{4,6},{5,7},{6,4},{7,5},{8,10},{9,11},{10,... | collective-permute-start | bytes 49160 | tf_op jit(solution)/shard_map/ppermute | solution.py:180
  4.0 5.9 %collective-permute-start.1 = (f32[64,64]{1,0:T(8,128)}, f32[64,64]{1,0:T(8,128)S(1)}, u32[]{:S(2)}, u32[]{:S(2)}) collective-permute-start(f32[64,64]{1,0:T(8,128)} %refs_0_.1), channel_id=1, source_target_pairs={{0,3},{1,2},{2,1},{3,0},{4,7},{5,6},{6,5},{7,4},{8,11},{9,10},{10,... | collective-permute-start | bytes 49160 | tf_op jit(solution)/shard_map/ppermute | solution.py:180
  5.4 4.6 %collective-permute-start.2 = (f32[64,64]{1,0:T(8,128)}, f32[64,64]{1,0:T(8,128)S(1)}, u32[]{:S(2)}, u32[]{:S(2)}) collective-permute-start(f32[64,64]{1,0:T(8,128)} %refs_0_.1), channel_id=1, source_target_pairs={{0,1},{1,0},{2,3},{3,2},{4,5},{5,4},{6,7},{7,6},{8,9},{9,8},{10,11... | collective-permute-start | bytes 49160 | tf_op jit(solution)/shard_map/ppermute | solution.py:180
  6.3 3.7 %copy-start.2 = (f32[64,64]{1,0:T(8,128)S(1)}, f32[64,64]{1,0:T(8,128)}, u32[]{:S(2)}) copy-start(f32[64,64]{1,0:T(8,128)} %refs_0_.1) | copy-start | bytes 49156
  6.3 3.7 %copy-start.3 = (s32[1,3,1]{1,2,0:T(1,128)S(1)}, s32[1,3,1]{1,2,0:T(1,128)}, u32[]{:S(2)}) copy-start(s32[1,3,1]{1,2,0:T(1,128)} %param.8) | copy-start | bytes 40
  8.3 9.8 %copy-start = (f32[1,3,64,1024]{3,2,1,0:T(8,128)S(1)}, f32[1,3,64,1024]{3,2,1,0:T(8,128)}, u32[]{:S(2)}) copy-start(f32[1,3,64,1024]{3,2,1,0:T(8,128)} %metric.3) | copy-start | bytes 2359300
  8.3 9.8 %copy-start.1 = (s32[1,3,1]{1,2,0:T(1,128)S(1)}, s32[1,3,1]{1,2,0:T(1,128)}, u32[]{:S(2)}) copy-start(s32[1,3,1]{1,2,0:T(1,128)} %param.12) | copy-start | bytes 40
  12.4 8.4 %collective-permute-start.3 = (bf16[64,1024]{1,0:T(8,128)(2,1)S(1)}, bf16[64,1024]{1,0:T(8,128)(2,1)S(1)}, u32[]{:S(2)}, u32[]{:S(2)}) collective-permute-start(bf16[64,1024]{1,0:T(8,128)(2,1)S(1)} %get-tuple-element.12), channel_id=1, source_target_pairs={{0,3},{1,2},{2,1},{3,0},{4,7},{5,6},{6,5},{7,4},{8,11},{9,10},{10,... | collective-permute-start | bytes 393224 | tf_op jit(solution)/shard_map/ppermute | solution.py:223
  14.5 10.6 %collective-permute-start.4 = (bf16[64,1024]{1,0:T(8,128)(2,1)S(1)}, bf16[64,1024]{1,0:T(8,128)(2,1)S(1)}, u32[]{:S(2)}, u32[]{:S(2)}) collective-permute-start(bf16[64,1024]{1,0:T(8,128)(2,1)S(1)} %get-tuple-element.13), channel_id=1, source_target_pairs={{0,1},{1,3},{2,0},{3,2},{4,5},{5,7},{6,4},{7,6},{8,9},{9,11},{10,8... | collective-permute-start | bytes 393224 | tf_op jit(solution)/shard_map/ppermute | solution.py:223
  14.5 10.6 %collective-permute-start.5 = (bf16[64,1024]{1,0:T(8,128)(2,1)S(1)}, bf16[64,1024]{1,0:T(8,128)(2,1)S(1)}, u32[]{:S(2)}, u32[]{:S(2)}) collective-permute-start(bf16[64,1024]{1,0:T(8,128)(2,1)S(1)} %get-tuple-element.14), channel_id=1, source_target_pairs={{0,2},{1,0},{2,3},{3,1},{4,6},{5,4},{6,7},{7,5},{8,10},{9,8},{10,1... | collective-permute-start | bytes 393224 | tf_op jit(solution)/shard_map/ppermute | solution.py:223

commit v12 on v11

--- a/solution.py
+++ b/solution.py
@@ -16,7 +16,7 @@
 
 
 DENSITY_ORDER = (2, 3, 1)
-FACTORS = (1, 4, 2, 3)
+FACTORS = (1, 2, 4, 3)
 
 
 def goes_to(factor, z):

time: 38.9 us -> 38.5 us (0.990)
  starting transfers between devices: 10.6 us -> 9.71 us
  blocking collectives: 12.4 us -> 12.9 us
    ppermute x3, starting transfers between devices: 5.01 us -> 4.09 us  [fast(): lax.ppermute(halves[s], 'mu', [(z, goes_to(FACTORS[s], z)) for z in range...]
    all_to_all x1, blocking collectives: 12.4 us -> 12.9 us  [fast(): parts = lax.all_to_all(parts, ('aux', 'mu'), 0, 0, axis_index_groups=[down])]
  transfers between devices with their start and end apart: 6 -> 6, of which waited for: 3 -> 2; matrix products, arithmetic and copies ran while one was open for 0% -> 0% of each run, Pallas kernels for 8% -> 8%
where the time goes in v12:
time: 38.5 us; the launch traced here: 38.4 us
  blocking collectives  12.9 us (34%)
  starting transfers between devices  9.71 us (25%)
  waiting for transfers between devices  7.66 us (20%)
  Pallas kernels  6.67 us (17%)
  between operations  1.4 us (4%)
    all_to_all x1, blocking collectives, fast(): parts = lax.all_to_all(parts, ('aux', 'mu'), 0, 0, axis_index_groups=[down])  12.9 us
    ppermute x3, waiting for transfers between devices, fast(): lax.ppermute(halves[s], 'mu', [(z, goes_to(FACTORS[s], z)) for z in range...  6.01 us
    ppermute x3, starting transfers between devices, fast(): lax.ppermute(density, 'mu', turns[s])  5.62 us
    ppermute x3, starting transfers between devices, fast(): lax.ppermute(halves[s], 'mu', [(z, goes_to(FACTORS[s], z)) for z in range...  4.09 us
    pallas_call x1, Pallas kernels, fast(): pl.pallas_call(functools.partial(half_kernel, n_mu), out_shape=(half_shap...  2.44 us
    pallas_call x1, Pallas kernels, fast(): pl.pallas_call(tensor_kernel, out_shape=t_shape, in_specs=[HBM], out_spec...  1.98 us
    ppermute x3, waiting for transfers between devices, fast(): lax.ppermute(density, 'mu', turns[s])  1.65 us
    pallas_call x1, Pallas kernels, fast(): pl.pallas_call(metric_kernel, out_shape=(m_shape, m_shape), in_specs=[SME...  1 us
  transfers between devices with their start and end apart: 6, of which 2 were waited for; matrix products, arithmetic and copies ran while one was open for 0% of the time, Pallas kernels for 8%

profile of v12, /device:TPU:0, one launch (start us, length us, event | category | flops | bytes accessed | tf_op | source)
XLA Modules:
  0.0 38.4 jit_solution(16562801962180680313)
XLA Ops:
  0.0 4.0 %collective-permute-start = (f32[64,64]{1,0:T(8,128)}, f32[64,64]{1,0:T(8,128)S(1)}, u32[]{:S(2)}, u32[]{:S(2)}) collective-permute-start(f32[64,64]{1,0:T(8,128)} %refs_0_.1), channel_id=1, source_target_pairs={{0,2},{1,3},{2,0},{3,1},{4,6},{5,7},{6,4},{7,5},{8,10},{9,11},{10,... | collective-permute-start | bytes 49160 | tf_op jit(solution)/shard_map/ppermute | solution.py:180
  4.0 1.3 %collective-permute-start.1 = (f32[64,64]{1,0:T(8,128)}, f32[64,64]{1,0:T(8,128)S(1)}, u32[]{:S(2)}, u32[]{:S(2)}) collective-permute-start(f32[64,64]{1,0:T(8,128)} %refs_0_.1), channel_id=1, source_target_pairs={{0,3},{1,2},{2,1},{3,0},{4,7},{5,6},{6,5},{7,4},{8,11},{9,10},{10,... | collective-permute-start | bytes 49160 | tf_op jit(solution)/shard_map/ppermute | solution.py:180
  5.4 0.2 collective-permute-start.2
  6.3 0.0 copy-start.2
  6.3 0.0 copy-start.3
  6.3 2.0 %tensor.2.refs_4_ = bf16[2048,768]{1,0:T(8,128)(2,1)S(1)} custom-call(f32[1,3,64,4096]{3,2,1,0:T(8,128)} %tensor.3), custom_call_target="tpu_custom_call" | custom-call | flops 10000000 | bytes 6000000 | tf_op jit(solution)/shard_map/tensor/pallas_call | solution.py:185
  8.3 0.0 copy-start
  8.3 0.0 copy-start.1
  8.3 0.0 collective-permute-done.refs_1_
  8.3 1.6 %collective-permute-done.1.refs_2_ = f32[64,64]{1,0:T(8,128)S(1)} collective-permute-done((f32[64,64]{1,0:T(8,128)}, f32[64,64]{1,0:T(8,128)S(1)}, u32[]{:S(2)}, u32[]{:S(2)}) %collective-permute-start.1) | collective-permute-done | bytes 16416 | tf_op jit(solution)/shard_map/ppermute | solution.py:180
  10.0 0.0 collective-permute-done.2.refs_3_
  10.0 0.0 copy-done.2
  10.0 0.0 copy-done.3
  10.0 2.4 %half.1 = (bf16[64,1024]{1,0:T(8,128)(2,1)S(1)}, bf16[64,1024]{1,0:T(8,128)(2,1)S(1)}, bf16[64,1024]{1,0:T(8,128)(2,1)S(1)}, bf16[64,1024]{1,0:T(8,128)(2,1)S(1)}) custom-call(s32[1,1,3]{2,1,0:T(1,128)S(1)} %bitcast.3, s32[1,1]{1,0:T(1,128)S(6)} %copy.8.nu_count, f32[64,64]{1,0:T(8,128)S(1)} %copy-done.2, f32[64,64]{1,0:T(8,128)S(1)} %collective-permute-done.refs_1_, ...), custom_call_target="tpu_custom_call" | custom-call | flops 1200000000 | bytes 4000000 | tf_op jit(solution)/shard_map/half/pallas_call | solution.py:199
  12.4 0.2 collective-permute-start.3
  12.7 2.5 %collective-permute-start.4 = (bf16[64,1024]{1,0:T(8,128)(2,1)S(1)}, bf16[64,1024]{1,0:T(8,128)(2,1)S(1)}, u32[]{:S(2)}, u32[]{:S(2)}) collective-permute-start(bf16[64,1024]{1,0:T(8,128)(2,1)S(1)} %get-tuple-element.13), channel_id=1, source_target_pairs={{0,3},{1,2},{2,1},{3,0},{4,7},{5,6},{6,5},{7,4},{8,11},{9,10},{10,... | collective-permute-start | bytes 393224 | tf_op jit(solution)/shard_map/ppermute | solution.py:223
  15.2 1.3 %collective-permute-start.5 = (bf16[64,1024]{1,0:T(8,128)(2,1)S(1)}, bf16[64,1024]{1,0:T(8,128)(2,1)S(1)}, u32[]{:S(2)}, u32[]{:S(2)}) collective-permute-start(bf16[64,1024]{1,0:T(8,128)(2,1)S(1)} %get-tuple-element.14), channel_id=1, source_target_pairs={{0,2},{1,0},{2,3},{3,1},{4,6},{5,4},{6,7},{7,5},{8,10},{9,8},{10,1... | collective-permute-start | bytes 393224 | tf_op jit(solution)/shard_map/ppermute | solution.py:223
  17.2 0.0 copy-done
  17.2 0.0 copy-done.1
  17.2 1.0 %metric.2 = (bf16[1024,256]{1,0:T(8,128)(2,1)S(1)}, bf16[1024,256]{1,0:T(8,128)(2,1)S(1)}) custom-call(s32[1,1,3]{2,1,0:T(1,128)S(1)} %bitcast.2, s32[1,1]{1,0:T(1,128)S(6)} %copy.9.sig_count, bf16[64,1024]{1,0:T(8,128)(2,1)S(1)} %get-tuple-element.11.after.refs_0_, f32[1,3,64,1024]{3,2,1,0:T(8,128)S(1)} %copy-done), custom_call_target="tpu_custom_call" | custom-call | flops 10000000 | bytes 2000000 | tf_op jit(solution)/shard_map/metric/pallas_call | solution.py:213
  18.2 6.0 %collective-permute-done.3.refs_1_ = bf16[64,1024]{1,0:T(8,128)(2,1)S(1)} collective-permute-done((bf16[64,1024]{1,0:T(8,128)(2,1)S(1)}, bf16[64,1024]{1,0:T(8,128)(2,1)S(1)}, u32[]{:S(2)}, u32[]{:S(2)}) %collective-permute-start.3) | collective-permute-done | bytes 131104 | tf_op jit(solution)/shard_map/ppermute | solution.py:223
  24.2 0.0 collective-permute-done.4.refs_2_
  24.2 0.0 collective-permute-done.5.refs_3_
  24.2 0.5 %exchange.1 = bf16[32,16,128]{2,1,0:T(8,128)(2,1)S(1)} custom-call(bf16[64,1024]{1,0:T(8,128)(2,1)S(1)} %get-tuple-element.11.after.refs_0_, bf16[64,1024]{1,0:T(8,128)(2,1)S(1)} %collective-permute-done.3.refs_1_, bf16[64,1024]{1,0:T(8,128)(2,1)S(1)} %collective-permute-done.4.refs_2_, bf16[64,1024]{1,0:T(8,128)(2,1)S(1)} %collective-permute-done.5.refs_3_, ...), custom_call_target="tpu_custom_call" | custom-call | flops 300000000 | bytes 2000000 | tf_op jit(solution)/shard_map/exchange/pallas_call | solution.py:227
  24.8 12.9 %all_to_all.5.parts = bf16[32,16,128]{2,1,0:T(8,128)(2,1)S(1)} all-to-all(bf16[32,16,128]{2,1,0:T(8,128)(2,1)S(1)} %exchange.1), channel_id=1, replica_groups={{31,30,29,28,27,26,25,24,23,22,21,20,19,18,17,16,15,14,13,12,11,10,9,8,..., dimensions={0} | all-to-all | bytes 262144 | tf_op jit(solution)/shard_map/all_to_all | solution.py:238
  37.7 0.7 %sum.1 = f32[32,64]{1,0:T(8,128)} custom-call(bf16[32,16,128]{2,1,0:T(8,128)(2,1)S(1)} %all_to_all.5.parts), custom_call_target="tpu_custom_call" | custom-call | tf_op jit(solution)/shard_map/sum/pallas_call | solution.py:239
Async XLA Ops:
  0.0 8.3 %collective-permute-start = (f32[64,64]{1,0:T(8,128)}, f32[64,64]{1,0:T(8,128)S(1)}, u32[]{:S(2)}, u32[]{:S(2)}) collective-permute-start(f32[64,64]{1,0:T(8,128)} %refs_0_.1), channel_id=1, source_target_pairs={{0,2},{1,3},{2,0},{3,1},{4,6},{5,7},{6,4},{7,5},{8,10},{9,11},{10,... | collective-permute-start | bytes 49160 | tf_op jit(solution)/shard_map/ppermute | solution.py:180
  4.0 5.9 %collective-permute-start.1 = (f32[64,64]{1,0:T(8,128)}, f32[64,64]{1,0:T(8,128)S(1)}, u32[]{:S(2)}, u32[]{:S(2)}) collective-permute-start(f32[64,64]{1,0:T(8,128)} %refs_0_.1), channel_id=1, source_target_pairs={{0,3},{1,2},{2,1},{3,0},{4,7},{5,6},{6,5},{7,4},{8,11},{9,10},{10,... | collective-permute-start | bytes 49160 | tf_op jit(solution)/shard_map/ppermute | solution.py:180
  5.4 4.6 %collective-permute-start.2 = (f32[64,64]{1,0:T(8,128)}, f32[64,64]{1,0:T(8,128)S(1)}, u32[]{:S(2)}, u32[]{:S(2)}) collective-permute-start(f32[64,64]{1,0:T(8,128)} %refs_0_.1), channel_id=1, source_target_pairs={{0,1},{1,0},{2,3},{3,2},{4,5},{5,4},{6,7},{7,6},{8,9},{9,8},{10,11... | collective-permute-start | bytes 49160 | tf_op jit(solution)/shard_map/ppermute | solution.py:180
  6.3 3.7 %copy-start.2 = (f32[64,64]{1,0:T(8,128)S(1)}, f32[64,64]{1,0:T(8,128)}, u32[]{:S(2)}) copy-start(f32[64,64]{1,0:T(8,128)} %refs_0_.1) | copy-start | bytes 49156
  6.3 3.7 %copy-start.3 = (s32[1,3,1]{1,2,0:T(1,128)S(1)}, s32[1,3,1]{1,2,0:T(1,128)}, u32[]{:S(2)}) copy-start(s32[1,3,1]{1,2,0:T(1,128)} %param.8) | copy-start | bytes 40
  8.3 8.9 %copy-start = (f32[1,3,64,1024]{3,2,1,0:T(8,128)S(1)}, f32[1,3,64,1024]{3,2,1,0:T(8,128)}, u32[]{:S(2)}) copy-start(f32[1,3,64,1024]{3,2,1,0:T(8,128)} %metric.3) | copy-start | bytes 2359300
  8.3 8.9 %copy-start.1 = (s32[1,3,1]{1,2,0:T(1,128)S(1)}, s32[1,3,1]{1,2,0:T(1,128)}, u32[]{:S(2)}) copy-start(s32[1,3,1]{1,2,0:T(1,128)} %param.12) | copy-start | bytes 40
  12.4 11.8 %collective-permute-start.3 = (bf16[64,1024]{1,0:T(8,128)(2,1)S(1)}, bf16[64,1024]{1,0:T(8,128)(2,1)S(1)}, u32[]{:S(2)}, u32[]{:S(2)}) collective-permute-start(bf16[64,1024]{1,0:T(8,128)(2,1)S(1)} %get-tuple-element.12), channel_id=1, source_target_pairs={{0,1},{1,3},{2,0},{3,2},{4,5},{5,7},{6,4},{7,6},{8,9},{9,11},{10,8... | collective-permute-start | bytes 393224 | tf_op jit(solution)/shard_map/ppermute | solution.py:223
  12.7 11.6 %collective-permute-start.4 = (bf16[64,1024]{1,0:T(8,128)(2,1)S(1)}, bf16[64,1024]{1,0:T(8,128)(2,1)S(1)}, u32[]{:S(2)}, u32[]{:S(2)}) collective-permute-start(bf16[64,1024]{1,0:T(8,128)(2,1)S(1)} %get-tuple-element.13), channel_id=1, source_target_pairs={{0,3},{1,2},{2,1},{3,0},{4,7},{5,6},{6,5},{7,4},{8,11},{9,10},{10,... | collective-permute-start | bytes 393224 | tf_op jit(solution)/shard_map/ppermute | solution.py:223
  15.2 9.0 %collective-permute-start.5 = (bf16[64,1024]{1,0:T(8,128)(2,1)S(1)}, bf16[64,1024]{1,0:T(8,128)(2,1)S(1)}, u32[]{:S(2)}, u32[]{:S(2)}) collective-permute-start(bf16[64,1024]{1,0:T(8,128)(2,1)S(1)} %get-tuple-element.14), channel_id=1, source_target_pairs={{0,2},{1,0},{2,3},{3,1},{4,6},{5,4},{6,7},{7,5},{8,10},{9,8},{10,1... | collective-permute-start | bytes 393224 | tf_op jit(solution)/shard_map/ppermute | solution.py:223

commit v13 on v12

--- a/solution.py
+++ b/solution.py
@@ -16,11 +16,7 @@
 
 
 DENSITY_ORDER = (2, 3, 1)
-FACTORS = (1, 2, 4, 3)
-
-
-def goes_to(factor, z):
-    return (z + 1) * factor % 5 - 1
+HALF_ORDER = (0, 2, 3, 1)
 
 
 def by_distance(refs, order):
@@ -101,7 +97,7 @@
     row, col = iota((lam_all, 128), 0), iota((lam_all, 128), 1)
     group = z
     for slot in range(1, n_mu):
-        group = jnp.where((col >> 3) & 3 == slot, lax.rem((z + 1) * FACTORS[slot], 5) - 1, group)
+        group = jnp.where((col >> 3) & 3 == slot, z ^ HALF_ORDER[slot], group)
     wanted = group * lam + (col >> 6) * 8 + (col & 7)
     choose = jnp.where(row == wanted, 1.0, 0.0).astype(BF16)
     for s in range(n_mu):
@@ -148,8 +144,7 @@
     product += jnp.dot(left, m_lo[...], preferred_element_type=F32)
     orb = halves[0].shape[0]
     for s in range(n_mu):
-        back = pow(FACTORS[s], -1, 5)
-        block = lax.rem((z + 1) * back, 5) - 1
+        block = z ^ HALF_ORDER[s]
         total[pl.ds(pl.multiple_of(block * orb, orb), orb), :] = product[s * orb:(s + 1) * orb]
     rows = out.shape[1]
     lower = iota((rows, 128), 1) < 64
@@ -220,8 +215,7 @@
         name="metric",
     )(sig_slots, sig_count, halves[0], metric_tensor)
     halves = [halves[0]] + [
-        lax.ppermute(halves[s], "mu", [(z, goes_to(FACTORS[s], z)) for z in range(n_mu)])
-        for s in range(1, n_mu)
+        lax.ppermute(halves[s], "mu", turns[HALF_ORDER[s]]) for s in range(1, n_mu)
     ]
     rows = n_mu * orb // n_aux
     parts = pl.pallas_call(

time: 38.5 us -> 38.5 us (level)
  starting transfers between devices: 9.71 us -> 9.17 us
  waiting for transfers between devices: 7.66 us -> 8.18 us
    ppermute x3, starting transfers between devices: 4.09 us -> 3.55 us  [fast(): lax.ppermute(halves[s], 'mu', turns[HALF_ORDER[s]])]
    ppermute x3, waiting for transfers between devices: 6.01 us -> 6.53 us  [fast(): lax.ppermute(halves[s], 'mu', turns[HALF_ORDER[s]])]
  transfers between devices with their start and end apart: 6 -> 6, of which waited for: 2 -> 3; matrix products, arithmetic and copies ran while one was open for 0% -> 0% of each run, Pallas kernels for 8% -> 8%
where the time goes in v13:
time: 38.5 us; the launch traced here: 38.4 us
  blocking collectives  12.9 us (34%)
  starting transfers between devices  9.17 us (24%)
  waiting for transfers between devices  8.18 us (21%)
  Pallas kernels  6.66 us (17%)
  between operations  1.4 us (4%)
    all_to_all x1, blocking collectives, fast(): parts = lax.all_to_all(parts, ('aux', 'mu'), 0, 0, axis_index_groups=[down])  12.9 us
    ppermute x3, waiting for transfers between devices, fast(): lax.ppermute(halves[s], 'mu', turns[HALF_ORDER[s]])  6.53 us
    ppermute x3, starting transfers between devices, fast(): lax.ppermute(density, 'mu', turns[s])  5.62 us
    ppermute x3, starting transfers between devices, fast(): lax.ppermute(halves[s], 'mu', turns[HALF_ORDER[s]])  3.55 us
    pallas_call x1, Pallas kernels, fast(): pl.pallas_call(functools.partial(half_kernel, n_mu), out_shape=(half_shap...  2.43 us
    pallas_call x1, Pallas kernels, fast(): pl.pallas_call(tensor_kernel, out_shape=t_shape, in_specs=[HBM], out_spec...  1.98 us
    ppermute x3, waiting for transfers between devices, fast(): lax.ppermute(density, 'mu', turns[s])  1.65 us
    pallas_call x1, Pallas kernels, fast(): pl.pallas_call(metric_kernel, out_shape=(m_shape, m_shape), in_specs=[SME...  1 us
  transfers between devices with their start and end apart: 6, of which 3 were waited for; matrix products, arithmetic and copies ran while one was open for 0% of the time, Pallas kernels for 8%

profile of v13, /device:TPU:0, one launch (start us, length us, event | category | flops | bytes accessed | tf_op | source)
XLA Modules:
  0.0 38.4 jit_solution(4562998823621067560)
XLA Ops:
  0.0 4.0 %collective-permute-start = (f32[64,64]{1,0:T(8,128)}, f32[64,64]{1,0:T(8,128)S(1)}, u32[]{:S(2)}, u32[]{:S(2)}) collective-permute-start(f32[64,64]{1,0:T(8,128)} %refs_0_.1), channel_id=1, source_target_pairs={{0,2},{1,3},{2,0},{3,1},{4,6},{5,7},{6,4},{7,5},{8,10},{9,11},{10,... | collective-permute-start | bytes 49160 | tf_op jit(solution)/shard_map/ppermute | solution.py:175
  4.0 1.3 %collective-permute-start.1 = (f32[64,64]{1,0:T(8,128)}, f32[64,64]{1,0:T(8,128)S(1)}, u32[]{:S(2)}, u32[]{:S(2)}) collective-permute-start(f32[64,64]{1,0:T(8,128)} %refs_0_.1), channel_id=1, source_target_pairs={{0,3},{1,2},{2,1},{3,0},{4,7},{5,6},{6,5},{7,4},{8,11},{9,10},{10,... | collective-permute-start | bytes 49160 | tf_op jit(solution)/shard_map/ppermute | solution.py:175
  5.4 0.2 collective-permute-start.2
  6.3 0.0 copy-start.2
  6.3 0.0 copy-start.3
  6.3 2.0 %tensor.2.refs_4_ = bf16[2048,768]{1,0:T(8,128)(2,1)S(1)} custom-call(f32[1,3,64,4096]{3,2,1,0:T(8,128)} %tensor.3), custom_call_target="tpu_custom_call" | custom-call | flops 10000000 | bytes 6000000 | tf_op jit(solution)/shard_map/tensor/pallas_call | solution.py:180
  8.3 0.0 copy-start
  8.3 0.0 copy-start.1
  8.3 0.0 collective-permute-done.refs_1_
  8.3 1.6 %collective-permute-done.1.refs_2_ = f32[64,64]{1,0:T(8,128)S(1)} collective-permute-done((f32[64,64]{1,0:T(8,128)}, f32[64,64]{1,0:T(8,128)S(1)}, u32[]{:S(2)}, u32[]{:S(2)}) %collective-permute-start.1) | collective-permute-done | bytes 16416 | tf_op jit(solution)/shard_map/ppermute | solution.py:175
  10.0 0.0 collective-permute-done.2.refs_3_
  10.0 0.0 copy-done.2
  10.0 0.0 copy-done.3
  10.0 2.4 %half.1 = (bf16[64,1024]{1,0:T(8,128)(2,1)S(1)}, bf16[64,1024]{1,0:T(8,128)(2,1)S(1)}, bf16[64,1024]{1,0:T(8,128)(2,1)S(1)}, bf16[64,1024]{1,0:T(8,128)(2,1)S(1)}) custom-call(s32[1,1,3]{2,1,0:T(1,128)S(1)} %bitcast.3, s32[1,1]{1,0:T(1,128)S(6)} %copy.8.nu_count, f32[64,64]{1,0:T(8,128)S(1)} %copy-done.2, f32[64,64]{1,0:T(8,128)S(1)} %collective-permute-done.refs_1_, ...), custom_call_target="tpu_custom_call" | custom-call | flops 1200000000 | bytes 4000000 | tf_op jit(solution)/shard_map/half/pallas_call | solution.py:194
  12.4 1.3 %collective-permute-start.3 = (bf16[64,1024]{1,0:T(8,128)(2,1)S(1)}, bf16[64,1024]{1,0:T(8,128)(2,1)S(1)}, u32[]{:S(2)}, u32[]{:S(2)}) collective-permute-start(bf16[64,1024]{1,0:T(8,128)(2,1)S(1)} %get-tuple-element.12), channel_id=1, source_target_pairs={{0,2},{1,3},{2,0},{3,1},{4,6},{5,7},{6,4},{7,5},{8,10},{9,11},{10,... | collective-permute-start | bytes 393224 | tf_op jit(solution)/shard_map/ppermute | solution.py:218
  13.7 1.3 %collective-permute-start.4 = (bf16[64,1024]{1,0:T(8,128)(2,1)S(1)}, bf16[64,1024]{1,0:T(8,128)(2,1)S(1)}, u32[]{:S(2)}, u32[]{:S(2)}) collective-permute-start(bf16[64,1024]{1,0:T(8,128)(2,1)S(1)} %get-tuple-element.13), channel_id=1, source_target_pairs={{0,3},{1,2},{2,1},{3,0},{4,7},{5,6},{6,5},{7,4},{8,11},{9,10},{10,... | collective-permute-start | bytes 393224 | tf_op jit(solution)/shard_map/ppermute | solution.py:218
  15.0 0.9 %collective-permute-start.5 = (bf16[64,1024]{1,0:T(8,128)(2,1)S(1)}, bf16[64,1024]{1,0:T(8,128)(2,1)S(1)}, u32[]{:S(2)}, u32[]{:S(2)}) collective-permute-start(bf16[64,1024]{1,0:T(8,128)(2,1)S(1)} %get-tuple-element.14), channel_id=1, source_target_pairs={{0,1},{1,0},{2,3},{3,2},{4,5},{5,4},{6,7},{7,6},{8,9},{9,8},{10,11... | collective-permute-start | bytes 393224 | tf_op jit(solution)/shard_map/ppermute | solution.py:218
  16.6 0.0 copy-done
  16.6 0.0 copy-done.1
  16.6 1.0 %metric.2 = (bf16[1024,256]{1,0:T(8,128)(2,1)S(1)}, bf16[1024,256]{1,0:T(8,128)(2,1)S(1)}) custom-call(s32[1,1,3]{2,1,0:T(1,128)S(1)} %bitcast.2, s32[1,1]{1,0:T(1,128)S(6)} %copy.9.sig_count, bf16[64,1024]{1,0:T(8,128)(2,1)S(1)} %get-tuple-element.11.after.refs_0_, f32[1,3,64,1024]{3,2,1,0:T(8,128)S(1)} %copy-done), custom_call_target="tpu_custom_call" | custom-call | flops 10000000 | bytes 2000000 | tf_op jit(solution)/shard_map/metric/pallas_call | solution.py:208
  17.6 6.1 %collective-permute-done.3.refs_1_ = bf16[64,1024]{1,0:T(8,128)(2,1)S(1)} collective-permute-done((bf16[64,1024]{1,0:T(8,128)(2,1)S(1)}, bf16[64,1024]{1,0:T(8,128)(2,1)S(1)}, u32[]{:S(2)}, u32[]{:S(2)}) %collective-permute-start.3) | collective-permute-done | bytes 131104 | tf_op jit(solution)/shard_map/ppermute | solution.py:218
  23.7 0.0 collective-permute-done.4.refs_2_
  23.7 0.4 %collective-permute-done.5.refs_3_ = bf16[64,1024]{1,0:T(8,128)(2,1)S(1)} collective-permute-done((bf16[64,1024]{1,0:T(8,128)(2,1)S(1)}, bf16[64,1024]{1,0:T(8,128)(2,1)S(1)}, u32[]{:S(2)}, u32[]{:S(2)}) %collective-permute-start.5) | collective-permute-done | bytes 131104 | tf_op jit(solution)/shard_map/ppermute | solution.py:218
  24.2 0.5 %exchange.1 = bf16[32,16,128]{2,1,0:T(8,128)(2,1)S(1)} custom-call(bf16[64,1024]{1,0:T(8,128)(2,1)S(1)} %get-tuple-element.11.after.refs_0_, bf16[64,1024]{1,0:T(8,128)(2,1)S(1)} %collective-permute-done.3.refs_1_, bf16[64,1024]{1,0:T(8,128)(2,1)S(1)} %collective-permute-done.4.refs_2_, bf16[64,1024]{1,0:T(8,128)(2,1)S(1)} %collective-permute-done.5.refs_3_, ...), custom_call_target="tpu_custom_call" | custom-call | flops 300000000 | bytes 2000000 | tf_op jit(solution)/shard_map/exchange/pallas_call | solution.py:221
  24.7 12.9 %all_to_all.5.parts = bf16[32,16,128]{2,1,0:T(8,128)(2,1)S(1)} all-to-all(bf16[32,16,128]{2,1,0:T(8,128)(2,1)S(1)} %exchange.1), channel_id=1, replica_groups={{31,30,29,28,27,26,25,24,23,22,21,20,19,18,17,16,15,14,13,12,11,10,9,8,..., dimensions={0} | all-to-all | bytes 262144 | tf_op jit(solution)/shard_map/all_to_all | solution.py:232
  37.7 0.7 %sum.1 = f32[32,64]{1,0:T(8,128)} custom-call(bf16[32,16,128]{2,1,0:T(8,128)(2,1)S(1)} %all_to_all.5.parts), custom_call_target="tpu_custom_call" | custom-call | tf_op jit(solution)/shard_map/sum/pallas_call | solution.py:233
Async XLA Ops:
  0.0 8.3 %collective-permute-start = (f32[64,64]{1,0:T(8,128)}, f32[64,64]{1,0:T(8,128)S(1)}, u32[]{:S(2)}, u32[]{:S(2)}) collective-permute-start(f32[64,64]{1,0:T(8,128)} %refs_0_.1), channel_id=1, source_target_pairs={{0,2},{1,3},{2,0},{3,1},{4,6},{5,7},{6,4},{7,5},{8,10},{9,11},{10,... | collective-permute-start | bytes 49160 | tf_op jit(solution)/shard_map/ppermute | solution.py:175
  4.0 5.9 %collective-permute-start.1 = (f32[64,64]{1,0:T(8,128)}, f32[64,64]{1,0:T(8,128)S(1)}, u32[]{:S(2)}, u32[]{:S(2)}) collective-permute-start(f32[64,64]{1,0:T(8,128)} %refs_0_.1), channel_id=1, source_target_pairs={{0,3},{1,2},{2,1},{3,0},{4,7},{5,6},{6,5},{7,4},{8,11},{9,10},{10,... | collective-permute-start | bytes 49160 | tf_op jit(solution)/shard_map/ppermute | solution.py:175
  5.4 4.6 %collective-permute-start.2 = (f32[64,64]{1,0:T(8,128)}, f32[64,64]{1,0:T(8,128)S(1)}, u32[]{:S(2)}, u32[]{:S(2)}) collective-permute-start(f32[64,64]{1,0:T(8,128)} %refs_0_.1), channel_id=1, source_target_pairs={{0,1},{1,0},{2,3},{3,2},{4,5},{5,4},{6,7},{7,6},{8,9},{9,8},{10,11... | collective-permute-start | bytes 49160 | tf_op jit(solution)/shard_map/ppermute | solution.py:175
  6.3 3.7 %copy-start.2 = (f32[64,64]{1,0:T(8,128)S(1)}, f32[64,64]{1,0:T(8,128)}, u32[]{:S(2)}) copy-start(f32[64,64]{1,0:T(8,128)} %refs_0_.1) | copy-start | bytes 49156
  6.3 3.7 %copy-start.3 = (s32[1,3,1]{1,2,0:T(1,128)S(1)}, s32[1,3,1]{1,2,0:T(1,128)}, u32[]{:S(2)}) copy-start(s32[1,3,1]{1,2,0:T(1,128)} %param.8) | copy-start | bytes 40
  8.3 8.3 %copy-start = (f32[1,3,64,1024]{3,2,1,0:T(8,128)S(1)}, f32[1,3,64,1024]{3,2,1,0:T(8,128)}, u32[]{:S(2)}) copy-start(f32[1,3,64,1024]{3,2,1,0:T(8,128)} %metric.3) | copy-start | bytes 2359300
  8.3 8.3 %copy-start.1 = (s32[1,3,1]{1,2,0:T(1,128)S(1)}, s32[1,3,1]{1,2,0:T(1,128)}, u32[]{:S(2)}) copy-start(s32[1,3,1]{1,2,0:T(1,128)} %param.12) | copy-start | bytes 40
  12.4 11.3 %collective-permute-start.3 = (bf16[64,1024]{1,0:T(8,128)(2,1)S(1)}, bf16[64,1024]{1,0:T(8,128)(2,1)S(1)}, u32[]{:S(2)}, u32[]{:S(2)}) collective-permute-start(bf16[64,1024]{1,0:T(8,128)(2,1)S(1)} %get-tuple-element.12), channel_id=1, source_target_pairs={{0,2},{1,3},{2,0},{3,1},{4,6},{5,7},{6,4},{7,5},{8,10},{9,11},{10,... | collective-permute-start | bytes 393224 | tf_op jit(solution)/shard_map/ppermute | solution.py:218
  13.7 10.0 %collective-permute-start.4 = (bf16[64,1024]{1,0:T(8,128)(2,1)S(1)}, bf16[64,1024]{1,0:T(8,128)(2,1)S(1)}, u32[]{:S(2)}, u32[]{:S(2)}) collective-permute-start(bf16[64,1024]{1,0:T(8,128)(2,1)S(1)} %get-tuple-element.13), channel_id=1, source_target_pairs={{0,3},{1,2},{2,1},{3,0},{4,7},{5,6},{6,5},{7,4},{8,11},{9,10},{10,... | collective-permute-start | bytes 393224 | tf_op jit(solution)/shard_map/ppermute | solution.py:218
  15.0 9.2 %collective-permute-start.5 = (bf16[64,1024]{1,0:T(8,128)(2,1)S(1)}, bf16[64,1024]{1,0:T(8,128)(2,1)S(1)}, u32[]{:S(2)}, u32[]{:S(2)}) collective-permute-start(bf16[64,1024]{1,0:T(8,128)(2,1)S(1)} %get-tuple-element.14), channel_id=1, source_target_pairs={{0,1},{1,0},{2,3},{3,2},{4,5},{5,4},{6,7},{7,6},{8,9},{9,8},{10,11... | collective-permute-start | bytes 393224 | tf_op jit(solution)/shard_map/ppermute | solution.py:218

commit v14 on v13

--- a/solution.py
+++ b/solution.py
@@ -100,10 +100,12 @@
         group = jnp.where((col >> 3) & 3 == slot, z ^ HALF_ORDER[slot], group)
     wanted = group * lam + (col >> 6) * 8 + (col & 7)
     choose = jnp.where(row == wanted, 1.0, 0.0).astype(BF16)
+    halves = [split(d[...]) for d in dens]
+    stacked = jnp.concatenate([half[part] for part in range(2) for half in halves], axis=0)
+    chosen = jnp.dot(stacked, choose, preferred_element_type=F32)
     for s in range(n_mu):
-        hi, lo = split(dens[s][...])
-        d_both[s, :, :128] = jnp.dot(hi, choose, preferred_element_type=F32)
-        d_both[s, :, 128:] = jnp.dot(lo, choose, preferred_element_type=F32)
+        d_both[s, :, :128] = chosen[s * orb:(s + 1) * orb]
+        d_both[s, :, 128:] = chosen[(n_mu + s) * orb:(n_mu + s + 1) * orb]
     orbital = (iota((orb, 256), 1) >> 5) & 1
     for k in range(slots):
         live = jnp.where(k < nu_count[0, 0], 1.0, 0.0)

time: 38.5 us -> 38.5 us (level)
  no operation moved by 1% of the time
where the time goes in v14:
time: 38.5 us; the launch traced here: 38.4 us
  blocking collectives  12.9 us (34%)
  starting transfers between devices  9.17 us (24%)
  waiting for transfers between devices  8.17 us (21%)
  Pallas kernels  6.66 us (17%)
  between operations  1.4 us (4%)
    all_to_all x1, blocking collectives, fast(): parts = lax.all_to_all(parts, ('aux', 'mu'), 0, 0, axis_index_groups=[down])  12.9 us
    ppermute x3, waiting for transfers between devices, fast(): lax.ppermute(halves[s], 'mu', turns[HALF_ORDER[s]])  6.52 us
    ppermute x3, starting transfers between devices, fast(): lax.ppermute(density, 'mu', turns[s])  5.62 us
    ppermute x3, starting transfers between devices, fast(): lax.ppermute(halves[s], 'mu', turns[HALF_ORDER[s]])  3.55 us
    pallas_call x1, Pallas kernels, fast(): pl.pallas_call(functools.partial(half_kernel, n_mu), out_shape=(half_shap...  2.43 us
    pallas_call x1, Pallas kernels, fast(): pl.pallas_call(tensor_kernel, out_shape=t_shape, in_specs=[HBM], out_spec...  1.98 us
    ppermute x3, waiting for transfers between devices, fast(): lax.ppermute(density, 'mu', turns[s])  1.65 us
    pallas_call x1, Pallas kernels, fast(): pl.pallas_call(metric_kernel, out_shape=(m_shape, m_shape), in_specs=[SME...  1 us
  transfers between devices with their start and end apart: 6, of which 3 were waited for; matrix products, arithmetic and copies ran while one was open for 0% of the time, Pallas kernels for 8%

profile of v14, /device:TPU:0, one launch (start us, length us, event | category | flops | bytes accessed | tf_op | source)
XLA Modules:
  0.0 38.4 jit_solution(4484788467224619623)
XLA Ops:
  0.0 4.0 %collective-permute-start = (f32[64,64]{1,0:T(8,128)}, f32[64,64]{1,0:T(8,128)S(1)}, u32[]{:S(2)}, u32[]{:S(2)}) collective-permute-start(f32[64,64]{1,0:T(8,128)} %refs_0_.1), channel_id=1, source_target_pairs={{0,2},{1,3},{2,0},{3,1},{4,6},{5,7},{6,4},{7,5},{8,10},{9,11},{10,... | collective-permute-start | bytes 49160 | tf_op jit(solution)/shard_map/ppermute | solution.py:177
  4.0 1.3 %collective-permute-start.1 = (f32[64,64]{1,0:T(8,128)}, f32[64,64]{1,0:T(8,128)S(1)}, u32[]{:S(2)}, u32[]{:S(2)}) collective-permute-start(f32[64,64]{1,0:T(8,128)} %refs_0_.1), channel_id=1, source_target_pairs={{0,3},{1,2},{2,1},{3,0},{4,7},{5,6},{6,5},{7,4},{8,11},{9,10},{10,... | collective-permute-start | bytes 49160 | tf_op jit(solution)/shard_map/ppermute | solution.py:177
  5.4 0.2 collective-permute-start.2
  6.3 0.0 copy-start.2
  6.3 0.0 copy-start.3
  6.3 2.0 %tensor.2.refs_4_ = bf16[2048,768]{1,0:T(8,128)(2,1)S(1)} custom-call(f32[1,3,64,4096]{3,2,1,0:T(8,128)} %tensor.3), custom_call_target="tpu_custom_call" | custom-call | flops 10000000 | bytes 6000000 | tf_op jit(solution)/shard_map/tensor/pallas_call | solution.py:182
  8.3 0.0 copy-start
  8.3 0.0 copy-start.1
  8.3 0.0 collective-permute-done.refs_1_
  8.3 1.6 %collective-permute-done.1.refs_2_ = f32[64,64]{1,0:T(8,128)S(1)} collective-permute-done((f32[64,64]{1,0:T(8,128)}, f32[64,64]{1,0:T(8,128)S(1)}, u32[]{:S(2)}, u32[]{:S(2)}) %collective-permute-start.1) | collective-permute-done | bytes 16416 | tf_op jit(solution)/shard_map/ppermute | solution.py:177
  10.0 0.0 collective-permute-done.2.refs_3_
  10.0 0.0 copy-done.2
  10.0 0.0 copy-done.3
  10.0 2.4 %half.1 = (bf16[64,1024]{1,0:T(8,128)(2,1)S(1)}, bf16[64,1024]{1,0:T(8,128)(2,1)S(1)}, bf16[64,1024]{1,0:T(8,128)(2,1)S(1)}, bf16[64,1024]{1,0:T(8,128)(2,1)S(1)}) custom-call(s32[1,1,3]{2,1,0:T(1,128)S(1)} %bitcast.3, s32[1,1]{1,0:T(1,128)S(6)} %copy.8.nu_count, f32[64,64]{1,0:T(8,128)S(1)} %copy-done.2, f32[64,64]{1,0:T(8,128)S(1)} %collective-permute-done.refs_1_, ...), custom_call_target="tpu_custom_call" | custom-call | flops 1200000000 | bytes 4000000 | tf_op jit(solution)/shard_map/half/pallas_call | solution.py:196
  12.4 1.3 %collective-permute-start.3 = (bf16[64,1024]{1,0:T(8,128)(2,1)S(1)}, bf16[64,1024]{1,0:T(8,128)(2,1)S(1)}, u32[]{:S(2)}, u32[]{:S(2)}) collective-permute-start(bf16[64,1024]{1,0:T(8,128)(2,1)S(1)} %get-tuple-element.12), channel_id=1, source_target_pairs={{0,2},{1,3},{2,0},{3,1},{4,6},{5,7},{6,4},{7,5},{8,10},{9,11},{10,... | collective-permute-start | bytes 393224 | tf_op jit(solution)/shard_map/ppermute | solution.py:220
  13.7 1.3 %collective-permute-start.4 = (bf16[64,1024]{1,0:T(8,128)(2,1)S(1)}, bf16[64,1024]{1,0:T(8,128)(2,1)S(1)}, u32[]{:S(2)}, u32[]{:S(2)}) collective-permute-start(bf16[64,1024]{1,0:T(8,128)(2,1)S(1)} %get-tuple-element.13), channel_id=1, source_target_pairs={{0,3},{1,2},{2,1},{3,0},{4,7},{5,6},{6,5},{7,4},{8,11},{9,10},{10,... | collective-permute-start | bytes 393224 | tf_op jit(solution)/shard_map/ppermute | solution.py:220
  15.0 1.0 %collective-permute-start.5 = (bf16[64,1024]{1,0:T(8,128)(2,1)S(1)}, bf16[64,1024]{1,0:T(8,128)(2,1)S(1)}, u32[]{:S(2)}, u32[]{:S(2)}) collective-permute-start(bf16[64,1024]{1,0:T(8,128)(2,1)S(1)} %get-tuple-element.14), channel_id=1, source_target_pairs={{0,1},{1,0},{2,3},{3,2},{4,5},{5,4},{6,7},{7,6},{8,9},{9,8},{10,11... | collective-permute-start | bytes 393224 | tf_op jit(solution)/shard_map/ppermute | solution.py:220
  16.6 0.0 copy-done
  16.6 0.0 copy-done.1
  16.6 1.0 %metric.2 = (bf16[1024,256]{1,0:T(8,128)(2,1)S(1)}, bf16[1024,256]{1,0:T(8,128)(2,1)S(1)}) custom-call(s32[1,1,3]{2,1,0:T(1,128)S(1)} %bitcast.2, s32[1,1]{1,0:T(1,128)S(6)} %copy.9.sig_count, bf16[64,1024]{1,0:T(8,128)(2,1)S(1)} %get-tuple-element.11.after.refs_0_, f32[1,3,64,1024]{3,2,1,0:T(8,128)S(1)} %copy-done), custom_call_target="tpu_custom_call" | custom-call | flops 10000000 | bytes 2000000 | tf_op jit(solution)/shard_map/metric/pallas_call | solution.py:210
  17.6 6.1 %collective-permute-done.3.refs_1_ = bf16[64,1024]{1,0:T(8,128)(2,1)S(1)} collective-permute-done((bf16[64,1024]{1,0:T(8,128)(2,1)S(1)}, bf16[64,1024]{1,0:T(8,128)(2,1)S(1)}, u32[]{:S(2)}, u32[]{:S(2)}) %collective-permute-start.3) | collective-permute-done | bytes 131104 | tf_op jit(solution)/shard_map/ppermute | solution.py:220
  23.7 0.0 collective-permute-done.4.refs_2_
  23.7 0.4 %collective-permute-done.5.refs_3_ = bf16[64,1024]{1,0:T(8,128)(2,1)S(1)} collective-permute-done((bf16[64,1024]{1,0:T(8,128)(2,1)S(1)}, bf16[64,1024]{1,0:T(8,128)(2,1)S(1)}, u32[]{:S(2)}, u32[]{:S(2)}) %collective-permute-start.5) | collective-permute-done | bytes 131104 | tf_op jit(solution)/shard_map/ppermute | solution.py:220
  24.2 0.5 %exchange.1 = bf16[32,16,128]{2,1,0:T(8,128)(2,1)S(1)} custom-call(bf16[64,1024]{1,0:T(8,128)(2,1)S(1)} %get-tuple-element.11.after.refs_0_, bf16[64,1024]{1,0:T(8,128)(2,1)S(1)} %collective-permute-done.3.refs_1_, bf16[64,1024]{1,0:T(8,128)(2,1)S(1)} %collective-permute-done.4.refs_2_, bf16[64,1024]{1,0:T(8,128)(2,1)S(1)} %collective-permute-done.5.refs_3_, ...), custom_call_target="tpu_custom_call" | custom-call | flops 300000000 | bytes 2000000 | tf_op jit(solution)/shard_map/exchange/pallas_call | solution.py:223
  24.7 12.9 %all_to_all.5.parts = bf16[32,16,128]{2,1,0:T(8,128)(2,1)S(1)} all-to-all(bf16[32,16,128]{2,1,0:T(8,128)(2,1)S(1)} %exchange.1), channel_id=1, replica_groups={{31,30,29,28,27,26,25,24,23,22,21,20,19,18,17,16,15,14,13,12,11,10,9,8,..., dimensions={0} | all-to-all | bytes 262144 | tf_op jit(solution)/shard_map/all_to_all | solution.py:234
  37.7 0.7 %sum.1 = f32[32,64]{1,0:T(8,128)} custom-call(bf16[32,16,128]{2,1,0:T(8,128)(2,1)S(1)} %all_to_all.5.parts), custom_call_target="tpu_custom_call" | custom-call | tf_op jit(solution)/shard_map/sum/pallas_call | solution.py:235
Async XLA Ops:
  0.0 8.3 %collective-permute-start = (f32[64,64]{1,0:T(8,128)}, f32[64,64]{1,0:T(8,128)S(1)}, u32[]{:S(2)}, u32[]{:S(2)}) collective-permute-start(f32[64,64]{1,0:T(8,128)} %refs_0_.1), channel_id=1, source_target_pairs={{0,2},{1,3},{2,0},{3,1},{4,6},{5,7},{6,4},{7,5},{8,10},{9,11},{10,... | collective-permute-start | bytes 49160 | tf_op jit(solution)/shard_map/ppermute | solution.py:177
  4.0 5.9 %collective-permute-start.1 = (f32[64,64]{1,0:T(8,128)}, f32[64,64]{1,0:T(8,128)S(1)}, u32[]{:S(2)}, u32[]{:S(2)}) collective-permute-start(f32[64,64]{1,0:T(8,128)} %refs_0_.1), channel_id=1, source_target_pairs={{0,3},{1,2},{2,1},{3,0},{4,7},{5,6},{6,5},{7,4},{8,11},{9,10},{10,... | collective-permute-start | bytes 49160 | tf_op jit(solution)/shard_map/ppermute | solution.py:177
  5.4 4.6 %collective-permute-start.2 = (f32[64,64]{1,0:T(8,128)}, f32[64,64]{1,0:T(8,128)S(1)}, u32[]{:S(2)}, u32[]{:S(2)}) collective-permute-start(f32[64,64]{1,0:T(8,128)} %refs_0_.1), channel_id=1, source_target_pairs={{0,1},{1,0},{2,3},{3,2},{4,5},{5,4},{6,7},{7,6},{8,9},{9,8},{10,11... | collective-permute-start | bytes 49160 | tf_op jit(solution)/shard_map/ppermute | solution.py:177
  6.3 3.7 %copy-start.2 = (f32[64,64]{1,0:T(8,128)S(1)}, f32[64,64]{1,0:T(8,128)}, u32[]{:S(2)}) copy-start(f32[64,64]{1,0:T(8,128)} %refs_0_.1) | copy-start | bytes 49156
  6.3 3.7 %copy-start.3 = (s32[1,3,1]{1,2,0:T(1,128)S(1)}, s32[1,3,1]{1,2,0:T(1,128)}, u32[]{:S(2)}) copy-start(s32[1,3,1]{1,2,0:T(1,128)} %param.8) | copy-start | bytes 40
  8.3 8.3 %copy-start = (f32[1,3,64,1024]{3,2,1,0:T(8,128)S(1)}, f32[1,3,64,1024]{3,2,1,0:T(8,128)}, u32[]{:S(2)}) copy-start(f32[1,3,64,1024]{3,2,1,0:T(8,128)} %metric.3) | copy-start | bytes 2359300
  8.3 8.3 %copy-start.1 = (s32[1,3,1]{1,2,0:T(1,128)S(1)}, s32[1,3,1]{1,2,0:T(1,128)}, u32[]{:S(2)}) copy-start(s32[1,3,1]{1,2,0:T(1,128)} %param.12) | copy-start | bytes 40
  12.4 11.3 %collective-permute-start.3 = (bf16[64,1024]{1,0:T(8,128)(2,1)S(1)}, bf16[64,1024]{1,0:T(8,128)(2,1)S(1)}, u32[]{:S(2)}, u32[]{:S(2)}) collective-permute-start(bf16[64,1024]{1,0:T(8,128)(2,1)S(1)} %get-tuple-element.12), channel_id=1, source_target_pairs={{0,2},{1,3},{2,0},{3,1},{4,6},{5,7},{6,4},{7,5},{8,10},{9,11},{10,... | collective-permute-start | bytes 393224 | tf_op jit(solution)/shard_map/ppermute | solution.py:220
  13.7 10.0 %collective-permute-start.4 = (bf16[64,1024]{1,0:T(8,128)(2,1)S(1)}, bf16[64,1024]{1,0:T(8,128)(2,1)S(1)}, u32[]{:S(2)}, u32[]{:S(2)}) collective-permute-start(bf16[64,1024]{1,0:T(8,128)(2,1)S(1)} %get-tuple-element.13), channel_id=1, source_target_pairs={{0,3},{1,2},{2,1},{3,0},{4,7},{5,6},{6,5},{7,4},{8,11},{9,10},{10,... | collective-permute-start | bytes 393224 | tf_op jit(solution)/shard_map/ppermute | solution.py:220
  15.0 9.2 %collective-permute-start.5 = (bf16[64,1024]{1,0:T(8,128)(2,1)S(1)}, bf16[64,1024]{1,0:T(8,128)(2,1)S(1)}, u32[]{:S(2)}, u32[]{:S(2)}) collective-permute-start(bf16[64,1024]{1,0:T(8,128)(2,1)S(1)} %get-tuple-element.14), channel_id=1, source_target_pairs={{0,1},{1,0},{2,3},{3,2},{4,5},{5,4},{6,7},{7,6},{8,9},{9,8},{10,11... | collective-permute-start | bytes 393224 | tf_op jit(solution)/shard_map/ppermute | solution.py:220

commit v15 on v13

--- a/solution.py
+++ b/solution.py
@@ -60,7 +60,9 @@
             packed[at:at + aux_width, k * 256 + 128:(k + 1) * 256] = lo
 
 
-def metric_kernel(sig_slots, sig_count, after, metric, m_hi, m_lo):
+def metric_kernel(sig_slots, sig_count, after, metric, placed):
+    depth = placed.shape[0] // 2
+    m_hi, m_lo = placed.at[pl.ds(0, depth)], placed.at[pl.ds(depth, depth)]
     _, sig, aux_width, width = metric.shape
     half = iota((aux_width, 128), 1) >= 64
     pair_of = jnp.where(half, 1, 0)
@@ -115,11 +117,14 @@
                 weights[at:at + orb, :] = block
     aux_width = outs[0].shape[1] // lam
     lower = iota((aux_width, 128), 1) < 64
-    per_group = 512 // (2 * aux_width)
+    group_rows = packed.shape[0] // 2
+    per_group = group_rows // (2 * aux_width)
     span = per_group * 4
-    for part in range(packed.shape[0] // 512):
+    for part in range(packed.shape[0] // group_rows):
         product = jnp.dot(
-            packed[part * 512:(part + 1) * 512, :], weights[...], preferred_element_type=F32
+            packed[part * group_rows:(part + 1) * group_rows, :],
+            weights[...],
+            preferred_element_type=F32,
         )
         total = product[:, :128] + product[:, 128:]
         for chunk in range(per_group):
@@ -137,11 +142,11 @@
 
 def exchange_kernel(n_mu, n_aux, *refs):
     halves = refs[:n_mu]
-    m_hi, m_lo, out, total = refs[n_mu:]
+    placed, out, total = refs[n_mu:]
     z = lax.axis_index("mu")
     left = jnp.concatenate([h[...] for h in halves], axis=0)
-    product = jnp.dot(left, m_hi[...], preferred_element_type=F32)
-    product += jnp.dot(left, m_lo[...], preferred_element_type=F32)
+    left = jnp.concatenate([left, left], axis=1)
+    product = jnp.dot(left, placed[...], preferred_element_type=F32)
     orb = halves[0].shape[0]
     for s in range(n_mu):
         block = z ^ HALF_ORDER[s]
@@ -176,7 +181,7 @@
     nu_slots, sig_slots = jnp.swapaxes(nu_slots, 1, 2), jnp.swapaxes(sig_slots, 1, 2)
     chunks = three_center.shape[3] // 256
     t_shape = jax.ShapeDtypeStruct((2 * chunks * aux_width, slots * 256), BF16)
-    m_shape = jax.ShapeDtypeStruct((lam * aux_width, n_mu * orb), BF16)
+    m_shape = jax.ShapeDtypeStruct((2 * lam * aux_width, n_mu * orb), BF16)
     packed = pl.pallas_call(
         tensor_kernel,
         out_shape=t_shape,
@@ -205,11 +210,11 @@
         cost_estimate=pl.CostEstimate(flops=1_200_000_000, bytes_accessed=4_000_000, transcendentals=0),
         name="half",
     )(nu_slots, nu_count, *dens, packed)
-    m_hi, m_lo = pl.pallas_call(
+    placed = pl.pallas_call(
         metric_kernel,
-        out_shape=(m_shape, m_shape),
+        out_shape=m_shape,
         in_specs=[SMEM, SMEM, ANY, VMEM],
-        out_specs=(VMEM, VMEM),
+        out_specs=VMEM,
         compiler_params=params(16),
         cost_estimate=pl.CostEstimate(flops=10_000_000, bytes_accessed=2_000_000, transcendentals=0),
         name="metric",
@@ -221,13 +226,13 @@
     parts = pl.pallas_call(
         functools.partial(exchange_kernel, n_mu, n_aux),
         out_shape=jax.ShapeDtypeStruct((n_aux * n_mu, rows // 2, 128), BF16),
-        in_specs=[VMEM] * (n_mu + 2),
+        in_specs=[VMEM] * (n_mu + 1),
         out_specs=VMEM,
         scratch_shapes=[pltpu.VMEM((n_mu * orb, n_mu * orb), F32)],
         compiler_params=params(16),
         cost_estimate=pl.CostEstimate(flops=300_000_000, bytes_accessed=2_000_000, transcendentals=0),
         name="exchange",
-    )(*halves, m_hi, m_lo)
+    )(*halves, placed)
     down = list(reversed(range(n_aux * n_mu)))
     parts = lax.all_to_all(parts, ("aux", "mu"), 0, 0, axis_index_groups=[down])
     return pl.pallas_call(

time: 38.5 us -> 38.8 us (level)
  no operation moved by 1% of the time
where the time goes in v15:
time: 38.8 us; the launch traced here: 38.7 us
  blocking collectives  12.9 us (33%)
  starting transfers between devices  9.17 us (24%)
  waiting for transfers between devices  8.17 us (21%)
  Pallas kernels  6.94 us (18%)
  between operations  1.4 us (4%)
    all_to_all x1, blocking collectives, fast(): parts = lax.all_to_all(parts, ('aux', 'mu'), 0, 0, axis_index_groups=[down])  12.9 us
    ppermute x3, waiting for transfers between devices, fast(): lax.ppermute(halves[s], 'mu', turns[HALF_ORDER[s]])  6.52 us
    ppermute x3, starting transfers between devices, fast(): lax.ppermute(density, 'mu', turns[s])  5.62 us
    ppermute x3, starting transfers between devices, fast(): lax.ppermute(halves[s], 'mu', turns[HALF_ORDER[s]])  3.55 us
    pallas_call x1, Pallas kernels, fast(): pl.pallas_call(functools.partial(half_kernel, n_mu), out_shape=(half_shap...  2.71 us
    pallas_call x1, Pallas kernels, fast(): pl.pallas_call(tensor_kernel, out_shape=t_shape, in_specs=[HBM], out_spec...  1.98 us
    ppermute x3, waiting for transfers between devices, fast(): lax.ppermute(density, 'mu', turns[s])  1.65 us
    pallas_call x1, Pallas kernels, fast(): pl.pallas_call(metric_kernel, out_shape=m_shape, in_specs=[SMEM, SMEM, AN...  1 us
  transfers between devices with their start and end apart: 6, of which 3 were waited for; matrix products, arithmetic and copies ran while one was open for 0% of the time, Pallas kernels for 8%

profile of v15, /device:TPU:0, one launch (start us, length us, event | category | flops | bytes accessed | tf_op | source)
XLA Modules:
  0.0 38.7 jit_solution(9585215019580108788)
XLA Ops:
  0.0 4.0 %collective-permute-start = (f32[64,64]{1,0:T(8,128)}, f32[64,64]{1,0:T(8,128)S(1)}, u32[]{:S(2)}, u32[]{:S(2)}) collective-permute-start(f32[64,64]{1,0:T(8,128)} %refs_0_.1), channel_id=1, source_target_pairs={{0,2},{1,3},{2,0},{3,1},{4,6},{5,7},{6,4},{7,5},{8,10},{9,11},{10,... | collective-permute-start | bytes 49160 | tf_op jit(solution)/shard_map/ppermute | solution.py:180
  4.0 1.3 %collective-permute-start.1 = (f32[64,64]{1,0:T(8,128)}, f32[64,64]{1,0:T(8,128)S(1)}, u32[]{:S(2)}, u32[]{:S(2)}) collective-permute-start(f32[64,64]{1,0:T(8,128)} %refs_0_.1), channel_id=1, source_target_pairs={{0,3},{1,2},{2,1},{3,0},{4,7},{5,6},{6,5},{7,4},{8,11},{9,10},{10,... | collective-permute-start | bytes 49160 | tf_op jit(solution)/shard_map/ppermute | solution.py:180
  5.4 0.2 collective-permute-start.2
  6.3 0.0 copy-start.2
  6.3 0.0 copy-start.3
  6.3 2.0 %tensor.2.refs_4_ = bf16[2048,768]{1,0:T(8,128)(2,1)S(1)} custom-call(f32[1,3,64,4096]{3,2,1,0:T(8,128)} %tensor.3), custom_call_target="tpu_custom_call" | custom-call | flops 10000000 | bytes 6000000 | tf_op jit(solution)/shard_map/tensor/pallas_call | solution.py:185
  8.3 0.0 copy-start
  8.3 0.0 copy-start.1
  8.3 0.0 collective-permute-done.refs_1_
  8.3 1.6 %collective-permute-done.1.refs_2_ = f32[64,64]{1,0:T(8,128)S(1)} collective-permute-done((f32[64,64]{1,0:T(8,128)}, f32[64,64]{1,0:T(8,128)S(1)}, u32[]{:S(2)}, u32[]{:S(2)}) %collective-permute-start.1) | collective-permute-done | bytes 16416 | tf_op jit(solution)/shard_map/ppermute | solution.py:180
  10.0 0.0 collective-permute-done.2.refs_3_
  10.0 0.0 copy-done.2
  10.0 0.0 copy-done.3
  10.0 2.7 %half.1 = (bf16[64,1024]{1,0:T(8,128)(2,1)S(1)}, bf16[64,1024]{1,0:T(8,128)(2,1)S(1)}, bf16[64,1024]{1,0:T(8,128)(2,1)S(1)}, bf16[64,1024]{1,0:T(8,128)(2,1)S(1)}) custom-call(s32[1,1,3]{2,1,0:T(1,128)S(1)} %bitcast.3, s32[1,1]{1,0:T(1,128)S(6)} %copy.8.nu_count, f32[64,64]{1,0:T(8,128)S(1)} %copy-done.2, f32[64,64]{1,0:T(8,128)S(1)} %collective-permute-done.refs_1_, ...), custom_call_target="tpu_custom_call" | custom-call | flops 1200000000 | bytes 4000000 | tf_op jit(solution)/shard_map/half/pallas_call | solution.py:199
  12.7 1.3 %collective-permute-start.3 = (bf16[64,1024]{1,0:T(8,128)(2,1)S(1)}, bf16[64,1024]{1,0:T(8,128)(2,1)S(1)}, u32[]{:S(2)}, u32[]{:S(2)}) collective-permute-start(bf16[64,1024]{1,0:T(8,128)(2,1)S(1)} %get-tuple-element.10), channel_id=1, source_target_pairs={{0,2},{1,3},{2,0},{3,1},{4,6},{5,7},{6,4},{7,5},{8,10},{9,11},{10,... | collective-permute-start | bytes 393224 | tf_op jit(solution)/shard_map/ppermute | solution.py:223
  14.0 1.3 %collective-permute-start.4 = (bf16[64,1024]{1,0:T(8,128)(2,1)S(1)}, bf16[64,1024]{1,0:T(8,128)(2,1)S(1)}, u32[]{:S(2)}, u32[]{:S(2)}) collective-permute-start(bf16[64,1024]{1,0:T(8,128)(2,1)S(1)} %get-tuple-element.11), channel_id=1, source_target_pairs={{0,3},{1,2},{2,1},{3,0},{4,7},{5,6},{6,5},{7,4},{8,11},{9,10},{10,... | collective-permute-start | bytes 393224 | tf_op jit(solution)/shard_map/ppermute | solution.py:223
  15.3 0.9 %collective-permute-start.5 = (bf16[64,1024]{1,0:T(8,128)(2,1)S(1)}, bf16[64,1024]{1,0:T(8,128)(2,1)S(1)}, u32[]{:S(2)}, u32[]{:S(2)}) collective-permute-start(bf16[64,1024]{1,0:T(8,128)(2,1)S(1)} %get-tuple-element.12), channel_id=1, source_target_pairs={{0,1},{1,0},{2,3},{3,2},{4,5},{5,4},{6,7},{7,6},{8,9},{9,8},{10,11... | collective-permute-start | bytes 393224 | tf_op jit(solution)/shard_map/ppermute | solution.py:223
  16.9 0.0 copy-done
  16.9 0.0 copy-done.1
  16.9 1.0 %metric.2.refs_4_ = bf16[2048,256]{1,0:T(8,128)(2,1)S(1)} custom-call(s32[1,1,3]{2,1,0:T(1,128)S(1)} %bitcast.2, s32[1,1]{1,0:T(1,128)S(6)} %copy.9.sig_count, bf16[64,1024]{1,0:T(8,128)(2,1)S(1)} %get-tuple-element.9.after.refs_0_, f32[1,3,64,1024]{3,2,1,0:T(8,128)S(1)} %copy-done), custom_call_target="tpu_custom_call" | custom-call | flops 10000000 | bytes 2000000 | tf_op jit(solution)/shard_map/metric/pallas_call | solution.py:213
  17.9 6.1 %collective-permute-done.3.refs_1_ = bf16[64,1024]{1,0:T(8,128)(2,1)S(1)} collective-permute-done((bf16[64,1024]{1,0:T(8,128)(2,1)S(1)}, bf16[64,1024]{1,0:T(8,128)(2,1)S(1)}, u32[]{:S(2)}, u32[]{:S(2)}) %collective-permute-start.3) | collective-permute-done | bytes 131104 | tf_op jit(solution)/shard_map/ppermute | solution.py:223
  24.0 0.0 collective-permute-done.4.refs_2_
  24.0 0.4 %collective-permute-done.5.refs_3_ = bf16[64,1024]{1,0:T(8,128)(2,1)S(1)} collective-permute-done((bf16[64,1024]{1,0:T(8,128)(2,1)S(1)}, bf16[64,1024]{1,0:T(8,128)(2,1)S(1)}, u32[]{:S(2)}, u32[]{:S(2)}) %collective-permute-start.5) | collective-permute-done | bytes 131104 | tf_op jit(solution)/shard_map/ppermute | solution.py:223
  24.4 0.5 %exchange.1 = bf16[32,16,128]{2,1,0:T(8,128)(2,1)S(1)} custom-call(bf16[64,1024]{1,0:T(8,128)(2,1)S(1)} %get-tuple-element.9.after.refs_0_, bf16[64,1024]{1,0:T(8,128)(2,1)S(1)} %collective-permute-done.3.refs_1_, bf16[64,1024]{1,0:T(8,128)(2,1)S(1)} %collective-permute-done.4.refs_2_, bf16[64,1024]{1,0:T(8,128)(2,1)S(1)} %collective-permute-done.5.refs_3_, ...), custom_call_target="tpu_custom_call" | custom-call | flops 300000000 | bytes 2000000 | tf_op jit(solution)/shard_map/exchange/pallas_call | solution.py:226
  25.0 12.9 %all_to_all.5.parts = bf16[32,16,128]{2,1,0:T(8,128)(2,1)S(1)} all-to-all(bf16[32,16,128]{2,1,0:T(8,128)(2,1)S(1)} %exchange.1), channel_id=1, replica_groups={{31,30,29,28,27,26,25,24,23,22,21,20,19,18,17,16,15,14,13,12,11,10,9,8,..., dimensions={0} | all-to-all | bytes 262144 | tf_op jit(solution)/shard_map/all_to_all | solution.py:237
  37.9 0.7 %sum.1 = f32[32,64]{1,0:T(8,128)} custom-call(bf16[32,16,128]{2,1,0:T(8,128)(2,1)S(1)} %all_to_all.5.parts), custom_call_target="tpu_custom_call" | custom-call | tf_op jit(solution)/shard_map/sum/pallas_call | solution.py:238
Async XLA Ops:
  0.0 8.3 %collective-permute-start = (f32[64,64]{1,0:T(8,128)}, f32[64,64]{1,0:T(8,128)S(1)}, u32[]{:S(2)}, u32[]{:S(2)}) collective-permute-start(f32[64,64]{1,0:T(8,128)} %refs_0_.1), channel_id=1, source_target_pairs={{0,2},{1,3},{2,0},{3,1},{4,6},{5,7},{6,4},{7,5},{8,10},{9,11},{10,... | collective-permute-start | bytes 49160 | tf_op jit(solution)/shard_map/ppermute | solution.py:180
  4.0 5.9 %collective-permute-start.1 = (f32[64,64]{1,0:T(8,128)}, f32[64,64]{1,0:T(8,128)S(1)}, u32[]{:S(2)}, u32[]{:S(2)}) collective-permute-start(f32[64,64]{1,0:T(8,128)} %refs_0_.1), channel_id=1, source_target_pairs={{0,3},{1,2},{2,1},{3,0},{4,7},{5,6},{6,5},{7,4},{8,11},{9,10},{10,... | collective-permute-start | bytes 49160 | tf_op jit(solution)/shard_map/ppermute | solution.py:180
  5.4 4.6 %collective-permute-start.2 = (f32[64,64]{1,0:T(8,128)}, f32[64,64]{1,0:T(8,128)S(1)}, u32[]{:S(2)}, u32[]{:S(2)}) collective-permute-start(f32[64,64]{1,0:T(8,128)} %refs_0_.1), channel_id=1, source_target_pairs={{0,1},{1,0},{2,3},{3,2},{4,5},{5,4},{6,7},{7,6},{8,9},{9,8},{10,11... | collective-permute-start | bytes 49160 | tf_op jit(solution)/shard_map/ppermute | solution.py:180
  6.3 3.7 %copy-start.2 = (f32[64,64]{1,0:T(8,128)S(1)}, f32[64,64]{1,0:T(8,128)}, u32[]{:S(2)}) copy-start(f32[64,64]{1,0:T(8,128)} %refs_0_.1) | copy-start | bytes 49156
  6.3 3.7 %copy-start.3 = (s32[1,3,1]{1,2,0:T(1,128)S(1)}, s32[1,3,1]{1,2,0:T(1,128)}, u32[]{:S(2)}) copy-start(s32[1,3,1]{1,2,0:T(1,128)} %param.8) | copy-start | bytes 40
  8.3 8.6 %copy-start = (f32[1,3,64,1024]{3,2,1,0:T(8,128)S(1)}, f32[1,3,64,1024]{3,2,1,0:T(8,128)}, u32[]{:S(2)}) copy-start(f32[1,3,64,1024]{3,2,1,0:T(8,128)} %metric.3) | copy-start | bytes 2359300
  8.3 8.6 %copy-start.1 = (s32[1,3,1]{1,2,0:T(1,128)S(1)}, s32[1,3,1]{1,2,0:T(1,128)}, u32[]{:S(2)}) copy-start(s32[1,3,1]{1,2,0:T(1,128)} %param.12) | copy-start | bytes 40
  12.7 11.3 %collective-permute-start.3 = (bf16[64,1024]{1,0:T(8,128)(2,1)S(1)}, bf16[64,1024]{1,0:T(8,128)(2,1)S(1)}, u32[]{:S(2)}, u32[]{:S(2)}) collective-permute-start(bf16[64,1024]{1,0:T(8,128)(2,1)S(1)} %get-tuple-element.10), channel_id=1, source_target_pairs={{0,2},{1,3},{2,0},{3,1},{4,6},{5,7},{6,4},{7,5},{8,10},{9,11},{10,... | collective-permute-start | bytes 393224 | tf_op jit(solution)/shard_map/ppermute | solution.py:223
  14.0 10.0 %collective-permute-start.4 = (bf16[64,1024]{1,0:T(8,128)(2,1)S(1)}, bf16[64,1024]{1,0:T(8,128)(2,1)S(1)}, u32[]{:S(2)}, u32[]{:S(2)}) collective-permute-start(bf16[64,1024]{1,0:T(8,128)(2,1)S(1)} %get-tuple-element.11), channel_id=1, source_target_pairs={{0,3},{1,2},{2,1},{3,0},{4,7},{5,6},{6,5},{7,4},{8,11},{9,10},{10,... | collective-permute-start | bytes 393224 | tf_op jit(solution)/shard_map/ppermute | solution.py:223
  15.3 9.1 %collective-permute-start.5 = (bf16[64,1024]{1,0:T(8,128)(2,1)S(1)}, bf16[64,1024]{1,0:T(8,128)(2,1)S(1)}, u32[]{:S(2)}, u32[]{:S(2)}) collective-permute-start(bf16[64,1024]{1,0:T(8,128)(2,1)S(1)} %get-tuple-element.12), channel_id=1, source_target_pairs={{0,1},{1,0},{2,3},{3,2},{4,5},{5,4},{6,7},{7,6},{8,9},{9,8},{10,11... | collective-permute-start | bytes 393224 | tf_op jit(solution)/shard_map/ppermute | solution.py:223

commit v16 on v13

--- a/solution.py
+++ b/solution.py
@@ -118,12 +118,14 @@
     per_group = 512 // (2 * aux_width)
     span = per_group * 4
     for part in range(packed.shape[0] // 512):
-        product = jnp.dot(
-            packed[part * 512:(part + 1) * 512, :], weights[...], preferred_element_type=F32
-        )
-        total = product[:, :128] + product[:, 128:]
         for chunk in range(per_group):
-            at = chunk * 2 * aux_width
+            if chunk % 2 == 0:
+                first = part * 512 + chunk * 2 * aux_width
+                product = jnp.dot(
+                    packed[first:first + 256, :], weights[...], preferred_element_type=F32
+                )
+                total = product[:, :128] + product[:, 128:]
+            at = chunk % 2 * 2 * aux_width
             one, two = total[at:at + aux_width], total[at + aux_width:at + 2 * aux_width]
             top = jnp.where(lower, one, pltpu.roll(two, 64, 1))
             bottom = jnp.where(lower, pltpu.roll(one, 64, 1), two)

time: 38.5 us -> 38.6 us (level)
  no operation moved by 1% of the time
where the time goes in v16:
time: 38.6 us; the launch traced here: 38.4 us
  blocking collectives  12.9 us (33%)
  starting transfers between devices  9.17 us (24%)
  waiting for transfers between devices  8.17 us (21%)
  Pallas kernels  6.68 us (17%)
  between operations  1.4 us (4%)
    all_to_all x1, blocking collectives, fast(): parts = lax.all_to_all(parts, ('aux', 'mu'), 0, 0, axis_index_groups=[down])  12.9 us
    ppermute x3, waiting for transfers between devices, fast(): lax.ppermute(halves[s], 'mu', turns[HALF_ORDER[s]])  6.52 us
    ppermute x3, starting transfers between devices, fast(): lax.ppermute(density, 'mu', turns[s])  5.62 us
    ppermute x3, starting transfers between devices, fast(): lax.ppermute(halves[s], 'mu', turns[HALF_ORDER[s]])  3.55 us
    pallas_call x1, Pallas kernels, fast(): pl.pallas_call(functools.partial(half_kernel, n_mu), out_shape=(half_shap...  2.45 us
    pallas_call x1, Pallas kernels, fast(): pl.pallas_call(tensor_kernel, out_shape=t_shape, in_specs=[HBM], out_spec...  1.98 us
    ppermute x3, waiting for transfers between devices, fast(): lax.ppermute(density, 'mu', turns[s])  1.65 us
    pallas_call x1, Pallas kernels, fast(): pl.pallas_call(metric_kernel, out_shape=(m_shape, m_shape), in_specs=[SME...  1 us
  transfers between devices with their start and end apart: 6, of which 3 were waited for; matrix products, arithmetic and copies ran while one was open for 0% of the time, Pallas kernels for 8%

profile of v16, /device:TPU:0, one launch (start us, length us, event | category | flops | bytes accessed | tf_op | source)
XLA Modules:
  0.0 38.4 jit_solution(707918043845107532)
XLA Ops:
  0.0 4.0 %collective-permute-start = (f32[64,64]{1,0:T(8,128)}, f32[64,64]{1,0:T(8,128)S(1)}, u32[]{:S(2)}, u32[]{:S(2)}) collective-permute-start(f32[64,64]{1,0:T(8,128)} %refs_0_.1), channel_id=1, source_target_pairs={{0,2},{1,3},{2,0},{3,1},{4,6},{5,7},{6,4},{7,5},{8,10},{9,11},{10,... | collective-permute-start | bytes 49160 | tf_op jit(solution)/shard_map/ppermute | solution.py:177
  4.0 1.3 %collective-permute-start.1 = (f32[64,64]{1,0:T(8,128)}, f32[64,64]{1,0:T(8,128)S(1)}, u32[]{:S(2)}, u32[]{:S(2)}) collective-permute-start(f32[64,64]{1,0:T(8,128)} %refs_0_.1), channel_id=1, source_target_pairs={{0,3},{1,2},{2,1},{3,0},{4,7},{5,6},{6,5},{7,4},{8,11},{9,10},{10,... | collective-permute-start | bytes 49160 | tf_op jit(solution)/shard_map/ppermute | solution.py:177
  5.4 0.2 collective-permute-start.2
  6.3 0.0 copy-start.2
  6.3 0.0 copy-start.3
  6.3 2.0 %tensor.2.refs_4_ = bf16[2048,768]{1,0:T(8,128)(2,1)S(1)} custom-call(f32[1,3,64,4096]{3,2,1,0:T(8,128)} %tensor.3), custom_call_target="tpu_custom_call" | custom-call | flops 10000000 | bytes 6000000 | tf_op jit(solution)/shard_map/tensor/pallas_call | solution.py:182
  8.3 0.0 copy-start
  8.3 0.0 copy-start.1
  8.3 0.0 collective-permute-done.refs_1_
  8.3 1.6 %collective-permute-done.1.refs_2_ = f32[64,64]{1,0:T(8,128)S(1)} collective-permute-done((f32[64,64]{1,0:T(8,128)}, f32[64,64]{1,0:T(8,128)S(1)}, u32[]{:S(2)}, u32[]{:S(2)}) %collective-permute-start.1) | collective-permute-done | bytes 16416 | tf_op jit(solution)/shard_map/ppermute | solution.py:177
  10.0 0.0 collective-permute-done.2.refs_3_
  10.0 0.0 copy-done.2
  10.0 0.0 copy-done.3
  10.0 2.4 %half.1 = (bf16[64,1024]{1,0:T(8,128)(2,1)S(1)}, bf16[64,1024]{1,0:T(8,128)(2,1)S(1)}, bf16[64,1024]{1,0:T(8,128)(2,1)S(1)}, bf16[64,1024]{1,0:T(8,128)(2,1)S(1)}) custom-call(s32[1,1,3]{2,1,0:T(1,128)S(1)} %bitcast.3, s32[1,1]{1,0:T(1,128)S(6)} %copy.8.nu_count, f32[64,64]{1,0:T(8,128)S(1)} %copy-done.2, f32[64,64]{1,0:T(8,128)S(1)} %collective-permute-done.refs_1_, ...), custom_call_target="tpu_custom_call" | custom-call | flops 1200000000 | bytes 4000000 | tf_op jit(solution)/shard_map/half/pallas_call | solution.py:196
  12.4 1.3 %collective-permute-start.3 = (bf16[64,1024]{1,0:T(8,128)(2,1)S(1)}, bf16[64,1024]{1,0:T(8,128)(2,1)S(1)}, u32[]{:S(2)}, u32[]{:S(2)}) collective-permute-start(bf16[64,1024]{1,0:T(8,128)(2,1)S(1)} %get-tuple-element.12), channel_id=1, source_target_pairs={{0,2},{1,3},{2,0},{3,1},{4,6},{5,7},{6,4},{7,5},{8,10},{9,11},{10,... | collective-permute-start | bytes 393224 | tf_op jit(solution)/shard_map/ppermute | solution.py:220
  13.7 1.3 %collective-permute-start.4 = (bf16[64,1024]{1,0:T(8,128)(2,1)S(1)}, bf16[64,1024]{1,0:T(8,128)(2,1)S(1)}, u32[]{:S(2)}, u32[]{:S(2)}) collective-permute-start(bf16[64,1024]{1,0:T(8,128)(2,1)S(1)} %get-tuple-element.13), channel_id=1, source_target_pairs={{0,3},{1,2},{2,1},{3,0},{4,7},{5,6},{6,5},{7,4},{8,11},{9,10},{10,... | collective-permute-start | bytes 393224 | tf_op jit(solution)/shard_map/ppermute | solution.py:220
  15.0 0.9 %collective-permute-start.5 = (bf16[64,1024]{1,0:T(8,128)(2,1)S(1)}, bf16[64,1024]{1,0:T(8,128)(2,1)S(1)}, u32[]{:S(2)}, u32[]{:S(2)}) collective-permute-start(bf16[64,1024]{1,0:T(8,128)(2,1)S(1)} %get-tuple-element.14), channel_id=1, source_target_pairs={{0,1},{1,0},{2,3},{3,2},{4,5},{5,4},{6,7},{7,6},{8,9},{9,8},{10,11... | collective-permute-start | bytes 393224 | tf_op jit(solution)/shard_map/ppermute | solution.py:220
  16.6 0.0 copy-done
  16.6 0.0 copy-done.1
  16.7 1.0 %metric.2 = (bf16[1024,256]{1,0:T(8,128)(2,1)S(1)}, bf16[1024,256]{1,0:T(8,128)(2,1)S(1)}) custom-call(s32[1,1,3]{2,1,0:T(1,128)S(1)} %bitcast.2, s32[1,1]{1,0:T(1,128)S(6)} %copy.9.sig_count, bf16[64,1024]{1,0:T(8,128)(2,1)S(1)} %get-tuple-element.11.after.refs_0_, f32[1,3,64,1024]{3,2,1,0:T(8,128)S(1)} %copy-done), custom_call_target="tpu_custom_call" | custom-call | flops 10000000 | bytes 2000000 | tf_op jit(solution)/shard_map/metric/pallas_call | solution.py:210
  17.7 6.1 %collective-permute-done.3.refs_1_ = bf16[64,1024]{1,0:T(8,128)(2,1)S(1)} collective-permute-done((bf16[64,1024]{1,0:T(8,128)(2,1)S(1)}, bf16[64,1024]{1,0:T(8,128)(2,1)S(1)}, u32[]{:S(2)}, u32[]{:S(2)}) %collective-permute-start.3) | collective-permute-done | bytes 131104 | tf_op jit(solution)/shard_map/ppermute | solution.py:220
  23.8 0.0 collective-permute-done.4.refs_2_
  23.8 0.4 %collective-permute-done.5.refs_3_ = bf16[64,1024]{1,0:T(8,128)(2,1)S(1)} collective-permute-done((bf16[64,1024]{1,0:T(8,128)(2,1)S(1)}, bf16[64,1024]{1,0:T(8,128)(2,1)S(1)}, u32[]{:S(2)}, u32[]{:S(2)}) %collective-permute-start.5) | collective-permute-done | bytes 131104 | tf_op jit(solution)/shard_map/ppermute | solution.py:220
  24.2 0.5 %exchange.1 = bf16[32,16,128]{2,1,0:T(8,128)(2,1)S(1)} custom-call(bf16[64,1024]{1,0:T(8,128)(2,1)S(1)} %get-tuple-element.11.after.refs_0_, bf16[64,1024]{1,0:T(8,128)(2,1)S(1)} %collective-permute-done.3.refs_1_, bf16[64,1024]{1,0:T(8,128)(2,1)S(1)} %collective-permute-done.4.refs_2_, bf16[64,1024]{1,0:T(8,128)(2,1)S(1)} %collective-permute-done.5.refs_3_, ...), custom_call_target="tpu_custom_call" | custom-call | flops 300000000 | bytes 2000000 | tf_op jit(solution)/shard_map/exchange/pallas_call | solution.py:223
  24.7 12.9 %all_to_all.5.parts = bf16[32,16,128]{2,1,0:T(8,128)(2,1)S(1)} all-to-all(bf16[32,16,128]{2,1,0:T(8,128)(2,1)S(1)} %exchange.1), channel_id=1, replica_groups={{31,30,29,28,27,26,25,24,23,22,21,20,19,18,17,16,15,14,13,12,11,10,9,8,..., dimensions={0} | all-to-all | bytes 262144 | tf_op jit(solution)/shard_map/all_to_all | solution.py:234
  37.7 0.7 %sum.1 = f32[32,64]{1,0:T(8,128)} custom-call(bf16[32,16,128]{2,1,0:T(8,128)(2,1)S(1)} %all_to_all.5.parts), custom_call_target="tpu_custom_call" | custom-call | tf_op jit(solution)/shard_map/sum/pallas_call | solution.py:235
Async XLA Ops:
  0.0 8.3 %collective-permute-start = (f32[64,64]{1,0:T(8,128)}, f32[64,64]{1,0:T(8,128)S(1)}, u32[]{:S(2)}, u32[]{:S(2)}) collective-permute-start(f32[64,64]{1,0:T(8,128)} %refs_0_.1), channel_id=1, source_target_pairs={{0,2},{1,3},{2,0},{3,1},{4,6},{5,7},{6,4},{7,5},{8,10},{9,11},{10,... | collective-permute-start | bytes 49160 | tf_op jit(solution)/shard_map/ppermute | solution.py:177
  4.0 5.9 %collective-permute-start.1 = (f32[64,64]{1,0:T(8,128)}, f32[64,64]{1,0:T(8,128)S(1)}, u32[]{:S(2)}, u32[]{:S(2)}) collective-permute-start(f32[64,64]{1,0:T(8,128)} %refs_0_.1), channel_id=1, source_target_pairs={{0,3},{1,2},{2,1},{3,0},{4,7},{5,6},{6,5},{7,4},{8,11},{9,10},{10,... | collective-permute-start | bytes 49160 | tf_op jit(solution)/shard_map/ppermute | solution.py:177
  5.4 4.6 %collective-permute-start.2 = (f32[64,64]{1,0:T(8,128)}, f32[64,64]{1,0:T(8,128)S(1)}, u32[]{:S(2)}, u32[]{:S(2)}) collective-permute-start(f32[64,64]{1,0:T(8,128)} %refs_0_.1), channel_id=1, source_target_pairs={{0,1},{1,0},{2,3},{3,2},{4,5},{5,4},{6,7},{7,6},{8,9},{9,8},{10,11... | collective-permute-start | bytes 49160 | tf_op jit(solution)/shard_map/ppermute | solution.py:177
  6.3 3.7 %copy-start.2 = (f32[64,64]{1,0:T(8,128)S(1)}, f32[64,64]{1,0:T(8,128)}, u32[]{:S(2)}) copy-start(f32[64,64]{1,0:T(8,128)} %refs_0_.1) | copy-start | bytes 49156
  6.3 3.7 %copy-start.3 = (s32[1,3,1]{1,2,0:T(1,128)S(1)}, s32[1,3,1]{1,2,0:T(1,128)}, u32[]{:S(2)}) copy-start(s32[1,3,1]{1,2,0:T(1,128)} %param.8) | copy-start | bytes 40
  8.3 8.4 %copy-start = (f32[1,3,64,1024]{3,2,1,0:T(8,128)S(1)}, f32[1,3,64,1024]{3,2,1,0:T(8,128)}, u32[]{:S(2)}) copy-start(f32[1,3,64,1024]{3,2,1,0:T(8,128)} %metric.3) | copy-start | bytes 2359300
  8.3 8.4 %copy-start.1 = (s32[1,3,1]{1,2,0:T(1,128)S(1)}, s32[1,3,1]{1,2,0:T(1,128)}, u32[]{:S(2)}) copy-start(s32[1,3,1]{1,2,0:T(1,128)} %param.12) | copy-start | bytes 40
  12.4 11.3 %collective-permute-start.3 = (bf16[64,1024]{1,0:T(8,128)(2,1)S(1)}, bf16[64,1024]{1,0:T(8,128)(2,1)S(1)}, u32[]{:S(2)}, u32[]{:S(2)}) collective-permute-start(bf16[64,1024]{1,0:T(8,128)(2,1)S(1)} %get-tuple-element.12), channel_id=1, source_target_pairs={{0,2},{1,3},{2,0},{3,1},{4,6},{5,7},{6,4},{7,5},{8,10},{9,11},{10,... | collective-permute-start | bytes 393224 | tf_op jit(solution)/shard_map/ppermute | solution.py:220
  13.7 10.0 %collective-permute-start.4 = (bf16[64,1024]{1,0:T(8,128)(2,1)S(1)}, bf16[64,1024]{1,0:T(8,128)(2,1)S(1)}, u32[]{:S(2)}, u32[]{:S(2)}) collective-permute-start(bf16[64,1024]{1,0:T(8,128)(2,1)S(1)} %get-tuple-element.13), channel_id=1, source_target_pairs={{0,3},{1,2},{2,1},{3,0},{4,7},{5,6},{6,5},{7,4},{8,11},{9,10},{10,... | collective-permute-start | bytes 393224 | tf_op jit(solution)/shard_map/ppermute | solution.py:220
  15.0 9.1 %collective-permute-start.5 = (bf16[64,1024]{1,0:T(8,128)(2,1)S(1)}, bf16[64,1024]{1,0:T(8,128)(2,1)S(1)}, u32[]{:S(2)}, u32[]{:S(2)}) collective-permute-start(bf16[64,1024]{1,0:T(8,128)(2,1)S(1)} %get-tuple-element.14), channel_id=1, source_target_pairs={{0,1},{1,0},{2,3},{3,2},{4,5},{5,4},{6,7},{7,6},{8,9},{9,8},{10,11... | collective-permute-start | bytes 393224 | tf_op jit(solution)/shard_map/ppermute | solution.py:220

commit v17 on v13

--- a/solution.py
+++ b/solution.py
@@ -153,9 +153,9 @@
             columns = slice(pair * 128, (pair + 1) * 128)
             top = total[a * 2 * rows:(a * 2 + 1) * rows, columns]
             bottom = total[(a * 2 + 1) * rows:(a * 2 + 2) * rows, columns]
-            at = n_aux * n_mu - 1 - (a * n_mu + pair * 2)
+            at = a * n_mu + pair * 2
             out[at] = jnp.where(lower, top, pltpu.roll(bottom, 64, 1)).astype(BF16)
-            out[at - 1] = jnp.where(lower, pltpu.roll(top, 64, 1), bottom).astype(BF16)
+            out[at + 1] = jnp.where(lower, pltpu.roll(top, 64, 1), bottom).astype(BF16)
 
 
 def sum_kernel(parts, out):
@@ -228,8 +228,7 @@
         cost_estimate=pl.CostEstimate(flops=300_000_000, bytes_accessed=2_000_000, transcendentals=0),
         name="exchange",
     )(*halves, m_hi, m_lo)
-    down = list(reversed(range(n_aux * n_mu)))
-    parts = lax.all_to_all(parts, ("aux", "mu"), 0, 0, axis_index_groups=[down])
+    parts = lax.all_to_all(parts, ("aux", "mu"), 0, 0)
     return pl.pallas_call(
         sum_kernel,
         out_shape=jax.ShapeDtypeStruct((rows, orb), F32),

time: 38.5 us -> 39.1 us (1.016)
  blocking collectives: 12.9 us -> 13.5 us
    all_to_all x1, blocking collectives: 12.9 us -> 13.5 us  [fast(): parts = lax.all_to_all(parts, ('aux', 'mu'), 0, 0)]
where the time goes in v17:
time: 39.1 us; the launch traced here: 38.9 us
  blocking collectives  13.5 us (35%)
  starting transfers between devices  9.17 us (23%)
  waiting for transfers between devices  8.17 us (21%)
  Pallas kernels  6.66 us (17%)
  between operations  1.4 us (4%)
    all_to_all x1, blocking collectives, fast(): parts = lax.all_to_all(parts, ('aux', 'mu'), 0, 0)  13.5 us
    ppermute x3, waiting for transfers between devices, fast(): lax.ppermute(halves[s], 'mu', turns[HALF_ORDER[s]])  6.52 us
    ppermute x3, starting transfers between devices, fast(): lax.ppermute(density, 'mu', turns[s])  5.62 us
    ppermute x3, starting transfers between devices, fast(): lax.ppermute(halves[s], 'mu', turns[HALF_ORDER[s]])  3.55 us
    pallas_call x1, Pallas kernels, fast(): pl.pallas_call(functools.partial(half_kernel, n_mu), out_shape=(half_shap...  2.43 us
    pallas_call x1, Pallas kernels, fast(): pl.pallas_call(tensor_kernel, out_shape=t_shape, in_specs=[HBM], out_spec...  1.98 us
    ppermute x3, waiting for transfers between devices, fast(): lax.ppermute(density, 'mu', turns[s])  1.65 us
    pallas_call x1, Pallas kernels, fast(): pl.pallas_call(metric_kernel, out_shape=(m_shape, m_shape), in_specs=[SME...  1 us
  transfers between devices with their start and end apart: 6, of which 3 were waited for; matrix products, arithmetic and copies ran while one was open for 0% of the time, Pallas kernels for 8%

profile of v17, /device:TPU:0, one launch (start us, length us, event | category | flops | bytes accessed | tf_op | source)
XLA Modules:
  0.0 38.9 jit_solution(1310213066038982575)
XLA Ops:
  0.0 4.0 %collective-permute-start = (f32[64,64]{1,0:T(8,128)}, f32[64,64]{1,0:T(8,128)S(1)}, u32[]{:S(2)}, u32[]{:S(2)}) collective-permute-start(f32[64,64]{1,0:T(8,128)} %refs_0_.1), channel_id=1, source_target_pairs={{0,2},{1,3},{2,0},{3,1},{4,6},{5,7},{6,4},{7,5},{8,10},{9,11},{10,... | collective-permute-start | bytes 49160 | tf_op jit(solution)/shard_map/ppermute | solution.py:175
  4.0 1.3 %collective-permute-start.1 = (f32[64,64]{1,0:T(8,128)}, f32[64,64]{1,0:T(8,128)S(1)}, u32[]{:S(2)}, u32[]{:S(2)}) collective-permute-start(f32[64,64]{1,0:T(8,128)} %refs_0_.1), channel_id=1, source_target_pairs={{0,3},{1,2},{2,1},{3,0},{4,7},{5,6},{6,5},{7,4},{8,11},{9,10},{10,... | collective-permute-start | bytes 49160 | tf_op jit(solution)/shard_map/ppermute | solution.py:175
  5.4 0.2 collective-permute-start.2
  6.3 0.0 copy-start.2
  6.3 0.0 copy-start.3
  6.3 2.0 %tensor.2.refs_4_ = bf16[2048,768]{1,0:T(8,128)(2,1)S(1)} custom-call(f32[1,3,64,4096]{3,2,1,0:T(8,128)} %tensor.3), custom_call_target="tpu_custom_call" | custom-call | flops 10000000 | bytes 6000000 | tf_op jit(solution)/shard_map/tensor/pallas_call | solution.py:180
  8.3 0.0 copy-start
  8.3 0.0 copy-start.1
  8.3 0.0 collective-permute-done.refs_1_
  8.3 1.6 %collective-permute-done.1.refs_2_ = f32[64,64]{1,0:T(8,128)S(1)} collective-permute-done((f32[64,64]{1,0:T(8,128)}, f32[64,64]{1,0:T(8,128)S(1)}, u32[]{:S(2)}, u32[]{:S(2)}) %collective-permute-start.1) | collective-permute-done | bytes 16416 | tf_op jit(solution)/shard_map/ppermute | solution.py:175
  10.0 0.0 collective-permute-done.2.refs_3_
  10.0 0.0 copy-done.2
  10.0 0.0 copy-done.3
  10.0 2.4 %half.1 = (bf16[64,1024]{1,0:T(8,128)(2,1)S(1)}, bf16[64,1024]{1,0:T(8,128)(2,1)S(1)}, bf16[64,1024]{1,0:T(8,128)(2,1)S(1)}, bf16[64,1024]{1,0:T(8,128)(2,1)S(1)}) custom-call(s32[1,1,3]{2,1,0:T(1,128)S(1)} %bitcast.3, s32[1,1]{1,0:T(1,128)S(6)} %copy.8.nu_count, f32[64,64]{1,0:T(8,128)S(1)} %copy-done.2, f32[64,64]{1,0:T(8,128)S(1)} %collective-permute-done.refs_1_, ...), custom_call_target="tpu_custom_call" | custom-call | flops 1200000000 | bytes 4000000 | tf_op jit(solution)/shard_map/half/pallas_call | solution.py:194
  12.4 1.3 %collective-permute-start.3 = (bf16[64,1024]{1,0:T(8,128)(2,1)S(1)}, bf16[64,1024]{1,0:T(8,128)(2,1)S(1)}, u32[]{:S(2)}, u32[]{:S(2)}) collective-permute-start(bf16[64,1024]{1,0:T(8,128)(2,1)S(1)} %get-tuple-element.12), channel_id=1, source_target_pairs={{0,2},{1,3},{2,0},{3,1},{4,6},{5,7},{6,4},{7,5},{8,10},{9,11},{10,... | collective-permute-start | bytes 393224 | tf_op jit(solution)/shard_map/ppermute | solution.py:218
  13.7 1.3 %collective-permute-start.4 = (bf16[64,1024]{1,0:T(8,128)(2,1)S(1)}, bf16[64,1024]{1,0:T(8,128)(2,1)S(1)}, u32[]{:S(2)}, u32[]{:S(2)}) collective-permute-start(bf16[64,1024]{1,0:T(8,128)(2,1)S(1)} %get-tuple-element.13), channel_id=1, source_target_pairs={{0,3},{1,2},{2,1},{3,0},{4,7},{5,6},{6,5},{7,4},{8,11},{9,10},{10,... | collective-permute-start | bytes 393224 | tf_op jit(solution)/shard_map/ppermute | solution.py:218
  15.0 0.9 %collective-permute-start.5 = (bf16[64,1024]{1,0:T(8,128)(2,1)S(1)}, bf16[64,1024]{1,0:T(8,128)(2,1)S(1)}, u32[]{:S(2)}, u32[]{:S(2)}) collective-permute-start(bf16[64,1024]{1,0:T(8,128)(2,1)S(1)} %get-tuple-element.14), channel_id=1, source_target_pairs={{0,1},{1,0},{2,3},{3,2},{4,5},{5,4},{6,7},{7,6},{8,9},{9,8},{10,11... | collective-permute-start | bytes 393224 | tf_op jit(solution)/shard_map/ppermute | solution.py:218
  16.6 0.0 copy-done
  16.6 0.0 copy-done.1
  16.6 1.0 %metric.2 = (bf16[1024,256]{1,0:T(8,128)(2,1)S(1)}, bf16[1024,256]{1,0:T(8,128)(2,1)S(1)}) custom-call(s32[1,1,3]{2,1,0:T(1,128)S(1)} %bitcast.2, s32[1,1]{1,0:T(1,128)S(6)} %copy.9.sig_count, bf16[64,1024]{1,0:T(8,128)(2,1)S(1)} %get-tuple-element.11.after.refs_0_, f32[1,3,64,1024]{3,2,1,0:T(8,128)S(1)} %copy-done), custom_call_target="tpu_custom_call" | custom-call | flops 10000000 | bytes 2000000 | tf_op jit(solution)/shard_map/metric/pallas_call | solution.py:208
  17.6 6.1 %collective-permute-done.3.refs_1_ = bf16[64,1024]{1,0:T(8,128)(2,1)S(1)} collective-permute-done((bf16[64,1024]{1,0:T(8,128)(2,1)S(1)}, bf16[64,1024]{1,0:T(8,128)(2,1)S(1)}, u32[]{:S(2)}, u32[]{:S(2)}) %collective-permute-start.3) | collective-permute-done | bytes 131104 | tf_op jit(solution)/shard_map/ppermute | solution.py:218
  23.7 0.0 collective-permute-done.4.refs_2_
  23.7 0.4 %collective-permute-done.5.refs_3_ = bf16[64,1024]{1,0:T(8,128)(2,1)S(1)} collective-permute-done((bf16[64,1024]{1,0:T(8,128)(2,1)S(1)}, bf16[64,1024]{1,0:T(8,128)(2,1)S(1)}, u32[]{:S(2)}, u32[]{:S(2)}) %collective-permute-start.5) | collective-permute-done | bytes 131104 | tf_op jit(solution)/shard_map/ppermute | solution.py:218
  24.2 0.5 %exchange.1 = bf16[32,16,128]{2,1,0:T(8,128)(2,1)S(1)} custom-call(bf16[64,1024]{1,0:T(8,128)(2,1)S(1)} %get-tuple-element.11.after.refs_0_, bf16[64,1024]{1,0:T(8,128)(2,1)S(1)} %collective-permute-done.3.refs_1_, bf16[64,1024]{1,0:T(8,128)(2,1)S(1)} %collective-permute-done.4.refs_2_, bf16[64,1024]{1,0:T(8,128)(2,1)S(1)} %collective-permute-done.5.refs_3_, ...), custom_call_target="tpu_custom_call" | custom-call | flops 300000000 | bytes 2000000 | tf_op jit(solution)/shard_map/exchange/pallas_call | solution.py:221
  24.7 13.5 %all_to_all.5.parts = bf16[32,16,128]{2,1,0:T(8,128)(2,1)S(1)} all-to-all(bf16[32,16,128]{2,1,0:T(8,128)(2,1)S(1)} %exchange.1), channel_id=1, replica_groups=mesh['aux'=8,'mu'=4] {'aux','mu'}, dimensions={0} | all-to-all | bytes 262144 | tf_op jit(solution)/shard_map/all_to_all | solution.py:231
  38.2 0.7 %sum.1 = f32[32,64]{1,0:T(8,128)} custom-call(bf16[32,16,128]{2,1,0:T(8,128)(2,1)S(1)} %all_to_all.5.parts), custom_call_target="tpu_custom_call" | custom-call | tf_op jit(solution)/shard_map/sum/pallas_call | solution.py:232
Async XLA Ops:
  0.0 8.3 %collective-permute-start = (f32[64,64]{1,0:T(8,128)}, f32[64,64]{1,0:T(8,128)S(1)}, u32[]{:S(2)}, u32[]{:S(2)}) collective-permute-start(f32[64,64]{1,0:T(8,128)} %refs_0_.1), channel_id=1, source_target_pairs={{0,2},{1,3},{2,0},{3,1},{4,6},{5,7},{6,4},{7,5},{8,10},{9,11},{10,... | collective-permute-start | bytes 49160 | tf_op jit(solution)/shard_map/ppermute | solution.py:175
  4.0 5.9 %collective-permute-start.1 = (f32[64,64]{1,0:T(8,128)}, f32[64,64]{1,0:T(8,128)S(1)}, u32[]{:S(2)}, u32[]{:S(2)}) collective-permute-start(f32[64,64]{1,0:T(8,128)} %refs_0_.1), channel_id=1, source_target_pairs={{0,3},{1,2},{2,1},{3,0},{4,7},{5,6},{6,5},{7,4},{8,11},{9,10},{10,... | collective-permute-start | bytes 49160 | tf_op jit(solution)/shard_map/ppermute | solution.py:175
  5.4 4.6 %collective-permute-start.2 = (f32[64,64]{1,0:T(8,128)}, f32[64,64]{1,0:T(8,128)S(1)}, u32[]{:S(2)}, u32[]{:S(2)}) collective-permute-start(f32[64,64]{1,0:T(8,128)} %refs_0_.1), channel_id=1, source_target_pairs={{0,1},{1,0},{2,3},{3,2},{4,5},{5,4},{6,7},{7,6},{8,9},{9,8},{10,11... | collective-permute-start | bytes 49160 | tf_op jit(solution)/shard_map/ppermute | solution.py:175
  6.3 3.7 %copy-start.2 = (f32[64,64]{1,0:T(8,128)S(1)}, f32[64,64]{1,0:T(8,128)}, u32[]{:S(2)}) copy-start(f32[64,64]{1,0:T(8,128)} %refs_0_.1) | copy-start | bytes 49156
  6.3 3.7 %copy-start.3 = (s32[1,3,1]{1,2,0:T(1,128)S(1)}, s32[1,3,1]{1,2,0:T(1,128)}, u32[]{:S(2)}) copy-start(s32[1,3,1]{1,2,0:T(1,128)} %param.8) | copy-start | bytes 40
  8.3 8.3 %copy-start = (f32[1,3,64,1024]{3,2,1,0:T(8,128)S(1)}, f32[1,3,64,1024]{3,2,1,0:T(8,128)}, u32[]{:S(2)}) copy-start(f32[1,3,64,1024]{3,2,1,0:T(8,128)} %metric.3) | copy-start | bytes 2359300
  8.3 8.3 %copy-start.1 = (s32[1,3,1]{1,2,0:T(1,128)S(1)}, s32[1,3,1]{1,2,0:T(1,128)}, u32[]{:S(2)}) copy-start(s32[1,3,1]{1,2,0:T(1,128)} %param.12) | copy-start | bytes 40
  12.4 11.3 %collective-permute-start.3 = (bf16[64,1024]{1,0:T(8,128)(2,1)S(1)}, bf16[64,1024]{1,0:T(8,128)(2,1)S(1)}, u32[]{:S(2)}, u32[]{:S(2)}) collective-permute-start(bf16[64,1024]{1,0:T(8,128)(2,1)S(1)} %get-tuple-element.12), channel_id=1, source_target_pairs={{0,2},{1,3},{2,0},{3,1},{4,6},{5,7},{6,4},{7,5},{8,10},{9,11},{10,... | collective-permute-start | bytes 393224 | tf_op jit(solution)/shard_map/ppermute | solution.py:218
  13.7 10.0 %collective-permute-start.4 = (bf16[64,1024]{1,0:T(8,128)(2,1)S(1)}, bf16[64,1024]{1,0:T(8,128)(2,1)S(1)}, u32[]{:S(2)}, u32[]{:S(2)}) collective-permute-start(bf16[64,1024]{1,0:T(8,128)(2,1)S(1)} %get-tuple-element.13), channel_id=1, source_target_pairs={{0,3},{1,2},{2,1},{3,0},{4,7},{5,6},{6,5},{7,4},{8,11},{9,10},{10,... | collective-permute-start | bytes 393224 | tf_op jit(solution)/shard_map/ppermute | solution.py:218
  15.0 9.1 %collective-permute-start.5 = (bf16[64,1024]{1,0:T(8,128)(2,1)S(1)}, bf16[64,1024]{1,0:T(8,128)(2,1)S(1)}, u32[]{:S(2)}, u32[]{:S(2)}) collective-permute-start(bf16[64,1024]{1,0:T(8,128)(2,1)S(1)} %get-tuple-element.14), channel_id=1, source_target_pairs={{0,1},{1,0},{2,3},{3,2},{4,5},{5,4},{6,7},{7,6},{8,9},{9,8},{10,11... | collective-permute-start | bytes 393224 | tf_op jit(solution)/shard_map/ppermute | solution.py:218

commit v18 on v13

--- a/solution.py
+++ b/solution.py
@@ -153,7 +153,7 @@
             columns = slice(pair * 128, (pair + 1) * 128)
             top = total[a * 2 * rows:(a * 2 + 1) * rows, columns]
             bottom = total[(a * 2 + 1) * rows:(a * 2 + 2) * rows, columns]
-            at = n_aux * n_mu - 1 - (a * n_mu + pair * 2)
+            at = a * n_mu + n_mu - 1 - pair * 2
             out[at] = jnp.where(lower, top, pltpu.roll(bottom, 64, 1)).astype(BF16)
             out[at - 1] = jnp.where(lower, pltpu.roll(top, 64, 1), bottom).astype(BF16)
 
@@ -228,7 +228,7 @@
         cost_estimate=pl.CostEstimate(flops=300_000_000, bytes_accessed=2_000_000, transcendentals=0),
         name="exchange",
     )(*halves, m_hi, m_lo)
-    down = list(reversed(range(n_aux * n_mu)))
+    down = [a * n_mu + z for a in range(n_aux) for z in reversed(range(n_mu))]
     parts = lax.all_to_all(parts, ("aux", "mu"), 0, 0, axis_index_groups=[down])
     return pl.pallas_call(
         sum_kernel,

time: 38.5 us -> 38.3 us (level); the launches traced: 38.4 us -> 37.8 us
  blocking collectives: 12.9 us -> 12.3 us
    all_to_all x1, blocking collectives: 12.9 us -> 12.3 us  [fast(): parts = lax.all_to_all(parts, ('aux', 'mu'), 0, 0, axis_index_groups=[down])]
where the time goes in v18:
time: 38.3 us; the launch traced here: 37.8 us
  blocking collectives  12.3 us (32%)
  starting transfers between devices  9.17 us (24%)
  waiting for transfers between devices  8.17 us (21%)
  Pallas kernels  6.66 us (17%)
  between operations  1.4 us (4%)
    all_to_all x1, blocking collectives, fast(): parts = lax.all_to_all(parts, ('aux', 'mu'), 0, 0, axis_index_groups=[down])  12.3 us
    ppermute x3, waiting for transfers between devices, fast(): lax.ppermute(halves[s], 'mu', turns[HALF_ORDER[s]])  6.52 us
    ppermute x3, starting transfers between devices, fast(): lax.ppermute(density, 'mu', turns[s])  5.62 us
    ppermute x3, starting transfers between devices, fast(): lax.ppermute(halves[s], 'mu', turns[HALF_ORDER[s]])  3.55 us
    pallas_call x1, Pallas kernels, fast(): pl.pallas_call(functools.partial(half_kernel, n_mu), out_shape=(half_shap...  2.43 us
    pallas_call x1, Pallas kernels, fast(): pl.pallas_call(tensor_kernel, out_shape=t_shape, in_specs=[HBM], out_spec...  1.98 us
    ppermute x3, waiting for transfers between devices, fast(): lax.ppermute(density, 'mu', turns[s])  1.65 us
    pallas_call x1, Pallas kernels, fast(): pl.pallas_call(metric_kernel, out_shape=(m_shape, m_shape), in_specs=[SME...  1 us
  transfers between devices with their start and end apart: 6, of which 3 were waited for; matrix products, arithmetic and copies ran while one was open for 0% of the time, Pallas kernels for 8%

profile of v18, /device:TPU:0, one launch (start us, length us, event | category | flops | bytes accessed | tf_op | source)
XLA Modules:
  0.0 37.8 jit_solution(16990831782183522110)
XLA Ops:
  0.0 4.0 %collective-permute-start = (f32[64,64]{1,0:T(8,128)}, f32[64,64]{1,0:T(8,128)S(1)}, u32[]{:S(2)}, u32[]{:S(2)}) collective-permute-start(f32[64,64]{1,0:T(8,128)} %refs_0_.1), channel_id=1, source_target_pairs={{0,2},{1,3},{2,0},{3,1},{4,6},{5,7},{6,4},{7,5},{8,10},{9,11},{10,... | collective-permute-start | bytes 49160 | tf_op jit(solution)/shard_map/ppermute | solution.py:175
  4.0 1.3 %collective-permute-start.1 = (f32[64,64]{1,0:T(8,128)}, f32[64,64]{1,0:T(8,128)S(1)}, u32[]{:S(2)}, u32[]{:S(2)}) collective-permute-start(f32[64,64]{1,0:T(8,128)} %refs_0_.1), channel_id=1, source_target_pairs={{0,3},{1,2},{2,1},{3,0},{4,7},{5,6},{6,5},{7,4},{8,11},{9,10},{10,... | collective-permute-start | bytes 49160 | tf_op jit(solution)/shard_map/ppermute | solution.py:175
  5.4 0.2 collective-permute-start.2
  6.3 0.0 copy-start.2
  6.3 0.0 copy-start.3
  6.3 2.0 %tensor.2.refs_4_ = bf16[2048,768]{1,0:T(8,128)(2,1)S(1)} custom-call(f32[1,3,64,4096]{3,2,1,0:T(8,128)} %tensor.3), custom_call_target="tpu_custom_call" | custom-call | flops 10000000 | bytes 6000000 | tf_op jit(solution)/shard_map/tensor/pallas_call | solution.py:180
  8.3 0.0 copy-start
  8.3 0.0 copy-start.1
  8.3 0.0 collective-permute-done.refs_1_
  8.3 1.6 %collective-permute-done.1.refs_2_ = f32[64,64]{1,0:T(8,128)S(1)} collective-permute-done((f32[64,64]{1,0:T(8,128)}, f32[64,64]{1,0:T(8,128)S(1)}, u32[]{:S(2)}, u32[]{:S(2)}) %collective-permute-start.1) | collective-permute-done | bytes 16416 | tf_op jit(solution)/shard_map/ppermute | solution.py:175
  10.0 0.0 collective-permute-done.2.refs_3_
  10.0 0.0 copy-done.2
  10.0 0.0 copy-done.3
  10.0 2.4 %half.1 = (bf16[64,1024]{1,0:T(8,128)(2,1)S(1)}, bf16[64,1024]{1,0:T(8,128)(2,1)S(1)}, bf16[64,1024]{1,0:T(8,128)(2,1)S(1)}, bf16[64,1024]{1,0:T(8,128)(2,1)S(1)}) custom-call(s32[1,1,3]{2,1,0:T(1,128)S(1)} %bitcast.3, s32[1,1]{1,0:T(1,128)S(6)} %copy.8.nu_count, f32[64,64]{1,0:T(8,128)S(1)} %copy-done.2, f32[64,64]{1,0:T(8,128)S(1)} %collective-permute-done.refs_1_, ...), custom_call_target="tpu_custom_call" | custom-call | flops 1200000000 | bytes 4000000 | tf_op jit(solution)/shard_map/half/pallas_call | solution.py:194
  12.4 1.3 %collective-permute-start.3 = (bf16[64,1024]{1,0:T(8,128)(2,1)S(1)}, bf16[64,1024]{1,0:T(8,128)(2,1)S(1)}, u32[]{:S(2)}, u32[]{:S(2)}) collective-permute-start(bf16[64,1024]{1,0:T(8,128)(2,1)S(1)} %get-tuple-element.12), channel_id=1, source_target_pairs={{0,2},{1,3},{2,0},{3,1},{4,6},{5,7},{6,4},{7,5},{8,10},{9,11},{10,... | collective-permute-start | bytes 393224 | tf_op jit(solution)/shard_map/ppermute | solution.py:218
  13.7 1.3 %collective-permute-start.4 = (bf16[64,1024]{1,0:T(8,128)(2,1)S(1)}, bf16[64,1024]{1,0:T(8,128)(2,1)S(1)}, u32[]{:S(2)}, u32[]{:S(2)}) collective-permute-start(bf16[64,1024]{1,0:T(8,128)(2,1)S(1)} %get-tuple-element.13), channel_id=1, source_target_pairs={{0,3},{1,2},{2,1},{3,0},{4,7},{5,6},{6,5},{7,4},{8,11},{9,10},{10,... | collective-permute-start | bytes 393224 | tf_op jit(solution)/shard_map/ppermute | solution.py:218
  15.0 0.9 %collective-permute-start.5 = (bf16[64,1024]{1,0:T(8,128)(2,1)S(1)}, bf16[64,1024]{1,0:T(8,128)(2,1)S(1)}, u32[]{:S(2)}, u32[]{:S(2)}) collective-permute-start(bf16[64,1024]{1,0:T(8,128)(2,1)S(1)} %get-tuple-element.14), channel_id=1, source_target_pairs={{0,1},{1,0},{2,3},{3,2},{4,5},{5,4},{6,7},{7,6},{8,9},{9,8},{10,11... | collective-permute-start | bytes 393224 | tf_op jit(solution)/shard_map/ppermute | solution.py:218
  16.6 0.0 copy-done
  16.6 0.0 copy-done.1
  16.6 1.0 %metric.2 = (bf16[1024,256]{1,0:T(8,128)(2,1)S(1)}, bf16[1024,256]{1,0:T(8,128)(2,1)S(1)}) custom-call(s32[1,1,3]{2,1,0:T(1,128)S(1)} %bitcast.2, s32[1,1]{1,0:T(1,128)S(6)} %copy.9.sig_count, bf16[64,1024]{1,0:T(8,128)(2,1)S(1)} %get-tuple-element.11.after.refs_0_, f32[1,3,64,1024]{3,2,1,0:T(8,128)S(1)} %copy-done), custom_call_target="tpu_custom_call" | custom-call | flops 10000000 | bytes 2000000 | tf_op jit(solution)/shard_map/metric/pallas_call | solution.py:208
  17.6 6.1 %collective-permute-done.3.refs_1_ = bf16[64,1024]{1,0:T(8,128)(2,1)S(1)} collective-permute-done((bf16[64,1024]{1,0:T(8,128)(2,1)S(1)}, bf16[64,1024]{1,0:T(8,128)(2,1)S(1)}, u32[]{:S(2)}, u32[]{:S(2)}) %collective-permute-start.3) | collective-permute-done | bytes 131104 | tf_op jit(solution)/shard_map/ppermute | solution.py:218
  23.7 0.0 collective-permute-done.4.refs_2_
  23.7 0.4 %collective-permute-done.5.refs_3_ = bf16[64,1024]{1,0:T(8,128)(2,1)S(1)} collective-permute-done((bf16[64,1024]{1,0:T(8,128)(2,1)S(1)}, bf16[64,1024]{1,0:T(8,128)(2,1)S(1)}, u32[]{:S(2)}, u32[]{:S(2)}) %collective-permute-start.5) | collective-permute-done | bytes 131104 | tf_op jit(solution)/shard_map/ppermute | solution.py:218
  24.2 0.5 %exchange.1 = bf16[32,16,128]{2,1,0:T(8,128)(2,1)S(1)} custom-call(bf16[64,1024]{1,0:T(8,128)(2,1)S(1)} %get-tuple-element.11.after.refs_0_, bf16[64,1024]{1,0:T(8,128)(2,1)S(1)} %collective-permute-done.3.refs_1_, bf16[64,1024]{1,0:T(8,128)(2,1)S(1)} %collective-permute-done.4.refs_2_, bf16[64,1024]{1,0:T(8,128)(2,1)S(1)} %collective-permute-done.5.refs_3_, ...), custom_call_target="tpu_custom_call" | custom-call | flops 300000000 | bytes 2000000 | tf_op jit(solution)/shard_map/exchange/pallas_call | solution.py:221
  24.7 12.3 %all_to_all.5.parts = bf16[32,16,128]{2,1,0:T(8,128)(2,1)S(1)} all-to-all(bf16[32,16,128]{2,1,0:T(8,128)(2,1)S(1)} %exchange.1), channel_id=1, replica_groups={{3,2,1,0,7,6,5,4,11,10,9,8,15,14,13,12,19,18,17,16,23,22,21,20,27,26,25..., dimensions={0} | all-to-all | bytes 262144 | tf_op jit(solution)/shard_map/all_to_all | solution.py:232
  37.0 0.7 %sum.1 = f32[32,64]{1,0:T(8,128)} custom-call(bf16[32,16,128]{2,1,0:T(8,128)(2,1)S(1)} %all_to_all.5.parts), custom_call_target="tpu_custom_call" | custom-call | tf_op jit(solution)/shard_map/sum/pallas_call | solution.py:233
Async XLA Ops:
  0.0 8.3 %collective-permute-start = (f32[64,64]{1,0:T(8,128)}, f32[64,64]{1,0:T(8,128)S(1)}, u32[]{:S(2)}, u32[]{:S(2)}) collective-permute-start(f32[64,64]{1,0:T(8,128)} %refs_0_.1), channel_id=1, source_target_pairs={{0,2},{1,3},{2,0},{3,1},{4,6},{5,7},{6,4},{7,5},{8,10},{9,11},{10,... | collective-permute-start | bytes 49160 | tf_op jit(solution)/shard_map/ppermute | solution.py:175
  4.0 5.9 %collective-permute-start.1 = (f32[64,64]{1,0:T(8,128)}, f32[64,64]{1,0:T(8,128)S(1)}, u32[]{:S(2)}, u32[]{:S(2)}) collective-permute-start(f32[64,64]{1,0:T(8,128)} %refs_0_.1), channel_id=1, source_target_pairs={{0,3},{1,2},{2,1},{3,0},{4,7},{5,6},{6,5},{7,4},{8,11},{9,10},{10,... | collective-permute-start | bytes 49160 | tf_op jit(solution)/shard_map/ppermute | solution.py:175
  5.4 4.6 %collective-permute-start.2 = (f32[64,64]{1,0:T(8,128)}, f32[64,64]{1,0:T(8,128)S(1)}, u32[]{:S(2)}, u32[]{:S(2)}) collective-permute-start(f32[64,64]{1,0:T(8,128)} %refs_0_.1), channel_id=1, source_target_pairs={{0,1},{1,0},{2,3},{3,2},{4,5},{5,4},{6,7},{7,6},{8,9},{9,8},{10,11... | collective-permute-start | bytes 49160 | tf_op jit(solution)/shard_map/ppermute | solution.py:175
  6.3 3.7 %copy-start.2 = (f32[64,64]{1,0:T(8,128)S(1)}, f32[64,64]{1,0:T(8,128)}, u32[]{:S(2)}) copy-start(f32[64,64]{1,0:T(8,128)} %refs_0_.1) | copy-start | bytes 49156
  6.3 3.7 %copy-start.3 = (s32[1,3,1]{1,2,0:T(1,128)S(1)}, s32[1,3,1]{1,2,0:T(1,128)}, u32[]{:S(2)}) copy-start(s32[1,3,1]{1,2,0:T(1,128)} %param.8) | copy-start | bytes 40
  8.3 8.3 %copy-start = (f32[1,3,64,1024]{3,2,1,0:T(8,128)S(1)}, f32[1,3,64,1024]{3,2,1,0:T(8,128)}, u32[]{:S(2)}) copy-start(f32[1,3,64,1024]{3,2,1,0:T(8,128)} %metric.3) | copy-start | bytes 2359300
  8.3 8.3 %copy-start.1 = (s32[1,3,1]{1,2,0:T(1,128)S(1)}, s32[1,3,1]{1,2,0:T(1,128)}, u32[]{:S(2)}) copy-start(s32[1,3,1]{1,2,0:T(1,128)} %param.12) | copy-start | bytes 40
  12.4 11.3 %collective-permute-start.3 = (bf16[64,1024]{1,0:T(8,128)(2,1)S(1)}, bf16[64,1024]{1,0:T(8,128)(2,1)S(1)}, u32[]{:S(2)}, u32[]{:S(2)}) collective-permute-start(bf16[64,1024]{1,0:T(8,128)(2,1)S(1)} %get-tuple-element.12), channel_id=1, source_target_pairs={{0,2},{1,3},{2,0},{3,1},{4,6},{5,7},{6,4},{7,5},{8,10},{9,11},{10,... | collective-permute-start | bytes 393224 | tf_op jit(solution)/shard_map/ppermute | solution.py:218
  13.7 10.0 %collective-permute-start.4 = (bf16[64,1024]{1,0:T(8,128)(2,1)S(1)}, bf16[64,1024]{1,0:T(8,128)(2,1)S(1)}, u32[]{:S(2)}, u32[]{:S(2)}) collective-permute-start(bf16[64,1024]{1,0:T(8,128)(2,1)S(1)} %get-tuple-element.13), channel_id=1, source_target_pairs={{0,3},{1,2},{2,1},{3,0},{4,7},{5,6},{6,5},{7,4},{8,11},{9,10},{10,... | collective-permute-start | bytes 393224 | tf_op jit(solution)/shard_map/ppermute | solution.py:218
  15.0 9.1 %collective-permute-start.5 = (bf16[64,1024]{1,0:T(8,128)(2,1)S(1)}, bf16[64,1024]{1,0:T(8,128)(2,1)S(1)}, u32[]{:S(2)}, u32[]{:S(2)}) collective-permute-start(bf16[64,1024]{1,0:T(8,128)(2,1)S(1)} %get-tuple-element.14), channel_id=1, source_target_pairs={{0,1},{1,0},{2,3},{3,2},{4,5},{5,4},{6,7},{7,6},{8,9},{9,8},{10,11... | collective-permute-start | bytes 393224 | tf_op jit(solution)/shard_map/ppermute | solution.py:218
